TPU v7x, 256 devices: a whole 4x4x8 slice. The times are simulated.
256 devices in a mesh: dp: 16 (over y, z_lo, core), space: 4 (over x), tensor: 4 (over z_hi).
Axes of the slice: x: 4, y: 4, z: 8 (z_hi: 4, z_lo: 2; z = z_hi * 2 + z_lo), core: 2. Of those that a mesh axis runs over, the one named last changes fastest.
Arguments:
- tokens: bfloat16 [16, 1024, 4096], P('dp', 'space'), may hold values from -4 to 4
- weights: bfloat16 [4096, 3, 2048], P('dp', None, 'tensor'), may hold values from -0.0625 to 0.0625
- cotangent: bfloat16 [16, 1024, 2048], P('dp', 'space', 'tensor'), may hold values from -6 to 6
Outputs:
- attended: bfloat16 [16, 1024, 2048], P('dp', 'space', 'tensor')
- token_grad: bfloat16 [16, 1024, 4096], P('dp', 'space', 'tensor')
- weight_grad: float32 [4096, 3, 2048], P('dp', None, 'tensor')
All inputs are finite; a program needn't handle non-finite values.
Results may differ from a plain program's by a relative error of at most 0.039.
Values may be sent and summed in bfloat16 or wider, within the bound.
No kernel may reach another device: no remote copies, remote signals or barrier semaphores. Data moves between devices by JAX's collectives and lax.ppermute only.
A program may use at most 128 MiB of HBM per device.

v0:
```python
import math

import jax
import jax.numpy as jnp
from jax import lax
from jax.sharding import PartitionSpec as P

HS = 128


def per_device(tokens, weights, cotangent):
    frames, row_count, model_width = tokens.shape
    local_cols = weights.shape[2]
    heads_local = local_cols // HS
    score_scale = 1.0 / math.sqrt(HS)
    tok_rows = frames * row_count
    tokens_f = tokens.astype(jnp.float32)
    root_ms = jnp.sqrt(jnp.mean(tokens_f * tokens_f, -1, keepdims=True) + 1e-05)
    unit_rows = tokens_f / root_ms
    normed = unit_rows.astype(jnp.bfloat16).reshape(tok_rows, model_width)
    full_w = lax.all_gather(weights, "dp", axis=0, tiled=True)
    flat_w = full_w.reshape(model_width, 3 * local_cols)
    proj = jnp.dot(normed, flat_w, preferred_element_type=jnp.float32).astype(jnp.bfloat16)
    proj = proj.reshape(frames, row_count, 3, heads_local, HS)
    query = proj[:, :, 0]
    key_own = proj[:, :, 1]
    value_own = proj[:, :, 2]
    key_all, value_all = (
        lax.all_gather(key_own, "space", axis=1, tiled=True),
        lax.all_gather(value_own, "space", axis=1, tiled=True),
    )
    scores = (
        jnp.einsum("fqhc,fkhc->fhqk", query, key_all, preferred_element_type=jnp.float32)
        * score_scale
    )
    attn_prob = jax.nn.softmax(scores, axis=-1)
    prob_bf = attn_prob.astype(jnp.bfloat16)
    attended = jnp.einsum(
        "fhqk,fkhc->fqhc", prob_bf, value_all, preferred_element_type=jnp.float32
    ).astype(jnp.bfloat16)
    dout = cotangent.reshape(frames, row_count, heads_local, HS)
    dprob = jnp.einsum("fqhc,fkhc->fhqk", dout, value_all, preferred_element_type=jnp.float32)
    row_dot = jnp.sum(dout.astype(jnp.float32) * attended.astype(jnp.float32), -1)
    dscore = (attn_prob * (dprob - jnp.transpose(row_dot, (0, 2, 1))[..., None])).astype(
        jnp.bfloat16
    )
    dquery = (
        jnp.einsum("fhqk,fkhc->fqhc", dscore, key_all, preferred_element_type=jnp.float32)
        * score_scale
    ).astype(jnp.bfloat16)
    dkey_part = (
        jnp.einsum("fhqk,fqhc->fkhc", dscore, query, preferred_element_type=jnp.float32)
        * score_scale
    )
    dval_part = jnp.einsum("fhqk,fqhc->fkhc", prob_bf, dout, preferred_element_type=jnp.float32)
    dkey, dvalue = (
        lax.psum_scatter(
            dkey_part.astype(jnp.bfloat16), "space", scatter_dimension=1, tiled=True
        ).astype(jnp.float32),
        lax.psum_scatter(
            dval_part.astype(jnp.bfloat16), "space", scatter_dimension=1, tiled=True
        ).astype(jnp.float32),
    )
    grads = jnp.stack([dquery, dkey.astype(jnp.bfloat16), dvalue.astype(jnp.bfloat16)], axis=2)
    grads = grads.reshape(tok_rows, 3 * local_cols)
    norm_part = lax.dot_general(
        grads, flat_w, (((1,), (1,)), ((), ())), preferred_element_type=jnp.float32
    )
    norm_part = norm_part.reshape(frames, row_count, model_width)
    norm_grad = lax.psum(norm_part.astype(jnp.bfloat16), "tensor").astype(jnp.float32)
    row_stat = jnp.mean(norm_grad * unit_rows, -1, keepdims=True)
    full_grad = (norm_grad - unit_rows * row_stat) / root_ms
    share = model_width // lax.axis_size("tensor")
    token_grad = lax.dynamic_slice_in_dim(
        full_grad, lax.axis_index("tensor") * share, share, 2
    ).astype(jnp.bfloat16)
    data_part = lax.psum_scatter(
        lax.dot_general(
            normed, grads, (((0,), (0,)), ((), ())), preferred_element_type=jnp.float32
        ).astype(jnp.bfloat16),
        "dp",
        scatter_dimension=0,
        tiled=True,
    )
    weight_grad = lax.psum(data_part, "space").astype(jnp.float32)
    attended_out = attended.reshape(frames, row_count, local_cols)
    return (attended_out, token_grad, weight_grad.reshape(weights.shape))


def solution(mesh):
    return jax.shard_map(
        per_device,
        mesh=mesh,
        in_specs=(P("dp", "space", None), P("dp", None, "tensor"), P("dp", "space", "tensor")),
        out_specs=(P("dp", "space", "tensor"), P("dp", "space", "tensor"), P("dp", None, "tensor")),
        check_vma=False,
    )
```

profile of v0, /device:TPU:8, one launch (start us, length us, event | category | flops | bytes accessed | tf_op | source)
XLA Modules:
  0.0 534.6 jit_solution(2369777991918421316)
XLA Ops:
  7.2 0.0 copy-start.2
  7.2 0.0 all-gather.6.cloned.1.call-start
  7.2 2.4 copy.20
  9.6 0.0 all-gather.6.cloned.1.call-update
  9.7 0.0 all-gather.10.cloned.1.call-start
  9.7 2.1 fusion.2
  11.8 83.1 %all-gather.6.cloned.1.call-done = bf16[4096,3,512]{0,2,1:T(8,128)(2,1)} async-done(((bf16[256,3,512]{0,2,1:T(8,128)(2,1)}), bf16[4096,3,512]{0,2,1:T(8,128)(2,1)}) %all-gather.6.cloned.1.call-update) | async-done | bytes 12582928 | tf_op jit(solution)/shard_map/all_gather | solution.py:21
  94.9 0.0 copy-done.2
  94.9 9.0 %convolution_convert_fusion.2 = bf16[256,1536]{1,0:T(8,128)(2,1)} fusion(bf16[4096,1536]{0,1:T(8,128)(2,1)} %bitcast.68, bf16[1,256,4096]{2,1,0:T(8,128)(2,1)S(1)} %copy-done.2, f32[256]{0:T(256)S(1)} %add_sqrt_fusion), kind=kOutput, calls=%fused_computation.13 | convolution fusion | flops 3224764416 | bytes 15467520 | tf_op jit(solution)/shard_map/dot_general | solution.py:23
  103.9 1.7 reshape.132
  105.6 0.3 fusion.27
  105.9 0.7 copy.44
  106.7 0.0 all-gather.10.cloned.1.call-update
  106.7 0.0 all-gather.8.cloned.1.call-start
  106.7 0.0 copy-done.6
  106.7 0.1 reshape.137
  106.8 0.0 copy-start.8
  106.8 0.9 copy.42
  107.7 0.0 all-gather.8.cloned.1.call-update
  107.7 0.0 reduce-scatter.6.cloned.1.call-start
  107.8 25.7 %all-gather.10.cloned.1.call-done = bf16[1,1024,1,4,128]{4,1,3,2,0:T(8,128)(2,1)} async-done(((bf16[1,256,1,4,128]{4,1,3,2,0:T(8,128)(2,1)}), bf16[1,1024,1,4,128]{4,1,3,2,0:T(8,128)(2,1)}) %all-gather.10.cloned.1.call-update) | async-done | bytes 1048592 | tf_op jit(solution)/shard_map/all_gather | solution.py:29
  133.4 1.9 fusion.18
  135.4 1.4 fusion.28
  136.8 0.0 copy-start
  136.8 1.9 copy-done
  138.7 0.5 fusion.10
  139.2 0.0 copy-done.8
  139.2 1.5 fusion.11
  140.7 0.0 reduce-scatter.6.cloned.1.call-update
  140.7 0.0 reduce-scatter.4.cloned.1.call-start
  140.8 0.1 copy.26
  140.9 23.7 %all-gather.8.cloned.1.call-done = bf16[1,1024,1,4,128]{1,4,3,2,0:T(8,128)(2,1)} async-done(((bf16[1,256,1,4,128]{1,4,3,2,0:T(8,128)(2,1)}), bf16[1,1024,1,4,128]{1,4,3,2,0:T(8,128)(2,1)}) %all-gather.8.cloned.1.call-update) | async-done | bytes 1048592 | tf_op jit(solution)/shard_map/all_gather | solution.py:30
  164.6 2.8 multiply_reduce_fusion.2
  167.4 0.0 copy-done.9
  167.4 3.3 fusion.3
  170.6 0.0 copy-start.4
  170.7 1.3 copy-done.4
  172.0 1.5 fusion.12
  173.5 0.0 reduce-scatter.4.cloned.1.call-update
  173.5 0.2 reduce-scatter.8.cloned.1.call-start
  173.7 0.0 copy-done.5
  173.8 2.4 fusion.14
  176.2 18.5 %reduce-scatter.6.cloned.1.call-done = bf16[1,256,4,128]{1,3,2,0:T(8,128)(2,1)} async-done(((bf16[1,1024,4,128]{1,3,2,0:T(8,128)(2,1)}), bf16[1,256,4,128]{1,3,2,0:T(8,128)(2,1)}) %reduce-scatter.6.cloned.1.call-update) | async-done | bytes 262160 | tf_op jit(solution)/shard_map/reduce_scatter | solution.py:60
  194.7 28.4 %reduce-scatter.4.cloned.1.call-done = bf16[1,256,4,128]{1,3,2,0:T(8,128)(2,1)} async-done(((bf16[1,1024,4,128]{1,3,2,0:T(8,128)(2,1)}), bf16[1,256,4,128]{1,3,2,0:T(8,128)(2,1)}) %reduce-scatter.4.cloned.1.call-update) | async-done | bytes 262160 | tf_op jit(solution)/shard_map/reduce_scatter | solution.py:57
  223.1 1.1 pad_maximum_fusion
  224.2 0.0 copy-done.3
  224.2 6.6 %convolution_convert_fusion = bf16[4096,1536]{1,0:T(8,128)(2,1)} fusion(bf16[256,1536]{0,1:T(8,128)(2,1)S(1)} %bitcast.70, bf16[1,256,4096]{2,1,0:T(8,128)(2,1)S(1)} %copy-done.3, f32[256]{0:T(256)S(1)} %add_sqrt_fusion), kind=kOutput, calls=%fused_computation.1 | convolution fusion | flops 3230662656 | bytes 15467520 | tf_op jit(solution)/shard_map/dot_general | solution.py:78
  230.8 0.0 reduce-scatter.8.cloned.1.call-update
  230.8 0.0 copy-start.7
  230.8 0.0 all-reduce.3.cloned.1.call-start
  230.9 9.2 %fusion.1 = bf16[1,256,4096]{2,1,0:T(8,128)(2,1)} fusion(bf16[256,1536]{0,1:T(8,128)(2,1)S(1)} %bitcast.71, bf16[4096,1536]{0,1:T(8,128)(2,1)} %bitcast.69), kind=kOutput, calls=%fused_computation.5 | convolution fusion | flops 3222274048 | bytes 15466496 | tf_op jit(solution)/shard_map/dot_general | solution.py:66
  240.1 0.0 all-reduce.3.cloned.1.call-update
  240.1 0.0 all-reduce.5.cloned.1.call-start
  240.2 0.8 copy.34
  241.1 130.2 %reduce-scatter.8.cloned.1.call-done = bf16[256,1536]{1,0:T(8,128)(2,1)} async-done(((bf16[4096,1536]{1,0:T(8,128)(2,1)}), bf16[256,1536]{1,0:T(8,128)(2,1)}) %reduce-scatter.8.cloned.1.call-update) | async-done | bytes 786448 | tf_op jit(solution)/shard_map/reduce_scatter | solution.py:77
  371.3 2.3 copy.33
  373.6 0.0 all-reduce.5.cloned.1.call-update
  373.6 100.0 %all-reduce.3.cloned.1.call-done = bf16[1,256,4096]{2,1,0:T(8,128)(2,1)} async-done(((bf16[1,256,4096]{2,1,0:T(8,128)(2,1)}), bf16[1,256,4096]{2,1,0:T(8,128)(2,1)}) %all-reduce.3.cloned.1.call-update) | async-done | bytes 2097168 | tf_op jit(solution)/shard_map/psum | solution.py:70
  473.7 2.6 multiply_reduce_fusion
  476.2 0.0 copy-done.1
  476.2 0.5 convert_element_type.116
  476.7 1.0 fusion.16
  477.8 47.4 %all-reduce.5.cloned.1.call-done = bf16[256,3,512]{0,2,1:T(8,128)(2,1)} async-done(((bf16[256,3,512]{0,2,1:T(8,128)(2,1)}), bf16[256,3,512]{0,2,1:T(8,128)(2,1)}) %all-reduce.5.cloned.1.call-update) | async-done | bytes 786448 | tf_op jit(solution)/shard_map/psum | solution.py:85
  525.2 2.6 copy.35
  (8 shorter events, 0.0 us)
Async XLA Ops:
  7.2 87.8 %copy-start.2 = (bf16[1,256,4096]{2,1,0:T(8,128)(2,1)S(1)}, bf16[1,256,4096]{2,1,0:T(8,128)(2,1)}, u32[]{:S(2)}) copy-start(bf16[1,256,4096]{2,1,0:T(8,128)(2,1)} %param.3) | copy-start | bytes 6291460
  7.2 87.7 %all-gather.6.cloned.1.call-start = ((), (), s32[]{:S(2)}) async-start(), calls=%async_computation.3 | async-start | bytes 13369344 | tf_op jit(solution)/shard_map/all_gather | solution.py:21
  9.7 123.8 %all-gather.10.cloned.1.call-start = ((), (), s32[]{:S(2)}) async-start(), calls=%async_computation.10 | async-start | bytes 1310720 | tf_op jit(solution)/shard_map/all_gather | solution.py:29
  94.9 11.8 %copy-start.6 = (bf16[1,256,512]{2,1,0:T(8,128)(2,1)S(1)}, bf16[1,256,512]{2,1,0:T(8,128)(2,1)}, u32[]{:S(2)}) copy-start(bf16[1,256,512]{2,1,0:T(8,128)(2,1)} %param.5) | copy-start | bytes 786436
  106.7 57.9 %all-gather.8.cloned.1.call-start = ((), (), s32[]{:S(2)}) async-start(), calls=%async_computation.9 | async-start | bytes 1310720 | tf_op jit(solution)/shard_map/all_gather | solution.py:30
  106.8 32.4 %copy-start.8 = (bf16[256,4,128]{2,1,0:T(4,128)(2,1)}, bf16[256,4,128]{2,1,0:T(4,128)(2,1)S(1)}, u32[]{:S(2)}) copy-start(bf16[256,4,128]{2,1,0:T(4,128)(2,1)S(1)} %reshape.137) | copy-start | bytes 786436
  107.7 87.0 %reduce-scatter.6.cloned.1.call-start = ((), (), s32[]{:S(2)}) async-start(), calls=%async_computation.5 | async-start | bytes 1310720 | tf_op jit(solution)/shard_map/reduce_scatter | solution.py:60
  136.8 1.9 copy-start
  140.7 26.7 %copy-start.9 = (bf16[256,4,128]{2,1,0:T(4,128)(2,1)S(1)}, bf16[256,4,128]{2,1,0:T(4,128)(2,1)}, u32[]{:S(2)}) copy-start(bf16[256,4,128]{2,1,0:T(4,128)(2,1)} %copy-done.8) | copy-start | bytes 786436
  140.7 82.4 %reduce-scatter.4.cloned.1.call-start = ((), (), s32[]{:S(2)}) async-start(), calls=%async_computation.4 | async-start | bytes 1310720 | tf_op jit(solution)/shard_map/reduce_scatter | solution.py:57
  170.6 1.3 copy-start.4
  172.0 1.8 copy-start.5
  172.0 52.3 %copy-start.3 = (bf16[1,256,4096]{2,1,0:T(8,128)(2,1)S(1)}, bf16[1,256,4096]{2,1,0:T(8,128)(2,1)}, u32[]{:S(2)}) copy-start(bf16[1,256,4096]{2,1,0:T(8,128)(2,1)} %param.3) | copy-start | bytes 6291460
  173.5 197.8 %reduce-scatter.8.cloned.1.call-start = ((), (), s32[]{:S(2)}) async-start(), calls=%async_computation.7 | async-start | bytes 13369344 | tf_op jit(solution)/shard_map/reduce_scatter | solution.py:77
  230.8 9.4 %copy-start.7 = (bf16[4,128,256]{2,1,0:T(8,128)(2,1)S(1)}, bf16[4,128,256]{2,1,0:T(8,128)(2,1)}, u32[]{:S(2)}) copy-start(bf16[4,128,256]{2,1,0:T(8,128)(2,1)} %get-tuple-element.17) | copy-start | bytes 786436
  230.8 242.8 %all-reduce.3.cloned.1.call-start = ((), (), s32[]{:S(2)}) async-start(), calls=%async_computation.6 | async-start | bytes 4194304 | tf_op jit(solution)/shard_map/psum | solution.py:70
  240.1 285.0 %all-reduce.5.cloned.1.call-start = ((), (), s32[]{:S(2)}) async-start(), calls=%async_computation.8 | async-start | bytes 1572864 | tf_op jit(solution)/shard_map/psum | solution.py:85
  473.7 2.6 copy-start.1
Sparse Core Ops, SparseCore 0:
  10.4 84.5 all-gather.5
  106.8 26.5 all-gather.9
  135.8 28.7 all-gather.7
  167.6 27.0 reduce-scatter.5
  197.3 25.8 reduce-scatter.3
  231.0 140.2 reduce-scatter.7
  374.0 99.6 all-reduce.2
  476.7 48.4 all-reduce.4
where the time goes:
time: 535 us
  waiting for transfers between devices  457 us (85%)
  matrix products  38.1 us (7%)
  local copies, waits for them, and re-layouts  15.2 us (3%)
  between operations  14.3 us (3%)
  other arithmetic  9.23 us (2%)
    reduce_scatter x1, waiting for transfers between devices, per_device(): lax.psum_scatter(lax.dot_general(normed, grads, (((0,), (0,)), ((), ())),...  130 us
    psum x1, waiting for transfers between devices, per_device(): lax.psum(norm_part.astype(jnp.bfloat16), 'tensor').astype(jnp.float32)  100 us
    all_gather x1, waiting for transfers between devices, per_device(): full_w = lax.all_gather(weights, 'dp', axis=0, tiled=True)  83.1 us
    psum x1, waiting for transfers between devices, per_device(): weight_grad = lax.psum(data_part, 'space').astype(jnp.float32)  47.4 us
    reduce_scatter x1, waiting for transfers between devices, per_device(): lax.psum_scatter(dkey_part.astype(jnp.bfloat16), 'space', scatter_dimensi...  28.4 us
    all_gather x1, waiting for transfers between devices, per_device(): lax.all_gather(key_own, 'space', axis=1, tiled=True)  25.7 us
    all_gather x1, waiting for transfers between devices, per_device(): lax.all_gather(value_own, 'space', axis=1, tiled=True)  23.7 us
    reduce_scatter x1, waiting for transfers between devices, per_device(): lax.psum_scatter(dval_part.astype(jnp.bfloat16), 'space', scatter_dimensi...  18.5 us
  transfers between devices with their start and end apart: 8, of which 8 were waited for; matrix products, arithmetic and copies ran while one was open for 7% of the time, Pallas kernels for 0%

commit v1 on v0

v1 whole, which is shorter than its diff:
```python
import functools
import math

import jax
import jax.numpy as jnp
from jax import lax
from jax.experimental import pallas as pl
from jax.experimental.pallas import tpu as pltpu
from jax.sharding import Mesh
from jax.sharding import PartitionSpec as P

HS = 128
BF = jnp.bfloat16
F32 = jnp.float32
VMEM_LIMIT = 48 * 1024 * 1024


def dot(a, b, ca, cb):
    return lax.dot_general(a, b, (((ca,), (cb,)), ((), ())), preferred_element_type=F32)


def attention_kernel(q_rows, qkv_ref, dout_ref, att_ref, grad_ref, dk_ref, dv_ref):
    scale = 1.0 / math.sqrt(HS)
    key = qkv_ref[:, HS : 2 * HS]
    value = qkv_ref[:, 2 * HS : 3 * HS]
    key_t = key.T
    value_t = value.T
    for i in range(qkv_ref.shape[0] // q_rows):
        rows = pl.ds(i * q_rows, q_rows)
        query = qkv_ref[rows, 0:HS]
        dout = dout_ref[rows, :]
        scores = dot(key, query, 1, 1) * (scale * math.log2(math.e))
        top = jnp.max(scores, axis=0, keepdims=True)
        expo = jnp.exp2(scores - top)
        prob = expo * (1.0 / jnp.sum(expo, axis=0, keepdims=True))
        prob_bf = prob.astype(BF)
        att = dot(value_t, prob_bf, 1, 0).T.astype(BF)
        att_ref[rows, :] = att
        row_dot = jnp.sum(
            dout.astype(F32).T * att.astype(F32).T, axis=0, keepdims=True
        )
        dprob = dot(value, dout, 1, 1)
        dscore = (prob * (dprob - row_dot)).astype(BF)
        grad_ref[rows, 0:HS] = (dot(key_t, dscore, 1, 0) * scale).T.astype(BF)
        dv = dot(prob_bf, dout, 1, 0)
        dk = dot(dscore, query, 1, 0)
        if i == 0:
            dv_ref[...] = dv
            dk_ref[...] = dk
        else:
            dv_ref[...] += dv
            dk_ref[...] += dk
    grad_ref[:, HS : 2 * HS] = (dk_ref[...] * scale).astype(BF)
    grad_ref[:, 2 * HS : 3 * HS] = dv_ref[...].astype(BF)


def attention(qkv, dout):
    n = qkv.shape[0]
    return pl.pallas_call(
        functools.partial(attention_kernel, min(256, n)),
        out_shape=(
            jax.ShapeDtypeStruct((n, HS), BF),
            jax.ShapeDtypeStruct((n, 3 * HS), BF),
        ),
        in_specs=[pl.BlockSpec(memory_space=pltpu.VMEM)] * 2,
        out_specs=(pl.BlockSpec(memory_space=pltpu.VMEM),) * 2,
        scratch_shapes=[pltpu.VMEM((n, HS), F32), pltpu.VMEM((n, HS), F32)],
        compiler_params=pltpu.CompilerParams(vmem_limit_bytes=VMEM_LIMIT),
        cost_estimate=pl.CostEstimate(
            flops=14 * n * n * HS, bytes_accessed=16 * n * HS, transcendentals=n * n
        ),
    )(qkv, dout)


def project_kernel(a_ref, w_ref, flat_ref, heads_ref, acc_ref):
    step = pl.program_id(0)
    part = jnp.dot(a_ref[...], w_ref[...], preferred_element_type=F32)

    @pl.when(step == 0)
    def _():
        acc_ref[...] = part

    @pl.when(step > 0)
    def _():
        acc_ref[...] += part

    @pl.when(step == pl.num_programs(0) - 1)
    def _():
        heads = heads_ref.shape[0]
        out = acc_ref[...].astype(BF)
        flat_ref[...] = out
        for j in range(3):
            for h in range(heads):
                at = (j * heads + h) * HS
                heads_ref[h, :, j * HS : (j + 1) * HS] = out[:, at : at + HS]


def project(normed, flat_w, heads):
    rows, depth = normed.shape
    cols = flat_w.shape[1]
    tile = 512
    return pl.pallas_call(
        project_kernel,
        grid=(depth // tile,),
        in_specs=[
            pl.BlockSpec((rows, tile), lambda i: (0, i)),
            pl.BlockSpec((tile, cols), lambda i: (i, 0)),
        ],
        out_specs=(
            pl.BlockSpec((rows, cols), lambda i: (0, 0)),
            pl.BlockSpec((heads, rows, 3 * HS), lambda i: (0, 0, 0)),
        ),
        out_shape=(
            jax.ShapeDtypeStruct((rows, cols), BF),
            jax.ShapeDtypeStruct((heads, rows, 3 * HS), BF),
        ),
        scratch_shapes=[pltpu.VMEM((rows, cols), F32)],
        compiler_params=pltpu.CompilerParams(vmem_limit_bytes=VMEM_LIMIT),
        cost_estimate=pl.CostEstimate(
            flops=2 * rows * depth * cols,
            bytes_accessed=2 * (depth * cols + rows * depth),
            transcendentals=0,
        ),
    )(normed, flat_w)


def norm_kernel(at_ref, g_ref, w_ref, out_ref):
    out_ref[...] = dot(g_ref[...], w_ref[...], 1, 1).astype(BF)


def norm_quarter(grads, flat_w, quarter, share):
    rows, cols = grads.shape
    tile = 256
    tiles = share // tile
    return pl.pallas_call(
        norm_kernel,
        grid_spec=pltpu.PrefetchScalarGridSpec(
            num_scalar_prefetch=1,
            grid=(tiles,),
            in_specs=[
                pl.BlockSpec((rows, cols), lambda i, at: (0, 0)),
                pl.BlockSpec((tile, cols), lambda i, at: (at[0] * tiles + i, 0)),
            ],
            out_specs=pl.BlockSpec((rows, tile), lambda i, at: (0, i)),
        ),
        out_shape=jax.ShapeDtypeStruct((rows, share), BF),
        compiler_params=pltpu.CompilerParams(vmem_limit_bytes=VMEM_LIMIT),
        cost_estimate=pl.CostEstimate(
            flops=2 * rows * share * cols,
            bytes_accessed=2 * (share * cols + rows * (share + cols)),
            transcendentals=0,
        ),
    )(quarter.reshape(1), grads, flat_w)


def shift(x, axis, by):
    n = lax.axis_size(axis)
    return lax.ppermute(x, axis, [(i, (i + by) % n) for i in range(n)])


def per_device(tokens, weights, cotangent):
    _, rows, width = tokens.shape
    w_rows, _, cols = weights.shape
    heads = cols // HS
    n_x = lax.axis_size("x")
    n_t = lax.axis_size("zh")
    at_core, at_x, at_t = (lax.axis_index(a) for a in ("core", "x", "zh"))
    share = width // n_t

    full_w = lax.all_gather(weights.reshape(w_rows, 3 * cols), ("y", "zl", "core"), axis=0, tiled=True)

    tokens_f = tokens[0].astype(F32)
    root_ms = jnp.sqrt(jnp.mean(tokens_f * tokens_f, -1, keepdims=True) + 1e-05)
    normed = (tokens_f / root_ms).astype(BF)

    dout = cotangent.reshape(rows, heads, HS).transpose(1, 0, 2)
    dout = lax.all_to_all(dout, "x", 0, 0, tiled=True).reshape(n_x * rows, HS)

    halves = normed.reshape(rows, width // (2 * w_rows), 2, w_rows)
    mine = lax.dynamic_index_in_dim(halves, at_core, 2, False).reshape(rows, width // 2)
    given = lax.dynamic_index_in_dim(halves, 1 - at_core, 2, False).reshape(rows, width // 2)
    theirs = shift(given, "core", 1)
    left_m, left_t = shift(mine, "x", 1), shift(theirs, "x", 1)
    right_m, right_t = shift(mine, "x", -1), shift(theirs, "x", -1)
    far_m, far_t = shift(left_m, "x", 1), shift(right_t, "x", -1)
    all_rows = jnp.concatenate([mine, left_m, right_m, far_m, theirs, left_t, right_t, far_t], 0)

    proj, by_head = project(normed, full_w, heads)
    qkv = lax.all_to_all(by_head, "x", 0, 0, tiled=True).reshape(n_x * rows, 3 * HS)
    att, head_grads = attention(qkv, dout)

    by_block = head_grads.reshape(n_x, rows, 3 * HS)
    grads = lax.all_to_all(by_block, "x", 0, 0, tiled=True)
    grads = grads.reshape(heads, rows, 3, HS).transpose(1, 2, 0, 3).reshape(rows, 3 * cols)

    stat = jnp.sum(grads.astype(F32) * proj.astype(F32), -1, keepdims=True) * (1.0 / width)
    stat = lax.psum(stat, "zh")

    far = norm_quarter(grads, full_w, (at_t + 2) % n_t, share)
    half = share // 2
    up = shift(far[:, :half], "zh", 1)
    down = shift(far[:, half:], "zh", -1)
    to_up = norm_quarter(grads, full_w, (at_t + 1) % n_t, share)
    to_down = norm_quarter(grads, full_w, (at_t + n_t - 1) % n_t, share)
    own = norm_quarter(grads, full_w, at_t, share)
    to_up = jnp.concatenate(
        [(to_up[:, :half].astype(F32) + up.astype(F32)).astype(BF), to_up[:, half:]], 1
    )
    to_down = jnp.concatenate(
        [to_down[:, :half], (to_down[:, half:].astype(F32) + down.astype(F32)).astype(BF)], 1
    )
    norm_grad = (
        own.astype(F32) + shift(to_up, "zh", 1).astype(F32) + shift(to_down, "zh", -1).astype(F32)
    )
    unit = lax.dynamic_slice_in_dim(tokens[0], at_t * share, share, 1).astype(F32) / root_ms
    token_grad = ((norm_grad - unit * stat) / root_ms).astype(BF)

    other_grads = shift(by_block, "core", 1)
    order = [at_x, (at_x + n_x - 1) % n_x, (at_x + 1) % n_x, (at_x + 2) % n_x]
    blocks = [lax.dynamic_index_in_dim(g, o, 0, False) for g in (by_block, other_grads) for o in order]
    part = dot(all_rows, jnp.concatenate(blocks, 0), 0, 0).astype(BF)
    part = lax.all_to_all(part, ("y", "zl"), 0, 0, tiled=True)
    part = jnp.sum(part.reshape(-1, w_rows, 3 * HS).astype(F32), 0).astype(BF)
    part = lax.all_to_all(jnp.broadcast_to(part, (n_x,) + part.shape), "x", 0, 0, tiled=True)
    weight_grad = part.reshape(heads, w_rows, 3, HS).transpose(1, 2, 0, 3).reshape(weights.shape)

    attended = lax.all_to_all(att.reshape(n_x, rows, HS), "x", 0, 0, tiled=True)
    attended = attended.transpose(1, 0, 2).reshape(1, rows, cols)
    return attended, token_grad[None], weight_grad.astype(F32)


def solution(mesh):
    fine = Mesh(mesh.devices.reshape(4, 2, 2, 4, 4), ("y", "zl", "core", "x", "zh"))
    dp = ("y", "zl", "core")
    return jax.shard_map(
        per_device,
        mesh=fine,
        in_specs=(P(dp, "x", None), P(dp, None, "zh"), P(dp, "x", "zh")),
        out_specs=(P(dp, "x", "zh"), P(dp, "x", "zh"), P(dp, None, "zh")),
        check_vma=False,
    )
```

time: 535 us -> 244 us (0.46)
  the two profiles are of different devices: /device:TPU:8 before, /device:TPU:34 now
where the time goes in v1:
time: 244 us; the launch traced here: 243 us
  waiting for transfers between devices  67.6 us (28%)
  local copies, waits for them, and re-layouts  51.8 us (21%)
  starting transfers between devices  43.4 us (18%)
  Pallas kernels  31.7 us (13%)
  between operations  14.3 us (6%)
  blocking collectives  12.7 us (5%)
  other arithmetic  11.8 us (5%)
  matrix products  9.51 us (4%)
    ppermute x12, waiting for transfers between devices, shift(): return lax.ppermute(x, axis, [(i, (i + by) % n) for i in range(n)])  54 us
    unnamed x22, local copies, waits for them, and re-layouts  24.3 us
    pallas_call x4, Pallas kernels, norm_quarter(): pl.pallas_call(norm_kernel, grid_spec=pltpu.PrefetchScalarGridSpec(num_sc...  14.5 us
    ppermute x12, starting transfers between devices, shift(): return lax.ppermute(x, axis, [(i, (i + by) % n) for i in range(n)])  13.7 us
    psum x1, blocking collectives, per_device(): stat = lax.psum(stat, 'zh')  12.7 us
    convert_element_type x2, local copies, waits for them, and re-layouts, per_device(): tokens_f = tokens[0].astype(F32)  12.4 us
    pallas_call x1, Pallas kernels, project(): pl.pallas_call(project_kernel, grid=(depth // tile,), in_specs=[pl.BlockS...  10.7 us
    dot_general x1, matrix products, dot(): lax.dot_general(a, b, (((ca,), (cb,)), ((), ())), preferred_element_type=...  9.51 us
  transfers between devices with their start and end apart: 19, of which 7 were waited for; matrix products, arithmetic and copies ran while one was open for 28% of the time, Pallas kernels for 13%

profile of v1, /device:TPU:34, one launch (start us, length us, event | category | flops | bytes accessed | tf_op | source)
XLA Modules:
  0.0 242.8 jit_solution(13034765819211039575)
XLA Ops:
  7.2 1.5 copy.25
  8.8 1.2 copy.26
  10.0 5.2 %reshape.113 = f32[256,8,2,256]{3,2,1,0:T(2,128)} reshape(bf16[1,256,4096]{2,1,0:T(8,128)(2,1)S(1)} %copy-done) | data formatting | bytes 6291456 | tf_op jit(solution)/shard_map/convert_element_type | solution.py:172
  15.1 7.2 %copy.31 = f32[256,8,2,256]{0,3,1,2:T(8,128)} copy(f32[256,8,2,256]{3,2,1,0:T(2,128)} %reshape.113) | data formatting | bytes 8388608 | tf_op jit(solution)/shard_map/convert_element_type | solution.py:172
  22.9 2.9 %divide_convert_fusion = bf16[256,8,2,256]{0,3,1,2:T(8,128)(2,1)S(1)} fusion(f32[256,8,2,256]{0,3,1,2:T(8,128)} %copy.31, f32[256]{0:T(256)S(1)} %add_sqrt_fusion), kind=kLoop, calls=%fused_computation.4 | loop fusion | flops 2097152 | bytes 6292480 | tf_op jit(solution)/shard_map/convert_element_type | solution.py:174
  25.8 1.2 constant_dynamic-slice_fusion
  27.0 1.5 collective-permute-start.4
  28.5 0.5 collective-permute-start.5
  29.1 0.7 copy.36
  29.8 5.1 %all-to-all-start.1 = ((bf16[4,256,128]{2,1,0:T(8,128)(2,1)}), bf16[4,256,128]{2,1,0:T(8,128)(2,1)S(1)}, u32[]{:S(2)}, u32[]{:S(2)}) async-start(bf16[4,256,128]{2,1,0:T(8,128)(2,1)} %bitcast.55), calls=%async_computation.1 | async-start | bytes 524288 | tf_op jit(solution)/shard_map/all_to_all | solution.py:177
  35.0 2.3 fusion.1.a_ref
  37.4 15.9 %collective-permute-done.4 = bf16[256,2048]{0,1:T(8,128)(2,1)} collective-permute-done((bf16[256,2048]{0,1:T(8,128)(2,1)}, bf16[256,2048]{0,1:T(8,128)(2,1)}, u32[]{:S(2)}, u32[]{:S(2)}) %collective-permute-start.4) | collective-permute-done | bytes 1048608 | tf_op jit(solution)/shard_map/ppermute | solution.py:158
  53.3 1.5 collective-permute-start.6
  54.8 2.3 constant_dynamic-update-slice_fusion.7
  57.1 1.2 collective-permute-start.8
  58.3 2.3 constant_dynamic-update-slice_fusion.6
  60.6 2.4 constant_dynamic-update-slice_fusion.5
  63.0 16.4 %collective-permute-done.9 = bf16[256,2048]{0,1:T(8,128)(2,1)} collective-permute-done((bf16[256,2048]{0,1:T(8,128)(2,1)}, bf16[256,2048]{0,1:T(8,128)(2,1)}, u32[]{:S(2)}, u32[]{:S(2)}) %collective-permute-start.9) | collective-permute-done | bytes 1048608 | tf_op jit(solution)/shard_map/ppermute | solution.py:158
  79.9 7.2 %all-gather.2.cloned.1.call-done.w_ref = bf16[4096,1536]{1,0:T(8,128)(2,1)} async-done(((bf16[256,1536]{1,0:T(8,128)(2,1)}), bf16[4096,1536]{1,0:T(8,128)(2,1)}) %all-gather.2.cloned.1.call-update) | async-done | bytes 12582928 | tf_op jit(solution)/shard_map/all_gather | solution.py:170
  87.1 10.7 %shard_map.58 = (bf16[256,1536]{1,0:T(8,128)(2,1)S(1)}, bf16[4,256,384]{2,1,0:T(8,128)(2,1)}) custom-call(bf16[256,4096]{1,0:T(8,128)(2,1)S(1)} %fusion.1.a_ref, bf16[4096,1536]{1,0:T(8,128)(2,1)} %all-gather.2.cloned.1.call-done.w_ref), custom_call_target="tpu_custom_call" | custom-call | flops 3221225472 | bytes 14680064 | tf_op jit(solution)/shard_map/pallas_call | solution.py:102
  97.8 4.8 %all-to-all-start = ((bf16[4,256,384]{2,1,0:T(8,128)(2,1)}), bf16[4,256,384]{2,1,0:T(8,128)(2,1)S(1)}, u32[]{:S(2)}, u32[]{:S(2)}) async-start(bf16[4,256,384]{2,1,0:T(8,128)(2,1)} %get-tuple-element.7), calls=%async_computation | async-start | bytes 1572864 | tf_op jit(solution)/shard_map/all_to_all | solution.py:189
  102.6 2.3 constant_dynamic-update-slice_fusion.4
  104.9 2.3 constant_dynamic-update-slice_fusion.3
  107.3 2.3 constant_dynamic-update-slice_fusion.2
  109.6 4.3 %all-to-all-done = bf16[4,256,384]{2,1,0:T(8,128)(2,1)S(1)} async-done(((bf16[4,256,384]{2,1,0:T(8,128)(2,1)}), bf16[4,256,384]{2,1,0:T(8,128)(2,1)S(1)}, u32[]{:S(2)}, u32[]{:S(2)}) %all-to-all-start) | async-done | bytes 786464 | tf_op jit(solution)/shard_map/all_to_all | solution.py:189
  113.9 6.5 %shard_map.59 = (bf16[1024,128]{1,0:T(8,128)(2,1)}, bf16[1024,384]{1,0:T(8,128)(2,1)S(1)}) custom-call(bf16[1024,384]{1,0:T(8,128)(2,1)S(1)} %bitcast.62, bf16[1024,128]{1,0:T(8,128)(2,1)S(1)} %bitcast.63), custom_call_target="tpu_custom_call" | custom-call | flops 1879048192 | bytes 2097152 | tf_op jit(solution)/shard_map/pallas_call | solution.py:59
  120.5 2.3 constant_dynamic-update-slice_fusion.1
  122.8 2.4 constant_dynamic-update-slice_fusion
  125.2 1.2 copy.29
  126.4 4.8 %all-to-all-start.2 = ((bf16[4,256,128]{2,1,0:T(8,128)(2,1)}), bf16[4,256,128]{2,1,0:T(8,128)(2,1)S(1)}, u32[]{:S(2)}, u32[]{:S(2)}) async-start(bf16[4,256,128]{2,1,0:T(8,128)(2,1)} %bitcast.5), calls=%async_computation.2 | async-start | bytes 524288 | tf_op jit(solution)/shard_map/all_to_all | solution.py:227
  131.2 0.7 bitcast_dynamic-update-slice_fusion.7
  131.9 0.7 bitcast_dynamic-update-slice_fusion.6
  132.6 0.7 bitcast_dynamic-update-slice_fusion.5
  133.3 0.7 bitcast_dynamic-update-slice_fusion.4
  134.0 0.7 bitcast_dynamic-update-slice_fusion.3
  134.7 0.7 bitcast_dynamic-update-slice_fusion.2
  135.4 0.7 bitcast_dynamic-update-slice_fusion.1
  136.1 0.7 bitcast_dynamic-update-slice_fusion
  136.8 0.6 all-to-all-done.2
  137.4 4.9 %all-to-all-start.3 = ((bf16[4,256,384]{1,2,0:T(8,128)(2,1)}), bf16[4,256,384]{1,2,0:T(8,128)(2,1)S(1)}, u32[]{:S(2)}, u32[]{:S(2)}) async-start(bf16[4,256,384]{1,2,0:T(8,128)(2,1)} %copy.29), calls=%async_computation.3 | async-start | bytes 1572864 | tf_op jit(solution)/shard_map/all_to_all | solution.py:193
  142.3 9.5 %convolution_convert_fusion = bf16[2048,384]{1,0:T(8,128)(2,1)} fusion(bf16[2048,2048]{0,1:T(8,128)(2,1)} %constant_dynamic-update-slice_fusion, bf16[2048,384]{1,0:T(8,128)(2,1)} %bitcast_dynamic-update-slice_fusion), kind=kOutput, calls=%fused_computation.5 | convolution fusion | flops 3222011904 | bytes 11534336 | tf_op jit(solution)/shard_map/dot_general | solution.py:19
  151.8 1.5 all-to-all-done.3
  153.3 5.1 %all-to-all-start.4 = ((bf16[8,256,384]{2,1,0:T(8,128)(2,1)}), bf16[8,256,384]{2,1,0:T(8,128)(2,1)S(1)}, u32[]{:S(2)}, u32[]{:S(2)}) async-start(bf16[8,256,384]{2,1,0:T(8,128)(2,1)} %bitcast.68), calls=%async_computation.4 | async-start | bytes 3145728 | tf_op jit(solution)/shard_map/all_to_all | solution.py:222
  158.3 1.3 copy.30
  159.6 1.7 reshape.104.g_ref
  161.3 3.6 %shard_map.62 = bf16[256,1024]{1,0:T(8,128)(2,1)S(1)} custom-call(s32[1]{0:T(128)} %bitcast.12.at_ref, bf16[256,1536]{1,0:T(8,128)(2,1)S(1)} %reshape.104.g_ref, bf16[4096,1536]{1,0:T(8,128)(2,1)} %all-gather.2.cloned.1.call-done.w_ref), custom_call_target="tpu_custom_call" | custom-call | flops 805306368 | bytes 4456448 | tf_op jit(solution)/shard_map/pallas_call | solution.py:135
  164.9 0.8 fusion.7
  165.8 4.9 %collective-permute-start.2 = (bf16[256,512]{1,0:T(8,128)(2,1)}, bf16[256,512]{1,0:T(8,128)(2,1)}, u32[]{:S(2)}, u32[]{:S(2)}) collective-permute-start(bf16[256,512]{1,0:T(8,128)(2,1)} %get-tuple-element.20), channel_id=1, source_target_pairs={{0,3},{1,0},{2,1},{3,2},{4,7},{5,4},{6,5},{7,6},{8,11},{9,8},{10,9... | collective-permute-start | bytes 786440 | tf_op jit(solution)/shard_map/ppermute | solution.py:158
  170.7 3.6 %shard_map.63 = bf16[256,1024]{1,0:T(8,128)(2,1)S(1)} custom-call(s32[1]{0:T(128)} %bitcast.13.at_ref, bf16[256,1536]{1,0:T(8,128)(2,1)S(1)} %reshape.104.g_ref, bf16[4096,1536]{1,0:T(8,128)(2,1)} %all-gather.2.cloned.1.call-done.w_ref), custom_call_target="tpu_custom_call" | custom-call | flops 805306368 | bytes 4456448 | tf_op jit(solution)/shard_map/pallas_call | solution.py:135
  174.4 3.7 %shard_map.61 = bf16[256,1024]{1,0:T(8,128)(2,1)S(1)} custom-call(s32[1]{0:T(128)} %bitcast.11.at_ref, bf16[256,1536]{1,0:T(8,128)(2,1)S(1)} %reshape.104.g_ref, bf16[4096,1536]{1,0:T(8,128)(2,1)} %all-gather.2.cloned.1.call-done.w_ref), custom_call_target="tpu_custom_call" | custom-call | flops 805306368 | bytes 4456448 | tf_op jit(solution)/shard_map/pallas_call | solution.py:135
  178.2 21.8 %collective-permute-done.2 = bf16[256,512]{1,0:T(8,128)(2,1)} collective-permute-done((bf16[256,512]{1,0:T(8,128)(2,1)}, bf16[256,512]{1,0:T(8,128)(2,1)}, u32[]{:S(2)}, u32[]{:S(2)}) %collective-permute-start.2) | collective-permute-done | bytes 262176 | tf_op jit(solution)/shard_map/ppermute | solution.py:158
  199.9 1.0 add_convert_fusion
  200.9 0.9 pad_maximum_fusion.1
  201.8 1.1 collective-permute-start.3
  203.0 0.9 pad_maximum_fusion
  203.9 2.1 collective-permute-start.1
  206.0 0.9 copy.28
  206.9 1.8 reshape.100
  209.4 0.9 broadcast_in_dim.9
  210.3 4.9 %all-to-all-start.5 = ((bf16[4,256,384]{1,2,0:T(8,128)(2,1)}), bf16[4,256,384]{1,2,0:T(8,128)(2,1)S(1)}, u32[]{:S(2)}, u32[]{:S(2)}) async-start(bf16[4,256,384]{1,2,0:T(8,128)(2,1)} %broadcast_in_dim.9), calls=%async_computation.5 | async-start | bytes 1572864 | tf_op jit(solution)/shard_map/all_to_all | solution.py:224
  215.2 12.7 %psum.7 = f32[256]{0:T(256)S(1)} all-reduce(f32[256]{0:T(256)S(1)} %broadcast_multiply_fusion), channel_id=1, replica_groups=mesh['y'=4,'zl'=2,'core'=2,'x'=4,'zh'=4] {'zh'}, use_global_device_ids=true, to_apply=%region_2.3 | all-reduce | flops 256 | bytes 2048 | tf_op jit(solution)/shard_map/psum | solution.py:197
  227.9 3.6 %shard_map.60 = bf16[256,1024]{1,0:T(8,128)(2,1)S(1)} custom-call(s32[1]{0:T(128)} %bitcast.7.at_ref, bf16[256,1536]{1,0:T(8,128)(2,1)S(1)} %reshape.104.g_ref, bf16[4096,1536]{1,0:T(8,128)(2,1)} %all-gather.2.cloned.1.call-done.w_ref), custom_call_target="tpu_custom_call" | custom-call | flops 805306368 | bytes 4456448 | tf_op jit(solution)/shard_map/pallas_call | solution.py:135
  231.5 2.5 %fusion.6 = bf16[1,256,1024]{2,1,0:T(8,128)(2,1)} fusion(f32[256]{0:T(256)S(1)} %psum.7, f32[256]{0:T(256)S(1)} %add_sqrt_fusion, bf16[1,256,4096]{2,1,0:T(8,128)(2,1)} %param.3, s32[]{:T(128)S(6)} %select_n.57, bf16[256,1024]{1,0:T(8,128)(2,1)} %collective-permute-done.3, bf16[256,1024]{1,0:T(8,128)(2,1)} %collective-permute-done.1, ...), kind=kLoop, calls=%fused_computation.17 | loop fusion | flops 2883584 | bytes 2623492 | tf_op jit(solution)/shard_map/broadcast_in_dim | solution.py:229
  234.4 1.6 copy.34
  (37 shorter events, 2.5 us)
Async XLA Ops:
  7.2 2.8 %copy-start = (bf16[1,256,4096]{2,1,0:T(8,128)(2,1)S(1)}, bf16[1,256,4096]{2,1,0:T(8,128)(2,1)}, u32[]{:S(2)}) copy-start(bf16[1,256,4096]{2,1,0:T(8,128)(2,1)} %param.3) | copy-start | bytes 6291460
  7.2 79.9 %all-gather.2.cloned.1.call-start = ((), (), s32[]{:S(2)}) async-start(), calls=%async_computation.6 | async-start | bytes 13369344 | tf_op jit(solution)/shard_map/all_gather | solution.py:170
  25.8 3.2 %copy-start.1 = (bf16[1,256,512]{2,1,0:T(8,128)(2,1)S(1)}, bf16[1,256,512]{2,1,0:T(8,128)(2,1)}, u32[]{:S(2)}) copy-start(bf16[1,256,512]{2,1,0:T(8,128)(2,1)} %param.5) | copy-start | bytes 786436
  27.0 7.9 %collective-permute-start.7 = (bf16[256,2048]{0,1:T(8,128)(2,1)S(1)}, bf16[256,2048]{0,1:T(8,128)(2,1)}, u32[]{:S(2)}, u32[]{:S(2)}) collective-permute-start(bf16[256,2048]{0,1:T(8,128)(2,1)S(1)} %bitcast.69), channel_id=1, source_target_pairs={{0,16},{16,0},{1,17},{17,1},{2,18},{18,2},{3,19},{19,3},{4,20},{20... | collective-permute-start | bytes 3145736 | tf_op jit(solution)/shard_map/ppermute | solution.py:158
  27.0 26.3 %collective-permute-start.4 = (bf16[256,2048]{0,1:T(8,128)(2,1)}, bf16[256,2048]{0,1:T(8,128)(2,1)}, u32[]{:S(2)}, u32[]{:S(2)}) collective-permute-start(bf16[256,2048]{0,1:T(8,128)(2,1)} %bitcast.16), channel_id=1, source_target_pairs={{0,4},{4,8},{8,12},{12,0},{1,5},{5,9},{9,13},{13,1},{2,6},{6,10},{... | collective-permute-start | bytes 3145736 | tf_op jit(solution)/shard_map/ppermute | solution.py:158
  28.5 32.2 %collective-permute-start.5 = (bf16[256,2048]{0,1:T(8,128)(2,1)}, bf16[256,2048]{0,1:T(8,128)(2,1)}, u32[]{:S(2)}, u32[]{:S(2)}) collective-permute-start(bf16[256,2048]{0,1:T(8,128)(2,1)} %bitcast.16), channel_id=1, source_target_pairs={{0,12},{4,0},{8,4},{12,8},{1,13},{5,1},{9,5},{13,9},{2,14},{6,2},{... | collective-permute-start | bytes 3145736 | tf_op jit(solution)/shard_map/ppermute | solution.py:158
  29.8 68.0 %all-to-all-start.1 = ((bf16[4,256,128]{2,1,0:T(8,128)(2,1)}), bf16[4,256,128]{2,1,0:T(8,128)(2,1)S(1)}, u32[]{:S(2)}, u32[]{:S(2)}) async-start(bf16[4,256,128]{2,1,0:T(8,128)(2,1)} %bitcast.55), calls=%async_computation.1 | async-start | bytes 524288 | tf_op jit(solution)/shard_map/all_to_all | solution.py:177
  34.9 44.5 %collective-permute-start.9 = (bf16[256,2048]{0,1:T(8,128)(2,1)}, bf16[256,2048]{0,1:T(8,128)(2,1)}, u32[]{:S(2)}, u32[]{:S(2)}) collective-permute-start(bf16[256,2048]{0,1:T(8,128)(2,1)} %collective-permute-done.7), channel_id=1, source_target_pairs={{0,12},{4,0},{8,4},{12,8},{1,13},{5,1},{9,5},{13,9},{2,14},{6,2},{... | collective-permute-start | bytes 3145736 | tf_op jit(solution)/shard_map/ppermute | solution.py:158
  53.3 49.4 %collective-permute-start.6 = (bf16[256,2048]{0,1:T(8,128)(2,1)}, bf16[256,2048]{0,1:T(8,128)(2,1)}, u32[]{:S(2)}, u32[]{:S(2)}) collective-permute-start(bf16[256,2048]{0,1:T(8,128)(2,1)} %collective-permute-done.4), channel_id=1, source_target_pairs={{0,4},{4,8},{8,12},{12,0},{1,5},{5,9},{9,13},{13,1},{2,6},{6,10},{... | collective-permute-start | bytes 3145736 | tf_op jit(solution)/shard_map/ppermute | solution.py:158
  57.1 50.2 %collective-permute-start.8 = (bf16[256,2048]{0,1:T(8,128)(2,1)}, bf16[256,2048]{0,1:T(8,128)(2,1)}, u32[]{:S(2)}, u32[]{:S(2)}) collective-permute-start(bf16[256,2048]{0,1:T(8,128)(2,1)} %collective-permute-done.7), channel_id=1, source_target_pairs={{0,4},{4,8},{8,12},{12,0},{1,5},{5,9},{9,13},{13,1},{2,6},{6,10},{... | collective-permute-start | bytes 3145736 | tf_op jit(solution)/shard_map/ppermute | solution.py:158
  79.4 43.4 %collective-permute-start.10 = (bf16[256,2048]{0,1:T(8,128)(2,1)}, bf16[256,2048]{0,1:T(8,128)(2,1)}, u32[]{:S(2)}, u32[]{:S(2)}) collective-permute-start(bf16[256,2048]{0,1:T(8,128)(2,1)} %collective-permute-done.9), channel_id=1, source_target_pairs={{0,12},{4,0},{8,4},{12,8},{1,13},{5,1},{9,5},{13,9},{2,14},{6,2},{... | collective-permute-start | bytes 3145736 | tf_op jit(solution)/shard_map/ppermute | solution.py:158
  97.8 16.1 %all-to-all-start = ((bf16[4,256,384]{2,1,0:T(8,128)(2,1)}), bf16[4,256,384]{2,1,0:T(8,128)(2,1)S(1)}, u32[]{:S(2)}, u32[]{:S(2)}) async-start(bf16[4,256,384]{2,1,0:T(8,128)(2,1)} %get-tuple-element.7), calls=%async_computation | async-start | bytes 1572864 | tf_op jit(solution)/shard_map/all_to_all | solution.py:189
  120.4 13.6 %collective-permute-start.11 = (bf16[4,256,384]{2,1,0:T(8,128)(2,1)S(1)}, bf16[4,256,384]{2,1,0:T(8,128)(2,1)S(1)}, u32[]{:S(2)}, u32[]{:S(2)}) collective-permute-start(bf16[4,256,384]{2,1,0:T(8,128)(2,1)S(1)} %bitcast.56), channel_id=1, source_target_pairs={{0,16},{16,0},{1,17},{17,1},{2,18},{18,2},{3,19},{19,3},{4,20},{20... | collective-permute-start | bytes 2359304 | tf_op jit(solution)/shard_map/ppermute | solution.py:158
  126.4 11.0 %all-to-all-start.2 = ((bf16[4,256,128]{2,1,0:T(8,128)(2,1)}), bf16[4,256,128]{2,1,0:T(8,128)(2,1)S(1)}, u32[]{:S(2)}, u32[]{:S(2)}) async-start(bf16[4,256,128]{2,1,0:T(8,128)(2,1)} %bitcast.5), calls=%async_computation.2 | async-start | bytes 524288 | tf_op jit(solution)/shard_map/all_to_all | solution.py:227
  137.4 15.9 %all-to-all-start.3 = ((bf16[4,256,384]{1,2,0:T(8,128)(2,1)}), bf16[4,256,384]{1,2,0:T(8,128)(2,1)S(1)}, u32[]{:S(2)}, u32[]{:S(2)}) async-start(bf16[4,256,384]{1,2,0:T(8,128)(2,1)} %copy.29), calls=%async_computation.3 | async-start | bytes 1572864 | tf_op jit(solution)/shard_map/all_to_all | solution.py:193
  153.3 55.7 %all-to-all-start.4 = ((bf16[8,256,384]{2,1,0:T(8,128)(2,1)}), bf16[8,256,384]{2,1,0:T(8,128)(2,1)S(1)}, u32[]{:S(2)}, u32[]{:S(2)}) async-start(bf16[8,256,384]{2,1,0:T(8,128)(2,1)} %bitcast.68), calls=%async_computation.4 | async-start | bytes 3145728 | tf_op jit(solution)/shard_map/all_to_all | solution.py:222
  165.8 34.2 %collective-permute-start.2 = (bf16[256,512]{1,0:T(8,128)(2,1)}, bf16[256,512]{1,0:T(8,128)(2,1)}, u32[]{:S(2)}, u32[]{:S(2)}) collective-permute-start(bf16[256,512]{1,0:T(8,128)(2,1)} %get-tuple-element.20), channel_id=1, source_target_pairs={{0,3},{1,0},{2,1},{3,2},{4,7},{5,4},{6,5},{7,6},{8,11},{9,8},{10,9... | collective-permute-start | bytes 786440 | tf_op jit(solution)/shard_map/ppermute | solution.py:158
  174.3 3.7 %copy-start.2 = (bf16[256,512]{1,0:T(8,128)(2,1)S(1)}, bf16[256,512]{1,0:T(8,128)(2,1)}, u32[]{:S(2)}) copy-start(bf16[256,512]{1,0:T(8,128)(2,1)} %get-tuple-element.19) | copy-start | bytes 786436
  178.1 24.9 %collective-permute-start = (bf16[256,512]{1,0:T(8,128)(2,1)S(1)}, bf16[256,512]{1,0:T(8,128)(2,1)S(1)}, u32[]{:S(2)}, u32[]{:S(2)}) collective-permute-start(bf16[256,512]{1,0:T(8,128)(2,1)S(1)} %copy-done.2), channel_id=1, source_target_pairs={{0,1},{1,2},{2,3},{3,0},{4,5},{5,6},{6,7},{7,4},{8,9},{9,10},{10,1... | collective-permute-start | bytes 786440 | tf_op jit(solution)/shard_map/ppermute | solution.py:158
  201.8 29.7 %collective-permute-start.3 = (bf16[256,1024]{1,0:T(8,128)(2,1)}, bf16[256,1024]{1,0:T(8,128)(2,1)}, u32[]{:S(2)}, u32[]{:S(2)}) collective-permute-start(bf16[256,1024]{1,0:T(8,128)(2,1)} %pad_maximum_fusion.1), channel_id=1, source_target_pairs={{0,3},{1,0},{2,1},{3,2},{4,7},{5,4},{6,5},{7,6},{8,11},{9,8},{10,9... | collective-permute-start | bytes 1572872 | tf_op jit(solution)/shard_map/ppermute | solution.py:158
  203.9 27.7 %collective-permute-start.1 = (bf16[256,1024]{1,0:T(8,128)(2,1)}, bf16[256,1024]{1,0:T(8,128)(2,1)}, u32[]{:S(2)}, u32[]{:S(2)}) collective-permute-start(bf16[256,1024]{1,0:T(8,128)(2,1)} %pad_maximum_fusion), channel_id=1, source_target_pairs={{0,1},{1,2},{2,3},{3,0},{4,5},{5,6},{6,7},{7,4},{8,9},{9,10},{10,1... | collective-permute-start | bytes 1572872 | tf_op jit(solution)/shard_map/ppermute | solution.py:158
  210.3 23.8 %all-to-all-start.5 = ((bf16[4,256,384]{1,2,0:T(8,128)(2,1)}), bf16[4,256,384]{1,2,0:T(8,128)(2,1)S(1)}, u32[]{:S(2)}, u32[]{:S(2)}) async-start(bf16[4,256,384]{1,2,0:T(8,128)(2,1)} %broadcast_in_dim.9), calls=%async_computation.5 | async-start | bytes 1572864 | tf_op jit(solution)/shard_map/all_to_all | solution.py:224
Sparse Core Ops, SparseCore 0:
  10.1 76.9 all-gather.1

commit v2 on v1

v2 whole, which is shorter than its diff:
```python
import functools
import math

import jax
import jax.numpy as jnp
from jax import lax
from jax.experimental import pallas as pl
from jax.experimental.pallas import tpu as pltpu
from jax.sharding import Mesh
from jax.sharding import PartitionSpec as P

HS = 128
BF = jnp.bfloat16
F32 = jnp.float32
PARAMS = pltpu.CompilerParams(vmem_limit_bytes=48 * 1024 * 1024)


def dot(a, b, ca, cb):
    return lax.dot_general(a, b, (((ca,), (cb,)), ((), ())), preferred_element_type=F32)


def cost(flops, nbytes, exps=0):
    return pl.CostEstimate(flops=flops, bytes_accessed=nbytes, transcendentals=exps)


def shape(*dims, dtype=BF):
    return jax.ShapeDtypeStruct(dims, dtype)


def unit_kernel(at_ref, tok_ref, normed_ref, root_ref, mine_ref, given_ref, *, band):
    tok = tok_ref[...].astype(F32)
    root = jnp.sqrt(jnp.mean(tok * tok, -1, keepdims=True) + 1e-05)
    normed_ref[...] = (tok / root).astype(BF)
    root_ref[...] = root
    core = at_ref[0]
    for i in range(mine_ref.shape[0] // band):
        for ref, which in ((mine_ref, core), (given_ref, 1 - core)):
            at = pl.multiple_of((2 * i + which) * band, band)
            ref[i * band : (i + 1) * band, :] = normed_ref[:, pl.ds(at, band)].T


def unit_rows(tokens, core, band):
    rows, width = tokens.shape
    tile = 128
    return pl.pallas_call(
        functools.partial(unit_kernel, band=band),
        grid_spec=pltpu.PrefetchScalarGridSpec(
            num_scalar_prefetch=1,
            grid=(rows // tile,),
            in_specs=[pl.BlockSpec((tile, width), lambda i, at: (i, 0))],
            out_specs=(
                pl.BlockSpec((tile, width), lambda i, at: (i, 0)),
                pl.BlockSpec((tile, 1), lambda i, at: (i, 0)),
                pl.BlockSpec((width // 2, tile), lambda i, at: (0, i)),
                pl.BlockSpec((width // 2, tile), lambda i, at: (0, i)),
            ),
        ),
        out_shape=(
            shape(rows, width),
            shape(rows, 1, dtype=F32),
            shape(width // 2, rows),
            shape(width // 2, rows),
        ),
        compiler_params=PARAMS,
        cost_estimate=cost(6 * rows * width, 6 * rows * width),
    )(core.reshape(1), tokens)


def project_kernel(a_ref, w_ref, heads_ref, acc_ref):
    step = pl.program_id(0)
    part = jnp.dot(a_ref[...], w_ref[...], preferred_element_type=F32)

    @pl.when(step == 0)
    def _():
        acc_ref[...] = part

    @pl.when(step > 0)
    def _():
        acc_ref[...] += part

    @pl.when(step == pl.num_programs(0) - 1)
    def _():
        heads = heads_ref.shape[0]
        for j in range(3):
            for h in range(heads):
                at = (j * heads + h) * HS
                heads_ref[h, :, j * HS : (j + 1) * HS] = acc_ref[:, at : at + HS].astype(BF)


def project(normed, flat_w, heads):
    rows, depth = normed.shape
    cols = flat_w.shape[1]
    tile = 512
    return pl.pallas_call(
        project_kernel,
        grid=(depth // tile,),
        in_specs=[
            pl.BlockSpec((rows, tile), lambda i: (0, i)),
            pl.BlockSpec((tile, cols), lambda i: (i, 0)),
        ],
        out_specs=pl.BlockSpec((heads, rows, 3 * HS), lambda i: (0, 0, 0)),
        out_shape=shape(heads, rows, 3 * HS),
        scratch_shapes=[pltpu.VMEM((rows, cols), F32)],
        compiler_params=PARAMS,
        cost_estimate=cost(2 * rows * depth * cols, 2 * (depth * cols + rows * depth)),
    )(normed, flat_w)


def attention_kernel(q_rows, qkv_ref, dout_ref, att_ref, grad_ref, dk_ref, dv_ref):
    scale = 1.0 / math.sqrt(HS)
    key = qkv_ref[:, HS : 2 * HS]
    value = qkv_ref[:, 2 * HS : 3 * HS]
    key_t = key.T
    value_t = value.T
    for i in range(qkv_ref.shape[0] // q_rows):
        rows = pl.ds(i * q_rows, q_rows)
        query = qkv_ref[rows, 0:HS]
        dout = dout_ref[rows, :]
        scores = dot(key, query, 1, 1) * (scale * math.log2(math.e))
        top = jnp.max(scores, axis=0, keepdims=True)
        expo = jnp.exp2(scores - top)
        prob = expo * (1.0 / jnp.sum(expo, axis=0, keepdims=True))
        prob_bf = prob.astype(BF)
        att = dot(value_t, prob_bf, 1, 0).T.astype(BF)
        att_ref[rows, :] = att
        row_dot = jnp.sum(
            dout.astype(F32).T * att.astype(F32).T, axis=0, keepdims=True
        )
        dprob = dot(value, dout, 1, 1)
        dscore = (prob * (dprob - row_dot)).astype(BF)
        grad_ref[rows, 0:HS] = (dot(key_t, dscore, 1, 0) * scale).T.astype(BF)
        dv = dot(prob_bf, dout, 1, 0)
        dk = dot(dscore, query, 1, 0)
        if i == 0:
            dv_ref[...] = dv
            dk_ref[...] = dk
        else:
            dv_ref[...] += dv
            dk_ref[...] += dk
    grad_ref[:, HS : 2 * HS] = (dk_ref[...] * scale).astype(BF)
    grad_ref[:, 2 * HS : 3 * HS] = dv_ref[...].astype(BF)


def attention(qkv, dout):
    n = qkv.shape[0]
    return pl.pallas_call(
        functools.partial(attention_kernel, min(256, n)),
        out_shape=(shape(n, HS), shape(n, 3 * HS)),
        in_specs=[pl.BlockSpec(memory_space=pltpu.VMEM)] * 2,
        out_specs=(pl.BlockSpec(memory_space=pltpu.VMEM),) * 2,
        scratch_shapes=[pltpu.VMEM((n, HS), F32), pltpu.VMEM((n, HS), F32)],
        compiler_params=PARAMS,
        cost_estimate=cost(14 * n * n * HS, 16 * n * HS, n * n),
    )(qkv, dout)


def norm_kernel(at_ref, g_ref, w_ref, out_ref, flat_ref):
    @pl.when(pl.program_id(0) == 0)
    def _():
        heads = g_ref.shape[0]
        for j in range(3):
            for h in range(heads):
                at = (j * heads + h) * HS
                flat_ref[:, at : at + HS] = g_ref[h, :, j * HS : (j + 1) * HS]

    out_ref[...] = dot(w_ref[...], flat_ref[...], 1, 1).astype(BF)


def norm_quarter(grads, flat_w, quarter, share):
    heads, rows, _ = grads.shape
    cols = flat_w.shape[1]
    tile = 512
    tiles = share // tile
    return pl.pallas_call(
        norm_kernel,
        grid_spec=pltpu.PrefetchScalarGridSpec(
            num_scalar_prefetch=1,
            grid=(tiles,),
            in_specs=[
                pl.BlockSpec(grads.shape, lambda i, at: (0, 0, 0)),
                pl.BlockSpec((tile, cols), lambda i, at: (at[0] * tiles + i, 0)),
            ],
            out_specs=pl.BlockSpec((tile, rows), lambda i, at: (i, 0)),
            scratch_shapes=[pltpu.VMEM((rows, cols), BF)],
        ),
        out_shape=shape(share, rows),
        compiler_params=PARAMS,
        cost_estimate=cost(2 * rows * share * cols, 2 * (share * cols + rows * (share + cols))),
    )(quarter.reshape(1), grads, flat_w)


def finish_kernel(at_ref, own_ref, a0_ref, a1_ref, b0_ref, b1_ref, tok_ref, root_ref, stat_ref, out_ref):
    half = a0_ref.shape[0]
    for i, refs in enumerate(((a0_ref, b0_ref), (a1_ref, b1_ref))):
        span = slice(i * half, (i + 1) * half)
        total = own_ref[span, :].astype(F32)
        for ref in refs:
            total += ref[...].astype(F32)
        unit = tok_ref[:, span].astype(F32) / root_ref[...]
        out_ref[:, span] = ((total.T - unit * stat_ref[...]) / root_ref[...]).astype(BF)


def finish(quarter, own, parts, tokens, root, stat):
    share, rows = own.shape
    whole = lambda a: pl.BlockSpec(a.shape, lambda i, at: (0, 0))
    return pl.pallas_call(
        finish_kernel,
        grid_spec=pltpu.PrefetchScalarGridSpec(
            num_scalar_prefetch=1,
            grid=(1,),
            in_specs=[whole(own)]
            + [whole(p) for p in parts]
            + [pl.BlockSpec((rows, share), lambda i, at: (0, at[0]))]
            + [whole(root), whole(stat)],
            out_specs=pl.BlockSpec((rows, share), lambda i, at: (0, 0)),
        ),
        out_shape=shape(rows, share),
        compiler_params=PARAMS,
        cost_estimate=cost(8 * rows * share, 10 * rows * share),
    )(quarter.reshape(1), own, *parts, tokens, root, stat)


def outer_kernel(at_ref, *refs):
    *blocks, mine_ref, other_ref, out_ref = refs
    n = mine_ref.shape[0]
    total = None
    for i, block in enumerate(blocks):
        g_ref = mine_ref if i < n else other_ref
        part = jnp.dot(block[...], g_ref[at_ref[i % n]], preferred_element_type=F32)
        total = part if total is None else total + part
    out_ref[...] = total.astype(BF)


def outer(blocks, order, mine, other):
    depth, rows = blocks[0].shape
    cols = mine.shape[2]
    tile = 256
    return pl.pallas_call(
        outer_kernel,
        grid_spec=pltpu.PrefetchScalarGridSpec(
            num_scalar_prefetch=1,
            grid=(depth // tile,),
            in_specs=[pl.BlockSpec((tile, rows), lambda i, at: (i, 0))] * len(blocks)
            + [pl.BlockSpec(mine.shape, lambda i, at: (0, 0, 0))] * 2,
            out_specs=pl.BlockSpec((tile, cols), lambda i, at: (i, 0)),
        ),
        out_shape=shape(depth, cols),
        compiler_params=PARAMS,
        cost_estimate=cost(
            2 * len(blocks) * depth * rows * cols, 2 * len(blocks) * depth * rows
        ),
    )(order, *blocks, mine, other)


def shift(x, axis, by):
    n = lax.axis_size(axis)
    return lax.ppermute(x, axis, [(i, (i + by) % n) for i in range(n)])


def per_device(tokens, weights, cotangent):
    _, rows, width = tokens.shape
    w_rows, _, cols = weights.shape
    heads = cols // HS
    n_x = lax.axis_size("x")
    n_t = lax.axis_size("zh")
    at_core, at_x, at_t = (lax.axis_index(a) for a in ("core", "x", "zh"))
    share = width // n_t
    tokens = tokens.reshape(rows, width)

    full_w = lax.all_gather(
        weights.reshape(w_rows, 3 * cols), ("y", "zl", "core"), axis=0, tiled=True
    )

    normed, root, mine, given = unit_rows(tokens, at_core, w_rows)
    theirs = shift(given, "core", 1)
    left_m, right_m = shift(mine, "x", 1), shift(mine, "x", -1)
    left_t, right_t = shift(theirs, "x", 1), shift(theirs, "x", -1)
    far_m, far_t = shift(left_m, "x", 1), shift(right_t, "x", -1)
    blocks = (mine, left_m, right_m, far_m, theirs, left_t, right_t, far_t)
    order = jnp.stack([(at_x + by) % n_x for by in (0, n_x - 1, 1, 2)])

    dout = cotangent.reshape(rows, heads, HS).transpose(1, 0, 2)
    dout = lax.all_to_all(dout, "x", 0, 0, tiled=True).reshape(n_x * rows, HS)

    proj = project(normed, full_w, heads)
    qkv = lax.all_to_all(proj, "x", 0, 0, tiled=True).reshape(n_x * rows, 3 * HS)
    att, head_grads = attention(qkv, dout)

    head_grads = head_grads.reshape(n_x, rows, 3 * HS)
    grads = lax.all_to_all(head_grads, "x", 0, 0, tiled=True)

    half = share // 2
    far = norm_quarter(grads, full_w, (at_t + 2) % n_t, share)
    up = shift(far[:half], "zh", 1)
    down = shift(far[half:], "zh", -1)
    to_up = norm_quarter(grads, full_w, (at_t + 1) % n_t, share)
    up_1 = shift(to_up[half:], "zh", 1)
    to_down = norm_quarter(grads, full_w, (at_t + n_t - 1) % n_t, share)
    down_0 = shift(to_down[:half], "zh", -1)
    own = norm_quarter(grads, full_w, at_t, share)
    stat = jnp.sum(grads.astype(F32) * proj.astype(F32), (0, 2)) * (1.0 / width)
    stat = stat + sum(shift(stat, "zh", by) for by in range(1, n_t))
    up_0 = shift((to_up[:half].astype(F32) + up.astype(F32)).astype(BF), "zh", 1)
    down_1 = shift((to_down[half:].astype(F32) + down.astype(F32)).astype(BF), "zh", -1)
    token_grad = finish(
        at_t, own, (up_0, up_1, down_0, down_1), tokens, root, stat.reshape(rows, 1)
    )

    other_grads = shift(head_grads, "core", 1)
    part = outer(blocks, order, head_grads, other_grads)
    part = lax.all_to_all(part, ("y", "zl"), 0, 0, tiled=True)
    part = jnp.sum(part.reshape(-1, w_rows, 3 * HS).astype(F32), 0).astype(BF)
    part = jnp.broadcast_to(part, (n_x,) + part.shape)
    last = jnp.concatenate([part, att.reshape(n_x, rows, HS)], 2)
    last = lax.all_to_all(last, "x", 0, 0, tiled=True)
    weight_grad = last[:, :, : 3 * HS].reshape(heads, w_rows, 3, HS).transpose(1, 2, 0, 3)
    attended = last[:, :, 3 * HS :].transpose(1, 0, 2).reshape(1, rows, cols)
    return attended, token_grad[None], weight_grad.reshape(weights.shape).astype(F32)


def solution(mesh):
    fine = Mesh(mesh.devices.reshape(4, 2, 2, 4, 4), ("y", "zl", "core", "x", "zh"))
    dp = ("y", "zl", "core")
    return jax.shard_map(
        per_device,
        mesh=fine,
        in_specs=(P(dp, "x", None), P(dp, None, "zh"), P(dp, "x", "zh")),
        out_specs=(P(dp, "x", "zh"), P(dp, "x", "zh"), P(dp, None, "zh")),
        check_vma=False,
    )
```

time: 244 us -> 252 us (1.033)
  the two profiles are of different devices: /device:TPU:34 before, /device:TPU:8 now
where the time goes in v2:
time: 252 us; the launch traced here: 249 us
  waiting for transfers between devices  116 us (46%)
  starting transfers between devices  51.3 us (20%)
  Pallas kernels  45.4 us (18%)
  between operations  14.2 us (6%)
  local copies, waits for them, and re-layouts  13.4 us (5%)
  other arithmetic  8.55 us (3%)
    all_gather x1, waiting for transfers between devices, per_device(): lax.all_gather(weights.reshape(w_rows, 3 * cols), ('y', 'zl', 'core'), ax...  64 us
    ppermute x17, waiting for transfers between devices, shift(): return lax.ppermute(x, axis, [(i, (i + by) % n) for i in range(n)])  45.1 us
    ppermute x17, starting transfers between devices, shift(): return lax.ppermute(x, axis, [(i, (i + by) % n) for i in range(n)])  30.2 us
    pallas_call x4, Pallas kernels, norm_quarter(): pl.pallas_call(norm_kernel, grid_spec=pltpu.PrefetchScalarGridSpec(num_sc...  11.3 us
    pallas_call x1, Pallas kernels, project(): pl.pallas_call(project_kernel, grid=(depth // tile,), in_specs=[pl.BlockS...  10.7 us
    pallas_call x1, Pallas kernels, outer(): pl.pallas_call(outer_kernel, grid_spec=pltpu.PrefetchScalarGridSpec(num_s...  10.4 us
    pallas_call x1, Pallas kernels, attention(): pl.pallas_call(functools.partial(attention_kernel, min(256, n)), out_shap...  7.42 us
    all_to_all x1, waiting for transfers between devices, per_device(): lax.all_to_all(proj, 'x', 0, 0, tiled=True).reshape(n_x * rows, 3 * HS)  7 us
  transfers between devices with their start and end apart: 23, of which 9 were waited for; matrix products, arithmetic and copies ran while one was open for 6% of the time, Pallas kernels for 18%

profile of v2, /device:TPU:8, one launch (start us, length us, event | category | flops | bytes accessed | tf_op | source)
XLA Modules:
  0.0 249.0 jit_solution(14792730517197720680)
XLA Ops:
  7.2 0.0 all-gather.2.cloned.1.call-start
  7.2 1.4 copy.23
  8.6 1.2 copy.24
  9.8 0.0 all-gather.2.cloned.1.call-update
  9.8 3.0 %shard_map.58 = (bf16[256,4096]{1,0:T(8,128)(2,1)S(1)}, f32[256,1]{1,0:T(8,128)S(1)}, bf16[2048,256]{1,0:T(8,128)(2,1)S(1)}, bf16[2048,256]{1,0:T(8,128)(2,1)S(1)}) custom-call(s32[1]{0:T(128)} %bitcast.4.at_ref, bf16[256,4096]{1,0:T(8,128)(2,1)} %bitcast.29), custom_call_target="tpu_custom_call" | custom-call | flops 6291456 | bytes 6291456 | tf_op jit(solution)/shard_map/pallas_call | solution.py:45
  12.8 0.1 collective-permute-start.3
  12.9 1.6 collective-permute-start
  14.5 1.2 collective-permute-done.3.refs_4_
  15.7 2.8 %collective-permute-start.5 = (bf16[2048,256]{1,0:T(8,128)(2,1)}, bf16[2048,256]{1,0:T(8,128)(2,1)}, u32[]{:S(2)}, u32[]{:S(2)}) collective-permute-start(bf16[2048,256]{1,0:T(8,128)(2,1)} %collective-permute-done.3.refs_4_), channel_id=1, source_target_pairs={{0,12},{4,0},{8,4},{12,8},{1,13},{5,1},{9,5},{13,9},{2,14},{6,2},{... | collective-permute-start | bytes 3145736 | tf_op jit(solution)/shard_map/ppermute | solution.py:257
  18.5 1.0 reshape.63
  19.5 0.7 copy.33
  20.2 3.4 %all-to-all-start.1 = ((bf16[4,256,128]{2,1,0:T(8,128)(2,1)}), bf16[4,256,128]{2,1,0:T(8,128)(2,1)S(1)}, u32[]{:S(2)}, u32[]{:S(2)}) async-start(bf16[4,256,128]{2,1,0:T(8,128)(2,1)} %bitcast.38), calls=%async_computation.1 | async-start | bytes 524288 | tf_op jit(solution)/shard_map/all_to_all | solution.py:283
  23.6 64.0 %all-gather.2.cloned.1.call-done.w_ref = bf16[4096,1536]{1,0:T(8,128)(2,1)} async-done(((bf16[256,1536]{1,0:T(8,128)(2,1)}), bf16[4096,1536]{1,0:T(8,128)(2,1)}) %all-gather.2.cloned.1.call-update) | async-done | bytes 12582928 | tf_op jit(solution)/shard_map/all_gather | solution.py:270
  87.6 10.7 %shard_map.59 = bf16[4,256,384]{2,1,0:T(8,128)(2,1)} custom-call(bf16[256,4096]{1,0:T(8,128)(2,1)S(1)} %get-tuple-element.11.a_ref, bf16[4096,1536]{1,0:T(8,128)(2,1)} %all-gather.2.cloned.1.call-done.w_ref), custom_call_target="tpu_custom_call" | custom-call | flops 3221225472 | bytes 14680064 | tf_op jit(solution)/shard_map/pallas_call | solution.py:94
  98.3 4.2 %all-to-all-start = ((bf16[4,256,384]{2,1,0:T(8,128)(2,1)}), bf16[4,256,384]{2,1,0:T(8,128)(2,1)S(1)}, u32[]{:S(2)}, u32[]{:S(2)}) async-start(bf16[4,256,384]{2,1,0:T(8,128)(2,1)} %shard_map.59), calls=%async_computation | async-start | bytes 1572864 | tf_op jit(solution)/shard_map/all_to_all | solution.py:286
  102.5 3.2 %collective-permute-start.1 = (bf16[2048,256]{1,0:T(8,128)(2,1)S(1)}, bf16[2048,256]{1,0:T(8,128)(2,1)S(1)}, u32[]{:S(2)}, u32[]{:S(2)}) collective-permute-start(bf16[2048,256]{1,0:T(8,128)(2,1)S(1)} %get-tuple-element.9.refs_0_), channel_id=1, source_target_pairs={{0,12},{4,0},{8,4},{12,8},{1,13},{5,1},{9,5},{13,9},{2,14},{6,2},{... | collective-permute-start | bytes 3145736 | tf_op jit(solution)/shard_map/ppermute | solution.py:257
  105.8 0.8 collective-permute-start.2
  106.6 2.7 %collective-permute-start.6 = (bf16[2048,256]{1,0:T(8,128)(2,1)}, bf16[2048,256]{1,0:T(8,128)(2,1)}, u32[]{:S(2)}, u32[]{:S(2)}) collective-permute-start(bf16[2048,256]{1,0:T(8,128)(2,1)} %collective-permute-done.5.refs_6_), channel_id=1, source_target_pairs={{0,12},{4,0},{8,4},{12,8},{1,13},{5,1},{9,5},{13,9},{2,14},{6,2},{... | collective-permute-start | bytes 3145736 | tf_op jit(solution)/shard_map/ppermute | solution.py:257
  109.3 7.0 %all-to-all-done = bf16[4,256,384]{2,1,0:T(8,128)(2,1)S(1)} async-done(((bf16[4,256,384]{2,1,0:T(8,128)(2,1)}), bf16[4,256,384]{2,1,0:T(8,128)(2,1)S(1)}, u32[]{:S(2)}, u32[]{:S(2)}) %all-to-all-start) | async-done | bytes 786464 | tf_op jit(solution)/shard_map/all_to_all | solution.py:286
  116.3 7.4 %shard_map.60 = (bf16[1024,128]{1,0:T(8,128)(2,1)S(1)}, bf16[1024,384]{1,0:T(8,128)(2,1)}) custom-call(bf16[1024,384]{1,0:T(8,128)(2,1)S(1)} %bitcast.31, bf16[1024,128]{1,0:T(8,128)(2,1)S(1)} %bitcast.33), custom_call_target="tpu_custom_call" | custom-call | flops 1879048192 | bytes 2097152 | tf_op jit(solution)/shard_map/pallas_call | solution.py:146
  123.7 3.5 %all-to-all-start.4 = ((bf16[4,256,384]{2,1,0:T(8,128)(2,1)}), bf16[4,256,384]{2,1,0:T(8,128)(2,1)S(1)}, u32[]{:S(2)}, u32[]{:S(2)}) async-start(bf16[4,256,384]{2,1,0:T(8,128)(2,1)} %bitcast.10.refs_8_), calls=%async_computation.4 | async-start | bytes 1572864 | tf_op jit(solution)/shard_map/all_to_all | solution.py:290
  127.2 0.1 pad_add_fusion.at_ref
  127.3 9.9 %collective-permute-done.1.refs_2_ = bf16[2048,256]{1,0:T(8,128)(2,1)S(1)} collective-permute-done((bf16[2048,256]{1,0:T(8,128)(2,1)S(1)}, bf16[2048,256]{1,0:T(8,128)(2,1)S(1)}, u32[]{:S(2)}, u32[]{:S(2)}) %collective-permute-start.1) | collective-permute-done | bytes 1048608 | tf_op jit(solution)/shard_map/ppermute | solution.py:257
  137.2 23.7 %collective-permute-done.2.refs_3_ = bf16[2048,256]{1,0:T(8,128)(2,1)} collective-permute-done((bf16[2048,256]{1,0:T(8,128)(2,1)}, bf16[2048,256]{1,0:T(8,128)(2,1)}, u32[]{:S(2)}, u32[]{:S(2)}) %collective-permute-start.2) | collective-permute-done | bytes 1048608 | tf_op jit(solution)/shard_map/ppermute | solution.py:257
  161.0 10.4 %shard_map.61 = bf16[2048,384]{1,0:T(8,128)(2,1)} custom-call(s32[4]{0:T(128)S(1)} %pad_add_fusion.at_ref, bf16[2048,256]{1,0:T(8,128)(2,1)S(1)} %get-tuple-element.9.refs_0_, bf16[2048,256]{1,0:T(8,128)(2,1)} %collective-permute-done.refs_1_, bf16[2048,256]{1,0:T(8,128)(2,1)S(1)} %collective-permute-done.1.refs_2_, ...), custom_call_target="tpu_custom_call" | custom-call | flops 3221225472 | bytes 8388608 | tf_op jit(solution)/shard_map/pallas_call | solution.py:238
  171.4 5.6 %all-to-all-start.2 = ((bf16[8,256,384]{2,1,0:T(8,128)(2,1)}), bf16[8,256,384]{2,1,0:T(8,128)(2,1)S(1)}, u32[]{:S(2)}, u32[]{:S(2)}) async-start(bf16[8,256,384]{2,1,0:T(8,128)(2,1)} %bitcast.37), calls=%async_computation.2 | async-start | bytes 3145728 | tf_op jit(solution)/shard_map/all_to_all | solution.py:311
  177.1 0.8 copy.27
  177.9 1.4 multiply_reduce_fusion
  179.4 0.6 broadcast_multiply_fusion
  179.9 2.5 %collective-permute-start.14 = (f32[256]{0:T(256)}, f32[256]{0:T(256)S(1)}, u32[]{:S(2)}, u32[]{:S(2)}) collective-permute-start(f32[256]{0:T(256)} %broadcast_multiply_fusion), channel_id=1, source_target_pairs={{0,1},{1,2},{2,3},{3,0},{4,5},{5,6},{6,7},{7,4},{8,9},{9,10},{10,1... | collective-permute-start | bytes 3080 | tf_op jit(solution)/shard_map/ppermute | solution.py:257
  182.5 3.0 %collective-permute-start.15 = (f32[256]{0:T(256)}, f32[256]{0:T(256)S(1)}, u32[]{:S(2)}, u32[]{:S(2)}) collective-permute-start(f32[256]{0:T(256)} %broadcast_multiply_fusion), channel_id=1, source_target_pairs={{0,2},{1,3},{2,0},{3,1},{4,6},{5,7},{6,4},{7,5},{8,10},{9,11},{10,... | collective-permute-start | bytes 3080 | tf_op jit(solution)/shard_map/ppermute | solution.py:257
  185.5 3.4 %collective-permute-start.16 = (f32[256]{0:T(256)}, f32[256]{0:T(256)S(1)}, u32[]{:S(2)}, u32[]{:S(2)}) collective-permute-start(f32[256]{0:T(256)} %broadcast_multiply_fusion), channel_id=1, source_target_pairs={{0,3},{1,0},{2,1},{3,2},{4,7},{5,4},{6,5},{7,6},{8,11},{9,8},{10,9... | collective-permute-start | bytes 3080 | tf_op jit(solution)/shard_map/ppermute | solution.py:257
  188.9 2.8 %shard_map.64 = bf16[1024,256]{1,0:T(8,128)(2,1)S(1)} custom-call(s32[1]{0:T(128)} %bitcast.17.at_ref, bf16[4,256,384]{2,1,0:T(8,128)(2,1)S(1)} %all-to-all-done.4.g_ref, bf16[4096,1536]{1,0:T(8,128)(2,1)} %all-gather.2.cloned.1.call-done.w_ref), custom_call_target="tpu_custom_call" | custom-call | flops 805306368 | bytes 4456448 | tf_op jit(solution)/shard_map/pallas_call | solution.py:174
  191.7 0.8 fusion
  192.5 0.1 collective-permute-start.12
  192.6 2.9 %collective-permute-start.8 = (bf16[512,256]{1,0:T(8,128)(2,1)}, bf16[512,256]{1,0:T(8,128)(2,1)}, u32[]{:S(2)}, u32[]{:S(2)}) collective-permute-start(bf16[512,256]{1,0:T(8,128)(2,1)} %get-tuple-element.25), channel_id=1, source_target_pairs={{0,1},{1,2},{2,3},{3,0},{4,5},{5,6},{6,7},{7,4},{8,9},{9,10},{10,1... | collective-permute-start | bytes 786440 | tf_op jit(solution)/shard_map/ppermute | solution.py:257
  195.4 2.8 %shard_map.63 = bf16[1024,256]{1,0:T(8,128)(2,1)S(1)} custom-call(s32[1]{0:T(128)} %bitcast.16.at_ref, bf16[4,256,384]{2,1,0:T(8,128)(2,1)S(1)} %all-to-all-done.4.g_ref, bf16[4096,1536]{1,0:T(8,128)(2,1)} %all-gather.2.cloned.1.call-done.w_ref), custom_call_target="tpu_custom_call" | custom-call | flops 805306368 | bytes 4456448 | tf_op jit(solution)/shard_map/pallas_call | solution.py:174
  198.2 0.7 slice.35
  198.9 2.8 %shard_map.65 = bf16[1024,256]{1,0:T(8,128)(2,1)S(1)} custom-call(s32[1]{0:T(128)} %bitcast.18.at_ref, bf16[4,256,384]{2,1,0:T(8,128)(2,1)S(1)} %all-to-all-done.4.g_ref, bf16[4096,1536]{1,0:T(8,128)(2,1)} %all-gather.2.cloned.1.call-done.w_ref), custom_call_target="tpu_custom_call" | custom-call | flops 805306368 | bytes 4456448 | tf_op jit(solution)/shard_map/pallas_call | solution.py:174
  201.7 0.7 slice.36
  202.5 0.9 reduce_sum.21
  203.4 1.1 copy.26
  204.5 0.1 broadcast_in_dim.6
  204.5 2.0 pad_maximum_fusion
  206.5 4.3 %all-to-all-start.3 = ((bf16[4,256,512]{1,2,0:T(8,128)(2,1)}), bf16[4,256,512]{1,2,0:T(8,128)(2,1)}, u32[]{:S(2)}, u32[]{:S(2)}) async-start(bf16[4,256,512]{1,2,0:T(8,128)(2,1)} %pad_maximum_fusion), calls=%async_computation.3 | async-start | bytes 2097152 | tf_op jit(solution)/shard_map/all_to_all | solution.py:315
  210.8 2.7 %collective-permute-start.10 = (bf16[512,256]{1,0:T(8,128)(2,1)}, bf16[512,256]{1,0:T(8,128)(2,1)}, u32[]{:S(2)}, u32[]{:S(2)}) collective-permute-start(bf16[512,256]{1,0:T(8,128)(2,1)} %slice.35), channel_id=1, source_target_pairs={{0,1},{1,2},{2,3},{3,0},{4,5},{5,6},{6,7},{7,4},{8,9},{9,10},{10,1... | collective-permute-start | bytes 786440 | tf_op jit(solution)/shard_map/ppermute | solution.py:257
  213.5 1.7 add_convert_fusion
  215.2 1.5 collective-permute-start.11
  216.7 1.7 add_convert_fusion.1
  218.4 2.1 collective-permute-start.13
  220.6 0.8 collective-permute-start.9
  221.4 2.9 %shard_map.62.own_ref = bf16[1024,256]{1,0:T(8,128)(2,1)S(1)} custom-call(s32[1]{0:T(128)} %bitcast.15.at_ref, bf16[4,256,384]{2,1,0:T(8,128)(2,1)S(1)} %all-to-all-done.4.g_ref, bf16[4096,1536]{1,0:T(8,128)(2,1)} %all-gather.2.cloned.1.call-done.w_ref), custom_call_target="tpu_custom_call" | custom-call | flops 805306368 | bytes 4456448 | tf_op jit(solution)/shard_map/pallas_call | solution.py:174
  224.3 0.1 copy.28.stat_ref
  224.5 2.5 %collective-permute-done.10.a1_ref = bf16[512,256]{1,0:T(8,128)(2,1)} collective-permute-done((bf16[512,256]{1,0:T(8,128)(2,1)}, bf16[512,256]{1,0:T(8,128)(2,1)}, u32[]{:S(2)}, u32[]{:S(2)}) %collective-permute-start.10) | collective-permute-done | bytes 262176 | tf_op jit(solution)/shard_map/ppermute | solution.py:257
  227.0 1.8 collective-permute-done.11.b0_ref
  228.8 5.0 %collective-permute-done.13.b1_ref = bf16[512,256]{1,0:T(8,128)(2,1)} collective-permute-done((bf16[512,256]{1,0:T(8,128)(2,1)}, bf16[512,256]{1,0:T(8,128)(2,1)}, u32[]{:S(2)}, u32[]{:S(2)}) %collective-permute-start.13) | collective-permute-done | bytes 262176 | tf_op jit(solution)/shard_map/ppermute | solution.py:257
  233.8 0.9 collective-permute-done.9.a0_ref
  234.7 2.6 %shard_map.66 = bf16[256,1024]{1,0:T(8,128)(2,1)} custom-call(s32[1]{0:T(128)} %bitcast.15.at_ref, bf16[1024,256]{1,0:T(8,128)(2,1)S(1)} %shard_map.62.own_ref, bf16[512,256]{1,0:T(8,128)(2,1)} %collective-permute-done.9.a0_ref, bf16[512,256]{1,0:T(8,128)(2,1)} %collective-permute-done.10.a1_ref, bf16[512,256]{1,0:T(8,128)(2,1)} %collective-permute-done.11.b0_ref, ...), custom_call_target="tpu_custom_call" | custom-call | flops 2097152 | bytes 2621440 | tf_op jit(solution)/shard_map/pallas_call | solution.py:206
  237.3 1.2 slice.39
  238.4 0.1 convert_bitcast_fusion
  238.6 0.1 copy.29
  238.7 1.6 copy.31
  240.3 1.0 slice.32
  241.3 0.8 copy.30
  (19 shorter events, 0.1 us)
Async XLA Ops:
  7.2 80.5 %all-gather.2.cloned.1.call-start = ((), (), s32[]{:S(2)}) async-start(), calls=%async_computation.5 | async-start | bytes 13369344 | tf_op jit(solution)/shard_map/all_gather | solution.py:270
  12.8 2.9 %collective-permute-start.3 = (bf16[2048,256]{1,0:T(8,128)(2,1)S(1)}, bf16[2048,256]{1,0:T(8,128)(2,1)}, u32[]{:S(2)}, u32[]{:S(2)}) collective-permute-start(bf16[2048,256]{1,0:T(8,128)(2,1)S(1)} %get-tuple-element.10), channel_id=1, source_target_pairs={{0,16},{16,0},{1,17},{17,1},{2,18},{18,2},{3,19},{19,3},{4,20},{20... | collective-permute-start | bytes 3145736 | tf_op jit(solution)/shard_map/ppermute | solution.py:257
  12.9 92.8 %collective-permute-start = (bf16[2048,256]{1,0:T(8,128)(2,1)S(1)}, bf16[2048,256]{1,0:T(8,128)(2,1)}, u32[]{:S(2)}, u32[]{:S(2)}) collective-permute-start(bf16[2048,256]{1,0:T(8,128)(2,1)S(1)} %get-tuple-element.9.refs_0_), channel_id=1, source_target_pairs={{0,4},{4,8},{8,12},{12,0},{1,5},{5,9},{9,13},{13,1},{2,6},{6,10},{... | collective-permute-start | bytes 3145736 | tf_op jit(solution)/shard_map/ppermute | solution.py:257
  15.7 90.9 %collective-permute-start.5 = (bf16[2048,256]{1,0:T(8,128)(2,1)}, bf16[2048,256]{1,0:T(8,128)(2,1)}, u32[]{:S(2)}, u32[]{:S(2)}) collective-permute-start(bf16[2048,256]{1,0:T(8,128)(2,1)} %collective-permute-done.3.refs_4_), channel_id=1, source_target_pairs={{0,12},{4,0},{8,4},{12,8},{1,13},{5,1},{9,5},{13,9},{2,14},{6,2},{... | collective-permute-start | bytes 3145736 | tf_op jit(solution)/shard_map/ppermute | solution.py:257
  20.2 78.1 %all-to-all-start.1 = ((bf16[4,256,128]{2,1,0:T(8,128)(2,1)}), bf16[4,256,128]{2,1,0:T(8,128)(2,1)S(1)}, u32[]{:S(2)}, u32[]{:S(2)}) async-start(bf16[4,256,128]{2,1,0:T(8,128)(2,1)} %bitcast.38), calls=%async_computation.1 | async-start | bytes 524288 | tf_op jit(solution)/shard_map/all_to_all | solution.py:283
  98.3 18.0 %all-to-all-start = ((bf16[4,256,384]{2,1,0:T(8,128)(2,1)}), bf16[4,256,384]{2,1,0:T(8,128)(2,1)S(1)}, u32[]{:S(2)}, u32[]{:S(2)}) async-start(bf16[4,256,384]{2,1,0:T(8,128)(2,1)} %shard_map.59), calls=%async_computation | async-start | bytes 1572864 | tf_op jit(solution)/shard_map/all_to_all | solution.py:286
  102.5 34.7 %collective-permute-start.1 = (bf16[2048,256]{1,0:T(8,128)(2,1)S(1)}, bf16[2048,256]{1,0:T(8,128)(2,1)S(1)}, u32[]{:S(2)}, u32[]{:S(2)}) collective-permute-start(bf16[2048,256]{1,0:T(8,128)(2,1)S(1)} %get-tuple-element.9.refs_0_), channel_id=1, source_target_pairs={{0,12},{4,0},{8,4},{12,8},{1,13},{5,1},{9,5},{13,9},{2,14},{6,2},{... | collective-permute-start | bytes 3145736 | tf_op jit(solution)/shard_map/ppermute | solution.py:257
  105.8 55.2 %collective-permute-start.4 = (bf16[2048,256]{1,0:T(8,128)(2,1)}, bf16[2048,256]{1,0:T(8,128)(2,1)}, u32[]{:S(2)}, u32[]{:S(2)}) collective-permute-start(bf16[2048,256]{1,0:T(8,128)(2,1)} %collective-permute-done.3.refs_4_), channel_id=1, source_target_pairs={{0,4},{4,8},{8,12},{12,0},{1,5},{5,9},{9,13},{13,1},{2,6},{6,10},{... | collective-permute-start | bytes 3145736 | tf_op jit(solution)/shard_map/ppermute | solution.py:257
  105.8 55.2 %collective-permute-start.2 = (bf16[2048,256]{1,0:T(8,128)(2,1)}, bf16[2048,256]{1,0:T(8,128)(2,1)}, u32[]{:S(2)}, u32[]{:S(2)}) collective-permute-start(bf16[2048,256]{1,0:T(8,128)(2,1)} %collective-permute-done.refs_1_), channel_id=1, source_target_pairs={{0,4},{4,8},{8,12},{12,0},{1,5},{5,9},{9,13},{13,1},{2,6},{6,10},{... | collective-permute-start | bytes 3145736 | tf_op jit(solution)/shard_map/ppermute | solution.py:257
  106.6 54.4 %collective-permute-start.6 = (bf16[2048,256]{1,0:T(8,128)(2,1)}, bf16[2048,256]{1,0:T(8,128)(2,1)}, u32[]{:S(2)}, u32[]{:S(2)}) collective-permute-start(bf16[2048,256]{1,0:T(8,128)(2,1)} %collective-permute-done.5.refs_6_), channel_id=1, source_target_pairs={{0,12},{4,0},{8,4},{12,8},{1,13},{5,1},{9,5},{13,9},{2,14},{6,2},{... | collective-permute-start | bytes 3145736 | tf_op jit(solution)/shard_map/ppermute | solution.py:257
  123.7 37.3 %collective-permute-start.7 = (bf16[4,256,384]{2,1,0:T(8,128)(2,1)}, bf16[4,256,384]{2,1,0:T(8,128)(2,1)}, u32[]{:S(2)}, u32[]{:S(2)}) collective-permute-start(bf16[4,256,384]{2,1,0:T(8,128)(2,1)} %bitcast.10.refs_8_), channel_id=1, source_target_pairs={{0,16},{16,0},{1,17},{17,1},{2,18},{18,2},{3,19},{19,3},{4,20},{20... | collective-permute-start | bytes 2359304 | tf_op jit(solution)/shard_map/ppermute | solution.py:257
  123.7 47.7 %all-to-all-start.4 = ((bf16[4,256,384]{2,1,0:T(8,128)(2,1)}), bf16[4,256,384]{2,1,0:T(8,128)(2,1)S(1)}, u32[]{:S(2)}, u32[]{:S(2)}) async-start(bf16[4,256,384]{2,1,0:T(8,128)(2,1)} %bitcast.10.refs_8_), calls=%async_computation.4 | async-start | bytes 1572864 | tf_op jit(solution)/shard_map/all_to_all | solution.py:290
  171.4 31.0 %all-to-all-start.2 = ((bf16[8,256,384]{2,1,0:T(8,128)(2,1)}), bf16[8,256,384]{2,1,0:T(8,128)(2,1)S(1)}, u32[]{:S(2)}, u32[]{:S(2)}) async-start(bf16[8,256,384]{2,1,0:T(8,128)(2,1)} %bitcast.37), calls=%async_computation.2 | async-start | bytes 3145728 | tf_op jit(solution)/shard_map/all_to_all | solution.py:311
  179.9 38.5 %collective-permute-start.14 = (f32[256]{0:T(256)}, f32[256]{0:T(256)S(1)}, u32[]{:S(2)}, u32[]{:S(2)}) collective-permute-start(f32[256]{0:T(256)} %broadcast_multiply_fusion), channel_id=1, source_target_pairs={{0,1},{1,2},{2,3},{3,0},{4,5},{5,6},{6,7},{7,4},{8,9},{9,10},{10,1... | collective-permute-start | bytes 3080 | tf_op jit(solution)/shard_map/ppermute | solution.py:257
  182.5 38.1 %collective-permute-start.15 = (f32[256]{0:T(256)}, f32[256]{0:T(256)S(1)}, u32[]{:S(2)}, u32[]{:S(2)}) collective-permute-start(f32[256]{0:T(256)} %broadcast_multiply_fusion), channel_id=1, source_target_pairs={{0,2},{1,3},{2,0},{3,1},{4,6},{5,7},{6,4},{7,5},{8,10},{9,11},{10,... | collective-permute-start | bytes 3080 | tf_op jit(solution)/shard_map/ppermute | solution.py:257
  185.5 38.8 %collective-permute-start.16 = (f32[256]{0:T(256)}, f32[256]{0:T(256)S(1)}, u32[]{:S(2)}, u32[]{:S(2)}) collective-permute-start(f32[256]{0:T(256)} %broadcast_multiply_fusion), channel_id=1, source_target_pairs={{0,3},{1,0},{2,1},{3,2},{4,7},{5,4},{6,5},{7,6},{8,11},{9,8},{10,9... | collective-permute-start | bytes 3080 | tf_op jit(solution)/shard_map/ppermute | solution.py:257
  192.5 18.3 %collective-permute-start.12 = (bf16[512,256]{1,0:T(8,128)(2,1)}, bf16[512,256]{1,0:T(8,128)(2,1)}, u32[]{:S(2)}, u32[]{:S(2)}) collective-permute-start(bf16[512,256]{1,0:T(8,128)(2,1)} %get-tuple-element.24), channel_id=1, source_target_pairs={{0,3},{1,0},{2,1},{3,2},{4,7},{5,4},{6,5},{7,6},{8,11},{9,8},{10,9... | collective-permute-start | bytes 786440 | tf_op jit(solution)/shard_map/ppermute | solution.py:257
  192.6 22.7 %collective-permute-start.8 = (bf16[512,256]{1,0:T(8,128)(2,1)}, bf16[512,256]{1,0:T(8,128)(2,1)}, u32[]{:S(2)}, u32[]{:S(2)}) collective-permute-start(bf16[512,256]{1,0:T(8,128)(2,1)} %get-tuple-element.25), channel_id=1, source_target_pairs={{0,1},{1,2},{2,3},{3,0},{4,5},{5,6},{6,7},{7,4},{8,9},{9,10},{10,1... | collective-permute-start | bytes 786440 | tf_op jit(solution)/shard_map/ppermute | solution.py:257
  206.5 30.7 %all-to-all-start.3 = ((bf16[4,256,512]{1,2,0:T(8,128)(2,1)}), bf16[4,256,512]{1,2,0:T(8,128)(2,1)}, u32[]{:S(2)}, u32[]{:S(2)}) async-start(bf16[4,256,512]{1,2,0:T(8,128)(2,1)} %pad_maximum_fusion), calls=%async_computation.3 | async-start | bytes 2097152 | tf_op jit(solution)/shard_map/all_to_all | solution.py:315
  210.8 16.2 %collective-permute-start.10 = (bf16[512,256]{1,0:T(8,128)(2,1)}, bf16[512,256]{1,0:T(8,128)(2,1)}, u32[]{:S(2)}, u32[]{:S(2)}) collective-permute-start(bf16[512,256]{1,0:T(8,128)(2,1)} %slice.35), channel_id=1, source_target_pairs={{0,1},{1,2},{2,3},{3,0},{4,5},{5,6},{6,7},{7,4},{8,9},{9,10},{10,1... | collective-permute-start | bytes 786440 | tf_op jit(solution)/shard_map/ppermute | solution.py:257
  215.2 13.6 %collective-permute-start.11 = (bf16[512,256]{1,0:T(8,128)(2,1)}, bf16[512,256]{1,0:T(8,128)(2,1)}, u32[]{:S(2)}, u32[]{:S(2)}) collective-permute-start(bf16[512,256]{1,0:T(8,128)(2,1)} %slice.36), channel_id=1, source_target_pairs={{0,3},{1,0},{2,1},{3,2},{4,7},{5,4},{6,5},{7,6},{8,11},{9,8},{10,9... | collective-permute-start | bytes 786440 | tf_op jit(solution)/shard_map/ppermute | solution.py:257
  218.4 15.4 %collective-permute-start.13 = (bf16[512,256]{1,0:T(8,128)(2,1)}, bf16[512,256]{1,0:T(8,128)(2,1)}, u32[]{:S(2)}, u32[]{:S(2)}) collective-permute-start(bf16[512,256]{1,0:T(8,128)(2,1)} %add_convert_fusion), channel_id=1, source_target_pairs={{0,3},{1,0},{2,1},{3,2},{4,7},{5,4},{6,5},{7,6},{8,11},{9,8},{10,9... | collective-permute-start | bytes 786440 | tf_op jit(solution)/shard_map/ppermute | solution.py:257
  220.6 14.1 %collective-permute-start.9 = (bf16[512,256]{1,0:T(8,128)(2,1)}, bf16[512,256]{1,0:T(8,128)(2,1)}, u32[]{:S(2)}, u32[]{:S(2)}) collective-permute-start(bf16[512,256]{1,0:T(8,128)(2,1)} %add_convert_fusion.1), channel_id=1, source_target_pairs={{0,1},{1,2},{2,3},{3,0},{4,5},{5,6},{6,7},{7,4},{8,9},{9,10},{10,1... | collective-permute-start | bytes 786440 | tf_op jit(solution)/shard_map/ppermute | solution.py:257
  221.4 13.3 %copy-start = (bf16[1,256,4096]{2,1,0:T(8,128)(2,1)S(1)}, bf16[1,256,4096]{2,1,0:T(8,128)(2,1)}, u32[]{:S(2)}) copy-start(bf16[1,256,4096]{2,1,0:T(8,128)(2,1)} %param.3) | copy-start | bytes 6291460
Sparse Core Ops, SparseCore 0:
  10.4 77.1 all-gather.1

commit v3 on v2

--- a/solution.py
+++ b/solution.py
@@ -66,44 +66,63 @@
     )(core.reshape(1), tokens)
 
 
-def project_kernel(a_ref, w_ref, heads_ref, acc_ref):
+def project_kernel(before, a_ref, w_ref, *refs):
+    *_, heads_ref, acc_ref = refs
     step = pl.program_id(0)
-    part = jnp.dot(a_ref[...], w_ref[...], preferred_element_type=F32)
-
-    @pl.when(step == 0)
-    def _():
-        acc_ref[...] = part
-
-    @pl.when(step > 0)
-    def _():
-        acc_ref[...] += part
+    tiles, kinds, depth, cols = w_ref.shape
+    for j in range(kinds):
+        span = slice(j * cols, (j + 1) * cols)
+        part = sum(
+            jnp.dot(
+                a_ref[:, i * depth : (i + 1) * depth],
+                w_ref[i, j],
+                preferred_element_type=F32,
+            )
+            for i in range(tiles)
+        )
+
+        @pl.when(step == 0)
+        def _(span=span, part=part):
+            acc_ref[:, span] = part
+
+        @pl.when(step > 0)
+        def _(span=span, part=part):
+            acc_ref[:, span] += part
 
     @pl.when(step == pl.num_programs(0) - 1)
     def _():
         heads = heads_ref.shape[0]
-        for j in range(3):
+        if before:
+            heads_ref[:, :, :before] = refs[0][...]
+        for j in range(kinds):
             for h in range(heads):
                 at = (j * heads + h) * HS
-                heads_ref[h, :, j * HS : (j + 1) * HS] = acc_ref[:, at : at + HS].astype(BF)
-
-
-def project(normed, flat_w, heads):
+                to = before + j * HS
+                heads_ref[h, :, to : to + HS] = acc_ref[:, at : at + HS].astype(BF)
+
+
+def project(normed, w, heads, earlier=None, after=()):
     rows, depth = normed.shape
-    cols = flat_w.shape[1]
-    tile = 512
-    return pl.pallas_call(
-        project_kernel,
-        grid=(depth // tile,),
+    n, kinds, band, cols = w.shape
+    tiles = 2
+    before = 0 if earlier is None else earlier.shape[2]
+    out = (heads, rows, before + kinds * HS)
+    more = () if earlier is None else (earlier,)
+    return pl.pallas_call(
+        functools.partial(project_kernel, before),
+        grid=(n // tiles,),
         in_specs=[
-            pl.BlockSpec((rows, tile), lambda i: (0, i)),
-            pl.BlockSpec((tile, cols), lambda i: (i, 0)),
-        ],
-        out_specs=pl.BlockSpec((heads, rows, 3 * HS), lambda i: (0, 0, 0)),
-        out_shape=shape(heads, rows, 3 * HS),
-        scratch_shapes=[pltpu.VMEM((rows, cols), F32)],
-        compiler_params=PARAMS,
-        cost_estimate=cost(2 * rows * depth * cols, 2 * (depth * cols + rows * depth)),
-    )(normed, flat_w)
+            pl.BlockSpec((rows, tiles * band), lambda i: (0, i)),
+            pl.BlockSpec((tiles, kinds, band, cols), lambda i: (i, 0, 0, 0)),
+        ]
+        + [pl.BlockSpec(m.shape, lambda i: (0, 0, 0)) for m in more]
+        + [pl.BlockSpec(memory_space=pl.ANY)] * len(after),
+        out_specs=pl.BlockSpec(out, lambda i: (0, 0, 0)),
+        out_shape=shape(*out),
+        scratch_shapes=[pltpu.VMEM((rows, kinds * cols), F32)],
+        compiler_params=PARAMS,
+        cost_estimate=cost(2 * rows * w.size, 2 * (w.size + rows * depth)),
+    )(normed, w, *more, *after)
 
 
 def attention_kernel(q_rows, qkv_ref, dout_ref, att_ref, grad_ref, dk_ref, dv_ref):
@@ -154,62 +173,136 @@
     )(qkv, dout)
 
 
-def norm_kernel(at_ref, g_ref, w_ref, out_ref, flat_ref):
-    @pl.when(pl.program_id(0) == 0)
+def write_stat(ref, at, stat):
+    ref[at:, :] = jnp.zeros((ref.shape[0] - at, ref.shape[1]), BF)
+    rest = stat
+    for i in range(3):
+        top = rest.astype(BF)
+        ref[at + i : at + i + 1, :] = top
+        rest = rest - top.astype(F32)
+
+
+def read_stat(ref, at):
+    return sum(ref[at + i : at + i + 1, :].astype(F32) for i in range(3))
+
+
+def norm_kernel(width, spots, carried, at_ref, g_ref, p_ref, qk_w, v_w, *refs):
+    refs = refs[carried:]
+    n_out = max(spot[0] for spot in spots) + 1
+    outs, stat_ref, flat_ref = refs[:n_out], refs[n_out], refs[-1]
+    step = pl.program_id(0)
+
+    @pl.when(step == 0)
     def _():
-        heads = g_ref.shape[0]
-        for j in range(3):
-            for h in range(heads):
+        heads, _, _ = g_ref.shape
+        for h in range(heads):
+            for j in range(3):
                 at = (j * heads + h) * HS
                 flat_ref[:, at : at + HS] = g_ref[h, :, j * HS : (j + 1) * HS]
-
-    out_ref[...] = dot(w_ref[...], flat_ref[...], 1, 1).astype(BF)
-
-
-def norm_quarter(grads, flat_w, quarter, share):
+        total = sum(
+            g_ref[h, :, j * HS : (j + 1) * HS].astype(F32)
+            * p_ref[h, :, j * HS : (j + 1) * HS].astype(F32)
+            for h in range(heads)
+            for j in range(3)
+        )
+        stat = jnp.sum(total.T, axis=0, keepdims=True) * (1.0 / width)
+        stat_ref[...] = stat
+        for ref in outs:
+            if ref.shape[0] % 128:
+                write_stat(ref, ref.shape[0] - 16, stat)
+
+    tiles, _, band, cols = qk_w.shape
+    pieces = [(qk_w, 0), (qk_w, 1), (v_w, 0)]
+    for i in range(tiles):
+        total = sum(
+            dot(ref[i, j], flat_ref[:, n * cols : (n + 1) * cols], 1, 1)
+            for n, (ref, j) in enumerate(pieces)
+        ).astype(BF)
+        for at_step, (which, at) in enumerate(spots):
+
+            @pl.when(step == at_step)
+            def _(ref=outs[which], at=at + i * band, total=total):
+                ref[at : at + band, :] = total
+
+
+def norm_halves(grads, proj, w_qk, w_v, halves, spots, sizes, width, carry=()):
     heads, rows, _ = grads.shape
-    cols = flat_w.shape[1]
-    tile = 512
-    tiles = share // tile
-    return pl.pallas_call(
-        norm_kernel,
+    n = len(spots)
+    _, _, band, cols = w_qk.shape
+    tiles = 2
+    whole = pl.BlockSpec(grads.shape, lambda i, at: (0, 0, 0))
+    w_spec = lambda w: pl.BlockSpec(
+        (tiles, w.shape[1], band, cols), lambda i, at: (at[i], 0, 0, 0)
+    )
+    sizes = (*sizes, 1)
+    return pl.pallas_call(
+        functools.partial(norm_kernel, width, spots, len(carry)),
         grid_spec=pltpu.PrefetchScalarGridSpec(
             num_scalar_prefetch=1,
-            grid=(tiles,),
-            in_specs=[
-                pl.BlockSpec(grads.shape, lambda i, at: (0, 0, 0)),
-                pl.BlockSpec((tile, cols), lambda i, at: (at[0] * tiles + i, 0)),
-            ],
-            out_specs=pl.BlockSpec((tile, rows), lambda i, at: (i, 0)),
-            scratch_shapes=[pltpu.VMEM((rows, cols), BF)],
+            grid=(n,),
+            in_specs=[whole, whole, w_spec(w_qk), w_spec(w_v)]
+            + [pl.BlockSpec(memory_space=pl.ANY)] * len(carry),
+            out_specs=tuple(pl.BlockSpec((s, rows), lambda i, at: (0, 0)) for s in sizes)
+            + (pl.BlockSpec(memory_space=pl.ANY),) * len(carry),
+            scratch_shapes=[pltpu.VMEM((rows, 3 * cols), BF)],
         ),
-        out_shape=shape(share, rows),
-        compiler_params=PARAMS,
-        cost_estimate=cost(2 * rows * share * cols, 2 * (share * cols + rows * (share + cols))),
-    )(quarter.reshape(1), grads, flat_w)
-
-
-def finish_kernel(at_ref, own_ref, a0_ref, a1_ref, b0_ref, b1_ref, tok_ref, root_ref, stat_ref, out_ref):
-    half = a0_ref.shape[0]
-    for i, refs in enumerate(((a0_ref, b0_ref), (a1_ref, b1_ref))):
+        out_shape=tuple(shape(s, rows) for s in sizes[:-1])
+        + (shape(1, rows, dtype=F32),)
+        + tuple(shape(*c.shape) for c in carry),
+        input_output_aliases={5 + i: len(sizes) + i for i in range(len(carry))},
+        compiler_params=PARAMS,
+        cost_estimate=cost(1, 1),
+    )(halves, grads, proj, w_qk, w_v, *carry)
+
+
+def add_kernel(up_part, up_in, down_part, down_in, stat_ref, after_ref, up_out, down_out):
+    half = up_part.shape[0]
+    for part, came, out in ((up_part, up_in, up_out), (down_part, down_in, down_out)):
+        out[:half, :] = (part[...].astype(F32) + came[:half, :].astype(F32)).astype(BF)
+    at = up_in.shape[0] - 16
+    write_stat(up_out, half, stat_ref[...] + read_stat(up_in, at))
+    write_stat(down_out, half, stat_ref[...])
+
+
+def add_messages(up_part, up_in, down_part, down_in, stat, after):
+    half, rows = up_part.shape
+    vmem = pl.BlockSpec(memory_space=pltpu.VMEM)
+    return pl.pallas_call(
+        add_kernel,
+        out_shape=(shape(half + 16, rows),) * 2,
+        in_specs=[vmem] * 5 + [pl.BlockSpec(memory_space=pl.ANY)],
+        out_specs=(vmem, vmem),
+        compiler_params=PARAMS,
+        cost_estimate=cost(2 * half * rows, 12 * half * rows),
+    )(up_part, up_in, down_part, down_in, stat, after)
+
+
+def finish_kernel(at_ref, own0, own1, up0, up1, down0, down1, tok_ref, root_ref, stat_ref, out_ref):
+    half = own0.shape[0]
+    stat = stat_ref[...] + read_stat(up0, half) + read_stat(down1, half)
+    stat = jnp.broadcast_to(stat, (HS, stat.shape[1])).T[:, 0:1]
+    root = root_ref[...]
+    parts = (
+        (own0[...], up0[:half, :], down0[half : 2 * half, :]),
+        (own1[...], up1[half : 2 * half, :], down1[:half, :]),
+    )
+    for i, part in enumerate(parts):
         span = slice(i * half, (i + 1) * half)
-        total = own_ref[span, :].astype(F32)
-        for ref in refs:
-            total += ref[...].astype(F32)
-        unit = tok_ref[:, span].astype(F32) / root_ref[...]
-        out_ref[:, span] = ((total.T - unit * stat_ref[...]) / root_ref[...]).astype(BF)
-
-
-def finish(quarter, own, parts, tokens, root, stat):
-    share, rows = own.shape
+        total = sum(p.astype(F32) for p in part)
+        unit = tok_ref[:, span].astype(F32) / root
+        out_ref[:, span] = ((total.T - unit * stat) / root).astype(BF)
+
+
+def finish(quarter, parts, tokens, root, stat):
+    half, rows = parts[0].shape
+    share = 2 * half
     whole = lambda a: pl.BlockSpec(a.shape, lambda i, at: (0, 0))
     return pl.pallas_call(
         finish_kernel,
         grid_spec=pltpu.PrefetchScalarGridSpec(
             num_scalar_prefetch=1,
             grid=(1,),
-            in_specs=[whole(own)]
-            + [whole(p) for p in parts]
+            in_specs=[whole(p) for p in parts]
             + [pl.BlockSpec((rows, share), lambda i, at: (0, at[0]))]
             + [whole(root), whole(stat)],
             out_specs=pl.BlockSpec((rows, share), lambda i, at: (0, 0)),
@@ -217,7 +310,7 @@
         out_shape=shape(rows, share),
         compiler_params=PARAMS,
         cost_estimate=cost(8 * rows * share, 10 * rows * share),
-    )(quarter.reshape(1), own, *parts, tokens, root, stat)
+    )(quarter.reshape(1), *parts, tokens, root, stat)
 
 
 def outer_kernel(at_ref, *refs):
@@ -234,7 +327,7 @@
 def outer(blocks, order, mine, other):
     depth, rows = blocks[0].shape
     cols = mine.shape[2]
-    tile = 256
+    tile = 1024
     return pl.pallas_call(
         outer_kernel,
         grid_spec=pltpu.PrefetchScalarGridSpec(
@@ -246,10 +339,48 @@
         ),
         out_shape=shape(depth, cols),
         compiler_params=PARAMS,
-        cost_estimate=cost(
-            2 * len(blocks) * depth * rows * cols, 2 * len(blocks) * depth * rows
-        ),
+        cost_estimate=cost(1, 1),
     )(order, *blocks, mine, other)
+
+
+def merge_kernel(part_ref, att_ref, after_ref, out_ref):
+    total = sum(part_ref[i].astype(F32) for i in range(part_ref.shape[0])).astype(BF)
+    cols = total.shape[1]
+    for i in range(out_ref.shape[0]):
+        out_ref[i, :, :cols] = total
+        out_ref[i, :, cols:] = att_ref[i]
+
+
+def merge(part, att, after):
+    _, rows, cols = part.shape
+    n, _, more = att.shape
+    vmem = pl.BlockSpec(memory_space=pltpu.VMEM)
+    return pl.pallas_call(
+        merge_kernel,
+        out_shape=shape(n, rows, cols + more),
+        in_specs=[vmem, vmem, pl.BlockSpec(memory_space=pl.ANY)],
+        out_specs=vmem,
+        compiler_params=PARAMS,
+        cost_estimate=cost(1, 1),
+    )(part, att, after)
+
+
+def unpack_kernel(in_ref, w_ref, att_ref):
+    for h in range(in_ref.shape[0]):
+        span = slice(h * HS, (h + 1) * HS)
+        for j in range(3):
+            w_ref[j, :, span] = in_ref[h, :, j * HS : (j + 1) * HS].astype(F32)
+        att_ref[:, span] = in_ref[h, :, 3 * HS :]
+
+
+def unpack(last):
+    heads, rows, _ = last.shape
+    return pl.pallas_call(
+        unpack_kernel,
+        out_shape=(shape(3, rows, heads * HS, dtype=F32), shape(rows, heads * HS)),
+        compiler_params=PARAMS,
+        cost_estimate=cost(last.size, 6 * last.size),
+    )(last)
 
 
 def shift(x, axis, by):
@@ -267,9 +398,10 @@
     share = width // n_t
     tokens = tokens.reshape(rows, width)
 
-    full_w = lax.all_gather(
-        weights.reshape(w_rows, 3 * cols), ("y", "zl", "core"), axis=0, tiled=True
-    )
+    w_kinds = weights.transpose(1, 0, 2)[None]
+    gather = lambda w: lax.all_gather(w, ("y", "zl", "core"), axis=0, tiled=True)
+    w_qk = gather(w_kinds[:, :2])
+    w_v = gather(w_kinds[:, 2:])
 
     normed, root, mine, given = unit_rows(tokens, at_core, w_rows)
     theirs = shift(given, "core", 1)
@@ -282,7 +414,8 @@
     dout = cotangent.reshape(rows, heads, HS).transpose(1, 0, 2)
     dout = lax.all_to_all(dout, "x", 0, 0, tiled=True).reshape(n_x * rows, HS)
 
-    proj = project(normed, full_w, heads)
+    proj = project(normed, w_qk, heads)
+    proj = project(normed, w_v, heads, proj, blocks)
     qkv = lax.all_to_all(proj, "x", 0, 0, tiled=True).reshape(n_x * rows, 3 * HS)
     att, head_grads = attention(qkv, dout)
 
@@ -290,32 +423,29 @@
     grads = lax.all_to_all(head_grads, "x", 0, 0, tiled=True)
 
     half = share // 2
-    far = norm_quarter(grads, full_w, (at_t + 2) % n_t, share)
-    up = shift(far[:half], "zh", 1)
-    down = shift(far[half:], "zh", -1)
-    to_up = norm_quarter(grads, full_w, (at_t + 1) % n_t, share)
-    up_1 = shift(to_up[half:], "zh", 1)
-    to_down = norm_quarter(grads, full_w, (at_t + n_t - 1) % n_t, share)
-    down_0 = shift(to_down[:half], "zh", -1)
-    own = norm_quarter(grads, full_w, at_t, share)
-    stat = jnp.sum(grads.astype(F32) * proj.astype(F32), (0, 2)) * (1.0 / width)
-    stat = stat + sum(shift(stat, "zh", by) for by in range(1, n_t))
-    up_0 = shift((to_up[:half].astype(F32) + up.astype(F32)).astype(BF), "zh", 1)
-    down_1 = shift((to_down[half:].astype(F32) + down.astype(F32)).astype(BF), "zh", -1)
-    token_grad = finish(
-        at_t, own, (up_0, up_1, down_0, down_1), tokens, root, stat.reshape(rows, 1)
-    )
-
-    other_grads = shift(head_grads, "core", 1)
-    part = outer(blocks, order, head_grads, other_grads)
+    norm = lambda at, spots, sizes, carry=(): norm_halves(
+        grads, proj, w_qk, w_v, jnp.stack(at), spots, sizes, width, carry
+    )
+    here, above, far, below = (2 * ((at_t + by) % n_t) for by in range(n_t))
+    part = outer(blocks, order, head_grads, shift(head_grads, "core", 1))
+    up, down, stat, part = norm(
+        [far, above + 1, far + 1, below],
+        ((0, 0), (0, half), (1, 0), (1, half)),
+        (share + 16, share),
+        (part,),
+    )
+    up, down = shift(up, "zh", 1), shift(down, "zh", -1)
     part = lax.all_to_all(part, ("y", "zl"), 0, 0, tiled=True)
-    part = jnp.sum(part.reshape(-1, w_rows, 3 * HS).astype(F32), 0).astype(BF)
-    part = jnp.broadcast_to(part, (n_x,) + part.shape)
-    last = jnp.concatenate([part, att.reshape(n_x, rows, HS)], 2)
+    up_part, down_part, own0, own1, _ = norm(
+        [above, below + 1, here, here + 1], ((0, 0), (1, 0), (2, 0), (3, 0)), (half,) * 4
+    )
+    last = merge(part.reshape(-1, w_rows, 3 * HS), att.reshape(n_x, rows, HS), own0)
+    up_2, down_2 = add_messages(up_part, up, down_part, down, stat, last)
+    up_2, down_2 = shift(up_2, "zh", 1), shift(down_2, "zh", -1)
     last = lax.all_to_all(last, "x", 0, 0, tiled=True)
-    weight_grad = last[:, :, : 3 * HS].reshape(heads, w_rows, 3, HS).transpose(1, 2, 0, 3)
-    attended = last[:, :, 3 * HS :].transpose(1, 0, 2).reshape(1, rows, cols)
-    return attended, token_grad[None], weight_grad.reshape(weights.shape).astype(F32)
+    token_grad = finish(at_t, (own0, own1, up_2, up, down, down_2), tokens, root, stat)
+    weight_grad, attended = unpack(last)
+    return attended[None], token_grad[None], weight_grad.transpose(1, 0, 2)
 
 
 def solution(mesh):

time: 252 us -> 251 us (level)
  starting transfers between devices: 51.3 us -> 33.7 us
  blocking collectives: 0 us -> 16.7 us
  Pallas kernels: 45.4 us -> 58 us
  other arithmetic: 8.55 us -> 0.23 us
  waiting for transfers between devices: 116 us -> 111 us
    all_gather x1 -> x2, waiting for transfers between devices: 64 us -> 36.7 us  [per_device(): lax.all_gather(w, ('y', 'zl', 'core'), axis=0, tiled=True)]
    all_to_all x1, waiting for transfers between devices: 0.01 us -> 18.3 us  [per_device(): part = lax.all_to_all(part, ('y', 'zl'), 0, 0, tiled=True)]
    all_to_all x0 -> x1, blocking collectives: none -> 16.7 us  [per_device(): lax.all_to_all(proj, 'x', 0, 0, tiled=True).reshape(n_x * rows, 3 * HS)]
    pallas_call x5 -> x7, Pallas kernels: 22 us -> 34.5 us  [the longest x2 15.3 us: project(): pl.pallas_call(functools.partial(project_kernel, before), grid=(n // tile...]
    ppermute x17 -> x12, starting transfers between devices: 30.2 us -> 17.9 us  [shift(): return lax.ppermute(x, axis, [(i, (i + by) % n) for i in range(n)])]
    ppermute x17 -> x12, waiting for transfers between devices: 45.1 us -> 52.3 us  [shift(): return lax.ppermute(x, axis, [(i, (i + by) % n) for i in range(n)])]
    all_to_all x1 -> x0, waiting for transfers between devices: 7 us -> none  [per_device(): lax.all_to_all(proj, 'x', 0, 0, tiled=True).reshape(n_x * rows, 3 * HS)]
    unnamed x5 -> x30, local copies, waits for them, and re-layouts: 3.87 us -> 9.23 us
  transfers between devices with their start and end apart: 23 -> 18, of which waited for: 9 -> 12; matrix products, arithmetic and copies ran while one was open for 6% -> 1% of each run, Pallas kernels for 18% -> 16%
where the time goes in v3:
time: 251 us; the launch traced here: 248 us
  waiting for transfers between devices  111 us (44%)
  Pallas kernels  58 us (23%)
  starting transfers between devices  33.7 us (13%)
  blocking collectives  16.7 us (7%)
  between operations  14.3 us (6%)
  local copies, waits for them, and re-layouts  13.6 us (5%)
    ppermute x12, waiting for transfers between devices, shift(): return lax.ppermute(x, axis, [(i, (i + by) % n) for i in range(n)])  52.3 us
    all_gather x2, waiting for transfers between devices, per_device(): lax.all_gather(w, ('y', 'zl', 'core'), axis=0, tiled=True)  36.7 us
    all_to_all x1, waiting for transfers between devices, per_device(): part = lax.all_to_all(part, ('y', 'zl'), 0, 0, tiled=True)  18.3 us
    ppermute x12, starting transfers between devices, shift(): return lax.ppermute(x, axis, [(i, (i + by) % n) for i in range(n)])  17.9 us
    all_to_all x1, blocking collectives, per_device(): lax.all_to_all(proj, 'x', 0, 0, tiled=True).reshape(n_x * rows, 3 * HS)  16.7 us
    pallas_call x2, Pallas kernels, project(): pl.pallas_call(functools.partial(project_kernel, before), grid=(n // tile...  15.3 us
    pallas_call x2, Pallas kernels, norm_halves(): pl.pallas_call(functools.partial(norm_kernel, width, spots, len(carry)),...  15.1 us
    unnamed x30, local copies, waits for them, and re-layouts  9.23 us
  transfers between devices with their start and end apart: 18, of which 12 were waited for; matrix products, arithmetic and copies ran while one was open for 1% of the time, Pallas kernels for 16%

profile of v3, /device:TPU:8, one launch (start us, length us, event | category | flops | bytes accessed | tf_op | source)
XLA Modules:
  0.0 247.8 jit_solution(6232912609744023265)
XLA Ops:
  7.2 0.0 all-gather.5.cloned.1.call-start
  7.2 1.9 slice.9
  9.1 0.0 all-gather.5.cloned.1.call-update
  9.2 0.0 all-gather.3.cloned.1.call-start
  9.2 1.7 slice.8
  10.9 0.0 all-gather.3.cloned.1.call-update
  10.9 3.6 %shard_map.58 = (bf16[256,4096]{1,0:T(8,128)(2,1)S(1)}, f32[256,1]{1,0:T(8,128)S(1)}, bf16[2048,256]{1,0:T(8,128)(2,1)}, bf16[2048,256]{1,0:T(8,128)(2,1)S(1)}) custom-call(s32[1]{0:T(128)} %bitcast.4.at_ref, bf16[256,4096]{1,0:T(8,128)(2,1)} %bitcast.30), custom_call_target="tpu_custom_call" | custom-call | flops 6291456 | bytes 6291456 | tf_op jit(solution)/shard_map/pallas_call | solution.py:45
  14.5 1.5 collective-permute-start
  16.0 1.3 collective-permute-done.3.refs_5_.refs_4_
  17.3 2.8 %collective-permute-start.5 = (bf16[2048,256]{1,0:T(8,128)(2,1)}, bf16[2048,256]{1,0:T(8,128)(2,1)}, u32[]{:S(2)}, u32[]{:S(2)}) collective-permute-start(bf16[2048,256]{1,0:T(8,128)(2,1)} %collective-permute-done.3.refs_5_.refs_4_), channel_id=1, source_target_pairs={{0,12},{4,0},{8,4},{12,8},{1,13},{5,1},{9,5},{13,9},{2,14},{6,2},{... | collective-permute-start | bytes 3145736 | tf_op jit(solution)/shard_map/ppermute | solution.py:388
  20.0 0.9 collective-permute-start.1
  20.9 1.2 collective-permute-start.4
  22.1 19.9 %collective-permute-done.refs_2_.refs_1_ = bf16[2048,256]{1,0:T(8,128)(2,1)} collective-permute-done((bf16[2048,256]{1,0:T(8,128)(2,1)}, bf16[2048,256]{1,0:T(8,128)(2,1)}, u32[]{:S(2)}, u32[]{:S(2)}) %collective-permute-start) | collective-permute-done | bytes 1048608 | tf_op jit(solution)/shard_map/ppermute | solution.py:388
  42.0 0.3 collective-permute-start.2
  42.3 1.6 collective-permute-done.5.refs_7_.refs_6_
  43.9 3.7 %collective-permute-start.6 = (bf16[2048,256]{1,0:T(8,128)(2,1)}, bf16[2048,256]{1,0:T(8,128)(2,1)}, u32[]{:S(2)}, u32[]{:S(2)}) collective-permute-start(bf16[2048,256]{1,0:T(8,128)(2,1)} %collective-permute-done.5.refs_7_.refs_6_), channel_id=1, source_target_pairs={{0,12},{4,0},{8,4},{12,8},{1,13},{5,1},{9,5},{13,9},{2,14},{6,2},{... | collective-permute-start | bytes 3145736 | tf_op jit(solution)/shard_map/ppermute | solution.py:388
  47.6 0.1 reshape.37
  47.6 0.7 copy.10
  48.4 4.0 %all-to-all-start.1 = ((bf16[4,256,128]{2,1,0:T(8,128)(2,1)}), bf16[4,256,128]{2,1,0:T(8,128)(2,1)}, u32[]{:S(2)}, u32[]{:S(2)}) async-start(bf16[4,256,128]{2,1,0:T(8,128)(2,1)} %bitcast.28), calls=%async_computation.1 | async-start | bytes 524288 | tf_op jit(solution)/shard_map/all_to_all | solution.py:415
  52.4 15.5 %all-gather.5.cloned.1.call-done.w_ref.qk_w = bf16[16,2,256,512]{3,2,1,0:T(8,128)(2,1)} async-done(((bf16[1,2,256,512]{3,2,1,0:T(8,128)(2,1)}), bf16[16,2,256,512]{3,2,1,0:T(8,128)(2,1)}) %all-gather.5.cloned.1.call-update) | async-done | bytes 8388624 | tf_op jit(solution)/shard_map/all_gather | solution.py:402
  67.9 8.8 %shard_map.59.refs_0_ = bf16[4,256,256]{2,1,0:T(8,128)(2,1)S(1)} custom-call(bf16[256,4096]{1,0:T(8,128)(2,1)S(1)} %get-tuple-element.21.a_ref, bf16[16,2,256,512]{3,2,1,0:T(8,128)(2,1)} %all-gather.5.cloned.1.call-done.w_ref.qk_w), custom_call_target="tpu_custom_call" | custom-call | flops 2147483648 | bytes 10485760 | tf_op jit(solution)/shard_map/pallas_call | solution.py:111
  76.7 10.2 %collective-permute-done.2.refs_4_.refs_3_ = bf16[2048,256]{1,0:T(8,128)(2,1)} collective-permute-done((bf16[2048,256]{1,0:T(8,128)(2,1)}, bf16[2048,256]{1,0:T(8,128)(2,1)}, u32[]{:S(2)}, u32[]{:S(2)}) %collective-permute-start.2) | collective-permute-done | bytes 1048608 | tf_op jit(solution)/shard_map/ppermute | solution.py:388
  86.9 3.2 %collective-permute-done.6.refs_8_.refs_7_ = bf16[2048,256]{1,0:T(8,128)(2,1)} collective-permute-done((bf16[2048,256]{1,0:T(8,128)(2,1)}, bf16[2048,256]{1,0:T(8,128)(2,1)}, u32[]{:S(2)}, u32[]{:S(2)}) %collective-permute-start.6) | collective-permute-done | bytes 1048608 | tf_op jit(solution)/shard_map/ppermute | solution.py:388
  90.1 21.2 %all-gather.3.cloned.1.call-done.w_ref.v_w = bf16[16,1,256,512]{3,2,1,0:T(8,128)(2,1)} async-done(((bf16[1,1,256,512]{3,2,1,0:T(8,128)(2,1)}), bf16[16,1,256,512]{3,2,1,0:T(8,128)(2,1)}) %all-gather.3.cloned.1.call-update) | async-done | bytes 4194320 | tf_op jit(solution)/shard_map/all_gather | solution.py:402
  111.3 6.5 %shard_map.60.p_ref = bf16[4,256,384]{2,1,0:T(8,128)(2,1)S(1)} custom-call(bf16[256,4096]{1,0:T(8,128)(2,1)} %copy-done.3, bf16[16,1,256,512]{3,2,1,0:T(8,128)(2,1)} %all-gather.3.cloned.1.call-done.w_ref.v_w, bf16[4,256,256]{2,1,0:T(8,128)(2,1)S(1)} %shard_map.59.refs_0_, bf16[2048,256]{1,0:T(8,128)(2,1)} %get-tuple-element.22.refs_1_.refs_0_, ...), custom_call_target="tpu_custom_call" | custom-call | flops 1073741824 | bytes 6291456 | tf_op jit(solution)/shard_map/pallas_call | solution.py:111
  117.8 0.0 all-to-all-done.1
  117.8 16.7 %all_to_all.29 = bf16[4,256,384]{2,1,0:T(8,128)(2,1)S(1)} all-to-all(bf16[4,256,384]{2,1,0:T(8,128)(2,1)S(1)} %shard_map.60.p_ref), channel_id=1, replica_groups=mesh['y'=4,'zl'=2,'core'=2,'x'=4,'zh'=4] {'x'}, dimensions={0} | all-to-all | bytes 1572864 | tf_op jit(solution)/shard_map/all_to_all | solution.py:419
  134.6 8.4 %shard_map.61 = (bf16[1024,128]{1,0:T(8,128)(2,1)S(1)}, bf16[1024,384]{1,0:T(8,128)(2,1)}) custom-call(bf16[1024,384]{1,0:T(8,128)(2,1)S(1)} %bitcast.32, bf16[1024,128]{1,0:T(8,128)(2,1)} %bitcast.11.dout_ref), custom_call_target="tpu_custom_call" | custom-call | flops 1879048192 | bytes 2097152 | tf_op jit(solution)/shard_map/pallas_call | solution.py:165
  142.9 0.7 copy-done.4
  143.6 0.0 collective-permute-start.7
  143.6 3.5 %all-to-all-start.2 = ((bf16[4,256,384]{2,1,0:T(8,128)(2,1)}), bf16[4,256,384]{2,1,0:T(8,128)(2,1)S(1)}, u32[]{:S(2)}, u32[]{:S(2)}) async-start(bf16[4,256,384]{2,1,0:T(8,128)(2,1)} %bitcast.12.refs_8_), calls=%async_computation.2 | async-start | bytes 1572864 | tf_op jit(solution)/shard_map/all_to_all | solution.py:423
  147.2 0.1 pad_add_fusion.at_ref
  147.3 0.1 pad_add_fusion.1.at_ref
  147.3 0.0 collective-permute-done.7.refs_9_
  147.4 9.0 %shard_map.62.refs_0_ = bf16[2048,384]{1,0:T(8,128)(2,1)} custom-call(s32[4]{0:T(128)S(1)} %pad_add_fusion.1.at_ref, bf16[2048,256]{1,0:T(8,128)(2,1)} %get-tuple-element.22.refs_1_.refs_0_, bf16[2048,256]{1,0:T(8,128)(2,1)} %collective-permute-done.refs_2_.refs_1_, bf16[2048,256]{1,0:T(8,128)(2,1)} %collective-permute-done.1.refs_3_.refs_2_, ...), custom_call_target="tpu_custom_call" | custom-call | flops 1 | bytes 1 | tf_op jit(solution)/shard_map/pallas_call | solution.py:331
  156.4 4.0 %all-to-all-done.2.g_ref = bf16[4,256,384]{2,1,0:T(8,128)(2,1)S(1)} async-done(((bf16[4,256,384]{2,1,0:T(8,128)(2,1)}), bf16[4,256,384]{2,1,0:T(8,128)(2,1)S(1)}, u32[]{:S(2)}, u32[]{:S(2)}) %all-to-all-start.2) | async-done | bytes 786464 | tf_op jit(solution)/shard_map/all_to_all | solution.py:423
  160.3 1.4 copy-done
  161.7 7.3 %shard_map.63 = (bf16[1040,256]{1,0:T(8,128)(2,1)S(1)}, bf16[1024,256]{1,0:T(8,128)(2,1)S(1)}, f32[1,256]{1,0:T(1,128)S(1)}, bf16[2048,384]{1,0:T(8,128)(2,1)S(1)}) custom-call(s32[4]{0:T(128)S(1)} %pad_add_fusion.at_ref, bf16[4,256,384]{2,1,0:T(8,128)(2,1)S(1)} %all-to-all-done.2.g_ref, ...), custom_call_target="tpu_custom_call", output_to_operand_aliasing={{3}: (5, {})} | custom-call | flops 1 | bytes 1 | tf_op jit(solution)/shard_map/pallas_call | solution.py:238
  169.0 0.0 copy-start.1
  169.1 1.1 copy-done.1
  170.2 0.8 copy-done.12
  171.0 0.2 copy-done.13
  171.2 4.5 %all-to-all-start.3 = ((bf16[8,256,384]{2,1,0:T(8,128)(2,1)}), bf16[8,256,384]{2,1,0:T(8,128)(2,1)S(1)}, u32[]{:S(2)}, u32[]{:S(2)}) async-start(bf16[8,256,384]{2,1,0:T(8,128)(2,1)} %bitcast.29), calls=%async_computation.3 | async-start | bytes 3145728 | tf_op jit(solution)/shard_map/all_to_all | solution.py:438
  175.7 3.5 %collective-permute-start.9 = (bf16[1024,256]{1,0:T(8,128)(2,1)}, bf16[1024,256]{1,0:T(8,128)(2,1)}, u32[]{:S(2)}, u32[]{:S(2)}) collective-permute-start(bf16[1024,256]{1,0:T(8,128)(2,1)} %copy-done.13), channel_id=1, source_target_pairs={{0,3},{1,0},{2,1},{3,2},{4,7},{5,4},{6,5},{7,6},{8,11},{9,8},{10,9... | collective-permute-start | bytes 1572872 | tf_op jit(solution)/shard_map/ppermute | solution.py:388
  179.2 0.0 collective-permute-start.8
  179.2 0.1 pad_add_fusion.2.at_ref
  179.2 7.8 %shard_map.64 = (bf16[512,256]{1,0:T(8,128)(2,1)S(1)}, bf16[512,256]{1,0:T(8,128)(2,1)S(1)}, bf16[512,256]{1,0:T(8,128)(2,1)S(1)}, bf16[512,256]{1,0:T(8,128)(2,1)S(1)}, f32[1,256]{1,0:T(1,128)}) custom-call(s32[4]{0:T(128)S(1)} %pad_add_fusion.2.at_ref, bf16[4,256,384]{2,1,0:T(8,128)(2,1)S(1)} %all-to-all-done.2.g_ref, ...), custom_call_target="tpu_custom_call" | custom-call | flops 1 | bytes 1 | tf_op jit(solution)/shard_map/pallas_call | solution.py:238
  187.0 0.7 copy-done.6
  187.7 0.7 copy-done.8
  188.4 0.7 copy-done.10
  189.2 18.3 %all-to-all-done.3.part_ref = bf16[8,256,384]{2,1,0:T(8,128)(2,1)S(1)} async-done(((bf16[8,256,384]{2,1,0:T(8,128)(2,1)}), bf16[8,256,384]{2,1,0:T(8,128)(2,1)S(1)}, u32[]{:S(2)}, u32[]{:S(2)}) %all-to-all-start.3) | async-done | bytes 1572896 | tf_op jit(solution)/shard_map/all_to_all | solution.py:438
  207.4 0.9 copy-done.5
  208.4 1.2 shard_map.65.after_ref
  209.6 3.6 %all-to-all-start.4 = ((bf16[4,256,512]{2,1,0:T(8,128)(2,1)}), bf16[4,256,512]{2,1,0:T(8,128)(2,1)S(1)}, u32[]{:S(2)}, u32[]{:S(2)}) async-start(bf16[4,256,512]{2,1,0:T(8,128)(2,1)} %shard_map.65.after_ref), calls=%async_computation.4 | async-start | bytes 2097152 | tf_op jit(solution)/shard_map/all_to_all | solution.py:445
  213.3 6.1 %collective-permute-done.8.up_in.up1 = bf16[1040,256]{1,0:T(8,128)(2,1)} collective-permute-done((bf16[1040,256]{1,0:T(8,128)(2,1)}, bf16[1040,256]{1,0:T(8,128)(2,1)}, u32[]{:S(2)}, u32[]{:S(2)}) %collective-permute-start.8) | collective-permute-done | bytes 532512 | tf_op jit(solution)/shard_map/ppermute | solution.py:388
  219.3 0.9 copy-done.9
  220.3 0.9 copy-done.11
  221.2 1.5 shard_map.67
  222.7 0.1 collective-permute-start.10
  222.8 4.1 %collective-permute-start.11 = (bf16[528,256]{1,0:T(8,128)(2,1)S(1)}, bf16[528,256]{1,0:T(8,128)(2,1)S(1)}, u32[]{:S(2)}, u32[]{:S(2)}) collective-permute-start(bf16[528,256]{1,0:T(8,128)(2,1)S(1)} %get-tuple-element.36), channel_id=1, source_target_pairs={{0,3},{1,0},{2,1},{3,2},{4,7},{5,4},{6,5},{7,6},{8,11},{9,8},{10,9... | collective-permute-start | bytes 811016 | tf_op jit(solution)/shard_map/ppermute | solution.py:388
  226.9 9.3 %collective-permute-done.10.up0 = bf16[528,256]{1,0:T(8,128)(2,1)S(1)} collective-permute-done((bf16[528,256]{1,0:T(8,128)(2,1)S(1)}, bf16[528,256]{1,0:T(8,128)(2,1)S(1)}, u32[]{:S(2)}, u32[]{:S(2)}) %collective-permute-start.10) | collective-permute-done | bytes 270368 | tf_op jit(solution)/shard_map/ppermute | solution.py:388
  236.2 0.7 collective-permute-done.11.down1
  236.9 2.5 %shard_map.68 = bf16[256,1024]{1,0:T(8,128)(2,1)} custom-call(s32[1]{0:T(128)} %bitcast.24.at_ref, bf16[512,256]{1,0:T(8,128)(2,1)S(1)} %get-tuple-element.27.after_ref.own0, bf16[512,256]{1,0:T(8,128)(2,1)S(1)} %copy-done.7, bf16[528,256]{1,0:T(8,128)(2,1)S(1)} %collective-permute-done.10.up0, bf16[1040,256]{1,0:T(8,128)(2,1)} %collective-permute-done.8.up_in.up1, ...), custom_call_target="tpu_custom_call" | custom-call | flops 2097152 | bytes 2621440 | tf_op jit(solution)/shard_map/pallas_call | solution.py:300
  239.5 1.5 shard_map.66
  (23 shorter events, 0.0 us)
Async XLA Ops:
  7.2 60.8 %all-gather.5.cloned.1.call-start = ((), (), s32[]{:S(2)}) async-start(), calls=%async_computation.6 | async-start | bytes 8912896 | tf_op jit(solution)/shard_map/all_gather | solution.py:402
  7.2 40.4 %copy-start.14 = (bf16[1,256,512]{2,1,0:T(8,128)(2,1)S(1)}, bf16[1,256,512]{2,1,0:T(8,128)(2,1)}, u32[]{:S(2)}) copy-start(bf16[1,256,512]{2,1,0:T(8,128)(2,1)} %param.5) | copy-start | bytes 786436
  9.2 102.1 %all-gather.3.cloned.1.call-start = ((), (), s32[]{:S(2)}) async-start(), calls=%async_computation.5 | async-start | bytes 4456448 | tf_op jit(solution)/shard_map/all_gather | solution.py:402
  14.5 62.2 %copy-start.3 = (bf16[256,4096]{1,0:T(8,128)(2,1)}, bf16[256,4096]{1,0:T(8,128)(2,1)S(1)}, u32[]{:S(2)}) copy-start(bf16[256,4096]{1,0:T(8,128)(2,1)S(1)} %get-tuple-element.21.a_ref) | copy-start | bytes 6291460
  14.5 2.8 %collective-permute-start.3 = (bf16[2048,256]{1,0:T(8,128)(2,1)S(1)}, bf16[2048,256]{1,0:T(8,128)(2,1)}, u32[]{:S(2)}, u32[]{:S(2)}) collective-permute-start(bf16[2048,256]{1,0:T(8,128)(2,1)S(1)} %get-tuple-element.23), channel_id=1, source_target_pairs={{0,16},{16,0},{1,17},{17,1},{2,18},{18,2},{3,19},{19,3},{4,20},{20... | collective-permute-start | bytes 3145736 | tf_op jit(solution)/shard_map/ppermute | solution.py:388
  14.5 27.5 %collective-permute-start = (bf16[2048,256]{1,0:T(8,128)(2,1)}, bf16[2048,256]{1,0:T(8,128)(2,1)}, u32[]{:S(2)}, u32[]{:S(2)}) collective-permute-start(bf16[2048,256]{1,0:T(8,128)(2,1)} %get-tuple-element.22.refs_1_.refs_0_), channel_id=1, source_target_pairs={{0,4},{4,8},{8,12},{12,0},{1,5},{5,9},{9,13},{13,1},{2,6},{6,10},{... | collective-permute-start | bytes 3145736 | tf_op jit(solution)/shard_map/ppermute | solution.py:388
  17.3 26.6 %collective-permute-start.5 = (bf16[2048,256]{1,0:T(8,128)(2,1)}, bf16[2048,256]{1,0:T(8,128)(2,1)}, u32[]{:S(2)}, u32[]{:S(2)}) collective-permute-start(bf16[2048,256]{1,0:T(8,128)(2,1)} %collective-permute-done.3.refs_5_.refs_4_), channel_id=1, source_target_pairs={{0,12},{4,0},{8,4},{12,8},{1,13},{5,1},{9,5},{13,9},{2,14},{6,2},{... | collective-permute-start | bytes 3145736 | tf_op jit(solution)/shard_map/ppermute | solution.py:388
  20.0 56.7 %collective-permute-start.1 = (bf16[2048,256]{1,0:T(8,128)(2,1)}, bf16[2048,256]{1,0:T(8,128)(2,1)}, u32[]{:S(2)}, u32[]{:S(2)}) collective-permute-start(bf16[2048,256]{1,0:T(8,128)(2,1)} %get-tuple-element.22.refs_1_.refs_0_), channel_id=1, source_target_pairs={{0,12},{4,0},{8,4},{12,8},{1,13},{5,1},{9,5},{13,9},{2,14},{6,2},{... | collective-permute-start | bytes 3145736 | tf_op jit(solution)/shard_map/ppermute | solution.py:388
  20.9 55.8 %collective-permute-start.4 = (bf16[2048,256]{1,0:T(8,128)(2,1)}, bf16[2048,256]{1,0:T(8,128)(2,1)}, u32[]{:S(2)}, u32[]{:S(2)}) collective-permute-start(bf16[2048,256]{1,0:T(8,128)(2,1)} %collective-permute-done.3.refs_5_.refs_4_), channel_id=1, source_target_pairs={{0,4},{4,8},{8,12},{12,0},{1,5},{5,9},{9,13},{13,1},{2,6},{6,10},{... | collective-permute-start | bytes 3145736 | tf_op jit(solution)/shard_map/ppermute | solution.py:388
  42.0 44.9 %collective-permute-start.2 = (bf16[2048,256]{1,0:T(8,128)(2,1)}, bf16[2048,256]{1,0:T(8,128)(2,1)}, u32[]{:S(2)}, u32[]{:S(2)}) collective-permute-start(bf16[2048,256]{1,0:T(8,128)(2,1)} %collective-permute-done.refs_2_.refs_1_), channel_id=1, source_target_pairs={{0,4},{4,8},{8,12},{12,0},{1,5},{5,9},{9,13},{13,1},{2,6},{6,10},{... | collective-permute-start | bytes 3145736 | tf_op jit(solution)/shard_map/ppermute | solution.py:388
  43.9 46.2 %collective-permute-start.6 = (bf16[2048,256]{1,0:T(8,128)(2,1)}, bf16[2048,256]{1,0:T(8,128)(2,1)}, u32[]{:S(2)}, u32[]{:S(2)}) collective-permute-start(bf16[2048,256]{1,0:T(8,128)(2,1)} %collective-permute-done.5.refs_7_.refs_6_), channel_id=1, source_target_pairs={{0,12},{4,0},{8,4},{12,8},{1,13},{5,1},{9,5},{13,9},{2,14},{6,2},{... | collective-permute-start | bytes 3145736 | tf_op jit(solution)/shard_map/ppermute | solution.py:388
  48.4 69.4 %all-to-all-start.1 = ((bf16[4,256,128]{2,1,0:T(8,128)(2,1)}), bf16[4,256,128]{2,1,0:T(8,128)(2,1)}, u32[]{:S(2)}, u32[]{:S(2)}) async-start(bf16[4,256,128]{2,1,0:T(8,128)(2,1)} %bitcast.28), calls=%async_computation.1 | async-start | bytes 524288 | tf_op jit(solution)/shard_map/all_to_all | solution.py:415
  142.9 0.7 copy-start.4
  143.6 3.7 %collective-permute-start.7 = (bf16[4,256,384]{2,1,0:T(8,128)(2,1)}, bf16[4,256,384]{2,1,0:T(8,128)(2,1)S(1)}, u32[]{:S(2)}, u32[]{:S(2)}) collective-permute-start(bf16[4,256,384]{2,1,0:T(8,128)(2,1)} %bitcast.12.refs_8_), channel_id=1, source_target_pairs={{0,16},{16,0},{1,17},{17,1},{2,18},{18,2},{3,19},{19,3},{4,20},{20... | collective-permute-start | bytes 2359304 | tf_op jit(solution)/shard_map/ppermute | solution.py:388
  143.6 16.7 %all-to-all-start.2 = ((bf16[4,256,384]{2,1,0:T(8,128)(2,1)}), bf16[4,256,384]{2,1,0:T(8,128)(2,1)S(1)}, u32[]{:S(2)}, u32[]{:S(2)}) async-start(bf16[4,256,384]{2,1,0:T(8,128)(2,1)} %bitcast.12.refs_8_), calls=%async_computation.2 | async-start | bytes 1572864 | tf_op jit(solution)/shard_map/all_to_all | solution.py:423
  160.3 1.4 copy-start
  169.0 1.1 copy-start.1
  170.2 0.8 copy-start.12
  170.2 1.0 copy-start.13
  171.2 36.3 %all-to-all-start.3 = ((bf16[8,256,384]{2,1,0:T(8,128)(2,1)}), bf16[8,256,384]{2,1,0:T(8,128)(2,1)S(1)}, u32[]{:S(2)}, u32[]{:S(2)}) async-start(bf16[8,256,384]{2,1,0:T(8,128)(2,1)} %bitcast.29), calls=%async_computation.3 | async-start | bytes 3145728 | tf_op jit(solution)/shard_map/all_to_all | solution.py:438
  175.7 37.6 %collective-permute-start.9 = (bf16[1024,256]{1,0:T(8,128)(2,1)}, bf16[1024,256]{1,0:T(8,128)(2,1)}, u32[]{:S(2)}, u32[]{:S(2)}) collective-permute-start(bf16[1024,256]{1,0:T(8,128)(2,1)} %copy-done.13), channel_id=1, source_target_pairs={{0,3},{1,0},{2,1},{3,2},{4,7},{5,4},{6,5},{7,6},{8,11},{9,8},{10,9... | collective-permute-start | bytes 1572872 | tf_op jit(solution)/shard_map/ppermute | solution.py:388
  179.2 40.2 %collective-permute-start.8 = (bf16[1040,256]{1,0:T(8,128)(2,1)}, bf16[1040,256]{1,0:T(8,128)(2,1)}, u32[]{:S(2)}, u32[]{:S(2)}) collective-permute-start(bf16[1040,256]{1,0:T(8,128)(2,1)} %copy-done.12), channel_id=1, source_target_pairs={{0,1},{1,2},{2,3},{3,0},{4,5},{5,6},{6,7},{7,4},{8,9},{9,10},{10,1... | collective-permute-start | bytes 1597448 | tf_op jit(solution)/shard_map/ppermute | solution.py:388
  187.0 0.7 copy-start.6
  187.7 0.7 copy-start.8
  188.4 0.7 copy-start.10
  207.4 1.0 copy-start.5
  209.6 27.4 %copy-start.2 = (bf16[1,256,4096]{2,1,0:T(8,128)(2,1)S(1)}, bf16[1,256,4096]{2,1,0:T(8,128)(2,1)}, u32[]{:S(2)}) copy-start(bf16[1,256,4096]{2,1,0:T(8,128)(2,1)} %param.3) | copy-start | bytes 6291460
  209.6 29.9 %all-to-all-start.4 = ((bf16[4,256,512]{2,1,0:T(8,128)(2,1)}), bf16[4,256,512]{2,1,0:T(8,128)(2,1)S(1)}, u32[]{:S(2)}, u32[]{:S(2)}) async-start(bf16[4,256,512]{2,1,0:T(8,128)(2,1)} %shard_map.65.after_ref), calls=%async_computation.4 | async-start | bytes 2097152 | tf_op jit(solution)/shard_map/all_to_all | solution.py:445
  213.2 23.7 %copy-start.7 = (bf16[512,256]{1,0:T(8,128)(2,1)S(1)}, bf16[512,256]{1,0:T(8,128)(2,1)}, u32[]{:S(2)}) copy-start(bf16[512,256]{1,0:T(8,128)(2,1)} %copy-done.6) | copy-start | bytes 786436
  219.3 1.0 copy-start.9
  220.3 0.9 copy-start.11
  222.7 13.5 %collective-permute-start.10 = (bf16[528,256]{1,0:T(8,128)(2,1)S(1)}, bf16[528,256]{1,0:T(8,128)(2,1)S(1)}, u32[]{:S(2)}, u32[]{:S(2)}) collective-permute-start(bf16[528,256]{1,0:T(8,128)(2,1)S(1)} %get-tuple-element.35), channel_id=1, source_target_pairs={{0,1},{1,2},{2,3},{3,0},{4,5},{5,6},{6,7},{7,4},{8,9},{9,10},{10,1... | collective-permute-start | bytes 811016 | tf_op jit(solution)/shard_map/ppermute | solution.py:388
  222.8 14.2 %collective-permute-start.11 = (bf16[528,256]{1,0:T(8,128)(2,1)S(1)}, bf16[528,256]{1,0:T(8,128)(2,1)S(1)}, u32[]{:S(2)}, u32[]{:S(2)}) collective-permute-start(bf16[528,256]{1,0:T(8,128)(2,1)S(1)} %get-tuple-element.36), channel_id=1, source_target_pairs={{0,3},{1,0},{2,1},{3,2},{4,7},{5,4},{6,5},{7,6},{8,11},{9,8},{10,9... | collective-permute-start | bytes 811016 | tf_op jit(solution)/shard_map/ppermute | solution.py:388
Sparse Core Ops, SparseCore 0:
  10.4 57.4 all-gather.4
  70.3 40.8 all-gather.2

commit v4 on v3

v4 whole, which is shorter than its diff:
```python
import functools
import math

import jax
import jax.numpy as jnp
from jax import lax
from jax.experimental import pallas as pl
from jax.experimental.pallas import tpu as pltpu
from jax.sharding import Mesh
from jax.sharding import PartitionSpec as P

HS = 128
CORE, X, T, Y, Z = range(5)
BF = jnp.bfloat16
F32 = jnp.float32
PARAMS = pltpu.CompilerParams(vmem_limit_bytes=60 * 1024 * 1024)


def dot(a, b, ca, cb):
    return lax.dot_general(a, b, (((ca,), (cb,)), ((), ())), preferred_element_type=F32)


def cost(flops, nbytes, exps=0):
    return pl.CostEstimate(flops=flops, bytes_accessed=nbytes, transcendentals=exps)


def shape(*dims, dtype=BF):
    return jax.ShapeDtypeStruct(dims, dtype)


def unit_kernel(at_ref, tok_ref, normed_ref, root_ref, mine_ref, given_ref, *, band):
    tok = tok_ref[...].astype(F32)
    root = jnp.sqrt(jnp.mean(tok * tok, -1, keepdims=True) + 1e-05)
    normed_ref[...] = (tok / root).astype(BF)
    root_ref[...] = root
    core = at_ref[CORE]
    for i in range(mine_ref.shape[0] // band):
        for ref, which in ((mine_ref, core), (given_ref, 1 - core)):
            at = pl.multiple_of((2 * i + which) * band, band)
            ref[i * band : (i + 1) * band, :] = normed_ref[:, pl.ds(at, band)].T


def unit_rows(ids, tokens, band):
    rows, width = tokens.shape
    tile = 128
    return pl.pallas_call(
        functools.partial(unit_kernel, band=band),
        grid_spec=pltpu.PrefetchScalarGridSpec(
            num_scalar_prefetch=1,
            grid=(rows // tile,),
            in_specs=[pl.BlockSpec((tile, width), lambda i, at: (i, 0))],
            out_specs=(
                pl.BlockSpec((tile, width), lambda i, at: (i, 0)),
                pl.BlockSpec((tile, 1), lambda i, at: (i, 0)),
                pl.BlockSpec((width // 2, tile), lambda i, at: (0, i)),
                pl.BlockSpec((width // 2, tile), lambda i, at: (0, i)),
            ),
        ),
        out_shape=(
            shape(rows, width),
            shape(rows, 1, dtype=F32),
            shape(width // 2, rows),
            shape(width // 2, rows),
        ),
        compiler_params=PARAMS,
        cost_estimate=cost(6 * rows * width, 6 * rows * width),
    )(ids, tokens)


def project_kernel(chunks, a_any, w_any, *refs):
    heads_ref, a_ref, w_ref, acc_ref, a_sem, w_sem = refs[-6:]
    bands, kinds, depth, cols = w_ref.shape
    n = bands // chunks
    copies = []
    for c in range(chunks):
        span = pl.ds(c * n * depth, n * depth)
        some = pl.ds(c * n, n)
        copies.append(
            (
                pltpu.make_async_copy(a_any.at[:, span], a_ref.at[:, span], a_sem.at[c]),
                pltpu.make_async_copy(w_any.at[some], w_ref.at[some], w_sem.at[c]),
            )
        )
        for copy in copies[-1]:
            copy.start()
    for c in range(chunks):
        for copy in copies[c]:
            copy.wait()
        band = a_ref[:, c * n * depth : (c + 1) * n * depth]
        for j in range(kinds):
            w = w_ref[c * n : (c + 1) * n, j].reshape(n * depth, cols)
            part = jnp.dot(band, w, preferred_element_type=F32)
            span = slice(j * cols, (j + 1) * cols)
            if c:
                part += acc_ref[:, span]
            if c < chunks - 1:
                acc_ref[:, span] = part
            else:
                for h in range(heads_ref.shape[0]):
                    heads_ref[h, :, j * HS : (j + 1) * HS] = part[:, h * HS : (h + 1) * HS].astype(BF)


def project(normed, w, heads, after):
    rows, depth = normed.shape
    bands, kinds, _, cols = w.shape
    chunks = 4
    free = pl.BlockSpec(memory_space=pl.ANY)
    return pl.pallas_call(
        functools.partial(project_kernel, chunks),
        in_specs=[free] * (2 + len(after)),
        out_specs=pl.BlockSpec(memory_space=pltpu.VMEM),
        out_shape=shape(heads, rows, kinds * cols // heads),
        scratch_shapes=[
            pltpu.VMEM(normed.shape, BF),
            pltpu.VMEM(w.shape, BF),
            pltpu.VMEM((rows, kinds * cols), F32),
            pltpu.SemaphoreType.DMA((chunks,)),
            pltpu.SemaphoreType.DMA((chunks,)),
        ],
        compiler_params=PARAMS,
        cost_estimate=cost(1, 1),
    )(normed, w, *after)


def attention_kernel(q_rows, qkv_ref, dout_ref, *refs):
    att_ref, grad_ref, dk_ref, dv_ref = refs[-4:]
    scale = 1.0 / math.sqrt(HS)
    key = qkv_ref[:, HS : 2 * HS]
    value = qkv_ref[:, 2 * HS : 3 * HS]
    key_t = key.T
    value_t = value.T
    for i in range(qkv_ref.shape[0] // q_rows):
        rows = pl.ds(i * q_rows, q_rows)
        query = qkv_ref[rows, 0:HS]
        dout = dout_ref[rows, :]
        scores = dot(key, query, 1, 1) * (scale * math.log2(math.e))
        top = jnp.max(scores, axis=0, keepdims=True)
        expo = jnp.exp2(scores - top)
        prob = expo * (1.0 / jnp.sum(expo, axis=0, keepdims=True))
        prob_bf = prob.astype(BF)
        att = dot(value_t, prob_bf, 1, 0).T.astype(BF)
        att_ref[rows, :] = att
        row_dot = jnp.sum(
            dout.astype(F32).T * att.astype(F32).T, axis=0, keepdims=True
        )
        dprob = dot(value, dout, 1, 1)
        dscore = (prob * (dprob - row_dot)).astype(BF)
        grad_ref[rows, 0:HS] = (dot(key_t, dscore, 1, 0) * scale).T.astype(BF)
        dv = dot(prob_bf, dout, 1, 0)
        dk = dot(dscore, query, 1, 0)
        if i == 0:
            dv_ref[...] = dv
            dk_ref[...] = dk
        else:
            dv_ref[...] += dv
            dk_ref[...] += dk
    grad_ref[:, HS : 2 * HS] = (dk_ref[...] * scale).astype(BF)
    grad_ref[:, 2 * HS : 3 * HS] = dv_ref[...].astype(BF)


def attention(qkv, dout, after=()):
    n = qkv.shape[0]
    return pl.pallas_call(
        functools.partial(attention_kernel, min(256, n)),
        out_shape=(shape(n, HS), shape(n, 3 * HS)),
        in_specs=[pl.BlockSpec(memory_space=pltpu.VMEM)] * 2
        + [pl.BlockSpec(memory_space=pl.ANY)] * len(after),
        out_specs=(pl.BlockSpec(memory_space=pltpu.VMEM),) * 2,
        scratch_shapes=[pltpu.VMEM((n, HS), F32), pltpu.VMEM((n, HS), F32)],
        compiler_params=PARAMS,
        cost_estimate=cost(1, 1),
    )(qkv, dout, *after)


def write_stat(ref, at, stat):
    ref[at:, :] = jnp.zeros((ref.shape[0] - at, ref.shape[1]), BF)
    rest = stat
    for i in range(3):
        top = rest.astype(BF)
        ref[at + i : at + i + 1, :] = top
        rest = rest - top.astype(F32)


def read_stat(ref, at):
    return sum(ref[at + i : at + i + 1, :].astype(F32) for i in range(3))


def norm_kernel(width, halves, spots, at_ref, g_ref, p_ref, w_any, *refs):
    n_out = max(spot[0] for spot in spots) + 1
    outs, stat_ref = refs[-4 - n_out : -4], refs[-4]
    w_ref, flat_ref, sems = refs[-3:]
    n, bands, kinds, depth, cols = w_ref.shape
    quarters = w_any.shape[0] // (2 * bands)
    copies = []
    for step, (by, half) in enumerate(halves):
        at = (lax.rem(at_ref[T] + by, quarters) * 2 + half) * bands
        copy = pltpu.make_async_copy(w_any.at[pl.ds(at, bands)], w_ref.at[step], sems.at[step])
        copy.start()
        copies.append(copy)

    heads, _, _ = g_ref.shape
    for h in range(heads):
        for j in range(kinds):
            at = (j * heads + h) * HS
            flat_ref[at : at + HS, :] = g_ref[h, :, j * HS : (j + 1) * HS].T
    total = sum(
        g_ref[h, :, j * HS : (j + 1) * HS].astype(F32)
        * p_ref[h, :, j * HS : (j + 1) * HS].astype(F32)
        for h in range(heads)
        for j in range(kinds)
    )
    stat = jnp.sum(total.T, axis=0, keepdims=True) * (1.0 / width)
    stat_ref[...] = stat
    for ref in outs:
        if ref.shape[0] % 128:
            write_stat(ref, ref.shape[0] - 16, stat)

    for step, (which, at) in enumerate(spots):
        copies[step].wait()
        total = sum(
            dot(
                w_ref[step, :, j].reshape(bands * depth, cols),
                flat_ref[j * cols : (j + 1) * cols, :],
                1,
                0,
            )
            for j in range(kinds)
        )
        outs[which][at : at + bands * depth, :] = total.astype(BF)


def norm_halves(ids, grads, proj, w, halves, spots, sizes, width, after=()):
    heads, rows, _ = grads.shape
    bands, kinds, depth, cols = w.shape
    n = len(spots)
    sizes = (*sizes, 1)
    vmem = pl.BlockSpec(memory_space=pltpu.VMEM)
    free = pl.BlockSpec(memory_space=pl.ANY)
    return pl.pallas_call(
        functools.partial(norm_kernel, width, halves, spots),
        in_specs=[pl.BlockSpec(memory_space=pltpu.SMEM), vmem, vmem, free] + [free] * len(after),
        out_specs=(vmem,) * len(sizes),
        out_shape=tuple(shape(s, rows) for s in sizes[:-1]) + (shape(1, rows, dtype=F32),),
        scratch_shapes=[
            pltpu.VMEM((n, bands // 8, kinds, depth, cols), BF),
            pltpu.VMEM((kinds * cols, rows), BF),
            pltpu.SemaphoreType.DMA((n,)),
        ],
        compiler_params=PARAMS,
        cost_estimate=cost(1, 1),
    )(ids, grads, proj, w, *after)


def add_kernel(up_part, up_in, stat_in, down_part, down_in, stat_ref, *refs):
    up_out, down_out = refs[-2:]
    half = up_part.shape[0]
    for part, came, out in ((up_part, up_in, up_out), (down_part, down_in, down_out)):
        out[:half, :] = (part[...].astype(F32) + came[...].astype(F32)).astype(BF)
    write_stat(up_out, half, stat_ref[...] + read_stat(stat_in, 0))
    write_stat(down_out, half, stat_ref[...])


def add_messages(up_part, up_in, down_part, down_in, stat, after=()):
    half, rows = up_part.shape
    block = pl.BlockSpec((half, rows), lambda i: (0, 0))
    out = pl.BlockSpec((half + 16, rows), lambda i: (0, 0))
    end = pl.BlockSpec((16, rows), lambda i: (2 * half // 16, 0))
    return pl.pallas_call(
        add_kernel,
        grid=(1,),
        out_shape=(shape(half + 16, rows),) * 2,
        in_specs=[block, block, end, block, block, pl.BlockSpec((1, rows), lambda i: (0, 0))]
        + [pl.BlockSpec(memory_space=pl.ANY)] * len(after),
        out_specs=(out, out),
        compiler_params=PARAMS,
        cost_estimate=cost(1, 1),
    )(up_part, up_in, up_in, down_part, down_in, stat, *after)


def finish_kernel(at_ref, own0, own1, up0, up1, down0, down1, tok_ref, root_ref, stat_ref, out_ref):
    half = own0.shape[0]
    stat = stat_ref[...] + read_stat(up0, half) + read_stat(down1, half)
    stat = jnp.broadcast_to(stat, (HS, stat.shape[1])).T[:, 0:1]
    root = root_ref[...]
    parts = (
        (own0[...], up0[:half, :], down0[half : 2 * half, :]),
        (own1[...], up1[half : 2 * half, :], down1[:half, :]),
    )
    for i, part in enumerate(parts):
        span = slice(i * half, (i + 1) * half)
        total = sum(p.astype(F32) for p in part)
        unit = tok_ref[:, span].astype(F32) / root
        out_ref[:, span] = ((total.T - unit * stat) / root).astype(BF)


def finish(ids, parts, tokens, root, stat):
    half, rows = parts[0].shape
    share = 2 * half
    tile = HS
    some = lambda a: pl.BlockSpec((a.shape[0], tile), lambda i, at: (0, i))
    return pl.pallas_call(
        finish_kernel,
        grid_spec=pltpu.PrefetchScalarGridSpec(
            num_scalar_prefetch=1,
            grid=(rows // tile,),
            in_specs=[some(p) for p in parts]
            + [pl.BlockSpec((tile, share), lambda i, at: (i, at[T]))]
            + [pl.BlockSpec((tile, 1), lambda i, at: (i, 0)), some(stat)],
            out_specs=pl.BlockSpec((tile, share), lambda i, at: (i, 0)),
        ),
        out_shape=shape(rows, share),
        compiler_params=PARAMS,
        cost_estimate=cost(1, 1),
    )(ids, *parts, tokens, root, stat)


def outer_kernel(tile, at_ref, *refs):
    blocks, (mine_ref, other_ref, out_ref, a_ref, g_ref, sems) = refs[:-6], refs[-6:]
    n, rows, _ = mine_ref.shape
    depth = a_ref.shape[0]
    copies = []
    for step in range(depth // tile):
        span = pl.ds(step * tile, tile)
        some = []
        for i, block in enumerate(blocks):
            to = a_ref.at[span, pl.ds(i * rows, rows)]
            some.append(pltpu.make_async_copy(block.at[span], to, sems.at[step, i]))
            some[-1].start()
        copies.append(some)
    for i, by in enumerate((0, n - 1, 1, 2)):
        at = lax.rem(at_ref[X] + by, n)
        g_ref[i * rows : (i + 1) * rows, :] = mine_ref[at]
        g_ref[(n + i) * rows : (n + i + 1) * rows, :] = other_ref[at]
    for step, some in enumerate(copies):
        for copy in some:
            copy.wait()
        span = slice(step * tile, (step + 1) * tile)
        out_ref[span, :] = jnp.dot(
            a_ref[span, :], g_ref[...], preferred_element_type=F32
        ).astype(BF)


def outer(ids, blocks, mine, other):
    depth, rows = blocks[0].shape
    cols = mine.shape[2]
    tile = 512
    vmem = pl.BlockSpec(memory_space=pltpu.VMEM)
    return pl.pallas_call(
        functools.partial(outer_kernel, tile),
        in_specs=[pl.BlockSpec(memory_space=pltpu.SMEM)]
        + [pl.BlockSpec(memory_space=pl.ANY)] * len(blocks)
        + [vmem, vmem],
        out_specs=vmem,
        out_shape=shape(depth, cols),
        scratch_shapes=[
            pltpu.VMEM((depth, len(blocks) * rows), BF),
            pltpu.VMEM((len(blocks) * rows, cols), BF),
            pltpu.SemaphoreType.DMA((depth // tile, len(blocks))),
        ],
        compiler_params=PARAMS,
        cost_estimate=cost(1, 1),
    )(ids, *blocks, mine, other)


def split_kernel(at_ref, part_ref, *refs):
    keep_ref, give_ref = refs[-2:]
    n, _, rows, _ = part_ref.shape
    for ref, which in ((keep_ref, at_ref[Z]), (give_ref, 1 - at_ref[Z])):
        ref[...] = sum(part_ref[i, which].astype(F32) for i in range(n)).astype(ref.dtype)


def split(ids, part, after=()):
    _, _, rows, cols = part.shape
    vmem = pl.BlockSpec(memory_space=pltpu.VMEM)
    return pl.pallas_call(
        split_kernel,
        in_specs=[pl.BlockSpec(memory_space=pltpu.SMEM), vmem]
        + [pl.BlockSpec(memory_space=pl.ANY)] * len(after),
        out_specs=(vmem, vmem),
        out_shape=(shape(rows, cols, dtype=F32), shape(rows, cols)),
        compiler_params=PARAMS,
        cost_estimate=cost(1, 1),
    )(ids, part, *after)


def merge_kernel(keep_ref, came_ref, att_ref, *refs):
    out_ref = refs[-1]
    total = (keep_ref[...] + came_ref[...].astype(F32)).astype(BF)
    cols = total.shape[1]
    for i in range(out_ref.shape[0]):
        out_ref[i, :, :cols] = total
        out_ref[i, :, cols:] = att_ref[i]


def merge(keep, came, att, after=()):
    rows, cols = keep.shape
    n, _, more = att.shape
    vmem = pl.BlockSpec(memory_space=pltpu.VMEM)
    return pl.pallas_call(
        merge_kernel,
        out_shape=shape(n, rows, cols + more),
        in_specs=[vmem] * 3 + [pl.BlockSpec(memory_space=pl.ANY)] * len(after),
        out_specs=vmem,
        compiler_params=PARAMS,
        cost_estimate=cost(1, 1),
    )(keep, came, att, *after)


def unpack_kernel(in_ref, w_ref, att_ref):
    for h in range(in_ref.shape[0]):
        span = slice(h * HS, (h + 1) * HS)
        for j in range(3):
            w_ref[j, :, span] = in_ref[h, :, j * HS : (j + 1) * HS].astype(F32)
        att_ref[:, span] = in_ref[h, :, 3 * HS :]


def unpack(last):
    heads, rows, more = last.shape
    tile = rows // 4
    return pl.pallas_call(
        unpack_kernel,
        grid=(rows // tile,),
        in_specs=[pl.BlockSpec((heads, tile, more), lambda i: (0, i, 0))],
        out_specs=(
            pl.BlockSpec((3, tile, heads * HS), lambda i: (0, i, 0)),
            pl.BlockSpec((tile, heads * HS), lambda i: (i, 0)),
        ),
        out_shape=(shape(3, rows, heads * HS, dtype=F32), shape(rows, heads * HS)),
        compiler_params=PARAMS,
        cost_estimate=cost(1, 1),
    )(last)


def shift(x, axis, by):
    n = lax.axis_size(axis)
    return lax.ppermute(x, axis, [(i, (i + by) % n) for i in range(n)])


def per_device(tokens, weights, cotangent):
    _, rows, width = tokens.shape
    w_rows, _, cols = weights.shape
    heads = cols // HS
    n_x, n_y = (lax.axis_size(a) for a in ("x", "y"))
    ids = jnp.stack([lax.axis_index(a) for a in ("core", "x", "zh", "y", "zl")])
    tokens = tokens.reshape(rows, width)
    half = width // lax.axis_size("zh") // 2

    w = lax.all_gather(weights.transpose(1, 0, 2)[None], ("y", "zl", "core"), axis=0, tiled=True)

    normed, root, mine, given = unit_rows(ids, tokens, w_rows)
    theirs = shift(given, "core", 1)
    left_m, right_m = shift(mine, "x", 1), shift(mine, "x", -1)
    left_t, right_t = shift(theirs, "x", 1), shift(theirs, "x", -1)
    far_m, far_t = shift(left_m, "x", 1), shift(right_t, "x", -1)
    blocks = (mine, left_m, right_m, far_m, theirs, left_t, right_t, far_t)

    dout = cotangent.reshape(rows, heads, HS).transpose(1, 0, 2)
    dout = lax.all_to_all(dout, "x", 0, 0, tiled=True).reshape(n_x * rows, HS)

    proj = project(normed, w, heads, (*blocks, dout))
    qkv = lax.all_to_all(proj, "x", 0, 0, tiled=True).reshape(n_x * rows, 3 * HS)
    att, head_grads = attention(qkv, dout)

    head_grads = head_grads.reshape(n_x, rows, 3 * HS)
    grads = lax.all_to_all(head_grads, "x", 0, 0, tiled=True)
    part = outer(ids, blocks, head_grads, shift(head_grads, "core", 1))

    up, down, stat = norm_halves(
        ids, grads, proj, w,
        ((2, 0), (1, 1), (2, 1), (3, 0)),
        ((0, 0), (0, half), (1, 0), (1, half)),
        (2 * half + 16, 2 * half),
        width,
    )
    up, down = shift(up, "zh", 1), shift(down, "zh", -1)
    up_part, down_part, own0, own1, _ = norm_halves(
        ids, grads, proj, w,
        ((1, 0), (3, 1), (0, 0), (0, 1)),
        ((0, 0), (1, 0), (2, 0), (3, 0)),
        (half,) * 4,
        width,
        (stat,),
    )
    part = lax.all_to_all(part, "y", 0, 0, tiled=True).reshape(n_y, 2, w_rows, 3 * HS)
    keep, give = split(ids, part, (own0,))
    came = shift(give, "zl", 1)
    up_2, down_2 = add_messages(up_part, up, down_part, down, stat, (give,))
    last = merge(keep, came, att.reshape(n_x, rows, HS), (up_2,))
    up_2, down_2 = shift(up_2, "zh", 1), shift(down_2, "zh", -1)
    last = lax.all_to_all(last, "x", 0, 0, tiled=True)
    token_grad = finish(ids, (own0, own1, up_2, up, down, down_2), tokens, root, stat)
    weight_grad, attended = unpack(last)
    return attended[None], token_grad[None], weight_grad.transpose(1, 0, 2)


def solution(mesh):
    fine = Mesh(mesh.devices.reshape(4, 2, 2, 4, 4), ("y", "zl", "core", "x", "zh"))
    dp = ("y", "zl", "core")
    return jax.shard_map(
        per_device,
        mesh=fine,
        in_specs=(P(dp, "x", None), P(dp, None, "zh"), P(dp, "x", "zh")),
        out_specs=(P(dp, "x", "zh"), P(dp, "x", "zh"), P(dp, None, "zh")),
        check_vma=False,
    )
```

time: 251 us -> 225 us (0.90)
  waiting for transfers between devices: 111 us -> 48.9 us
  blocking collectives: 16.7 us -> 59.2 us
  local copies, waits for them, and re-layouts: 13.6 us -> 7.19 us
    all_to_all x0 -> x1, blocking collectives: none -> 42.2 us  [per_device(): dout = lax.all_to_all(dout, 'x', 0, 0, tiled=True).reshape(n_x * rows, HS)]
    all_gather x2 -> x1, waiting for transfers between devices: 36.7 us -> 0.02 us  [per_device(): lax.all_gather(weights.transpose(1, 0, 2)[None], ('y', 'zl', 'core'), axi...]
    all_to_all x2 -> x1, waiting for transfers between devices: 18.3 us -> 0.01 us  [per_device(): lax.all_to_all(part, 'y', 0, 0, tiled=True).reshape(n_y, 2, w_rows, 3 * HS)]
    ppermute x12 -> x13, waiting for transfers between devices: 52.3 us -> 45.3 us  [shift(): return lax.ppermute(x, axis, [(i, (i + by) % n) for i in range(n)])]
    ppermute x12 -> x13, starting transfers between devices: 17.9 us -> 22.2 us  [shift(): return lax.ppermute(x, axis, [(i, (i + by) % n) for i in range(n)])]
    unnamed x30 -> x28, local copies, waits for them, and re-layouts: 9.23 us -> 5.44 us
    all_to_all x2 -> x1, starting transfers between devices: 8.57 us -> 4.91 us  [per_device(): lax.all_to_all(part, 'y', 0, 0, tiled=True).reshape(n_y, 2, w_rows, 3 * HS)]
    slice x2 -> x0, local copies, waits for them, and re-layouts: 3.59 us -> none  [the longest x1 1.91 us: per_device(): w_qk = gather(w_kinds[:, :2])]
  transfers between devices with their start and end apart: 18 -> 17, of which waited for: 12 -> 8; matrix products, arithmetic and copies ran while one was open for 1% -> 1% of each run, Pallas kernels for 16% -> 17%
where the time goes in v4:
time: 225 us; the launch traced here: 222 us
  blocking collectives  59.2 us (26%)
  Pallas kernels  58.5 us (26%)
  waiting for transfers between devices  48.9 us (22%)
  starting transfers between devices  34.1 us (15%)
  between operations  14.2 us (6%)
  local copies, waits for them, and re-layouts  7.19 us (3%)
    ppermute x13, waiting for transfers between devices, shift(): return lax.ppermute(x, axis, [(i, (i + by) % n) for i in range(n)])  45.3 us
    all_to_all x1, blocking collectives, per_device(): dout = lax.all_to_all(dout, 'x', 0, 0, tiled=True).reshape(n_x * rows, HS)  42.2 us
    ppermute x13, starting transfers between devices, shift(): return lax.ppermute(x, axis, [(i, (i + by) % n) for i in range(n)])  22.2 us
    all_to_all x1, blocking collectives, per_device(): lax.all_to_all(proj, 'x', 0, 0, tiled=True).reshape(n_x * rows, 3 * HS)  17.1 us
    pallas_call x2, Pallas kernels, norm_halves(): pl.pallas_call(functools.partial(norm_kernel, width, halves, spots), in_s...  14.9 us
    pallas_call x1, Pallas kernels, outer(): pl.pallas_call(functools.partial(outer_kernel, tile), in_specs=[pl.BlockS...  9.34 us
    pallas_call x1, Pallas kernels, attention(): pl.pallas_call(functools.partial(attention_kernel, min(256, n)), out_shap...  8.61 us
    pallas_call x1, Pallas kernels, project(): pl.pallas_call(functools.partial(project_kernel, chunks), in_specs=[free]...  7.2 us
  transfers between devices with their start and end apart: 17, of which 8 were waited for; matrix products, arithmetic and copies ran while one was open for 1% of the time, Pallas kernels for 17%

profile of v4, /device:TPU:8, one launch (start us, length us, event | category | flops | bytes accessed | tf_op | source)
XLA Modules:
  0.0 222.2 jit_solution(4629640247544694125)
XLA Ops:
  7.2 0.0 all-gather.3.cloned.1.call-start
  7.2 0.7 all-gather.3.cloned.1.call-update
  7.9 0.7 stack.23.at_ref
  8.6 4.6 %shard_map.58 = (bf16[256,4096]{1,0:T(8,128)(2,1)}, f32[256,1]{1,0:T(8,128)}, bf16[2048,256]{1,0:T(8,128)(2,1)}, bf16[2048,256]{1,0:T(8,128)(2,1)}) custom-call(s32[5]{0:T(128)} %stack.23.at_ref, bf16[256,4096]{1,0:T(8,128)(2,1)} %bitcast.23), custom_call_target="tpu_custom_call" | custom-call | flops 6291456 | bytes 6291456 | tf_op jit(solution)/shard_map/pallas_call | solution.py:46
  13.2 0.0 collective-permute-start.3
  13.2 1.5 collective-permute-start
  14.7 1.4 collective-permute-done.3.refs_4_
  16.1 2.8 %collective-permute-start.5 = (bf16[2048,256]{1,0:T(8,128)(2,1)S(1)}, bf16[2048,256]{1,0:T(8,128)(2,1)S(1)}, u32[]{:S(2)}, u32[]{:S(2)}) collective-permute-start(bf16[2048,256]{1,0:T(8,128)(2,1)S(1)} %collective-permute-done.3.refs_4_), channel_id=1, source_target_pairs={{0,12},{4,0},{8,4},{12,8},{1,13},{5,1},{9,5},{13,9},{2,14},{6,2},{... | collective-permute-start | bytes 3145736 | tf_op jit(solution)/shard_map/ppermute | solution.py:436
  18.8 0.9 collective-permute-start.1
  19.7 1.2 collective-permute-start.4
  20.8 19.7 %collective-permute-done.refs_1_ = bf16[2048,256]{1,0:T(8,128)(2,1)S(1)} collective-permute-done((bf16[2048,256]{1,0:T(8,128)(2,1)}, bf16[2048,256]{1,0:T(8,128)(2,1)S(1)}, u32[]{:S(2)}, u32[]{:S(2)}) %collective-permute-start) | collective-permute-done | bytes 1048608 | tf_op jit(solution)/shard_map/ppermute | solution.py:436
  40.6 0.3 collective-permute-start.2
  40.8 1.5 collective-permute-done.5.refs_6_
  42.3 3.7 %collective-permute-start.6 = (bf16[2048,256]{1,0:T(8,128)(2,1)S(1)}, bf16[2048,256]{1,0:T(8,128)(2,1)}, u32[]{:S(2)}, u32[]{:S(2)}) collective-permute-start(bf16[2048,256]{1,0:T(8,128)(2,1)S(1)} %collective-permute-done.5.refs_6_), channel_id=1, source_target_pairs={{0,12},{4,0},{8,4},{12,8},{1,13},{5,1},{9,5},{13,9},{2,14},{6,2},{... | collective-permute-start | bytes 3145736 | tf_op jit(solution)/shard_map/ppermute | solution.py:436
  46.0 1.0 reshape.31
  47.1 42.2 %all_to_all.29 = bf16[4,256,128]{2,1,0:T(8,128)(2,1)} all-to-all(bf16[4,256,128]{2,1,0:T(8,128)(2,1)S(1)} %bitcast.33), channel_id=1, replica_groups=mesh['y'=4,'zl'=2,'core'=2,'x'=4,'zh'=4] {'x'}, dimensions={0} | all-to-all | bytes 524288 | tf_op jit(solution)/shard_map/all_to_all | solution.py:458
  89.3 0.0 collective-permute-done.1.refs_2_
  89.3 0.0 collective-permute-done.2.refs_3_
  89.3 0.0 collective-permute-done.4.refs_5_
  89.3 0.0 collective-permute-done.6.refs_7_
  89.3 0.0 all-gather.3.cloned.1.call-done
  89.3 0.0 copy-done.3
  89.3 0.0 copy-done.4
  89.4 0.0 copy-done.5
  89.4 7.2 %shard_map.59.p_ref = bf16[4,256,384]{2,1,0:T(8,128)(2,1)} custom-call(bf16[256,4096]{1,0:T(8,128)(2,1)} %get-tuple-element.24.a_any, bf16[16,3,256,512]{3,2,1,0:T(8,128)(2,1)} %bitcast.20, bf16[2048,256]{1,0:T(8,128)(2,1)} %get-tuple-element.22.refs_0_, bf16[2048,256]{1,0:T(8,128)(2,1)} %copy-done.4, bf16[2048,256]{1,0:T(8,128)(2,1)} %collective-permute-done.1.refs_2_, ...), custom_call_target="tpu_custom_call" | custom-call | flops 1 | bytes 1 | tf_op jit(solution)/shard_map/pallas_call | solution.py:108
  96.6 17.1 %all_to_all.30 = bf16[4,256,384]{2,1,0:T(8,128)(2,1)} all-to-all(bf16[4,256,384]{2,1,0:T(8,128)(2,1)} %shard_map.59.p_ref), channel_id=1, replica_groups=mesh['y'=4,'zl'=2,'core'=2,'x'=4,'zh'=4] {'x'}, dimensions={0} | all-to-all | bytes 1572864 | tf_op jit(solution)/shard_map/all_to_all | solution.py:461
  113.6 8.6 %shard_map.60 = (bf16[1024,128]{1,0:T(8,128)(2,1)}, bf16[1024,384]{1,0:T(8,128)(2,1)}) custom-call(bf16[1024,384]{1,0:T(8,128)(2,1)} %bitcast.30, bf16[1024,128]{1,0:T(8,128)(2,1)} %bitcast.32), custom_call_target="tpu_custom_call" | custom-call | flops 1 | bytes 1 | tf_op jit(solution)/shard_map/pallas_call | solution.py:163
  122.2 0.0 collective-permute-start.7
  122.2 3.5 %all-to-all-start.3 = ((bf16[4,256,384]{2,1,0:T(8,128)(2,1)}), bf16[4,256,384]{2,1,0:T(8,128)(2,1)S(1)}, u32[]{:S(2)}, u32[]{:S(2)}) async-start(bf16[4,256,384]{2,1,0:T(8,128)(2,1)} %bitcast.28), calls=%async_computation.3 | async-start | bytes 1572864 | tf_op jit(solution)/shard_map/all_to_all | solution.py:465
  125.7 0.0 collective-permute-done.7.refs_9_
  125.7 0.0 copy-start.8
  125.8 0.9 copy-done.8
  126.6 9.3 %shard_map.61 = bf16[2048,384]{1,0:T(8,128)(2,1)} custom-call(s32[5]{0:T(128)} %stack.23.at_ref, bf16[2048,256]{1,0:T(8,128)(2,1)} %get-tuple-element.22.refs_0_, bf16[2048,256]{1,0:T(8,128)(2,1)} %copy-done.4, bf16[2048,256]{1,0:T(8,128)(2,1)} %collective-permute-done.1.refs_2_, bf16[2048,256]{1,0:T(8,128)(2,1)} %collective-permute-done.2.refs_3_, ...), custom_call_target="tpu_custom_call" | custom-call | flops 1 | bytes 1 | tf_op jit(solution)/shard_map/pallas_call | solution.py:348
  136.0 3.0 %all-to-all-done.3.g_ref = bf16[4,256,384]{2,1,0:T(8,128)(2,1)S(1)} async-done(((bf16[4,256,384]{2,1,0:T(8,128)(2,1)}), bf16[4,256,384]{2,1,0:T(8,128)(2,1)S(1)}, u32[]{:S(2)}, u32[]{:S(2)}) %all-to-all-start.3) | async-done | bytes 786464 | tf_op jit(solution)/shard_map/all_to_all | solution.py:465
  138.9 4.9 %all-to-all-start.2 = ((bf16[4,512,384]{2,1,0:T(8,128)(2,1)}), bf16[4,512,384]{2,1,0:T(8,128)(2,1)S(1)}, u32[]{:S(2)}, u32[]{:S(2)}) async-start(bf16[4,512,384]{2,1,0:T(8,128)(2,1)} %bitcast.26), calls=%async_computation.2 | async-start | bytes 3145728 | tf_op jit(solution)/shard_map/all_to_all | solution.py:484
  143.9 7.5 %shard_map.62 = (bf16[1040,256]{1,0:T(8,128)(2,1)}, bf16[1024,256]{1,0:T(8,128)(2,1)}, f32[1,256]{1,0:T(1,128)}) custom-call(s32[5]{0:T(128)} %stack.23.at_ref, bf16[4,256,384]{2,1,0:T(8,128)(2,1)} %copy-done, bf16[4,256,384]{2,1,0:T(8,128)(2,1)} %shard_map.59.p_ref, bf16[16,3,256,512]{3,2,1,0:T(8,128)(2,1)} %bitcast.21), custom_call_target="tpu_custom_call" | custom-call | flops 1 | bytes 1 | tf_op jit(solution)/shard_map/pallas_call | solution.py:239
  151.3 3.6 %collective-permute-start.9 = (bf16[1040,256]{1,0:T(8,128)(2,1)}, bf16[1040,256]{1,0:T(8,128)(2,1)S(1)}, u32[]{:S(2)}, u32[]{:S(2)}) collective-permute-start(bf16[1040,256]{1,0:T(8,128)(2,1)} %get-tuple-element.32), channel_id=1, source_target_pairs={{0,1},{1,2},{2,3},{3,0},{4,5},{5,6},{6,7},{7,4},{8,9},{9,10},{10,1... | collective-permute-start | bytes 1597448 | tf_op jit(solution)/shard_map/ppermute | solution.py:436
  154.9 3.1 %collective-permute-start.10 = (bf16[1024,256]{1,0:T(8,128)(2,1)}, bf16[1024,256]{1,0:T(8,128)(2,1)S(1)}, u32[]{:S(2)}, u32[]{:S(2)}) collective-permute-start(bf16[1024,256]{1,0:T(8,128)(2,1)} %get-tuple-element.34), channel_id=1, source_target_pairs={{0,3},{1,0},{2,1},{3,2},{4,7},{5,4},{6,5},{7,6},{8,11},{9,8},{10,9... | collective-permute-start | bytes 1572872 | tf_op jit(solution)/shard_map/ppermute | solution.py:436
  158.0 7.4 %shard_map.63 = (bf16[512,256]{1,0:T(8,128)(2,1)}, bf16[512,256]{1,0:T(8,128)(2,1)}, bf16[512,256]{1,0:T(8,128)(2,1)}, bf16[512,256]{1,0:T(8,128)(2,1)}, f32[1,256]{1,0:T(1,128)}) custom-call(s32[5]{0:T(128)} %stack.23.at_ref, bf16[4,256,384]{2,1,0:T(8,128)(2,1)} %copy-done, bf16[4,256,384]{2,1,0:T(8,128)(2,1)} %shard_map.59.p_ref, ...), custom_call_target="tpu_custom_call" | custom-call | flops 1 | bytes 1 | tf_op jit(solution)/shard_map/pallas_call | solution.py:239
  165.4 0.0 all-to-all-done.2
  165.4 0.0 copy-start.1
  165.4 1.1 copy-done.1
  166.6 2.3 %shard_map.64 = (f32[256,384]{1,0:T(8,128)}, bf16[256,384]{1,0:T(8,128)(2,1)}) custom-call(s32[5]{0:T(128)} %stack.23.at_ref, bf16[4,2,256,384]{3,2,1,0:T(8,128)(2,1)} %bitcast.25, bf16[512,256]{1,0:T(8,128)(2,1)} %get-tuple-element.27.refs_0_.own0), custom_call_target="tpu_custom_call" | custom-call | flops 1 | bytes 1 | tf_op jit(solution)/shard_map/pallas_call | solution.py:375
  168.9 1.0 collective-permute-start.8
  169.9 11.8 %collective-permute-done.10.down_in.down0 = bf16[1024,256]{1,0:T(8,128)(2,1)S(1)} collective-permute-done((bf16[1024,256]{1,0:T(8,128)(2,1)}, bf16[1024,256]{1,0:T(8,128)(2,1)S(1)}, u32[]{:S(2)}, u32[]{:S(2)}) %collective-permute-start.10) | collective-permute-done | bytes 524320 | tf_op jit(solution)/shard_map/ppermute | solution.py:436
  181.8 0.1 collective-permute-done.9.up_in.stat_in.up1
  181.8 0.8 copy-done.7
  182.6 0.2 copy-done.2
  182.8 2.2 %shard_map.65 = (bf16[528,256]{1,0:T(8,128)(2,1)}, bf16[528,256]{1,0:T(8,128)(2,1)}) custom-call(bf16[512,256]{1,0:T(8,128)(2,1)} %get-tuple-element.31.up_part, bf16[1040,256]{1,0:T(8,128)(2,1)} %copy-done.2, bf16[1040,256]{1,0:T(8,128)(2,1)} %copy-done.2, bf16[512,256]{1,0:T(8,128)(2,1)} %get-tuple-element.33.down_part, bf16[1024,256]{1,0:T(8,128)(2,1)} %copy-done.7, ...), custom_call_target="tpu_custom_call" | custom-call | flops 1 | bytes 1 | tf_op jit(solution)/shard_map/pallas_call | solution.py:268
  185.0 0.7 collective-permute-done.8.came_ref
  185.7 0.7 copy-done.12
  186.4 2.3 %shard_map.66 = bf16[4,256,512]{2,1,0:T(8,128)(2,1)} custom-call(f32[256,384]{1,0:T(8,128)} %get-tuple-element.28.keep_ref, bf16[256,384]{1,0:T(8,128)(2,1)} %copy-done.12, bf16[4,256,128]{2,1,0:T(8,128)(2,1)} %bitcast.36, bf16[528,256]{1,0:T(8,128)(2,1)} %get-tuple-element.35.refs_0_), custom_call_target="tpu_custom_call" | custom-call | flops 1 | bytes 1 | tf_op jit(solution)/shard_map/pallas_call | solution.py:399
  188.7 3.5 %all-to-all-start.4 = ((bf16[4,256,512]{2,1,0:T(8,128)(2,1)}), bf16[4,256,512]{2,1,0:T(8,128)(2,1)S(1)}, u32[]{:S(2)}, u32[]{:S(2)}) async-start(bf16[4,256,512]{2,1,0:T(8,128)(2,1)} %shard_map.66), calls=%async_computation.4 | async-start | bytes 2097152 | tf_op jit(solution)/shard_map/all_to_all | solution.py:490
  192.2 0.0 copy-done.9
  192.2 2.3 %collective-permute-start.11 = (bf16[528,256]{1,0:T(8,128)(2,1)S(1)}, bf16[528,256]{1,0:T(8,128)(2,1)S(1)}, u32[]{:S(2)}, u32[]{:S(2)}) collective-permute-start(bf16[528,256]{1,0:T(8,128)(2,1)S(1)} %copy-done.9), channel_id=1, source_target_pairs={{0,1},{1,2},{2,3},{3,0},{4,5},{5,6},{6,7},{7,4},{8,9},{9,10},{10,1... | collective-permute-start | bytes 811016 | tf_op jit(solution)/shard_map/ppermute | solution.py:436
  194.5 1.9 collective-permute-start.12
  196.4 10.1 %collective-permute-done.11.up0 = bf16[528,256]{1,0:T(8,128)(2,1)S(1)} collective-permute-done((bf16[528,256]{1,0:T(8,128)(2,1)S(1)}, bf16[528,256]{1,0:T(8,128)(2,1)S(1)}, u32[]{:S(2)}, u32[]{:S(2)}) %collective-permute-start.11) | collective-permute-done | bytes 270368 | tf_op jit(solution)/shard_map/ppermute | solution.py:436
  206.5 0.0 collective-permute-done.12.down1
  206.5 0.7 copy-done.10
  207.2 0.1 copy-done.11
  207.3 3.5 %shard_map.68 = bf16[256,1024]{1,0:T(8,128)(2,1)} custom-call(s32[5]{0:T(128)} %stack.23.at_ref, bf16[512,256]{1,0:T(8,128)(2,1)} %get-tuple-element.27.refs_0_.own0, bf16[512,256]{1,0:T(8,128)(2,1)} %get-tuple-element.37.own1, bf16[528,256]{1,0:T(8,128)(2,1)} %copy-done.10, bf16[1040,256]{1,0:T(8,128)(2,1)} %copy-done.2, bf16[1024,256]{1,0:T(8,128)(2,1)} %copy-done.7, ...), custom_call_target="tpu_custom_call" | custom-call | flops 1 | bytes 1 | tf_op jit(solution)/shard_map/pallas_call | solution.py:301
  210.8 0.0 all-to-all-done.4.in_ref
  210.8 1.0 copy-done.6
  211.8 3.5 %shard_map.67 = (f32[3,256,512]{2,1,0:T(8,128)}, bf16[256,512]{1,0:T(8,128)(2,1)}) custom-call(bf16[4,256,512]{2,1,0:T(8,128)(2,1)} %copy-done.6), custom_call_target="tpu_custom_call" | custom-call | flops 1 | bytes 1 | tf_op jit(solution)/shard_map/pallas_call | solution.py:420
  (15 shorter events, 0.1 us)
Async XLA Ops:
  7.2 82.2 %all-gather.3.cloned.1.call-start = ((), (), s32[]{:S(2)}) async-start(), calls=%async_computation.5 | async-start | bytes 13369344 | tf_op jit(solution)/shard_map/all_gather | solution.py:448
  13.2 2.9 %collective-permute-start.3 = (bf16[2048,256]{1,0:T(8,128)(2,1)}, bf16[2048,256]{1,0:T(8,128)(2,1)S(1)}, u32[]{:S(2)}, u32[]{:S(2)}) collective-permute-start(bf16[2048,256]{1,0:T(8,128)(2,1)} %get-tuple-element.23), channel_id=1, source_target_pairs={{0,16},{16,0},{1,17},{17,1},{2,18},{18,2},{3,19},{19,3},{4,20},{20... | collective-permute-start | bytes 3145736 | tf_op jit(solution)/shard_map/ppermute | solution.py:436
  13.2 27.4 %collective-permute-start = (bf16[2048,256]{1,0:T(8,128)(2,1)}, bf16[2048,256]{1,0:T(8,128)(2,1)S(1)}, u32[]{:S(2)}, u32[]{:S(2)}) collective-permute-start(bf16[2048,256]{1,0:T(8,128)(2,1)} %get-tuple-element.22.refs_0_), channel_id=1, source_target_pairs={{0,4},{4,8},{8,12},{12,0},{1,5},{5,9},{9,13},{13,1},{2,6},{6,10},{... | collective-permute-start | bytes 3145736 | tf_op jit(solution)/shard_map/ppermute | solution.py:436
  16.0 73.3 %copy-start.3 = (bf16[2048,256]{1,0:T(8,128)(2,1)}, bf16[2048,256]{1,0:T(8,128)(2,1)S(1)}, u32[]{:S(2)}) copy-start(bf16[2048,256]{1,0:T(8,128)(2,1)S(1)} %collective-permute-done.3.refs_4_) | copy-start | bytes 3145732
  16.1 26.3 %collective-permute-start.5 = (bf16[2048,256]{1,0:T(8,128)(2,1)S(1)}, bf16[2048,256]{1,0:T(8,128)(2,1)S(1)}, u32[]{:S(2)}, u32[]{:S(2)}) collective-permute-start(bf16[2048,256]{1,0:T(8,128)(2,1)S(1)} %collective-permute-done.3.refs_4_), channel_id=1, source_target_pairs={{0,12},{4,0},{8,4},{12,8},{1,13},{5,1},{9,5},{13,9},{2,14},{6,2},{... | collective-permute-start | bytes 3145736 | tf_op jit(solution)/shard_map/ppermute | solution.py:436
  18.8 70.5 %collective-permute-start.1 = (bf16[2048,256]{1,0:T(8,128)(2,1)}, bf16[2048,256]{1,0:T(8,128)(2,1)}, u32[]{:S(2)}, u32[]{:S(2)}) collective-permute-start(bf16[2048,256]{1,0:T(8,128)(2,1)} %get-tuple-element.22.refs_0_), channel_id=1, source_target_pairs={{0,12},{4,0},{8,4},{12,8},{1,13},{5,1},{9,5},{13,9},{2,14},{6,2},{... | collective-permute-start | bytes 3145736 | tf_op jit(solution)/shard_map/ppermute | solution.py:436
  19.7 69.6 %collective-permute-start.4 = (bf16[2048,256]{1,0:T(8,128)(2,1)S(1)}, bf16[2048,256]{1,0:T(8,128)(2,1)}, u32[]{:S(2)}, u32[]{:S(2)}) collective-permute-start(bf16[2048,256]{1,0:T(8,128)(2,1)S(1)} %collective-permute-done.3.refs_4_), channel_id=1, source_target_pairs={{0,4},{4,8},{8,12},{12,0},{1,5},{5,9},{9,13},{13,1},{2,6},{6,10},{... | collective-permute-start | bytes 3145736 | tf_op jit(solution)/shard_map/ppermute | solution.py:436
  40.6 48.8 %copy-start.4 = (bf16[2048,256]{1,0:T(8,128)(2,1)}, bf16[2048,256]{1,0:T(8,128)(2,1)S(1)}, u32[]{:S(2)}) copy-start(bf16[2048,256]{1,0:T(8,128)(2,1)S(1)} %collective-permute-done.refs_1_) | copy-start | bytes 3145732
  40.6 48.7 %collective-permute-start.2 = (bf16[2048,256]{1,0:T(8,128)(2,1)S(1)}, bf16[2048,256]{1,0:T(8,128)(2,1)}, u32[]{:S(2)}, u32[]{:S(2)}) collective-permute-start(bf16[2048,256]{1,0:T(8,128)(2,1)S(1)} %collective-permute-done.refs_1_), channel_id=1, source_target_pairs={{0,4},{4,8},{8,12},{12,0},{1,5},{5,9},{9,13},{13,1},{2,6},{6,10},{... | collective-permute-start | bytes 3145736 | tf_op jit(solution)/shard_map/ppermute | solution.py:436
  42.3 47.0 %copy-start.5 = (bf16[2048,256]{1,0:T(8,128)(2,1)}, bf16[2048,256]{1,0:T(8,128)(2,1)S(1)}, u32[]{:S(2)}) copy-start(bf16[2048,256]{1,0:T(8,128)(2,1)S(1)} %collective-permute-done.5.refs_6_) | copy-start | bytes 3145732
  42.3 47.0 %collective-permute-start.6 = (bf16[2048,256]{1,0:T(8,128)(2,1)S(1)}, bf16[2048,256]{1,0:T(8,128)(2,1)}, u32[]{:S(2)}, u32[]{:S(2)}) collective-permute-start(bf16[2048,256]{1,0:T(8,128)(2,1)S(1)} %collective-permute-done.5.refs_6_), channel_id=1, source_target_pairs={{0,12},{4,0},{8,4},{12,8},{1,13},{5,1},{9,5},{13,9},{2,14},{6,2},{... | collective-permute-start | bytes 3145736 | tf_op jit(solution)/shard_map/ppermute | solution.py:436
  122.2 3.5 %collective-permute-start.7 = (bf16[4,256,384]{2,1,0:T(8,128)(2,1)}, bf16[4,256,384]{2,1,0:T(8,128)(2,1)S(1)}, u32[]{:S(2)}, u32[]{:S(2)}) collective-permute-start(bf16[4,256,384]{2,1,0:T(8,128)(2,1)} %bitcast.27), channel_id=1, source_target_pairs={{0,16},{16,0},{1,17},{17,1},{2,18},{18,2},{3,19},{19,3},{4,20},{20... | collective-permute-start | bytes 2359304 | tf_op jit(solution)/shard_map/ppermute | solution.py:436
  122.2 16.7 %all-to-all-start.3 = ((bf16[4,256,384]{2,1,0:T(8,128)(2,1)}), bf16[4,256,384]{2,1,0:T(8,128)(2,1)S(1)}, u32[]{:S(2)}, u32[]{:S(2)}) async-start(bf16[4,256,384]{2,1,0:T(8,128)(2,1)} %bitcast.28), calls=%async_computation.3 | async-start | bytes 1572864 | tf_op jit(solution)/shard_map/all_to_all | solution.py:465
  125.7 0.9 copy-start.8
  138.9 4.9 %copy-start = (bf16[4,256,384]{2,1,0:T(8,128)(2,1)}, bf16[4,256,384]{2,1,0:T(8,128)(2,1)S(1)}, u32[]{:S(2)}) copy-start(bf16[4,256,384]{2,1,0:T(8,128)(2,1)S(1)} %all-to-all-done.3.g_ref) | copy-start | bytes 2359300
  138.9 26.5 %all-to-all-start.2 = ((bf16[4,512,384]{2,1,0:T(8,128)(2,1)}), bf16[4,512,384]{2,1,0:T(8,128)(2,1)S(1)}, u32[]{:S(2)}, u32[]{:S(2)}) async-start(bf16[4,512,384]{2,1,0:T(8,128)(2,1)} %bitcast.26), calls=%async_computation.2 | async-start | bytes 3145728 | tf_op jit(solution)/shard_map/all_to_all | solution.py:484
  151.3 30.5 %collective-permute-start.9 = (bf16[1040,256]{1,0:T(8,128)(2,1)}, bf16[1040,256]{1,0:T(8,128)(2,1)S(1)}, u32[]{:S(2)}, u32[]{:S(2)}) collective-permute-start(bf16[1040,256]{1,0:T(8,128)(2,1)} %get-tuple-element.32), channel_id=1, source_target_pairs={{0,1},{1,2},{2,3},{3,0},{4,5},{5,6},{6,7},{7,4},{8,9},{9,10},{10,1... | collective-permute-start | bytes 1597448 | tf_op jit(solution)/shard_map/ppermute | solution.py:436
  154.9 26.9 %collective-permute-start.10 = (bf16[1024,256]{1,0:T(8,128)(2,1)}, bf16[1024,256]{1,0:T(8,128)(2,1)S(1)}, u32[]{:S(2)}, u32[]{:S(2)}) collective-permute-start(bf16[1024,256]{1,0:T(8,128)(2,1)} %get-tuple-element.34), channel_id=1, source_target_pairs={{0,3},{1,0},{2,1},{3,2},{4,7},{5,4},{6,5},{7,6},{8,11},{9,8},{10,9... | collective-permute-start | bytes 1572872 | tf_op jit(solution)/shard_map/ppermute | solution.py:436
  165.4 1.1 copy-start.1
  168.9 16.7 %collective-permute-start.8 = (bf16[256,384]{1,0:T(8,128)(2,1)}, bf16[256,384]{1,0:T(8,128)(2,1)S(1)}, u32[]{:S(2)}, u32[]{:S(2)}) collective-permute-start(bf16[256,384]{1,0:T(8,128)(2,1)} %get-tuple-element.29.refs_0_), channel_id=1, source_target_pairs={{0,32},{32,0},{1,33},{33,1},{2,34},{34,2},{3,35},{35,3},{4,36},{36... | collective-permute-start | bytes 589832 | tf_op jit(solution)/shard_map/ppermute | solution.py:436
  181.8 0.8 copy-start.7
  181.8 0.9 copy-start.2
  185.7 0.7 copy-start.12
  186.4 5.8 %copy-start.9 = (bf16[528,256]{1,0:T(8,128)(2,1)S(1)}, bf16[528,256]{1,0:T(8,128)(2,1)}, u32[]{:S(2)}) copy-start(bf16[528,256]{1,0:T(8,128)(2,1)} %get-tuple-element.35.refs_0_) | copy-start | bytes 811012
  186.4 8.1 %copy-start.13 = (bf16[528,256]{1,0:T(8,128)(2,1)S(1)}, bf16[528,256]{1,0:T(8,128)(2,1)}, u32[]{:S(2)}) copy-start(bf16[528,256]{1,0:T(8,128)(2,1)} %get-tuple-element.38) | copy-start | bytes 811012
  188.7 22.1 %all-to-all-start.4 = ((bf16[4,256,512]{2,1,0:T(8,128)(2,1)}), bf16[4,256,512]{2,1,0:T(8,128)(2,1)S(1)}, u32[]{:S(2)}, u32[]{:S(2)}) async-start(bf16[4,256,512]{2,1,0:T(8,128)(2,1)} %shard_map.66), calls=%async_computation.4 | async-start | bytes 2097152 | tf_op jit(solution)/shard_map/all_to_all | solution.py:490
  192.2 14.3 %collective-permute-start.11 = (bf16[528,256]{1,0:T(8,128)(2,1)S(1)}, bf16[528,256]{1,0:T(8,128)(2,1)S(1)}, u32[]{:S(2)}, u32[]{:S(2)}) collective-permute-start(bf16[528,256]{1,0:T(8,128)(2,1)S(1)} %copy-done.9), channel_id=1, source_target_pairs={{0,1},{1,2},{2,3},{3,0},{4,5},{5,6},{6,7},{7,4},{8,9},{9,10},{10,1... | collective-permute-start | bytes 811016 | tf_op jit(solution)/shard_map/ppermute | solution.py:436
  194.5 12.0 %collective-permute-start.12 = (bf16[528,256]{1,0:T(8,128)(2,1)S(1)}, bf16[528,256]{1,0:T(8,128)(2,1)S(1)}, u32[]{:S(2)}, u32[]{:S(2)}) collective-permute-start(bf16[528,256]{1,0:T(8,128)(2,1)S(1)} %copy-done.13), channel_id=1, source_target_pairs={{0,3},{1,0},{2,1},{3,2},{4,7},{5,4},{6,5},{7,6},{8,11},{9,8},{10,9... | collective-permute-start | bytes 811016 | tf_op jit(solution)/shard_map/ppermute | solution.py:436
  206.5 0.7 copy-start.10
  206.5 0.8 copy-start.11
  210.8 1.0 copy-start.6
Sparse Core Ops, SparseCore 0:
  9.8 77.1 all-gather.2

commit v5 on v4

--- a/solution.py
+++ b/solution.py
@@ -12,6 +12,7 @@
 HS = 128
 CORE, X, T, Y, Z = range(5)
 BF = jnp.bfloat16
+BUSY = 2 * 10**10
 F32 = jnp.float32
 PARAMS = pltpu.CompilerParams(vmem_limit_bytes=60 * 1024 * 1024)
 
@@ -28,98 +29,118 @@
     return jax.ShapeDtypeStruct(dims, dtype)
 
 
-def unit_kernel(at_ref, tok_ref, normed_ref, root_ref, mine_ref, given_ref, *, band):
-    tok = tok_ref[...].astype(F32)
-    root = jnp.sqrt(jnp.mean(tok * tok, -1, keepdims=True) + 1e-05)
-    normed_ref[...] = (tok / root).astype(BF)
-    root_ref[...] = root
+def unit_kernel(at_ref, tok_ref, other_ref, root_ref, mine_ref, given_ref, theirs_ref, both_ref, *, band):
     core = at_ref[CORE]
-    for i in range(mine_ref.shape[0] // band):
-        for ref, which in ((mine_ref, core), (given_ref, 1 - core)):
-            at = pl.multiple_of((2 * i + which) * band, band)
-            ref[i * band : (i + 1) * band, :] = normed_ref[:, pl.ds(at, band)].T
-
-
-def unit_rows(ids, tokens, band):
+    for n, ref in enumerate((tok_ref, other_ref)):
+        tok = ref[...].astype(F32)
+        root = jnp.sqrt(jnp.mean(tok * tok, -1, keepdims=True) + 1e-05)
+        outs = [(theirs_ref, core)]
+        if n == 0:
+            root_ref[...] = root
+            outs = [(mine_ref, core), (given_ref, 1 - core)]
+        for i in range(mine_ref.shape[1] // band):
+            for k, (out, which) in enumerate(outs):
+                at = pl.multiple_of((2 * i + which) * band, band)
+                unit = (ref[:, pl.ds(at, band)].astype(F32) / root).astype(BF)
+                out[:, i * band : (i + 1) * band] = unit
+                if k == 0:
+                    both_ref[n, i * band : (i + 1) * band, :] = unit.T
+
+
+def unit_rows(ids, tokens, others, band):
     rows, width = tokens.shape
     tile = 128
+    half = width // 2
+    row = pl.BlockSpec((tile, width), lambda i, at: (i, 0))
     return pl.pallas_call(
         functools.partial(unit_kernel, band=band),
         grid_spec=pltpu.PrefetchScalarGridSpec(
             num_scalar_prefetch=1,
             grid=(rows // tile,),
-            in_specs=[pl.BlockSpec((tile, width), lambda i, at: (i, 0))],
-            out_specs=(
-                pl.BlockSpec((tile, width), lambda i, at: (i, 0)),
-                pl.BlockSpec((tile, 1), lambda i, at: (i, 0)),
-                pl.BlockSpec((width // 2, tile), lambda i, at: (0, i)),
-                pl.BlockSpec((width // 2, tile), lambda i, at: (0, i)),
-            ),
+            in_specs=[row, row],
+            out_specs=(pl.BlockSpec((tile, 1), lambda i, at: (i, 0)),)
+            + (pl.BlockSpec((tile, half), lambda i, at: (i, 0)),) * 3
+            + (pl.BlockSpec((2, half, tile), lambda i, at: (0, 0, i)),),
         ),
+        out_shape=(shape(rows, 1, dtype=F32),)
+        + (shape(rows, half),) * 3
+        + (shape(2, half, rows),),
+        compiler_params=PARAMS,
+        cost_estimate=cost(BUSY, 1),
+    )(ids, tokens, others)
+
+
+def project_kernel(offsets, first, at_ref, mine_ref, theirs_ref, *refs):
+    keep_ref, give_ref, stack_ref, sems = refs[-4:]
+    n = len(offsets)
+    shards, sums = refs[:n], refs[n:-4]
+    copies = [pltpu.make_async_copy(w, stack_ref.at[i], sems.at[i]) for i, w in enumerate(shards)]
+    for copy in copies:
+        copy.start()
+    kinds, depth, cols = shards[0].shape
+    bands = [
+        pl.ds(pl.multiple_of(place_of(at_ref, *offset) * depth, depth), depth) for offset in offsets
+    ]
+    for i, (rows, out) in enumerate(((mine_ref, keep_ref), (theirs_ref, give_ref))):
+        for j in range(kinds):
+            span = slice(j * cols, (j + 1) * cols)
+            total = None if first else sums[i][:, span]
+            for band, shard in zip(bands, shards):
+                part = jnp.dot(rows[:, band], shard[j], preferred_element_type=F32)
+                total = part if total is None else total + part
+            out[:, span] = total.astype(out.dtype)
+    for copy in copies:
+        copy.wait()
+
+
+def place_of(at_ref, y, z):
+    return lax.rem(at_ref[Y] + y, 4) * 2 + lax.rem(at_ref[Z] + z, 2)
+
+
+def project(ids, mine, theirs, shards, offsets, sums=(), give=F32):
+    rows, _ = mine.shape
+    n = len(shards)
+    vmem = pl.BlockSpec(memory_space=pltpu.VMEM)
+    cols = 3 * shards[0].shape[-1]
+    return pl.pallas_call(
+        functools.partial(project_kernel, offsets, not sums),
+        in_specs=[pl.BlockSpec(memory_space=pltpu.SMEM)] + [vmem] * (2 + n + len(sums)),
+        out_specs=(vmem, vmem, pl.BlockSpec(memory_space=pl.ANY)),
         out_shape=(
-            shape(rows, width),
-            shape(rows, 1, dtype=F32),
-            shape(width // 2, rows),
-            shape(width // 2, rows),
+            shape(rows, cols, dtype=F32),
+            shape(rows, cols, dtype=give),
+            shape(n, *shards[0].shape),
         ),
-        compiler_params=PARAMS,
-        cost_estimate=cost(6 * rows * width, 6 * rows * width),
-    )(ids, tokens)
-
-
-def project_kernel(chunks, a_any, w_any, *refs):
-    heads_ref, a_ref, w_ref, acc_ref, a_sem, w_sem = refs[-6:]
-    bands, kinds, depth, cols = w_ref.shape
-    n = bands // chunks
-    copies = []
-    for c in range(chunks):
-        span = pl.ds(c * n * depth, n * depth)
-        some = pl.ds(c * n, n)
-        copies.append(
-            (
-                pltpu.make_async_copy(a_any.at[:, span], a_ref.at[:, span], a_sem.at[c]),
-                pltpu.make_async_copy(w_any.at[some], w_ref.at[some], w_sem.at[c]),
-            )
-        )
-        for copy in copies[-1]:
-            copy.start()
-    for c in range(chunks):
-        for copy in copies[c]:
-            copy.wait()
-        band = a_ref[:, c * n * depth : (c + 1) * n * depth]
-        for j in range(kinds):
-            w = w_ref[c * n : (c + 1) * n, j].reshape(n * depth, cols)
-            part = jnp.dot(band, w, preferred_element_type=F32)
-            span = slice(j * cols, (j + 1) * cols)
-            if c:
-                part += acc_ref[:, span]
-            if c < chunks - 1:
-                acc_ref[:, span] = part
-            else:
-                for h in range(heads_ref.shape[0]):
-                    heads_ref[h, :, j * HS : (j + 1) * HS] = part[:, h * HS : (h + 1) * HS].astype(BF)
-
-
-def project(normed, w, heads, after):
-    rows, depth = normed.shape
-    bands, kinds, _, cols = w.shape
-    chunks = 4
-    free = pl.BlockSpec(memory_space=pl.ANY)
-    return pl.pallas_call(
-        functools.partial(project_kernel, chunks),
-        in_specs=[free] * (2 + len(after)),
-        out_specs=pl.BlockSpec(memory_space=pltpu.VMEM),
-        out_shape=shape(heads, rows, kinds * cols // heads),
-        scratch_shapes=[
-            pltpu.VMEM(normed.shape, BF),
-            pltpu.VMEM(w.shape, BF),
-            pltpu.VMEM((rows, kinds * cols), F32),
-            pltpu.SemaphoreType.DMA((chunks,)),
-            pltpu.SemaphoreType.DMA((chunks,)),
-        ],
-        compiler_params=PARAMS,
-        cost_estimate=cost(1, 1),
-    )(normed, w, *after)
+        scratch_shapes=[pltpu.SemaphoreType.DMA((n,))],
+        compiler_params=PARAMS,
+        cost_estimate=cost(BUSY, 1),
+    )(ids, mine, theirs, *shards, *sums)
+
+
+def project_last_kernel(offset, at_ref, mine_ref, given_ref, keep_ref, came_ref, *refs):
+    shards, heads_ref = refs[:-1], refs[-1]
+    depth, cols = shards[0].shape[-2:]
+    band = pl.ds(pl.multiple_of(place_of(at_ref, *offset) * depth, depth), depth)
+    for j in range(3):
+        span = slice(j * cols, (j + 1) * cols)
+        total = keep_ref[:, span] + came_ref[:, span].astype(F32)
+        total += jnp.dot(mine_ref[:, band], shards[j][0], preferred_element_type=F32)
+        total += jnp.dot(given_ref[:, band], shards[3 + j][0], preferred_element_type=F32)
+        for h in range(heads_ref.shape[0]):
+            heads_ref[h, :, j * HS : (j + 1) * HS] = total[:, h * HS : (h + 1) * HS].astype(BF)
+
+
+def project_last(ids, mine, given, keep, came, pieces, offset, heads):
+    rows, cols = keep.shape
+    vmem = pl.BlockSpec(memory_space=pltpu.VMEM)
+    return pl.pallas_call(
+        functools.partial(project_last_kernel, offset),
+        in_specs=[pl.BlockSpec(memory_space=pltpu.SMEM)] + [vmem] * (4 + len(pieces)),
+        out_specs=vmem,
+        out_shape=shape(heads, rows, cols // heads),
+        compiler_params=PARAMS,
+        cost_estimate=cost(1, 1),
+    )(ids, mine, given, keep, came, *pieces)
 
 
 def attention_kernel(q_rows, qkv_ref, dout_ref, *refs):
@@ -185,18 +206,30 @@
     return sum(ref[at + i : at + i + 1, :].astype(F32) for i in range(3))
 
 
-def norm_kernel(width, halves, spots, at_ref, g_ref, p_ref, w_any, *refs):
+def norm_kernel(width, halves, spots, places, n_in, at_ref, g_ref, p_ref, *refs):
+    shards = refs[:n_in]
     n_out = max(spot[0] for spot in spots) + 1
     outs, stat_ref = refs[-4 - n_out : -4], refs[-4]
     w_ref, flat_ref, sems = refs[-3:]
-    n, bands, kinds, depth, cols = w_ref.shape
-    quarters = w_any.shape[0] // (2 * bands)
-    copies = []
+    _, kinds, depth, cols = w_ref.shape
+    band = depth // 2
+    quarters = len(places) // 2
+
+    def copy(step, core, j, source):
+        to = lax.rem(at_ref[CORE] + core, 2)
+        at = pl.ds(pl.multiple_of(to * band, band), band)
+        return pltpu.make_async_copy(source, w_ref.at[step, j, at], sems.at[step, core, j])
+
     for step, (by, half) in enumerate(halves):
-        at = (lax.rem(at_ref[T] + by, quarters) * 2 + half) * bands
-        copy = pltpu.make_async_copy(w_any.at[pl.ds(at, bands)], w_ref.at[step], sems.at[step])
-        copy.start()
-        copies.append(copy)
+        y_off = lax.rem(at_ref[T] + (by + quarters) - at_ref[Y], quarters)
+        where = y_off * 2 + lax.rem(at_ref[Z] + half, 2)
+        for place, cores in enumerate(places):
+
+            @pl.when(where == place)
+            def _(step=step, cores=cores):
+                for core, pieces in enumerate(cores):
+                    for j, (which, at) in enumerate(pieces):
+                        copy(step, core, j, shards[which].at[*at]).start()
 
     heads, _, _ = g_ref.shape
     for h in range(heads):
@@ -216,39 +249,38 @@
             write_stat(ref, ref.shape[0] - 16, stat)
 
     for step, (which, at) in enumerate(spots):
-        copies[step].wait()
+        for core in range(2):
+            for j in range(kinds):
+                copy(step, core, j, shards[0].at[0]).wait()
         total = sum(
-            dot(
-                w_ref[step, :, j].reshape(bands * depth, cols),
-                flat_ref[j * cols : (j + 1) * cols, :],
-                1,
-                0,
-            )
+            dot(w_ref[step, j], flat_ref[j * cols : (j + 1) * cols, :], 1, 0)
             for j in range(kinds)
         )
-        outs[which][at : at + bands * depth, :] = total.astype(BF)
-
-
-def norm_halves(ids, grads, proj, w, halves, spots, sizes, width, after=()):
+        outs[which][at : at + depth, :] = total.astype(BF)
+
+
+def norm_halves(ids, grads, proj, shards, places, halves, spots, sizes, width, after=()):
     heads, rows, _ = grads.shape
-    bands, kinds, depth, cols = w.shape
+    kinds = 3
+    band, cols = shards[0].shape[-2:]
     n = len(spots)
     sizes = (*sizes, 1)
     vmem = pl.BlockSpec(memory_space=pltpu.VMEM)
     free = pl.BlockSpec(memory_space=pl.ANY)
     return pl.pallas_call(
-        functools.partial(norm_kernel, width, halves, spots),
-        in_specs=[pl.BlockSpec(memory_space=pltpu.SMEM), vmem, vmem, free] + [free] * len(after),
+        functools.partial(norm_kernel, width, halves, spots, places, len(shards)),
+        in_specs=[pl.BlockSpec(memory_space=pltpu.SMEM), vmem, vmem]
+        + [free] * (len(shards) + len(after)),
         out_specs=(vmem,) * len(sizes),
         out_shape=tuple(shape(s, rows) for s in sizes[:-1]) + (shape(1, rows, dtype=F32),),
         scratch_shapes=[
-            pltpu.VMEM((n, bands // 8, kinds, depth, cols), BF),
+            pltpu.VMEM((n, kinds, 2 * band, cols), BF),
             pltpu.VMEM((kinds * cols, rows), BF),
-            pltpu.SemaphoreType.DMA((n,)),
+            pltpu.SemaphoreType.DMA((n, 2, kinds)),
         ],
         compiler_params=PARAMS,
         cost_estimate=cost(1, 1),
-    )(ids, grads, proj, w, *after)
+    )(ids, grads, proj, *shards, *after)
 
 
 def add_kernel(up_part, up_in, stat_in, down_part, down_in, stat_ref, *refs):
@@ -314,23 +346,21 @@
     )(ids, *parts, tokens, root, stat)
 
 
-def outer_kernel(tile, at_ref, *refs):
-    blocks, (mine_ref, other_ref, out_ref, a_ref, g_ref, sems) = refs[:-6], refs[-6:]
+def outer_kernel(tile, blocks_any, mine_ref, other_ref, out_ref, a_ref, g_ref, sems):
     n, rows, _ = mine_ref.shape
     depth = a_ref.shape[0]
     copies = []
     for step in range(depth // tile):
         span = pl.ds(step * tile, tile)
         some = []
-        for i, block in enumerate(blocks):
+        for i in range(2 * n):
             to = a_ref.at[span, pl.ds(i * rows, rows)]
-            some.append(pltpu.make_async_copy(block.at[span], to, sems.at[step, i]))
+            some.append(pltpu.make_async_copy(blocks_any.at[i, span], to, sems.at[step, i]))
             some[-1].start()
         copies.append(some)
-    for i, by in enumerate((0, n - 1, 1, 2)):
-        at = lax.rem(at_ref[X] + by, n)
-        g_ref[i * rows : (i + 1) * rows, :] = mine_ref[at]
-        g_ref[(n + i) * rows : (n + i + 1) * rows, :] = other_ref[at]
+    for i in range(n):
+        g_ref[2 * i * rows : (2 * i + 1) * rows, :] = mine_ref[i]
+        g_ref[(2 * i + 1) * rows : (2 * i + 2) * rows, :] = other_ref[i]
     for step, some in enumerate(copies):
         for copy in some:
             copy.wait()
@@ -340,26 +370,24 @@
         ).astype(BF)
 
 
-def outer(ids, blocks, mine, other):
-    depth, rows = blocks[0].shape
+def outer(blocks, mine, other):
+    n, depth, rows = blocks.shape
     cols = mine.shape[2]
     tile = 512
     vmem = pl.BlockSpec(memory_space=pltpu.VMEM)
     return pl.pallas_call(
         functools.partial(outer_kernel, tile),
-        in_specs=[pl.BlockSpec(memory_space=pltpu.SMEM)]
-        + [pl.BlockSpec(memory_space=pl.ANY)] * len(blocks)
-        + [vmem, vmem],
+        in_specs=[pl.BlockSpec(memory_space=pl.ANY), vmem, vmem],
         out_specs=vmem,
         out_shape=shape(depth, cols),
         scratch_shapes=[
-            pltpu.VMEM((depth, len(blocks) * rows), BF),
-            pltpu.VMEM((len(blocks) * rows, cols), BF),
-            pltpu.SemaphoreType.DMA((depth // tile, len(blocks))),
+            pltpu.VMEM((depth, n * rows), BF),
+            pltpu.VMEM((n * rows, cols), BF),
+            pltpu.SemaphoreType.DMA((depth // tile, n)),
         ],
         compiler_params=PARAMS,
         cost_estimate=cost(1, 1),
-    )(ids, *blocks, mine, other)
+    )(blocks, mine, other)
 
 
 def split_kernel(at_ref, part_ref, *refs):
@@ -431,6 +459,34 @@
     )(last)
 
 
+def gate(arrays, after=(), pieces=()):
+    n, m = len(arrays), len(arrays) + len(after)
+    free = pl.BlockSpec(memory_space=pl.ANY)
+
+    def kernel(*refs):
+        outs, sems = refs[m + n : -1], refs[-1]
+        copies = [
+            pltpu.make_async_copy(refs[which].at[pl.ds(at, 1)], out, sems.at[i])
+            for i, ((which, at), out) in enumerate(zip(pieces, outs))
+        ]
+        for copy in copies:
+            copy.start()
+        for copy in copies:
+            copy.wait()
+
+    return pl.pallas_call(
+        kernel,
+        in_specs=[free] * m,
+        out_specs=(free,) * (n + len(pieces)),
+        out_shape=tuple(shape(*a.shape) for a in arrays)
+        + tuple(shape(1, *arrays[which].shape[1:]) for which, _ in pieces),
+        scratch_shapes=[pltpu.SemaphoreType.DMA((max(len(pieces), 1),))],
+        input_output_aliases={i: i for i in range(n)},
+        compiler_params=PARAMS,
+        cost_estimate=cost(1, 1),
+    )(*arrays, *after)
+
+
 def shift(x, axis, by):
     n = lax.axis_size(axis)
     return lax.ppermute(x, axis, [(i, (i + by) % n) for i in range(n)])
@@ -445,28 +501,48 @@
     tokens = tokens.reshape(rows, width)
     half = width // lax.axis_size("zh") // 2
 
-    w = lax.all_gather(weights.transpose(1, 0, 2)[None], ("y", "zl", "core"), axis=0, tiled=True)
-
-    normed, root, mine, given = unit_rows(ids, tokens, w_rows)
-    theirs = shift(given, "core", 1)
-    left_m, right_m = shift(mine, "x", 1), shift(mine, "x", -1)
-    left_t, right_t = shift(theirs, "x", 1), shift(theirs, "x", -1)
-    far_m, far_t = shift(left_m, "x", 1), shift(right_t, "x", -1)
-    blocks = (mine, left_m, right_m, far_m, theirs, left_t, right_t, far_t)
+    swap = lambda a: shift(a, "core", 1)
+    own = weights.transpose(1, 0, 2)
+    left, right, other = shift(own, "y", 1), shift(own, "y", -1), shift(own, "zl", 1)
+    root, mine, given, theirs, pair = unit_rows(ids, tokens, swap(tokens), w_rows)
+    left, right, other = gate((left, right, other), (pair,))
+
+    blocks = lax.all_gather(pair, "x", axis=0, tiled=True)
 
     dout = cotangent.reshape(rows, heads, HS).transpose(1, 0, 2)
     dout = lax.all_to_all(dout, "x", 0, 0, tiled=True).reshape(n_x * rows, HS)
-
-    proj = project(normed, w, heads, (*blocks, dout))
+    near = ((0, 0), (3, 0), (1, 0), (0, 1))
+    *sums, stack_0 = project(ids, mine, theirs, (own, left, right, other), near)
+    far, other_left, other_right, *pieces = gate(
+        (shift(left, "y", 1), shift(left, "zl", 1), shift(other, "y", -1)),
+        (dout, *sums),
+        ((0, 0), (1, 1), (2, 2)),
+    )
+    then = ((2, 0), (3, 1), (1, 1))
+    keep, give, stack_1 = project(
+        ids, mine, theirs, (far, other_left, other_right), then, sums, BF
+    )
+    *pieces, give = gate(
+        (shift(pieces[0], "zl", 1), shift(pieces[1], "y", 1), shift(pieces[2], "y", -1), give)
+    )
+    pieces = (*pieces, *(swap(p) for p in pieces))
+    proj = project_last(ids, mine, given, keep, swap(give), pieces, (2, 1), heads)
+
+    shards = (*pieces, stack_0, swap(stack_0), stack_1, swap(stack_1))
+    places = {(2, 1): [[(3 * core + j, (0,)) for j in range(3)] for core in range(2)]}
+    for first, keys in ((6, near), (8, then)):
+        for i, key in enumerate(keys):
+            places[key] = [[(first + core, (i, j)) for j in range(3)] for core in range(2)]
+    places = [places[(by, z)] for by in range(n_y) for z in range(2)]
     qkv = lax.all_to_all(proj, "x", 0, 0, tiled=True).reshape(n_x * rows, 3 * HS)
     att, head_grads = attention(qkv, dout)
 
     head_grads = head_grads.reshape(n_x, rows, 3 * HS)
     grads = lax.all_to_all(head_grads, "x", 0, 0, tiled=True)
-    part = outer(ids, blocks, head_grads, shift(head_grads, "core", 1))
+    part = outer(blocks, head_grads, swap(head_grads))
 
     up, down, stat = norm_halves(
-        ids, grads, proj, w,
+        ids, grads, proj, shards, places,
         ((2, 0), (1, 1), (2, 1), (3, 0)),
         ((0, 0), (0, half), (1, 0), (1, half)),
         (2 * half + 16, 2 * half),
@@ -474,7 +550,7 @@
     )
     up, down = shift(up, "zh", 1), shift(down, "zh", -1)
     up_part, down_part, own0, own1, _ = norm_halves(
-        ids, grads, proj, w,
+        ids, grads, proj, shards, places,
         ((1, 0), (3, 1), (0, 0), (0, 1)),
         ((0, 0), (1, 0), (2, 0), (3, 0)),
         (half,) * 4,

time: 225 us -> 240 us (1.067)
  blocking collectives: 59.2 us -> 17.1 us
  Pallas kernels: 58.5 us -> 94.1 us
  waiting for transfers between devices: 48.9 us -> 60 us
  starting transfers between devices: 34.1 us -> 41.9 us
  local copies, waits for them, and re-layouts: 7.19 us -> 10.1 us
    all_to_all x1 -> x0, blocking collectives: 42.2 us -> none  [per_device(): dout = lax.all_to_all(dout, 'x', 0, 0, tiled=True).reshape(n_x * rows, HS)]
    pallas_call x3 -> x8, Pallas kernels: 22.1 us -> 56.8 us  [the longest x3 25 us: gate(): pl.pallas_call(kernel, in_specs=[free] * m, out_specs=(free,) * (n + len(...]
    ppermute x13 -> x22, waiting for transfers between devices: 45.3 us -> 56 us  [shift(): return lax.ppermute(x, axis, [(i, (i + by) % n) for i in range(n)])]
    all_to_all x0 -> x1, starting transfers between devices: none -> 4.29 us  [per_device(): dout = lax.all_to_all(dout, 'x', 0, 0, tiled=True).reshape(n_x * rows, HS)]
    unnamed x28 -> x42, local copies, waits for them, and re-layouts: 5.44 us -> 8.68 us
    ppermute x13 -> x22, starting transfers between devices: 22.2 us -> 23.2 us  [shift(): return lax.ppermute(x, axis, [(i, (i + by) % n) for i in range(n)])]
  transfers between devices with their start and end apart: 17 -> 27, of which waited for: 8 -> 17; matrix products, arithmetic and copies ran while one was open for 1% -> 1% of each run, Pallas kernels for 17% -> 35%
where the time goes in v5:
time: 240 us; the launch traced here: 238 us
  Pallas kernels  94.1 us (39%)
  waiting for transfers between devices  60 us (25%)
  starting transfers between devices  41.9 us (17%)
  blocking collectives  17.1 us (7%)
  between operations  14.3 us (6%)
  local copies, waits for them, and re-layouts  10.1 us (4%)
    ppermute x22, waiting for transfers between devices, shift(): return lax.ppermute(x, axis, [(i, (i + by) % n) for i in range(n)])  56 us
    pallas_call x3, Pallas kernels, gate(): pl.pallas_call(kernel, in_specs=[free] * m, out_specs=(free,) * (n + len(...  25 us
    ppermute x22, starting transfers between devices, shift(): return lax.ppermute(x, axis, [(i, (i + by) % n) for i in range(n)])  23.2 us
    all_to_all x1, blocking collectives, per_device(): lax.all_to_all(proj, 'x', 0, 0, tiled=True).reshape(n_x * rows, 3 * HS)  17.1 us
    pallas_call x2, Pallas kernels, norm_halves(): pl.pallas_call(functools.partial(norm_kernel, width, halves, spots, place...  15.2 us
    pallas_call x2, Pallas kernels, project(): pl.pallas_call(functools.partial(project_kernel, offsets, not sums), in_s...  12.5 us
    pallas_call x1, Pallas kernels, outer(): pl.pallas_call(functools.partial(outer_kernel, tile), in_specs=[pl.BlockS...  9.33 us
    unnamed x42, local copies, waits for them, and re-layouts  8.68 us
  transfers between devices with their start and end apart: 27, of which 17 were waited for; matrix products, arithmetic and copies ran while one was open for 1% of the time, Pallas kernels for 35%

profile of v5, /device:TPU:8, one launch (start us, length us, event | category | flops | bytes accessed | tf_op | source)
XLA Modules:
  0.0 237.5 jit_solution(4912343660940705891)
XLA Ops:
  7.3 0.6 stack.23.at_ref
  7.9 3.7 %collective-permute-done.other_ref = bf16[256,4096]{1,0:T(8,128)(2,1)S(1)} collective-permute-done((bf16[256,4096]{1,0:T(8,128)(2,1)}, bf16[256,4096]{1,0:T(8,128)(2,1)S(1)}, u32[]{:S(2)}, u32[]{:S(2)}) %collective-permute-start) | collective-permute-done | bytes 2097184 | tf_op jit(solution)/shard_map/ppermute | solution.py:492
  11.7 1.3 copy-done.19
  13.0 5.4 %shard_map.58 = (f32[256,1]{1,0:T(8,128)}, bf16[256,2048]{1,0:T(8,128)(2,1)}, bf16[256,2048]{1,0:T(8,128)(2,1)}, bf16[256,2048]{1,0:T(8,128)(2,1)}, bf16[2,2048,256]{2,1,0:T(8,128)(2,1)}) custom-call(s32[5]{0:T(128)} %stack.23.at_ref, bf16[256,4096]{1,0:T(8,128)(2,1)} %bitcast.27, bf16[256,4096]{1,0:T(8,128)(2,1)} %copy-done.19), custom_call_target="tpu_custom_call" | custom-call | flops 20000000000 | bytes 1 | tf_op jit(solution)/shard_map/pallas_call | solution.py:55
  18.5 1.7 collective-permute-start.1
  20.1 0.7 collective-permute-start.2
  20.8 1.7 collective-permute-start.3
  22.6 0.7 copy.19
  23.3 4.3 %all-to-all-start = ((bf16[4,256,128]{2,1,0:T(8,128)(2,1)}), bf16[4,256,128]{2,1,0:T(8,128)(2,1)S(1)}, u32[]{:S(2)}, u32[]{:S(2)}) async-start(bf16[4,256,128]{2,1,0:T(8,128)(2,1)} %bitcast.18), calls=%async_computation | async-start | bytes 524288 | tf_op jit(solution)/shard_map/all_to_all | solution.py:513
  27.6 11.2 %collective-permute-done.1.refs_0_ = bf16[3,256,512]{2,1,0:T(8,128)(2,1)S(1)} collective-permute-done((bf16[3,256,512]{2,1,0:T(8,128)(2,1)}, bf16[3,256,512]{2,1,0:T(8,128)(2,1)S(1)}, u32[]{:S(2)}, u32[]{:S(2)}) %collective-permute-start.1) | collective-permute-done | bytes 786464 | tf_op jit(solution)/shard_map/ppermute | solution.py:492
  38.8 0.8 collective-permute-done.2.refs_1_
  39.6 0.7 collective-permute-done.3.refs_2_
  40.5 0.9 copy-done.13
  41.4 1.6 collective-permute-start.4
  43.1 1.7 collective-permute-start.5
  44.7 0.7 collective-permute-start.6
  45.5 6.4 %shard_map.60 = (f32[256,1536]{1,0:T(8,128)}, f32[256,1536]{1,0:T(8,128)}, bf16[4,3,256,512]{3,2,1,0:T(8,128)(2,1)}) custom-call(s32[5]{0:T(128)} %stack.23.at_ref, bf16[256,2048]{1,0:T(8,128)(2,1)} %get-tuple-element.43.mine_ref, bf16[256,2048]{1,0:T(8,128)(2,1)} %get-tuple-element.45.theirs_ref, bf16[3,256,512]{2,1,0:T(8,128)(2,1)} %bitcast.6.refs_0_, ...), custom_call_target="tpu_custom_call" | custom-call | flops 20000000000 | bytes 1 | tf_op jit(solution)/shard_map/pallas_call | solution.py:105
  52.0 9.3 %collective-permute-done.4.refs_0_ = bf16[3,256,512]{2,1,0:T(8,128)(2,1)} collective-permute-done((bf16[3,256,512]{2,1,0:T(8,128)(2,1)}, bf16[3,256,512]{2,1,0:T(8,128)(2,1)}, u32[]{:S(2)}, u32[]{:S(2)}) %collective-permute-start.4) | collective-permute-done | bytes 786464 | tf_op jit(solution)/shard_map/ppermute | solution.py:492
  61.3 0.5 collective-permute-done.5.refs_1_
  61.8 1.1 collective-permute-done.6.refs_2_
  62.9 24.9 %shard_map.61 = (bf16[3,256,512]{2,1,0:T(8,128)(2,1)}, bf16[3,256,512]{2,1,0:T(8,128)(2,1)}, bf16[3,256,512]{2,1,0:T(8,128)(2,1)}, bf16[1,256,512]{2,1,0:T(8,128...) custom-call(bf16[3,256,512]{2,1,0:T(8,128)(2,1)} %collective-permute, ...), custom_call_target="tpu_custom_call", output_to_operand_aliasing={{0}: (0, {}), {1}: (1, {}), {2}: (2, {})} | custom-call | flops 1 | bytes 1 | tf_op jit(solution)/shard_map/pallas_call | solution.py:477
  87.9 1.7 collective-permute-start.7
  89.6 1.7 collective-permute-start.8
  91.3 0.3 collective-permute-start.9
  91.6 6.1 %shard_map.62 = (f32[256,1536]{1,0:T(8,128)}, bf16[256,1536]{1,0:T(8,128)(2,1)}, bf16[3,3,256,512]{3,2,1,0:T(8,128)(2,1)}) custom-call(s32[5]{0:T(128)} %stack.23.at_ref, bf16[256,2048]{1,0:T(8,128)(2,1)} %get-tuple-element.43.mine_ref, bf16[256,2048]{1,0:T(8,128)(2,1)} %get-tuple-element.45.theirs_ref, bf16[3,256,512]{2,1,0:T(8,128)(2,1)} %get-tuple-element.51.refs_0_, ...), custom_call_target="tpu_custom_call" | custom-call | flops 20000000000 | bytes 1 | tf_op jit(solution)/shard_map/pallas_call | solution.py:105
  98.0 0.4 copy-done.2
  98.8 0.5 collective-permute-start.11
  99.3 0.3 collective-permute-start.12
  99.8 1.8 collective-permute-done.11.refs_3_
  101.8 0.2 collective-permute-done.12.refs_4_
  102.0 0.4 collective-permute-done.13.refs_5_
  102.4 0.3 copy-done.7
  102.8 0.4 copy-done.8
  103.1 4.2 %shard_map.64.p_ref = bf16[4,256,384]{2,1,0:T(8,128)(2,1)} custom-call(s32[5]{0:T(128)} %stack.23.at_ref, bf16[256,2048]{1,0:T(8,128)(2,1)} %get-tuple-element.43.mine_ref, bf16[256,2048]{1,0:T(8,128)(2,1)} %get-tuple-element.44.given_ref, f32[256,1536]{1,0:T(8,128)} %get-tuple-element.54.keep_ref, bf16[256,1536]{1,0:T(8,128)(2,1)} %collective-permute-done.10.came_ref, ...), custom_call_target="tpu_custom_call" | custom-call | flops 1 | bytes 1 | tf_op jit(solution)/shard_map/pallas_call | solution.py:136
  107.3 17.1 %all_to_all.29 = bf16[4,256,384]{2,1,0:T(8,128)(2,1)} all-to-all(bf16[4,256,384]{2,1,0:T(8,128)(2,1)} %shard_map.64.p_ref), channel_id=1, replica_groups=mesh['y'=4,'zl'=2,'core'=2,'x'=4,'zh'=4] {'x'}, dimensions={0} | all-to-all | bytes 1572864 | tf_op jit(solution)/shard_map/all_to_all | solution.py:537
  124.5 8.6 %shard_map.65 = (bf16[1024,128]{1,0:T(8,128)(2,1)}, bf16[1024,384]{1,0:T(8,128)(2,1)}) custom-call(bf16[1024,384]{1,0:T(8,128)(2,1)} %bitcast.23, bf16[1024,128]{1,0:T(8,128)(2,1)} %bitcast.25), custom_call_target="tpu_custom_call" | custom-call | flops 1 | bytes 1 | tf_op jit(solution)/shard_map/pallas_call | solution.py:184
  133.1 4.2 %all-to-all-start.3 = ((bf16[4,256,384]{2,1,0:T(8,128)(2,1)}), bf16[4,256,384]{2,1,0:T(8,128)(2,1)}, u32[]{:S(2)}, u32[]{:S(2)}) async-start(bf16[4,256,384]{2,1,0:T(8,128)(2,1)} %bitcast.21), calls=%async_computation.3 | async-start | bytes 1572864 | tf_op jit(solution)/shard_map/all_to_all | solution.py:541
  137.3 9.3 %shard_map.66 = bf16[2048,384]{1,0:T(8,128)(2,1)} custom-call(bf16[8,2048,256]{2,1,0:T(8,128)(2,1)} %all-gather.2.cloned.1.call-done.blocks_any, bf16[4,256,384]{2,1,0:T(8,128)(2,1)} %bitcast.22, bf16[4,256,384]{2,1,0:T(8,128)(2,1)} %collective-permute-done.14.other_ref), custom_call_target="tpu_custom_call" | custom-call | flops 1 | bytes 1 | tf_op jit(solution)/shard_map/pallas_call | solution.py:378
  146.7 3.9 %all-to-all-done.3.g_ref = bf16[4,256,384]{2,1,0:T(8,128)(2,1)} async-done(((bf16[4,256,384]{2,1,0:T(8,128)(2,1)}), bf16[4,256,384]{2,1,0:T(8,128)(2,1)}, u32[]{:S(2)}, u32[]{:S(2)}) %all-to-all-start.3) | async-done | bytes 786464 | tf_op jit(solution)/shard_map/all_to_all | solution.py:541
  150.6 6.6 %all-to-all-start.2 = ((bf16[4,512,384]{2,1,0:T(8,128)(2,1)}), bf16[4,512,384]{2,1,0:T(8,128)(2,1)}, u32[]{:S(2)}, u32[]{:S(2)}) async-start(bf16[4,512,384]{2,1,0:T(8,128)(2,1)} %bitcast.19), calls=%async_computation.2 | async-start | bytes 3145728 | tf_op jit(solution)/shard_map/all_to_all | solution.py:560
  157.2 1.6 copy-done
  158.8 7.6 %shard_map.67 = (bf16[1040,256]{1,0:T(8,128)(2,1)}, bf16[1024,256]{1,0:T(8,128)(2,1)}, f32[1,256]{1,0:T(1,128)}) custom-call(s32[5]{0:T(128)} %stack.23.at_ref, bf16[4,256,384]{2,1,0:T(8,128)(2,1)} %all-to-all-done.3.g_ref, bf16[4,256,384]{2,1,0:T(8,128)(2,1)} %shard_map.64.p_ref, bf16[1,256,512]{2,1,0:T(8,128)(2,1)} %get-tuple-element.60.refs_0_, ...), custom_call_target="tpu_custom_call" | custom-call | flops 1 | bytes 1 | tf_op jit(solution)/shard_map/pallas_call | solution.py:270
  166.5 2.2 collective-permute-start.18
  168.7 2.6 %collective-permute-start.19 = (bf16[1024,256]{1,0:T(8,128)(2,1)}, bf16[1024,256]{1,0:T(8,128)(2,1)S(1)}, u32[]{:S(2)}, u32[]{:S(2)}) collective-permute-start(bf16[1024,256]{1,0:T(8,128)(2,1)} %get-tuple-element.74), channel_id=1, source_target_pairs={{0,3},{1,0},{2,1},{3,2},{4,7},{5,4},{6,5},{7,6},{8,11},{9,8},{10,9... | collective-permute-start | bytes 1572872 | tf_op jit(solution)/shard_map/ppermute | solution.py:492
  171.3 7.5 %shard_map.68 = (bf16[512,256]{1,0:T(8,128)(2,1)}, bf16[512,256]{1,0:T(8,128)(2,1)}, bf16[512,256]{1,0:T(8,128)(2,1)}, bf16[512,256]{1,0:T(8,128)(2,1)}, f32[1,256]{1,0:T(1,128)}) custom-call(s32[5]{0:T(128)} %stack.23.at_ref, bf16[4,256,384]{2,1,0:T(8,128)(2,1)} %all-to-all-done.3.g_ref, bf16[4,256,384]{2,1,0:T(8,128)(2,1)} %shard_map.64.p_ref, ...), custom_call_target="tpu_custom_call" | custom-call | flops 1 | bytes 1 | tf_op jit(solution)/shard_map/pallas_call | solution.py:270
  178.9 2.3 shard_map.69
  181.2 1.0 collective-permute-start.17
  182.2 13.3 %collective-permute-done.19.down_in.down0 = bf16[1024,256]{1,0:T(8,128)(2,1)S(1)} collective-permute-done((bf16[1024,256]{1,0:T(8,128)(2,1)}, bf16[1024,256]{1,0:T(8,128)(2,1)S(1)}, u32[]{:S(2)}, u32[]{:S(2)}) %collective-permute-start.19) | collective-permute-done | bytes 524320 | tf_op jit(solution)/shard_map/ppermute | solution.py:492
  195.5 0.4 collective-permute-done.18.up_in.stat_in.up1
  195.9 0.4 copy-done.10
  196.3 0.4 copy-done.1
  196.7 2.2 shard_map.70
  198.9 0.3 collective-permute-done.17.came_ref
  199.2 0.7 copy-done.18
  199.9 2.3 shard_map.71
  202.2 3.5 %all-to-all-start.4 = ((bf16[4,256,512]{2,1,0:T(8,128)(2,1)}), bf16[4,256,512]{2,1,0:T(8,128)(2,1)S(1)}, u32[]{:S(2)}, u32[]{:S(2)}) async-start(bf16[4,256,512]{2,1,0:T(8,128)(2,1)} %shard_map.71), calls=%async_computation.4 | async-start | bytes 2097152 | tf_op jit(solution)/shard_map/all_to_all | solution.py:566
  205.7 2.6 %collective-permute-start.20 = (bf16[528,256]{1,0:T(8,128)(2,1)S(1)}, bf16[528,256]{1,0:T(8,128)(2,1)S(1)}, u32[]{:S(2)}, u32[]{:S(2)}) collective-permute-start(bf16[528,256]{1,0:T(8,128)(2,1)S(1)} %copy-done.14), channel_id=1, source_target_pairs={{0,1},{1,2},{2,3},{3,0},{4,5},{5,6},{6,7},{7,4},{8,9},{9,10},{10,1... | collective-permute-start | bytes 811016 | tf_op jit(solution)/shard_map/ppermute | solution.py:492
  208.3 1.6 collective-permute-start.21
  209.9 9.9 %collective-permute-done.20.up0 = bf16[528,256]{1,0:T(8,128)(2,1)S(1)} collective-permute-done((bf16[528,256]{1,0:T(8,128)(2,1)S(1)}, bf16[528,256]{1,0:T(8,128)(2,1)S(1)}, u32[]{:S(2)}, u32[]{:S(2)}) %collective-permute-start.20) | collective-permute-done | bytes 270368 | tf_op jit(solution)/shard_map/ppermute | solution.py:492
  219.9 2.1 collective-permute-done.21.down1
  221.9 0.7 copy-done.16
  222.6 3.5 %shard_map.73 = bf16[256,1024]{1,0:T(8,128)(2,1)} custom-call(s32[5]{0:T(128)} %stack.23.at_ref, bf16[512,256]{1,0:T(8,128)(2,1)} %get-tuple-element.67.refs_0_.own0, bf16[512,256]{1,0:T(8,128)(2,1)} %get-tuple-element.77.own1, bf16[528,256]{1,0:T(8,128)(2,1)} %copy-done.15, bf16[1040,256]{1,0:T(8,128)(2,1)} %copy-done.1, bf16[1024,256]{1,0:T(8,128)(2,1)} %copy-done.10, ...), custom_call_target="tpu_custom_call" | custom-call | flops 1 | bytes 1 | tf_op jit(solution)/shard_map/pallas_call | solution.py:333
  226.1 1.0 copy-done.5
  227.1 3.5 %shard_map.72 = (f32[3,256,512]{2,1,0:T(8,128)}, bf16[256,512]{1,0:T(8,128)(2,1)}) custom-call(bf16[4,256,512]{2,1,0:T(8,128)(2,1)} %copy-done.5), custom_call_target="tpu_custom_call" | custom-call | flops 1 | bytes 1 | tf_op jit(solution)/shard_map/pallas_call | solution.py:448
  (53 shorter events, 1.5 us)
Async XLA Ops:
  7.2 130.1 %all-gather.2.cloned.1.call-start = ((), (), s32[]{:S(2)}) async-start(), calls=%async_computation.5 | async-start | bytes 10485760 | tf_op jit(solution)/shard_map/all_gather | solution.py:510
  7.2 4.5 %collective-permute-start = (bf16[256,4096]{1,0:T(8,128)(2,1)}, bf16[256,4096]{1,0:T(8,128)(2,1)S(1)}, u32[]{:S(2)}, u32[]{:S(2)}) collective-permute-start(bf16[256,4096]{1,0:T(8,128)(2,1)} %bitcast.26), channel_id=1, source_target_pairs={{0,16},{16,0},{1,17},{17,1},{2,18},{18,2},{3,19},{19,3},{4,20},{20... | collective-permute-start | bytes 6291464 | tf_op jit(solution)/shard_map/ppermute | solution.py:492
  11.7 1.3 copy-start.19
  18.4 4.1 %copy-start.17 = (bf16[1,256,512]{2,1,0:T(8,128)(2,1)S(1)}, bf16[1,256,512]{2,1,0:T(8,128)(2,1)}, u32[]{:S(2)}) copy-start(bf16[1,256,512]{2,1,0:T(8,128)(2,1)} %param.5) | copy-start | bytes 786436
  18.5 20.3 %collective-permute-start.1 = (bf16[3,256,512]{2,1,0:T(8,128)(2,1)}, bf16[3,256,512]{2,1,0:T(8,128)(2,1)S(1)}, u32[]{:S(2)}, u32[]{:S(2)}) collective-permute-start(bf16[3,256,512]{2,1,0:T(8,128)(2,1)} %bitcast.6.refs_0_), channel_id=1, source_target_pairs={{0,64},{64,128},{128,192},{192,0},{1,65},{65,129},{129,193},{193,1... | collective-permute-start | bytes 2359304 | tf_op jit(solution)/shard_map/ppermute | solution.py:492
  20.1 19.5 %collective-permute-start.2 = (bf16[3,256,512]{2,1,0:T(8,128)(2,1)}, bf16[3,256,512]{2,1,0:T(8,128)(2,1)S(1)}, u32[]{:S(2)}, u32[]{:S(2)}) collective-permute-start(bf16[3,256,512]{2,1,0:T(8,128)(2,1)} %bitcast.6.refs_0_), channel_id=1, source_target_pairs={{0,192},{64,0},{128,64},{192,128},{1,193},{65,1},{129,65},{193,129... | collective-permute-start | bytes 2359304 | tf_op jit(solution)/shard_map/ppermute | solution.py:492
  20.8 19.5 %collective-permute-start.3 = (bf16[3,256,512]{2,1,0:T(8,128)(2,1)}, bf16[3,256,512]{2,1,0:T(8,128)(2,1)S(1)}, u32[]{:S(2)}, u32[]{:S(2)}) collective-permute-start(bf16[3,256,512]{2,1,0:T(8,128)(2,1)} %bitcast.6.refs_0_), channel_id=1, source_target_pairs={{0,32},{32,0},{1,33},{33,1},{2,34},{34,2},{3,35},{35,3},{4,36},{36... | collective-permute-start | bytes 2359304 | tf_op jit(solution)/shard_map/ppermute | solution.py:492
  23.3 28.7 %all-to-all-start = ((bf16[4,256,128]{2,1,0:T(8,128)(2,1)}), bf16[4,256,128]{2,1,0:T(8,128)(2,1)S(1)}, u32[]{:S(2)}, u32[]{:S(2)}) async-start(bf16[4,256,128]{2,1,0:T(8,128)(2,1)} %bitcast.18), calls=%async_computation | async-start | bytes 524288 | tf_op jit(solution)/shard_map/all_to_all | solution.py:513
  38.8 1.6 copy-start.11
  39.6 0.9 copy-start.12
  40.5 0.9 copy-start.13
  41.4 19.9 %collective-permute-start.4 = (bf16[3,256,512]{2,1,0:T(8,128)(2,1)}, bf16[3,256,512]{2,1,0:T(8,128)(2,1)}, u32[]{:S(2)}, u32[]{:S(2)}) collective-permute-start(bf16[3,256,512]{2,1,0:T(8,128)(2,1)} %get-tuple-element.46.refs_1_), channel_id=1, source_target_pairs={{0,64},{64,128},{128,192},{192,0},{1,65},{65,129},{129,193},{193,1... | collective-permute-start | bytes 2359304 | tf_op jit(solution)/shard_map/ppermute | solution.py:492
  43.1 18.7 %collective-permute-start.5 = (bf16[3,256,512]{2,1,0:T(8,128)(2,1)}, bf16[3,256,512]{2,1,0:T(8,128)(2,1)}, u32[]{:S(2)}, u32[]{:S(2)}) collective-permute-start(bf16[3,256,512]{2,1,0:T(8,128)(2,1)} %get-tuple-element.46.refs_1_), channel_id=1, source_target_pairs={{0,32},{32,0},{1,33},{33,1},{2,34},{34,2},{3,35},{35,3},{4,36},{36... | collective-permute-start | bytes 2359304 | tf_op jit(solution)/shard_map/ppermute | solution.py:492
  44.7 18.2 %collective-permute-start.6 = (bf16[3,256,512]{2,1,0:T(8,128)(2,1)}, bf16[3,256,512]{2,1,0:T(8,128)(2,1)}, u32[]{:S(2)}, u32[]{:S(2)}) collective-permute-start(bf16[3,256,512]{2,1,0:T(8,128)(2,1)} %get-tuple-element.47.refs_3_), channel_id=1, source_target_pairs={{0,192},{64,0},{128,64},{192,128},{1,193},{65,1},{129,65},{193,129... | collective-permute-start | bytes 2359304 | tf_op jit(solution)/shard_map/ppermute | solution.py:492
  51.9 105.4 %collective-permute-start.15 = (bf16[4,3,256,512]{3,2,1,0:T(8,128)(2,1)}, bf16[4,3,256,512]{3,2,1,0:T(8,128)(2,1)S(1)}, u32[]{:S(2)}, u32[]{:S(2)}) collective-permute-start(bf16[4,3,256,512]{3,2,1,0:T(8,128)(2,1)} %get-tuple-element.64.refs_6_), channel_id=1, source_target_pairs={{0,16},{16,0},{1,17},{17,1},{2,18},{18,2},{3,19},{19,3},{4,20},{20... | collective-permute-start | bytes 9437192 | tf_op jit(solution)/shard_map/ppermute | solution.py:492
  52.0 10.9 %copy-start.9 = (bf16[4,256,128]{2,1,0:T(8,128)(2,1)}, bf16[4,256,128]{2,1,0:T(8,128)(2,1)S(1)}, u32[]{:S(2)}) copy-start(bf16[4,256,128]{2,1,0:T(8,128)(2,1)S(1)} %all-to-all-done) | copy-start | bytes 786436
  87.9 9.9 %collective-permute-start.7 = (bf16[1,256,512]{2,1,0:T(8,128)(2,1)}, bf16[1,256,512]{2,1,0:T(8,128)(2,1)S(1)}, u32[]{:S(2)}, u32[]{:S(2)}) collective-permute-start(bf16[1,256,512]{2,1,0:T(8,128)(2,1)} %get-tuple-element.55), channel_id=1, source_target_pairs={{0,32},{32,0},{1,33},{33,1},{2,34},{34,2},{3,35},{35,3},{4,36},{36... | collective-permute-start | bytes 786440 | tf_op jit(solution)/shard_map/ppermute | solution.py:492
  89.6 8.2 %collective-permute-start.8 = (bf16[1,256,512]{2,1,0:T(8,128)(2,1)}, bf16[1,256,512]{2,1,0:T(8,128)(2,1)S(1)}, u32[]{:S(2)}, u32[]{:S(2)}) collective-permute-start(bf16[1,256,512]{2,1,0:T(8,128)(2,1)} %get-tuple-element.56), channel_id=1, source_target_pairs={{0,64},{64,128},{128,192},{192,0},{1,65},{65,129},{129,193},{193,1... | collective-permute-start | bytes 786440 | tf_op jit(solution)/shard_map/ppermute | solution.py:492
  91.3 6.7 %collective-permute-start.9 = (bf16[1,256,512]{2,1,0:T(8,128)(2,1)}, bf16[1,256,512]{2,1,0:T(8,128)(2,1)S(1)}, u32[]{:S(2)}, u32[]{:S(2)}) collective-permute-start(bf16[1,256,512]{2,1,0:T(8,128)(2,1)} %get-tuple-element.57), channel_id=1, source_target_pairs={{0,192},{64,0},{128,64},{192,128},{1,193},{65,1},{129,65},{193,129... | collective-permute-start | bytes 786440 | tf_op jit(solution)/shard_map/ppermute | solution.py:492
  97.7 0.7 copy-start.2
  97.8 0.8 copy-start.3
  98.0 0.7 copy-start.4
  98.7 3.7 %collective-permute-start.10 = (bf16[256,1536]{1,0:T(8,128)(2,1)}, bf16[256,1536]{1,0:T(8,128)(2,1)}, u32[]{:S(2)}, u32[]{:S(2)}) collective-permute-start(bf16[256,1536]{1,0:T(8,128)(2,1)} %get-tuple-element.59), channel_id=1, source_target_pairs={{0,16},{16,0},{1,17},{17,1},{2,18},{18,2},{3,19},{19,3},{4,20},{20... | collective-permute-start | bytes 2359304 | tf_op jit(solution)/shard_map/ppermute | solution.py:492
  98.8 2.9 %collective-permute-start.11 = (bf16[1,256,512]{2,1,0:T(8,128)(2,1)}, bf16[1,256,512]{2,1,0:T(8,128)(2,1)S(1)}, u32[]{:S(2)}, u32[]{:S(2)}) collective-permute-start(bf16[1,256,512]{2,1,0:T(8,128)(2,1)} %get-tuple-element.60.refs_0_), channel_id=1, source_target_pairs={{0,16},{16,0},{1,17},{17,1},{2,18},{18,2},{3,19},{19,3},{4,20},{20... | collective-permute-start | bytes 786440 | tf_op jit(solution)/shard_map/ppermute | solution.py:492
  99.3 2.7 %collective-permute-start.12 = (bf16[1,256,512]{2,1,0:T(8,128)(2,1)}, bf16[1,256,512]{2,1,0:T(8,128)(2,1)S(1)}, u32[]{:S(2)}, u32[]{:S(2)}) collective-permute-start(bf16[1,256,512]{2,1,0:T(8,128)(2,1)} %get-tuple-element.61.refs_1_), channel_id=1, source_target_pairs={{0,16},{16,0},{1,17},{17,1},{2,18},{18,2},{3,19},{19,3},{4,20},{20... | collective-permute-start | bytes 786440 | tf_op jit(solution)/shard_map/ppermute | solution.py:492
  99.6 2.8 %collective-permute-start.13 = (bf16[1,256,512]{2,1,0:T(8,128)(2,1)}, bf16[1,256,512]{2,1,0:T(8,128)(2,1)S(1)}, u32[]{:S(2)}, u32[]{:S(2)}) collective-permute-start(bf16[1,256,512]{2,1,0:T(8,128)(2,1)} %get-tuple-element.62.refs_2_), channel_id=1, source_target_pairs={{0,16},{16,0},{1,17},{17,1},{2,18},{18,2},{3,19},{19,3},{4,20},{20... | collective-permute-start | bytes 786440 | tf_op jit(solution)/shard_map/ppermute | solution.py:492
  101.7 0.8 copy-start.6
  101.7 55.6 %collective-permute-start.16 = (bf16[3,3,256,512]{3,2,1,0:T(8,128)(2,1)}, bf16[3,3,256,512]{3,2,1,0:T(8,128)(2,1)}, u32[]{:S(2)}, u32[]{:S(2)}) collective-permute-start(bf16[3,3,256,512]{3,2,1,0:T(8,128)(2,1)} %get-tuple-element.65.refs_8_), channel_id=1, source_target_pairs={{0,16},{16,0},{1,17},{17,1},{2,18},{18,2},{3,19},{19,3},{4,20},{20... | collective-permute-start | bytes 7077896 | tf_op jit(solution)/shard_map/ppermute | solution.py:492
  102.0 0.7 copy-start.7
  102.4 0.7 copy-start.8
  133.1 4.2 %collective-permute-start.14 = (bf16[4,256,384]{2,1,0:T(8,128)(2,1)}, bf16[4,256,384]{2,1,0:T(8,128)(2,1)}, u32[]{:S(2)}, u32[]{:S(2)}) collective-permute-start(bf16[4,256,384]{2,1,0:T(8,128)(2,1)} %bitcast.20), channel_id=1, source_target_pairs={{0,16},{16,0},{1,17},{17,1},{2,18},{18,2},{3,19},{19,3},{4,20},{20... | collective-permute-start | bytes 2359304 | tf_op jit(solution)/shard_map/ppermute | solution.py:492
  133.1 17.5 %all-to-all-start.3 = ((bf16[4,256,384]{2,1,0:T(8,128)(2,1)}), bf16[4,256,384]{2,1,0:T(8,128)(2,1)}, u32[]{:S(2)}, u32[]{:S(2)}) async-start(bf16[4,256,384]{2,1,0:T(8,128)(2,1)} %bitcast.21), calls=%async_computation.3 | async-start | bytes 1572864 | tf_op jit(solution)/shard_map/all_to_all | solution.py:541
  150.6 28.3 %all-to-all-start.2 = ((bf16[4,512,384]{2,1,0:T(8,128)(2,1)}), bf16[4,512,384]{2,1,0:T(8,128)(2,1)}, u32[]{:S(2)}, u32[]{:S(2)}) async-start(bf16[4,512,384]{2,1,0:T(8,128)(2,1)} %bitcast.19), calls=%async_computation.2 | async-start | bytes 3145728 | tf_op jit(solution)/shard_map/all_to_all | solution.py:560
  157.2 1.6 copy-start
  166.5 29.4 %collective-permute-start.18 = (bf16[1040,256]{1,0:T(8,128)(2,1)}, bf16[1040,256]{1,0:T(8,128)(2,1)S(1)}, u32[]{:S(2)}, u32[]{:S(2)}) collective-permute-start(bf16[1040,256]{1,0:T(8,128)(2,1)} %get-tuple-element.72), channel_id=1, source_target_pairs={{0,1},{1,2},{2,3},{3,0},{4,5},{5,6},{6,7},{7,4},{8,9},{9,10},{10,1... | collective-permute-start | bytes 1597448 | tf_op jit(solution)/shard_map/ppermute | solution.py:492
  168.7 26.7 %collective-permute-start.19 = (bf16[1024,256]{1,0:T(8,128)(2,1)}, bf16[1024,256]{1,0:T(8,128)(2,1)S(1)}, u32[]{:S(2)}, u32[]{:S(2)}) collective-permute-start(bf16[1024,256]{1,0:T(8,128)(2,1)} %get-tuple-element.74), channel_id=1, source_target_pairs={{0,3},{1,0},{2,1},{3,2},{4,7},{5,4},{6,5},{7,6},{8,11},{9,8},{10,9... | collective-permute-start | bytes 1572872 | tf_op jit(solution)/shard_map/ppermute | solution.py:492
  181.2 18.0 %collective-permute-start.17 = (bf16[256,384]{1,0:T(8,128)(2,1)}, bf16[256,384]{1,0:T(8,128)(2,1)S(1)}, u32[]{:S(2)}, u32[]{:S(2)}) collective-permute-start(bf16[256,384]{1,0:T(8,128)(2,1)} %get-tuple-element.69.refs_0_), channel_id=1, source_target_pairs={{0,32},{32,0},{1,33},{33,1},{2,34},{34,2},{3,35},{35,3},{4,36},{36... | collective-permute-start | bytes 589832 | tf_op jit(solution)/shard_map/ppermute | solution.py:492
  195.5 0.8 copy-start.10
  195.9 0.8 copy-start.1
  199.2 0.7 copy-start.18
  199.9 5.8 %copy-start.14 = (bf16[528,256]{1,0:T(8,128)(2,1)S(1)}, bf16[528,256]{1,0:T(8,128)(2,1)}, u32[]{:S(2)}) copy-start(bf16[528,256]{1,0:T(8,128)(2,1)} %get-tuple-element.75.refs_0_) | copy-start | bytes 811012
  199.9 8.4 %copy-start.20 = (bf16[528,256]{1,0:T(8,128)(2,1)S(1)}, bf16[528,256]{1,0:T(8,128)(2,1)}, u32[]{:S(2)}) copy-start(bf16[528,256]{1,0:T(8,128)(2,1)} %get-tuple-element.78) | copy-start | bytes 811012
  202.2 23.9 %all-to-all-start.4 = ((bf16[4,256,512]{2,1,0:T(8,128)(2,1)}), bf16[4,256,512]{2,1,0:T(8,128)(2,1)S(1)}, u32[]{:S(2)}, u32[]{:S(2)}) async-start(bf16[4,256,512]{2,1,0:T(8,128)(2,1)} %shard_map.71), calls=%async_computation.4 | async-start | bytes 2097152 | tf_op jit(solution)/shard_map/all_to_all | solution.py:566
  205.7 14.1 %collective-permute-start.20 = (bf16[528,256]{1,0:T(8,128)(2,1)S(1)}, bf16[528,256]{1,0:T(8,128)(2,1)S(1)}, u32[]{:S(2)}, u32[]{:S(2)}) collective-permute-start(bf16[528,256]{1,0:T(8,128)(2,1)S(1)} %copy-done.14), channel_id=1, source_target_pairs={{0,1},{1,2},{2,3},{3,0},{4,5},{5,6},{6,7},{7,4},{8,9},{9,10},{10,1... | collective-permute-start | bytes 811016 | tf_op jit(solution)/shard_map/ppermute | solution.py:492
  208.3 13.6 %collective-permute-start.21 = (bf16[528,256]{1,0:T(8,128)(2,1)S(1)}, bf16[528,256]{1,0:T(8,128)(2,1)S(1)}, u32[]{:S(2)}, u32[]{:S(2)}) collective-permute-start(bf16[528,256]{1,0:T(8,128)(2,1)S(1)} %copy-done.20), channel_id=1, source_target_pairs={{0,3},{1,0},{2,1},{3,2},{4,7},{5,4},{6,5},{7,6},{8,11},{9,8},{10,9... | collective-permute-start | bytes 811016 | tf_op jit(solution)/shard_map/ppermute | solution.py:492
  219.9 2.1 copy-start.15
  221.9 0.7 copy-start.16
  226.1 1.0 copy-start.5
Sparse Core Ops, SparseCore 0:
  18.6 88.5 all-gather.1

commit v6 on v5

--- a/solution.py
+++ b/solution.py
@@ -113,7 +113,7 @@
         ),
         scratch_shapes=[pltpu.SemaphoreType.DMA((n,))],
         compiler_params=PARAMS,
-        cost_estimate=cost(BUSY, 1),
+        cost_estimate=cost(1, 1),
     )(ids, mine, theirs, *shards, *sums)
 
 
@@ -143,8 +143,9 @@
     )(ids, mine, given, keep, came, *pieces)
 
 
-def attention_kernel(q_rows, qkv_ref, dout_ref, *refs):
-    att_ref, grad_ref, dk_ref, dv_ref = refs[-4:]
+def attention_kernel(q_rows, carried, qkv_ref, dout_ref, *refs):
+    att_ref, grad_ref = refs[-4 - carried : -2 - carried]
+    dk_ref, dv_ref = refs[-2:]
     scale = 1.0 / math.sqrt(HS)
     key = qkv_ref[:, HS : 2 * HS]
     value = qkv_ref[:, 2 * HS : 3 * HS]
@@ -179,18 +180,20 @@
     grad_ref[:, 2 * HS : 3 * HS] = dv_ref[...].astype(BF)
 
 
-def attention(qkv, dout, after=()):
+def attention(qkv, dout, carry, after):
     n = qkv.shape[0]
-    return pl.pallas_call(
-        functools.partial(attention_kernel, min(256, n)),
-        out_shape=(shape(n, HS), shape(n, 3 * HS)),
-        in_specs=[pl.BlockSpec(memory_space=pltpu.VMEM)] * 2
-        + [pl.BlockSpec(memory_space=pl.ANY)] * len(after),
-        out_specs=(pl.BlockSpec(memory_space=pltpu.VMEM),) * 2,
+    vmem = pl.BlockSpec(memory_space=pltpu.VMEM)
+    free = pl.BlockSpec(memory_space=pl.ANY)
+    return pl.pallas_call(
+        functools.partial(attention_kernel, min(256, n), len(carry)),
+        out_shape=(shape(n, HS), shape(n, 3 * HS)) + tuple(shape(*c.shape) for c in carry),
+        in_specs=[vmem] * 2 + [free] * (len(carry) + len(after)),
+        out_specs=(vmem,) * 2 + (free,) * len(carry),
         scratch_shapes=[pltpu.VMEM((n, HS), F32), pltpu.VMEM((n, HS), F32)],
-        compiler_params=PARAMS,
-        cost_estimate=cost(1, 1),
-    )(qkv, dout, *after)
+        input_output_aliases={2 + i: 2 + i for i in range(len(carry))},
+        compiler_params=PARAMS,
+        cost_estimate=cost(BUSY, 1),
+    )(qkv, dout, *carry, *after)
 
 
 def write_stat(ref, at, stat):
@@ -309,7 +312,8 @@
     )(up_part, up_in, up_in, down_part, down_in, stat, *after)
 
 
-def finish_kernel(at_ref, own0, own1, up0, up1, down0, down1, tok_ref, root_ref, stat_ref, out_ref):
+def finish_kernel(at_ref, own0, own1, up0, up1, down0, down1, tok_ref, root_ref, stat_ref, *refs):
+    out_ref = refs[-1]
     half = own0.shape[0]
     stat = stat_ref[...] + read_stat(up0, half) + read_stat(down1, half)
     stat = jnp.broadcast_to(stat, (HS, stat.shape[1])).T[:, 0:1]
@@ -325,7 +329,7 @@
         out_ref[:, span] = ((total.T - unit * stat) / root).astype(BF)
 
 
-def finish(ids, parts, tokens, root, stat):
+def finish(ids, parts, tokens, root, stat, after=()):
     half, rows = parts[0].shape
     share = 2 * half
     tile = HS
@@ -337,30 +341,32 @@
             grid=(rows // tile,),
             in_specs=[some(p) for p in parts]
             + [pl.BlockSpec((tile, share), lambda i, at: (i, at[T]))]
-            + [pl.BlockSpec((tile, 1), lambda i, at: (i, 0)), some(stat)],
+            + [pl.BlockSpec((tile, 1), lambda i, at: (i, 0)), some(stat)]
+            + [pl.BlockSpec(memory_space=pl.ANY)] * len(after),
             out_specs=pl.BlockSpec((tile, share), lambda i, at: (i, 0)),
         ),
         out_shape=shape(rows, share),
         compiler_params=PARAMS,
-        cost_estimate=cost(1, 1),
-    )(ids, *parts, tokens, root, stat)
-
-
-def outer_kernel(tile, blocks_any, mine_ref, other_ref, out_ref, a_ref, g_ref, sems):
+        cost_estimate=cost(BUSY, 1),
+    )(ids, *parts, tokens, root, stat, *after)
+
+
+def outer_kernel(tile, spots, at_ref, *refs):
+    arrays, (mine_ref, other_ref, out_ref, a_ref, g_ref, sems) = refs[:-6], refs[-6:]
     n, rows, _ = mine_ref.shape
     depth = a_ref.shape[0]
     copies = []
     for step in range(depth // tile):
         span = pl.ds(step * tile, tile)
         some = []
-        for i in range(2 * n):
+        for i, (which, at, _, _) in enumerate(spots):
             to = a_ref.at[span, pl.ds(i * rows, rows)]
-            some.append(pltpu.make_async_copy(blocks_any.at[i, span], to, sems.at[step, i]))
+            some.append(pltpu.make_async_copy(arrays[which].at[at, span], to, sems.at[step, i]))
             some[-1].start()
         copies.append(some)
-    for i in range(n):
-        g_ref[2 * i * rows : (2 * i + 1) * rows, :] = mine_ref[i]
-        g_ref[(2 * i + 1) * rows : (2 * i + 2) * rows, :] = other_ref[i]
+    for i, (_, _, by, frame) in enumerate(spots):
+        ref = other_ref if frame else mine_ref
+        g_ref[i * rows : (i + 1) * rows, :] = ref[lax.rem(at_ref[X] + by, n)]
     for step, some in enumerate(copies):
         for copy in some:
             copy.wait()
@@ -370,14 +376,17 @@
         ).astype(BF)
 
 
-def outer(blocks, mine, other):
-    n, depth, rows = blocks.shape
+def outer(ids, arrays, spots, mine, other):
+    _, depth, rows = arrays[0].shape
     cols = mine.shape[2]
+    n = len(spots)
     tile = 512
     vmem = pl.BlockSpec(memory_space=pltpu.VMEM)
     return pl.pallas_call(
-        functools.partial(outer_kernel, tile),
-        in_specs=[pl.BlockSpec(memory_space=pl.ANY), vmem, vmem],
+        functools.partial(outer_kernel, tile, spots),
+        in_specs=[pl.BlockSpec(memory_space=pltpu.SMEM)]
+        + [pl.BlockSpec(memory_space=pl.ANY)] * len(arrays)
+        + [vmem, vmem],
         out_specs=vmem,
         out_shape=shape(depth, cols),
         scratch_shapes=[
@@ -387,7 +396,7 @@
         ],
         compiler_params=PARAMS,
         cost_estimate=cost(1, 1),
-    )(blocks, mine, other)
+    )(ids, *arrays, mine, other)
 
 
 def split_kernel(at_ref, part_ref, *refs):
@@ -477,7 +486,7 @@
     return pl.pallas_call(
         kernel,
         in_specs=[free] * m,
-        out_specs=(free,) * (n + len(pieces)),
+        out_specs=(free,) * n + (pl.BlockSpec(memory_space=pltpu.VMEM),) * len(pieces),
         out_shape=tuple(shape(*a.shape) for a in arrays)
         + tuple(shape(1, *arrays[which].shape[1:]) for which, _ in pieces),
         scratch_shapes=[pltpu.SemaphoreType.DMA((max(len(pieces), 1),))],
@@ -507,7 +516,7 @@
     root, mine, given, theirs, pair = unit_rows(ids, tokens, swap(tokens), w_rows)
     left, right, other = gate((left, right, other), (pair,))
 
-    blocks = lax.all_gather(pair, "x", axis=0, tiled=True)
+    x_left, x_right = shift(pair, "x", 1), shift(pair, "x", -1)
 
     dout = cotangent.reshape(rows, heads, HS).transpose(1, 0, 2)
     dout = lax.all_to_all(dout, "x", 0, 0, tiled=True).reshape(n_x * rows, HS)
@@ -528,18 +537,25 @@
     pieces = (*pieces, *(swap(p) for p in pieces))
     proj = project_last(ids, mine, given, keep, swap(give), pieces, (2, 1), heads)
 
+    x_left, x_right, far_0, far_1 = gate((x_left, x_right), pieces=((0, 0), (1, 1)))
+    far_0, far_1 = shift(far_0, "x", 1), shift(far_1, "x", -1)
+    blocks = (pair, x_left, x_right, far_0, far_1)
+    spots = ((0, 0, 0, 0), (0, 1, 0, 1), (1, 0, 3, 0), (1, 1, 3, 1), (2, 0, 1, 0), (2, 1, 1, 1), (3, 0, 2, 0), (4, 0, 2, 1))
+    qkv = lax.all_to_all(proj, "x", 0, 0, tiled=True).reshape(n_x * rows, 3 * HS)
+    att, head_grads, stack_0, stack_1 = attention(
+        qkv, dout, (stack_0, stack_1), (far_0, far_1)
+    )
+
     shards = (*pieces, stack_0, swap(stack_0), stack_1, swap(stack_1))
     places = {(2, 1): [[(3 * core + j, (0,)) for j in range(3)] for core in range(2)]}
     for first, keys in ((6, near), (8, then)):
         for i, key in enumerate(keys):
             places[key] = [[(first + core, (i, j)) for j in range(3)] for core in range(2)]
     places = [places[(by, z)] for by in range(n_y) for z in range(2)]
-    qkv = lax.all_to_all(proj, "x", 0, 0, tiled=True).reshape(n_x * rows, 3 * HS)
-    att, head_grads = attention(qkv, dout)
 
     head_grads = head_grads.reshape(n_x, rows, 3 * HS)
     grads = lax.all_to_all(head_grads, "x", 0, 0, tiled=True)
-    part = outer(blocks, head_grads, swap(head_grads))
+    part = outer(ids, blocks, spots, head_grads, swap(head_grads))
 
     up, down, stat = norm_halves(
         ids, grads, proj, shards, places,
@@ -560,8 +576,8 @@
     part = lax.all_to_all(part, "y", 0, 0, tiled=True).reshape(n_y, 2, w_rows, 3 * HS)
     keep, give = split(ids, part, (own0,))
     came = shift(give, "zl", 1)
-    up_2, down_2 = add_messages(up_part, up, down_part, down, stat, (give,))
-    last = merge(keep, came, att.reshape(n_x, rows, HS), (up_2,))
+    up_2, down_2 = add_messages(up_part, up, down_part, down, stat, (came,))
+    last = merge(keep, came, att.reshape(n_x, rows, HS))
     up_2, down_2 = shift(up_2, "zh", 1), shift(down_2, "zh", -1)
     last = lax.all_to_all(last, "x", 0, 0, tiled=True)
     token_grad = finish(ids, (own0, own1, up_2, up, down, down_2), tokens, root, stat)

time: 240 us -> 232 us (0.967)
  Pallas kernels: 94.1 us -> 73.8 us
  between operations: 14.3 us -> 0.9 us
  waiting for transfers between devices: 60 us -> 69 us
  blocking collectives: 17.1 us -> 25.3 us
  starting transfers between devices: 41.9 us -> 49.7 us
    all_to_all x1, waiting for transfers between devices: 0.01 us -> 26.8 us  [per_device(): dout = lax.all_to_all(dout, 'x', 0, 0, tiled=True).reshape(n_x * rows, HS)]
    pallas_call x5 -> x6, Pallas kernels: 42.9 us -> 22.8 us  [the longest x1 9.34 us: outer(): pl.pallas_call(functools.partial(outer_kernel, tile, spots), in_specs=[pl...]
    ppermute x22 -> x26, waiting for transfers between devices: 56 us -> 38 us  [shift(): return lax.ppermute(x, axis, [(i, (i + by) % n) for i in range(n)])]
    all_to_all x1, blocking collectives: 17.1 us -> 25.3 us  [per_device(): lax.all_to_all(proj, 'x', 0, 0, tiled=True).reshape(n_x * rows, 3 * HS)]
    ppermute x22 -> x26, starting transfers between devices: 23.2 us -> 30 us  [shift(): return lax.ppermute(x, axis, [(i, (i + by) % n) for i in range(n)])]
    all_to_all x1, waiting for transfers between devices: 0.01 us -> 4.13 us  [per_device(): last = lax.all_to_all(last, 'x', 0, 0, tiled=True)]
    all_to_all x1, waiting for transfers between devices: 3.92 us -> 0.01 us  [per_device(): grads = lax.all_to_all(head_grads, 'x', 0, 0, tiled=True)]
    unnamed x42 -> x46, local copies, waits for them, and re-layouts: 8.68 us -> 10.9 us
  transfers between devices with their start and end apart: 27 -> 30, of which waited for: 17 -> 12; matrix products, arithmetic and copies ran while one was open for 1% -> 1% of each run, Pallas kernels for 35% -> 26%
where the time goes in v6:
time: 232 us; the launch traced here: 231 us
  Pallas kernels  73.8 us (32%)
  waiting for transfers between devices  69 us (30%)
  starting transfers between devices  49.7 us (21%)
  blocking collectives  25.3 us (11%)
  local copies, waits for them, and re-layouts  12.3 us (5%)
    ppermute x26, waiting for transfers between devices, shift(): return lax.ppermute(x, axis, [(i, (i + by) % n) for i in range(n)])  38 us
    ppermute x26, starting transfers between devices, shift(): return lax.ppermute(x, axis, [(i, (i + by) % n) for i in range(n)])  30 us
    all_to_all x1, waiting for transfers between devices, per_device(): dout = lax.all_to_all(dout, 'x', 0, 0, tiled=True).reshape(n_x * rows, HS)  26.8 us
    all_to_all x1, blocking collectives, per_device(): lax.all_to_all(proj, 'x', 0, 0, tiled=True).reshape(n_x * rows, 3 * HS)  25.3 us
    pallas_call x2, Pallas kernels, norm_halves(): pl.pallas_call(functools.partial(norm_kernel, width, halves, spots, place...  15.2 us
    pallas_call x2, Pallas kernels, project(): pl.pallas_call(functools.partial(project_kernel, offsets, not sums), in_s...  12.4 us
    unnamed x46, local copies, waits for them, and re-layouts  10.9 us
    pallas_call x1, Pallas kernels, outer(): pl.pallas_call(functools.partial(outer_kernel, tile, spots), in_specs=[pl...  9.34 us
  transfers between devices with their start and end apart: 30, of which 12 were waited for; matrix products, arithmetic and copies ran while one was open for 1% of the time, Pallas kernels for 26%

profile of v6, /device:TPU:8, one launch (start us, length us, event | category | flops | bytes accessed | tf_op | source)
XLA Modules:
  0.0 231.0 jit_solution(4711422591717470354)
XLA Ops:
  0.7 1.7 collective-permute-start.5
  2.4 0.7 collective-permute-start.6
  3.1 1.7 collective-permute-start.7
  4.8 0.6 stack.23.at_ref
  5.4 1.3 copy-done.20
  6.7 5.4 %shard_map.58 = (f32[256,1]{1,0:T(8,128)}, bf16[256,2048]{1,0:T(8,128)(2,1)}, bf16[256,2048]{1,0:T(8,128)(2,1)}, bf16[256,2048]{1,0:T(8,128)(2,1)}, bf16[2,2048,256]{2,1,0:T(8,128)(2,1)}) custom-call(s32[5]{0:T(128)} %stack.23.at_ref, bf16[256,4096]{1,0:T(8,128)(2,1)} %bitcast.32, bf16[256,4096]{1,0:T(8,128)(2,1)} %copy-done.20), custom_call_target="tpu_custom_call" | custom-call | flops 20000000000 | bytes 1 | tf_op jit(solution)/shard_map/pallas_call | solution.py:55
  12.2 1.5 collective-permute-start.1
  13.7 1.7 collective-permute-start.2
  15.4 5.9 %collective-permute-done.5.refs_0_ = bf16[3,256,512]{2,1,0:T(8,128)(2,1)S(1)} collective-permute-done((bf16[3,256,512]{2,1,0:T(8,128)(2,1)}, bf16[3,256,512]{2,1,0:T(8,128)(2,1)S(1)}, u32[]{:S(2)}, u32[]{:S(2)}) %collective-permute-start.5) | collective-permute-done | bytes 786464 | tf_op jit(solution)/shard_map/ppermute | solution.py:501
  21.3 1.0 collective-permute-done.6.refs_1_
  22.3 0.6 collective-permute-done.7.refs_2_
  22.9 1.4 collective-permute-start.8
  24.4 1.7 collective-permute-start.9
  26.1 0.5 collective-permute-start.10
  26.6 0.7 copy.22
  27.3 4.3 %all-to-all-start = ((bf16[4,256,128]{2,1,0:T(8,128)(2,1)}), bf16[4,256,128]{2,1,0:T(8,128)(2,1)S(1)}, u32[]{:S(2)}, u32[]{:S(2)}) async-start(bf16[4,256,128]{2,1,0:T(8,128)(2,1)} %bitcast.18), calls=%async_computation | async-start | bytes 524288 | tf_op jit(solution)/shard_map/all_to_all | solution.py:522
  31.6 6.3 %shard_map.61 = (f32[256,1536]{1,0:T(8,128)}, f32[256,1536]{1,0:T(8,128)}, bf16[4,3,256,512]{3,2,1,0:T(8,128)(2,1)}) custom-call(s32[5]{0:T(128)} %stack.23.at_ref, bf16[256,2048]{1,0:T(8,128)(2,1)} %get-tuple-element.53.mine_ref, bf16[256,2048]{1,0:T(8,128)(2,1)} %get-tuple-element.55.theirs_ref, bf16[3,256,512]{2,1,0:T(8,128)(2,1)} %bitcast.29, ...), custom_call_target="tpu_custom_call" | custom-call | flops 1 | bytes 1 | tf_op jit(solution)/shard_map/pallas_call | solution.py:105
  37.9 26.8 %all-to-all-done = bf16[4,256,128]{2,1,0:T(8,128)(2,1)S(1)} async-done(((bf16[4,256,128]{2,1,0:T(8,128)(2,1)}), bf16[4,256,128]{2,1,0:T(8,128)(2,1)S(1)}, u32[]{:S(2)}, u32[]{:S(2)}) %all-to-all-start) | async-done | bytes 262176 | tf_op jit(solution)/shard_map/all_to_all | solution.py:522
  64.8 0.7 copy-done.16
  65.7 2.0 shard_map.62
  67.7 2.0 collective-permute-start.11
  69.7 1.6 collective-permute-start.12
  71.3 0.4 collective-permute-start.13
  71.7 6.1 %shard_map.63 = (f32[256,1536]{1,0:T(8,128)}, bf16[256,1536]{1,0:T(8,128)(2,1)}, bf16[3,3,256,512]{3,2,1,0:T(8,128)(2,1)}) custom-call(s32[5]{0:T(128)} %stack.23.at_ref, bf16[256,2048]{1,0:T(8,128)(2,1)} %get-tuple-element.53.mine_ref, bf16[256,2048]{1,0:T(8,128)(2,1)} %get-tuple-element.55.theirs_ref, bf16[3,256,512]{2,1,0:T(8,128)(2,1)} %get-tuple-element.61.refs_0_, ...), custom_call_target="tpu_custom_call" | custom-call | flops 1 | bytes 1 | tf_op jit(solution)/shard_map/pallas_call | solution.py:105
  78.2 0.5 copy-done.2
  79.2 0.5 collective-permute-start.15
  79.7 1.3 copy-done.1
  81.0 2.9 %shard_map.59 = (bf16[2,2048,256]{2,1,0:T(8,128)(2,1)}, bf16[2,2048,256]{2,1,0:T(8,128)(2,1)}, bf16[1,2048,256]{2,1,0:T(8,128)(2,1)}, bf16[1,2048,256]{2,1,0:T(8,128)(2,1)}) custom-call(bf16[2,2048,256]{2,1,0:T(8,128)(2,1)} %copy-done.1, bf16[2,2048,256]{2,1,0:T(8,128)(2,1)} %collective-permute-done.2.refs_1_), custom_call_target="tpu_custom_call", output_to_operand_aliasing={{0}: (0, {}), {1}: (1, {})} | custom-call | flops 1 | bytes 1 | tf_op jit(solution)/shard_map/pallas_call | solution.py:486
  83.9 1.2 collective-permute-start.3
  85.0 2.1 collective-permute-start.4
  87.2 0.6 collective-permute-start.17
  87.8 0.9 collective-permute-done.16.refs_4_
  89.4 0.4 copy-done.12
  89.8 4.2 %shard_map.65.p_ref = bf16[4,256,384]{2,1,0:T(8,128)(2,1)} custom-call(s32[5]{0:T(128)} %stack.23.at_ref, bf16[256,2048]{1,0:T(8,128)(2,1)} %get-tuple-element.53.mine_ref, bf16[256,2048]{1,0:T(8,128)(2,1)} %get-tuple-element.54.given_ref, f32[256,1536]{1,0:T(8,128)} %get-tuple-element.64.keep_ref, bf16[256,1536]{1,0:T(8,128)(2,1)} %collective-permute-done.14.came_ref, ...), custom_call_target="tpu_custom_call" | custom-call | flops 1 | bytes 1 | tf_op jit(solution)/shard_map/pallas_call | solution.py:136
  94.0 25.3 %all_to_all.29 = bf16[4,256,384]{2,1,0:T(8,128)(2,1)} all-to-all(bf16[4,256,384]{2,1,0:T(8,128)(2,1)} %shard_map.65.p_ref), channel_id=1, replica_groups=mesh['y'=4,'zl'=2,'core'=2,'x'=4,'zh'=4] {'x'}, dimensions={0} | all-to-all | bytes 1572864 | tf_op jit(solution)/shard_map/all_to_all | solution.py:544
  119.2 1.0 copy-done.14
  120.2 0.4 copy-done.15
  120.6 8.6 %shard_map.66 = (bf16[1024,128]{1,0:T(8,128)(2,1)}, bf16[1024,384]{1,0:T(8,128)(2,1)}, bf16[4,3,256,512]{3,2,1,0:T(8,128)(2,1)}, bf16[3,3,256,512]{3,2,1,0:T(8,128)(2,1)}) custom-call(bf16[1024,384]{1,0:T(8,128)(2,1)} %bitcast.25, bf16[1024,128]{1,0:T(8,128)(2,1)} %bitcast.24, ...), custom_call_target="tpu_custom_call", output_to_operand_aliasing={{2}: (2, {}), {3}: (3, {})} | custom-call | flops 20000000000 | bytes 1 | tf_op jit(solution)/shard_map/pallas_call | solution.py:187
  129.2 0.5 collective-permute-start.20
  129.7 4.4 %all-to-all-start.3 = ((bf16[4,256,384]{2,1,0:T(8,128)(2,1)}), bf16[4,256,384]{2,1,0:T(8,128)(2,1)}, u32[]{:S(2)}, u32[]{:S(2)}) async-start(bf16[4,256,384]{2,1,0:T(8,128)(2,1)} %bitcast.21), calls=%async_computation.3 | async-start | bytes 1572864 | tf_op jit(solution)/shard_map/all_to_all | solution.py:557
  134.1 5.6 %collective-permute-done.18.refs_6_ = bf16[4,256,384]{2,1,0:T(8,128)(2,1)} collective-permute-done((bf16[4,256,384]{2,1,0:T(8,128)(2,1)}, bf16[4,256,384]{2,1,0:T(8,128)(2,1)}, u32[]{:S(2)}, u32[]{:S(2)}) %collective-permute-start.18) | collective-permute-done | bytes 786464 | tf_op jit(solution)/shard_map/ppermute | solution.py:501
  139.7 9.3 %shard_map.67 = bf16[2048,384]{1,0:T(8,128)(2,1)} custom-call(s32[5]{0:T(128)} %stack.23.at_ref, bf16[2,2048,256]{2,1,0:T(8,128)(2,1)} %get-tuple-element.48.refs_3_.refs_0_, bf16[2,2048,256]{2,1,0:T(8,128)(2,1)} %get-tuple-element.49.refs_1_, bf16[2,2048,256]{2,1,0:T(8,128)(2,1)} %get-tuple-element.50.refs_2_, bf16[1,2048,256]{2,1,0:T(8,128)(2,1)} %copy-done.14, ...), custom_call_target="tpu_custom_call" | custom-call | flops 1 | bytes 1 | tf_op jit(solution)/shard_map/pallas_call | solution.py:385
  149.0 6.9 %all-to-all-start.2 = ((bf16[4,512,384]{2,1,0:T(8,128)(2,1)}), bf16[4,512,384]{2,1,0:T(8,128)(2,1)}, u32[]{:S(2)}, u32[]{:S(2)}) async-start(bf16[4,512,384]{2,1,0:T(8,128)(2,1)} %bitcast.19), calls=%async_computation.2 | async-start | bytes 3145728 | tf_op jit(solution)/shard_map/all_to_all | solution.py:576
  155.9 1.7 copy-done
  157.6 7.6 %shard_map.68 = (bf16[1040,256]{1,0:T(8,128)(2,1)}, bf16[1024,256]{1,0:T(8,128)(2,1)}, f32[1,256]{1,0:T(1,128)}) custom-call(s32[5]{0:T(128)} %stack.23.at_ref, bf16[4,256,384]{2,1,0:T(8,128)(2,1)} %all-to-all-done.3.g_ref, bf16[4,256,384]{2,1,0:T(8,128)(2,1)} %shard_map.65.p_ref, bf16[1,256,512]{2,1,0:T(8,128)(2,1)} %get-tuple-element.70.refs_0_, ...), custom_call_target="tpu_custom_call" | custom-call | flops 1 | bytes 1 | tf_op jit(solution)/shard_map/pallas_call | solution.py:273
  165.3 2.5 %collective-permute-start.22 = (bf16[1040,256]{1,0:T(8,128)(2,1)}, bf16[1040,256]{1,0:T(8,128)(2,1)S(1)}, u32[]{:S(2)}, u32[]{:S(2)}) collective-permute-start(bf16[1040,256]{1,0:T(8,128)(2,1)} %get-tuple-element.86), channel_id=1, source_target_pairs={{0,1},{1,2},{2,3},{3,0},{4,5},{5,6},{6,7},{7,4},{8,9},{9,10},{10,1... | collective-permute-start | bytes 1597448 | tf_op jit(solution)/shard_map/ppermute | solution.py:501
  167.7 2.3 collective-permute-start.23
  170.0 7.5 %shard_map.69 = (bf16[512,256]{1,0:T(8,128)(2,1)}, bf16[512,256]{1,0:T(8,128)(2,1)}, bf16[512,256]{1,0:T(8,128)(2,1)}, bf16[512,256]{1,0:T(8,128)(2,1)}, f32[1,256]{1,0:T(1,128)}) custom-call(s32[5]{0:T(128)} %stack.23.at_ref, bf16[4,256,384]{2,1,0:T(8,128)(2,1)} %all-to-all-done.3.g_ref, bf16[4,256,384]{2,1,0:T(8,128)(2,1)} %shard_map.65.p_ref, ...), custom_call_target="tpu_custom_call" | custom-call | flops 1 | bytes 1 | tf_op jit(solution)/shard_map/pallas_call | solution.py:273
  177.6 2.3 %shard_map.70 = (f32[256,384]{1,0:T(8,128)}, bf16[256,384]{1,0:T(8,128)(2,1)}) custom-call(s32[5]{0:T(128)} %stack.23.at_ref, bf16[4,2,256,384]{3,2,1,0:T(8,128)(2,1)} %bitcast.12.part_ref, bf16[512,256]{1,0:T(8,128)(2,1)} %get-tuple-element.79.refs_0_.own0), custom_call_target="tpu_custom_call" | custom-call | flops 1 | bytes 1 | tf_op jit(solution)/shard_map/pallas_call | solution.py:412
  179.9 1.0 collective-permute-start.21
  180.9 17.4 %collective-permute-done.21.came_ref.refs_0_ = bf16[256,384]{1,0:T(8,128)(2,1)S(1)} collective-permute-done((bf16[256,384]{1,0:T(8,128)(2,1)}, bf16[256,384]{1,0:T(8,128)(2,1)S(1)}, u32[]{:S(2)}, u32[]{:S(2)}) %collective-permute-start.21) | collective-permute-done | bytes 196640 | tf_op jit(solution)/shard_map/ppermute | solution.py:501
  198.4 0.7 copy-done.17
  199.5 2.2 shard_map.73
  201.7 1.5 collective-permute-start.24
  203.2 2.6 %collective-permute-start.25 = (bf16[528,256]{1,0:T(8,128)(2,1)}, bf16[528,256]{1,0:T(8,128)(2,1)S(1)}, u32[]{:S(2)}, u32[]{:S(2)}) collective-permute-start(bf16[528,256]{1,0:T(8,128)(2,1)} %get-tuple-element.90), channel_id=1, source_target_pairs={{0,3},{1,0},{2,1},{3,2},{4,7},{5,4},{6,5},{7,6},{8,11},{9,8},{10,9... | collective-permute-start | bytes 811016 | tf_op jit(solution)/shard_map/ppermute | solution.py:501
  205.9 2.2 shard_map.71
  208.1 4.0 %all-to-all-start.4 = ((bf16[4,256,512]{2,1,0:T(8,128)(2,1)}), bf16[4,256,512]{2,1,0:T(8,128)(2,1)S(1)}, u32[]{:S(2)}, u32[]{:S(2)}) async-start(bf16[4,256,512]{2,1,0:T(8,128)(2,1)} %shard_map.71), calls=%async_computation.4 | async-start | bytes 2097152 | tf_op jit(solution)/shard_map/all_to_all | solution.py:582
  212.1 4.3 %collective-permute-done.24.up0 = bf16[528,256]{1,0:T(8,128)(2,1)S(1)} collective-permute-done((bf16[528,256]{1,0:T(8,128)(2,1)}, bf16[528,256]{1,0:T(8,128)(2,1)S(1)}, u32[]{:S(2)}, u32[]{:S(2)}) %collective-permute-start.24) | collective-permute-done | bytes 270368 | tf_op jit(solution)/shard_map/ppermute | solution.py:501
  216.5 1.6 collective-permute-done.25.down1
  218.1 0.7 copy-done.22
  218.8 3.5 %shard_map.74 = bf16[256,1024]{1,0:T(8,128)(2,1)} custom-call(s32[5]{0:T(128)} %stack.23.at_ref, bf16[512,256]{1,0:T(8,128)(2,1)} %get-tuple-element.79.refs_0_.own0, bf16[512,256]{1,0:T(8,128)(2,1)} %get-tuple-element.84.own1, bf16[528,256]{1,0:T(8,128)(2,1)} %copy-done.21, bf16[1040,256]{1,0:T(8,128)(2,1)} %copy-done.13, bf16[1024,256]{1,0:T(8,128)(2,1)} %copy-done.18, ...), custom_call_target="tpu_custom_call" | custom-call | flops 20000000000 | bytes 1 | tf_op jit(solution)/shard_map/pallas_call | solution.py:337
  222.3 4.1 %all-to-all-done.4.in_ref = bf16[4,256,512]{2,1,0:T(8,128)(2,1)S(1)} async-done(((bf16[4,256,512]{2,1,0:T(8,128)(2,1)}), bf16[4,256,512]{2,1,0:T(8,128)(2,1)S(1)}, u32[]{:S(2)}, u32[]{:S(2)}) %all-to-all-start.4) | async-done | bytes 1048608 | tf_op jit(solution)/shard_map/all_to_all | solution.py:582
  226.4 1.0 copy-done.7
  227.4 3.5 %shard_map.72 = (f32[3,256,512]{2,1,0:T(8,128)}, bf16[256,512]{1,0:T(8,128)(2,1)}) custom-call(bf16[4,256,512]{2,1,0:T(8,128)(2,1)} %copy-done.7), custom_call_target="tpu_custom_call" | custom-call | flops 1 | bytes 1 | tf_op jit(solution)/shard_map/pallas_call | solution.py:457
  (63 shorter events, 2.4 us)
Async XLA Ops:
  0.6 4.8 %collective-permute-start = (bf16[256,4096]{1,0:T(8,128)(2,1)}, bf16[256,4096]{1,0:T(8,128)(2,1)S(1)}, u32[]{:S(2)}, u32[]{:S(2)}) collective-permute-start(bf16[256,4096]{1,0:T(8,128)(2,1)} %bitcast.31), channel_id=1, source_target_pairs={{0,16},{16,0},{1,17},{17,1},{2,18},{18,2},{3,19},{19,3},{4,20},{20... | collective-permute-start | bytes 6291464 | tf_op jit(solution)/shard_map/ppermute | solution.py:501
  0.7 20.6 %collective-permute-start.5 = (bf16[3,256,512]{2,1,0:T(8,128)(2,1)}, bf16[3,256,512]{2,1,0:T(8,128)(2,1)S(1)}, u32[]{:S(2)}, u32[]{:S(2)}) collective-permute-start(bf16[3,256,512]{2,1,0:T(8,128)(2,1)} %bitcast.26), channel_id=1, source_target_pairs={{0,64},{64,128},{128,192},{192,0},{1,65},{65,129},{129,193},{193,1... | collective-permute-start | bytes 2359304 | tf_op jit(solution)/shard_map/ppermute | solution.py:501
  2.4 19.9 %collective-permute-start.6 = (bf16[3,256,512]{2,1,0:T(8,128)(2,1)}, bf16[3,256,512]{2,1,0:T(8,128)(2,1)}, u32[]{:S(2)}, u32[]{:S(2)}) collective-permute-start(bf16[3,256,512]{2,1,0:T(8,128)(2,1)} %bitcast.27), channel_id=1, source_target_pairs={{0,192},{64,0},{128,64},{192,128},{1,193},{65,1},{129,65},{193,129... | collective-permute-start | bytes 2359304 | tf_op jit(solution)/shard_map/ppermute | solution.py:501
  3.1 19.8 %collective-permute-start.7 = (bf16[3,256,512]{2,1,0:T(8,128)(2,1)}, bf16[3,256,512]{2,1,0:T(8,128)(2,1)}, u32[]{:S(2)}, u32[]{:S(2)}) collective-permute-start(bf16[3,256,512]{2,1,0:T(8,128)(2,1)} %bitcast.28), channel_id=1, source_target_pairs={{0,32},{32,0},{1,33},{33,1},{2,34},{34,2},{3,35},{35,3},{4,36},{36... | collective-permute-start | bytes 2359304 | tf_op jit(solution)/shard_map/ppermute | solution.py:501
  5.4 1.3 copy-start.20
  12.2 14.3 %copy-start.19 = (bf16[1,256,512]{2,1,0:T(8,128)(2,1)S(1)}, bf16[1,256,512]{2,1,0:T(8,128)(2,1)}, u32[]{:S(2)}) copy-start(bf16[1,256,512]{2,1,0:T(8,128)(2,1)} %param.5) | copy-start | bytes 786436
  12.2 67.5 %collective-permute-start.1 = (bf16[2,2048,256]{2,1,0:T(8,128)(2,1)}, bf16[2,2048,256]{2,1,0:T(8,128)(2,1)S(1)}, u32[]{:S(2)}, u32[]{:S(2)}) collective-permute-start(bf16[2,2048,256]{2,1,0:T(8,128)(2,1)} %get-tuple-element.48.refs_3_.refs_0_), channel_id=1, source_target_pairs={{0,4},{4,8},{8,12},{12,0},{1,5},{5,9},{9,13},{13,1},{2,6},{6,10},{... | collective-permute-start | bytes 6291464 | tf_op jit(solution)/shard_map/ppermute | solution.py:501
  13.7 66.0 %collective-permute-start.2 = (bf16[2,2048,256]{2,1,0:T(8,128)(2,1)}, bf16[2,2048,256]{2,1,0:T(8,128)(2,1)}, u32[]{:S(2)}, u32[]{:S(2)}) collective-permute-start(bf16[2,2048,256]{2,1,0:T(8,128)(2,1)} %get-tuple-element.48.refs_3_.refs_0_), channel_id=1, source_target_pairs={{0,12},{4,0},{8,4},{12,8},{1,13},{5,1},{9,5},{13,9},{2,14},{6,2},{... | collective-permute-start | bytes 6291464 | tf_op jit(solution)/shard_map/ppermute | solution.py:501
  21.3 1.6 copy-start.9
  22.9 41.8 %collective-permute-start.8 = (bf16[3,256,512]{2,1,0:T(8,128)(2,1)}, bf16[3,256,512]{2,1,0:T(8,128)(2,1)S(1)}, u32[]{:S(2)}, u32[]{:S(2)}) collective-permute-start(bf16[3,256,512]{2,1,0:T(8,128)(2,1)} %get-tuple-element.56.refs_1_), channel_id=1, source_target_pairs={{0,64},{64,128},{128,192},{192,0},{1,65},{65,129},{129,193},{193,1... | collective-permute-start | bytes 2359304 | tf_op jit(solution)/shard_map/ppermute | solution.py:501
  24.4 40.4 %collective-permute-start.9 = (bf16[3,256,512]{2,1,0:T(8,128)(2,1)}, bf16[3,256,512]{2,1,0:T(8,128)(2,1)}, u32[]{:S(2)}, u32[]{:S(2)}) collective-permute-start(bf16[3,256,512]{2,1,0:T(8,128)(2,1)} %get-tuple-element.56.refs_1_), channel_id=1, source_target_pairs={{0,32},{32,0},{1,33},{33,1},{2,34},{34,2},{3,35},{35,3},{4,36},{36... | collective-permute-start | bytes 2359304 | tf_op jit(solution)/shard_map/ppermute | solution.py:501
  26.1 38.7 %collective-permute-start.10 = (bf16[3,256,512]{2,1,0:T(8,128)(2,1)}, bf16[3,256,512]{2,1,0:T(8,128)(2,1)}, u32[]{:S(2)}, u32[]{:S(2)}) collective-permute-start(bf16[3,256,512]{2,1,0:T(8,128)(2,1)} %get-tuple-element.57.refs_3_), channel_id=1, source_target_pairs={{0,192},{64,0},{128,64},{192,128},{1,193},{65,1},{129,65},{193,129... | collective-permute-start | bytes 2359304 | tf_op jit(solution)/shard_map/ppermute | solution.py:501
  27.3 37.4 %all-to-all-start = ((bf16[4,256,128]{2,1,0:T(8,128)(2,1)}), bf16[4,256,128]{2,1,0:T(8,128)(2,1)S(1)}, u32[]{:S(2)}, u32[]{:S(2)}) async-start(bf16[4,256,128]{2,1,0:T(8,128)(2,1)} %bitcast.18), calls=%async_computation | async-start | bytes 524288 | tf_op jit(solution)/shard_map/all_to_all | solution.py:522
  64.7 0.7 copy-start.16
  64.8 0.9 copy-start.8
  67.7 10.2 %collective-permute-start.11 = (bf16[1,256,512]{2,1,0:T(8,128)(2,1)}, bf16[1,256,512]{2,1,0:T(8,128)(2,1)S(1)}, u32[]{:S(2)}, u32[]{:S(2)}) collective-permute-start(bf16[1,256,512]{2,1,0:T(8,128)(2,1)} %get-tuple-element.65), channel_id=1, source_target_pairs={{0,32},{32,0},{1,33},{33,1},{2,34},{34,2},{3,35},{35,3},{4,36},{36... | collective-permute-start | bytes 786440 | tf_op jit(solution)/shard_map/ppermute | solution.py:501
  69.7 8.2 %collective-permute-start.12 = (bf16[1,256,512]{2,1,0:T(8,128)(2,1)}, bf16[1,256,512]{2,1,0:T(8,128)(2,1)S(1)}, u32[]{:S(2)}, u32[]{:S(2)}) collective-permute-start(bf16[1,256,512]{2,1,0:T(8,128)(2,1)} %get-tuple-element.66), channel_id=1, source_target_pairs={{0,64},{64,128},{128,192},{192,0},{1,65},{65,129},{129,193},{193,1... | collective-permute-start | bytes 786440 | tf_op jit(solution)/shard_map/ppermute | solution.py:501
  71.3 6.9 %collective-permute-start.13 = (bf16[1,256,512]{2,1,0:T(8,128)(2,1)}, bf16[1,256,512]{2,1,0:T(8,128)(2,1)S(1)}, u32[]{:S(2)}, u32[]{:S(2)}) collective-permute-start(bf16[1,256,512]{2,1,0:T(8,128)(2,1)} %get-tuple-element.67), channel_id=1, source_target_pairs={{0,192},{64,0},{128,64},{192,128},{1,193},{65,1},{129,65},{193,129... | collective-permute-start | bytes 786440 | tf_op jit(solution)/shard_map/ppermute | solution.py:501
  77.9 0.7 copy-start.2
  77.9 0.8 copy-start.3
  78.2 0.7 copy-start.5
  78.9 10.2 %collective-permute-start.14 = (bf16[256,1536]{1,0:T(8,128)(2,1)}, bf16[256,1536]{1,0:T(8,128)(2,1)}, u32[]{:S(2)}, u32[]{:S(2)}) collective-permute-start(bf16[256,1536]{1,0:T(8,128)(2,1)} %get-tuple-element.69), channel_id=1, source_target_pairs={{0,16},{16,0},{1,17},{17,1},{2,18},{18,2},{3,19},{19,3},{4,20},{20... | collective-permute-start | bytes 2359304 | tf_op jit(solution)/shard_map/ppermute | solution.py:501
  79.1 8.0 %copy-start.4 = (bf16[1,256,512]{2,1,0:T(8,128)(2,1)S(1)}, bf16[1,256,512]{2,1,0:T(8,128)(2,1)}, u32[]{:S(2)}) copy-start(bf16[1,256,512]{2,1,0:T(8,128)(2,1)} %get-tuple-element.71.refs_1_) | copy-start | bytes 786436
  79.2 8.0 %copy-start.6 = (bf16[1,256,512]{2,1,0:T(8,128)(2,1)S(1)}, bf16[1,256,512]{2,1,0:T(8,128)(2,1)}, u32[]{:S(2)}) copy-start(bf16[1,256,512]{2,1,0:T(8,128)(2,1)} %get-tuple-element.72.refs_2_) | copy-start | bytes 786436
  79.2 8.0 %collective-permute-start.15 = (bf16[1,256,512]{2,1,0:T(8,128)(2,1)}, bf16[1,256,512]{2,1,0:T(8,128)(2,1)S(1)}, u32[]{:S(2)}, u32[]{:S(2)}) collective-permute-start(bf16[1,256,512]{2,1,0:T(8,128)(2,1)} %get-tuple-element.70.refs_0_), channel_id=1, source_target_pairs={{0,16},{16,0},{1,17},{17,1},{2,18},{18,2},{3,19},{19,3},{4,20},{20... | collective-permute-start | bytes 786440 | tf_op jit(solution)/shard_map/ppermute | solution.py:501
  79.6 1.3 copy-start.1
  83.9 35.4 %collective-permute-start.3 = (bf16[1,2048,256]{2,1,0:T(8,128)(2,1)}, bf16[1,2048,256]{2,1,0:T(8,128)(2,1)S(1)}, u32[]{:S(2)}, u32[]{:S(2)}) collective-permute-start(bf16[1,2048,256]{2,1,0:T(8,128)(2,1)} %get-tuple-element.51), channel_id=1, source_target_pairs={{0,4},{4,8},{8,12},{12,0},{1,5},{5,9},{9,13},{13,1},{2,6},{6,10},{... | collective-permute-start | bytes 3145736 | tf_op jit(solution)/shard_map/ppermute | solution.py:501
  85.0 34.2 %collective-permute-start.4 = (bf16[1,2048,256]{2,1,0:T(8,128)(2,1)}, bf16[1,2048,256]{2,1,0:T(8,128)(2,1)S(1)}, u32[]{:S(2)}, u32[]{:S(2)}) collective-permute-start(bf16[1,2048,256]{2,1,0:T(8,128)(2,1)} %get-tuple-element.52), channel_id=1, source_target_pairs={{0,12},{4,0},{8,4},{12,8},{1,13},{5,1},{9,5},{13,9},{2,14},{6,2},{... | collective-permute-start | bytes 3145736 | tf_op jit(solution)/shard_map/ppermute | solution.py:501
  87.2 1.5 collective-permute-start.16
  87.2 1.9 copy-start.10
  87.2 1.9 collective-permute-start.17
  88.7 0.7 copy-start.11
  89.1 0.7 copy-start.12
  119.2 1.0 copy-start.14
  119.2 1.4 copy-start.15
  129.2 26.7 %collective-permute-start.19 = (bf16[4,3,256,512]{3,2,1,0:T(8,128)(2,1)}, bf16[4,3,256,512]{3,2,1,0:T(8,128)(2,1)S(1)}, u32[]{:S(2)}, u32[]{:S(2)}) collective-permute-start(bf16[4,3,256,512]{3,2,1,0:T(8,128)(2,1)} %get-tuple-element.76.refs_6_), channel_id=1, source_target_pairs={{0,16},{16,0},{1,17},{17,1},{2,18},{18,2},{3,19},{19,3},{4,20},{20... | collective-permute-start | bytes 9437192 | tf_op jit(solution)/shard_map/ppermute | solution.py:501
  129.2 26.7 %collective-permute-start.20 = (bf16[3,3,256,512]{3,2,1,0:T(8,128)(2,1)}, bf16[3,3,256,512]{3,2,1,0:T(8,128)(2,1)}, u32[]{:S(2)}, u32[]{:S(2)}) collective-permute-start(bf16[3,3,256,512]{3,2,1,0:T(8,128)(2,1)} %get-tuple-element.77.refs_8_), channel_id=1, source_target_pairs={{0,16},{16,0},{1,17},{17,1},{2,18},{18,2},{3,19},{19,3},{4,20},{20... | collective-permute-start | bytes 7077896 | tf_op jit(solution)/shard_map/ppermute | solution.py:501
  129.7 10.0 %collective-permute-start.18 = (bf16[4,256,384]{2,1,0:T(8,128)(2,1)}, bf16[4,256,384]{2,1,0:T(8,128)(2,1)}, u32[]{:S(2)}, u32[]{:S(2)}) collective-permute-start(bf16[4,256,384]{2,1,0:T(8,128)(2,1)} %bitcast.20), channel_id=1, source_target_pairs={{0,16},{16,0},{1,17},{17,1},{2,18},{18,2},{3,19},{19,3},{4,20},{20... | collective-permute-start | bytes 2359304 | tf_op jit(solution)/shard_map/ppermute | solution.py:501
  129.7 19.3 %all-to-all-start.3 = ((bf16[4,256,384]{2,1,0:T(8,128)(2,1)}), bf16[4,256,384]{2,1,0:T(8,128)(2,1)}, u32[]{:S(2)}, u32[]{:S(2)}) async-start(bf16[4,256,384]{2,1,0:T(8,128)(2,1)} %bitcast.21), calls=%async_computation.3 | async-start | bytes 1572864 | tf_op jit(solution)/shard_map/all_to_all | solution.py:557
  149.0 28.5 %all-to-all-start.2 = ((bf16[4,512,384]{2,1,0:T(8,128)(2,1)}), bf16[4,512,384]{2,1,0:T(8,128)(2,1)}, u32[]{:S(2)}, u32[]{:S(2)}) async-start(bf16[4,512,384]{2,1,0:T(8,128)(2,1)} %bitcast.19), calls=%async_computation.2 | async-start | bytes 3145728 | tf_op jit(solution)/shard_map/all_to_all | solution.py:576
  155.9 1.7 copy-start
  165.3 33.1 %collective-permute-start.22 = (bf16[1040,256]{1,0:T(8,128)(2,1)}, bf16[1040,256]{1,0:T(8,128)(2,1)S(1)}, u32[]{:S(2)}, u32[]{:S(2)}) collective-permute-start(bf16[1040,256]{1,0:T(8,128)(2,1)} %get-tuple-element.86), channel_id=1, source_target_pairs={{0,1},{1,2},{2,3},{3,0},{4,5},{5,6},{6,7},{7,4},{8,9},{9,10},{10,1... | collective-permute-start | bytes 1597448 | tf_op jit(solution)/shard_map/ppermute | solution.py:501
  167.7 30.6 %collective-permute-start.23 = (bf16[1024,256]{1,0:T(8,128)(2,1)}, bf16[1024,256]{1,0:T(8,128)(2,1)S(1)}, u32[]{:S(2)}, u32[]{:S(2)}) collective-permute-start(bf16[1024,256]{1,0:T(8,128)(2,1)} %get-tuple-element.88), channel_id=1, source_target_pairs={{0,3},{1,0},{2,1},{3,2},{4,7},{5,4},{6,5},{7,6},{8,11},{9,8},{10,9... | collective-permute-start | bytes 1572872 | tf_op jit(solution)/shard_map/ppermute | solution.py:501
  179.9 18.5 %collective-permute-start.21 = (bf16[256,384]{1,0:T(8,128)(2,1)}, bf16[256,384]{1,0:T(8,128)(2,1)S(1)}, u32[]{:S(2)}, u32[]{:S(2)}) collective-permute-start(bf16[256,384]{1,0:T(8,128)(2,1)} %get-tuple-element.81), channel_id=1, source_target_pairs={{0,32},{32,0},{1,33},{33,1},{2,34},{34,2},{3,35},{35,3},{4,36},{36... | collective-permute-start | bytes 589832 | tf_op jit(solution)/shard_map/ppermute | solution.py:501
  198.4 0.7 copy-start.17
  198.4 0.9 copy-start.18
  198.4 1.1 copy-start.13
  201.7 14.7 %collective-permute-start.24 = (bf16[528,256]{1,0:T(8,128)(2,1)}, bf16[528,256]{1,0:T(8,128)(2,1)S(1)}, u32[]{:S(2)}, u32[]{:S(2)}) collective-permute-start(bf16[528,256]{1,0:T(8,128)(2,1)} %get-tuple-element.89), channel_id=1, source_target_pairs={{0,1},{1,2},{2,3},{3,0},{4,5},{5,6},{6,7},{7,4},{8,9},{9,10},{10,1... | collective-permute-start | bytes 811016 | tf_op jit(solution)/shard_map/ppermute | solution.py:501
  203.2 14.9 %collective-permute-start.25 = (bf16[528,256]{1,0:T(8,128)(2,1)}, bf16[528,256]{1,0:T(8,128)(2,1)S(1)}, u32[]{:S(2)}, u32[]{:S(2)}) collective-permute-start(bf16[528,256]{1,0:T(8,128)(2,1)} %get-tuple-element.90), channel_id=1, source_target_pairs={{0,3},{1,0},{2,1},{3,2},{4,7},{5,4},{6,5},{7,6},{8,11},{9,8},{10,9... | collective-permute-start | bytes 811016 | tf_op jit(solution)/shard_map/ppermute | solution.py:501
  208.1 18.3 %all-to-all-start.4 = ((bf16[4,256,512]{2,1,0:T(8,128)(2,1)}), bf16[4,256,512]{2,1,0:T(8,128)(2,1)S(1)}, u32[]{:S(2)}, u32[]{:S(2)}) async-start(bf16[4,256,512]{2,1,0:T(8,128)(2,1)} %shard_map.71), calls=%async_computation.4 | async-start | bytes 2097152 | tf_op jit(solution)/shard_map/all_to_all | solution.py:582
  216.5 1.6 copy-start.21
  218.1 0.7 copy-start.22
  226.4 1.0 copy-start.7

commit v7 on v6

--- a/solution.py
+++ b/solution.py
@@ -117,35 +117,42 @@
     )(ids, mine, theirs, *shards, *sums)
 
 
-def project_last_kernel(offset, at_ref, mine_ref, given_ref, keep_ref, came_ref, *refs):
-    shards, heads_ref = refs[:-1], refs[-1]
+def project_last_kernel(offset, carried, at_ref, mine_ref, given_ref, keep_ref, came_ref, cot_ref, *refs):
+    shards, heads_ref = refs[:6], refs[-1 - carried]
     depth, cols = shards[0].shape[-2:]
     band = pl.ds(pl.multiple_of(place_of(at_ref, *offset) * depth, depth), depth)
+    heads = range(heads_ref.shape[0])
     for j in range(3):
         span = slice(j * cols, (j + 1) * cols)
         total = keep_ref[:, span] + came_ref[:, span].astype(F32)
         total += jnp.dot(mine_ref[:, band], shards[j][0], preferred_element_type=F32)
         total += jnp.dot(given_ref[:, band], shards[3 + j][0], preferred_element_type=F32)
-        for h in range(heads_ref.shape[0]):
+        for h in heads:
             heads_ref[h, :, j * HS : (j + 1) * HS] = total[:, h * HS : (h + 1) * HS].astype(BF)
-
-
-def project_last(ids, mine, given, keep, came, pieces, offset, heads):
+    for h in heads:
+        heads_ref[h, :, 3 * HS :] = cot_ref[:, h * HS : (h + 1) * HS]
+
+
+def project_last(ids, mine, given, keep, came, cotangent, pieces, offset, heads, carry):
     rows, cols = keep.shape
+    n = len(carry)
     vmem = pl.BlockSpec(memory_space=pltpu.VMEM)
-    return pl.pallas_call(
-        functools.partial(project_last_kernel, offset),
-        in_specs=[pl.BlockSpec(memory_space=pltpu.SMEM)] + [vmem] * (4 + len(pieces)),
-        out_specs=vmem,
-        out_shape=shape(heads, rows, cols // heads),
-        compiler_params=PARAMS,
-        cost_estimate=cost(1, 1),
-    )(ids, mine, given, keep, came, *pieces)
-
-
-def attention_kernel(q_rows, carried, qkv_ref, dout_ref, *refs):
-    att_ref, grad_ref = refs[-4 - carried : -2 - carried]
-    dk_ref, dv_ref = refs[-2:]
+    free = pl.BlockSpec(memory_space=pl.ANY)
+    return pl.pallas_call(
+        functools.partial(project_last_kernel, offset, n),
+        in_specs=[pl.BlockSpec(memory_space=pltpu.SMEM)]
+        + [vmem] * (5 + len(pieces))
+        + [free] * n,
+        out_specs=(vmem,) + (free,) * n,
+        out_shape=(shape(heads, rows, cols // heads + HS),) + tuple(shape(*c.shape) for c in carry),
+        input_output_aliases={6 + len(pieces) + i: 1 + i for i in range(n)},
+        compiler_params=PARAMS,
+        cost_estimate=cost(1, 1),
+    )(ids, mine, given, keep, came, cotangent, *pieces, *carry)
+
+
+def attention_kernel(q_rows, qkv_ref, *refs):
+    att_ref, grad_ref, dk_ref, dv_ref = refs[-4:]
     scale = 1.0 / math.sqrt(HS)
     key = qkv_ref[:, HS : 2 * HS]
     value = qkv_ref[:, 2 * HS : 3 * HS]
@@ -154,7 +161,7 @@
     for i in range(qkv_ref.shape[0] // q_rows):
         rows = pl.ds(i * q_rows, q_rows)
         query = qkv_ref[rows, 0:HS]
-        dout = dout_ref[rows, :]
+        dout = qkv_ref[rows, 3 * HS :]
         scores = dot(key, query, 1, 1) * (scale * math.log2(math.e))
         top = jnp.max(scores, axis=0, keepdims=True)
         expo = jnp.exp2(scores - top)
@@ -180,20 +187,18 @@
     grad_ref[:, 2 * HS : 3 * HS] = dv_ref[...].astype(BF)
 
 
-def attention(qkv, dout, carry, after):
+def attention(qkv, after):
     n = qkv.shape[0]
     vmem = pl.BlockSpec(memory_space=pltpu.VMEM)
-    free = pl.BlockSpec(memory_space=pl.ANY)
-    return pl.pallas_call(
-        functools.partial(attention_kernel, min(256, n), len(carry)),
-        out_shape=(shape(n, HS), shape(n, 3 * HS)) + tuple(shape(*c.shape) for c in carry),
-        in_specs=[vmem] * 2 + [free] * (len(carry) + len(after)),
-        out_specs=(vmem,) * 2 + (free,) * len(carry),
+    return pl.pallas_call(
+        functools.partial(attention_kernel, min(256, n)),
+        out_shape=(shape(n, HS), shape(n, 3 * HS)),
+        in_specs=[vmem] + [pl.BlockSpec(memory_space=pl.ANY)] * len(after),
+        out_specs=(vmem,) * 2,
         scratch_shapes=[pltpu.VMEM((n, HS), F32), pltpu.VMEM((n, HS), F32)],
-        input_output_aliases={2 + i: 2 + i for i in range(len(carry))},
         compiler_params=PARAMS,
         cost_estimate=cost(BUSY, 1),
-    )(qkv, dout, *carry, *after)
+    )(qkv, *after)
 
 
 def write_stat(ref, at, stat):
@@ -518,13 +523,11 @@
 
     x_left, x_right = shift(pair, "x", 1), shift(pair, "x", -1)
 
-    dout = cotangent.reshape(rows, heads, HS).transpose(1, 0, 2)
-    dout = lax.all_to_all(dout, "x", 0, 0, tiled=True).reshape(n_x * rows, HS)
     near = ((0, 0), (3, 0), (1, 0), (0, 1))
     *sums, stack_0 = project(ids, mine, theirs, (own, left, right, other), near)
     far, other_left, other_right, *pieces = gate(
         (shift(left, "y", 1), shift(left, "zl", 1), shift(other, "y", -1)),
-        (dout, *sums),
+        sums,
         ((0, 0), (1, 1), (2, 2)),
     )
     then = ((2, 0), (3, 1), (1, 1))
@@ -535,16 +538,17 @@
         (shift(pieces[0], "zl", 1), shift(pieces[1], "y", 1), shift(pieces[2], "y", -1), give)
     )
     pieces = (*pieces, *(swap(p) for p in pieces))
-    proj = project_last(ids, mine, given, keep, swap(give), pieces, (2, 1), heads)
-
-    x_left, x_right, far_0, far_1 = gate((x_left, x_right), pieces=((0, 0), (1, 1)))
+    proj, stack_0, stack_1 = project_last(
+        ids, mine, given, keep, swap(give), cotangent.reshape(rows, cols), pieces, (2, 1), heads,
+        (stack_0, stack_1),
+    )
+
+    x_left, x_right, far_0, far_1 = gate((x_left, x_right), (proj,), ((0, 0), (1, 1)))
     far_0, far_1 = shift(far_0, "x", 1), shift(far_1, "x", -1)
     blocks = (pair, x_left, x_right, far_0, far_1)
     spots = ((0, 0, 0, 0), (0, 1, 0, 1), (1, 0, 3, 0), (1, 1, 3, 1), (2, 0, 1, 0), (2, 1, 1, 1), (3, 0, 2, 0), (4, 0, 2, 1))
-    qkv = lax.all_to_all(proj, "x", 0, 0, tiled=True).reshape(n_x * rows, 3 * HS)
-    att, head_grads, stack_0, stack_1 = attention(
-        qkv, dout, (stack_0, stack_1), (far_0, far_1)
-    )
+    qkv = lax.all_to_all(proj, "x", 0, 0, tiled=True).reshape(n_x * rows, 4 * HS)
+    att, head_grads = attention(qkv, (x_left, x_right))
 
     shards = (*pieces, stack_0, swap(stack_0), stack_1, swap(stack_1))
     places = {(2, 1): [[(3 * core + j, (0,)) for j in range(3)] for core in range(2)]}

time: 232 us -> 203 us (0.88)
  blocking collectives: 25.3 us -> 0 us
  local copies, waits for them, and re-layouts: 12.3 us -> 8.79 us
    all_to_all x1 -> x0, blocking collectives: 25.3 us -> none  [per_device(): lax.all_to_all(proj, 'x', 0, 0, tiled=True).reshape(n_x * rows, 3 * HS)]
    ppermute x26, waiting for transfers between devices: 38 us -> 58.4 us  [shift(): return lax.ppermute(x, axis, [(i, (i + by) % n) for i in range(n)])]
    all_to_all x1, waiting for transfers between devices: 26.8 us -> 6.76 us  [per_device(): lax.all_to_all(proj, 'x', 0, 0, tiled=True).reshape(n_x * rows, 4 * HS)]
    unnamed x46 -> x40, local copies, waits for them, and re-layouts: 10.9 us -> 8.18 us
  transfers between devices with their start and end apart: 30 -> 30, of which waited for: 12 -> 16; matrix products, arithmetic and copies ran while one was open for 1% -> 0% of each run, Pallas kernels for 26% -> 34%
where the time goes in v7:
time: 203 us; the launch traced here: 202 us
  Pallas kernels  74.3 us (37%)
  waiting for transfers between devices  69 us (34%)
  starting transfers between devices  49 us (24%)
  local copies, waits for them, and re-layouts  8.79 us (4%)
    ppermute x26, waiting for transfers between devices, shift(): return lax.ppermute(x, axis, [(i, (i + by) % n) for i in range(n)])  58.4 us
    ppermute x26, starting transfers between devices, shift(): return lax.ppermute(x, axis, [(i, (i + by) % n) for i in range(n)])  29.2 us
    pallas_call x2, Pallas kernels, norm_halves(): pl.pallas_call(functools.partial(norm_kernel, width, halves, spots, place...  15.4 us
    pallas_call x2, Pallas kernels, project(): pl.pallas_call(functools.partial(project_kernel, offsets, not sums), in_s...  12.5 us
    pallas_call x1, Pallas kernels, outer(): pl.pallas_call(functools.partial(outer_kernel, tile, spots), in_specs=[pl...  9.34 us
    pallas_call x1, Pallas kernels, attention(): pl.pallas_call(functools.partial(attention_kernel, min(256, n)), out_shap...  8.62 us
    unnamed x40, local copies, waits for them, and re-layouts  8.18 us
    all_to_all x1, starting transfers between devices, per_device(): lax.all_to_all(part, 'y', 0, 0, tiled=True).reshape(n_y, 2, w_rows, 3 * HS)  7.53 us
  transfers between devices with their start and end apart: 30, of which 16 were waited for; matrix products, arithmetic and copies ran while one was open for 0% of the time, Pallas kernels for 34%

profile of v7, /device:TPU:8, one launch (start us, length us, event | category | flops | bytes accessed | tf_op | source)
XLA Modules:
  0.0 202.0 jit_solution(4299843265900844599)
XLA Ops:
  0.7 2.0 collective-permute-start.5
  2.7 0.4 collective-permute-start.4
  3.2 1.6 collective-permute-start.3
  4.8 0.6 stack.23.at_ref
  5.4 5.4 %shard_map.58 = (f32[256,1]{1,0:T(8,128)}, bf16[256,2048]{1,0:T(8,128)(2,1)}, bf16[256,2048]{1,0:T(8,128)(2,1)}, bf16[256,2048]{1,0:T(8,128)(2,1)}, bf16[2,2048,256]{2,1,0:T(8,128)(2,1)}) custom-call(s32[5]{0:T(128)} %stack.23.at_ref, bf16[256,4096]{1,0:T(8,128)(2,1)} %bitcast.27, bf16[256,4096]{1,0:T(8,128)(2,1)} %collective-permute-done.other_ref), custom_call_target="tpu_custom_call" | custom-call | flops 20000000000 | bytes 1 | tf_op jit(solution)/shard_map/pallas_call | solution.py:55
  10.8 10.2 %collective-permute-done.5.refs_2_ = bf16[3,256,512]{2,1,0:T(8,128)(2,1)S(1)} collective-permute-done((bf16[3,256,512]{2,1,0:T(8,128)(2,1)}, bf16[3,256,512]{2,1,0:T(8,128)(2,1)S(1)}, u32[]{:S(2)}, u32[]{:S(2)}) %collective-permute-start.5) | collective-permute-done | bytes 786464 | tf_op jit(solution)/shard_map/ppermute | solution.py:506
  21.1 1.5 collective-permute-done.4.refs_1_
  22.5 1.5 collective-permute-done.3.refs_0_
  24.0 0.9 copy-done.10
  24.9 3.0 %collective-permute-start.8 = (bf16[3,256,512]{2,1,0:T(8,128)(2,1)}, bf16[3,256,512]{2,1,0:T(8,128)(2,1)S(1)}, u32[]{:S(2)}, u32[]{:S(2)}) collective-permute-start(bf16[3,256,512]{2,1,0:T(8,128)(2,1)} %get-tuple-element.54.refs_3_), channel_id=1, source_target_pairs={{0,192},{64,0},{128,64},{192,128},{1,193},{65,1},{129,65},{193,129... | collective-permute-start | bytes 2359304 | tf_op jit(solution)/shard_map/ppermute | solution.py:506
  27.9 0.3 collective-permute-start.7
  28.2 2.8 %collective-permute-start.2 = (bf16[2,2048,256]{2,1,0:T(8,128)(2,1)}, bf16[2,2048,256]{2,1,0:T(8,128)(2,1)}, u32[]{:S(2)}, u32[]{:S(2)}) collective-permute-start(bf16[2,2048,256]{2,1,0:T(8,128)(2,1)} %get-tuple-element.49.refs_3_.refs_0_), channel_id=1, source_target_pairs={{0,12},{4,0},{8,4},{12,8},{1,13},{5,1},{9,5},{13,9},{2,14},{6,2},{... | collective-permute-start | bytes 6291464 | tf_op jit(solution)/shard_map/ppermute | solution.py:506
  31.0 6.4 %shard_map.60 = (f32[256,1536]{1,0:T(8,128)}, f32[256,1536]{1,0:T(8,128)}, bf16[4,3,256,512]{3,2,1,0:T(8,128)(2,1)}) custom-call(s32[5]{0:T(128)} %stack.23.at_ref, bf16[256,2048]{1,0:T(8,128)(2,1)} %get-tuple-element.50.mine_ref, bf16[256,2048]{1,0:T(8,128)(2,1)} %get-tuple-element.52.theirs_ref, bf16[3,256,512]{2,1,0:T(8,128)(2,1)} %bitcast.23, ...), custom_call_target="tpu_custom_call" | custom-call | flops 1 | bytes 1 | tf_op jit(solution)/shard_map/pallas_call | solution.py:105
  37.3 6.9 %collective-permute-done.8.refs_2_ = bf16[3,256,512]{2,1,0:T(8,128)(2,1)S(1)} collective-permute-done((bf16[3,256,512]{2,1,0:T(8,128)(2,1)}, bf16[3,256,512]{2,1,0:T(8,128)(2,1)S(1)}, u32[]{:S(2)}, u32[]{:S(2)}) %collective-permute-start.8) | collective-permute-done | bytes 786464 | tf_op jit(solution)/shard_map/ppermute | solution.py:506
  44.2 2.1 %collective-permute-done.7.refs_1_ = bf16[3,256,512]{2,1,0:T(8,128)(2,1)S(1)} collective-permute-done((bf16[3,256,512]{2,1,0:T(8,128)(2,1)}, bf16[3,256,512]{2,1,0:T(8,128)(2,1)S(1)}, u32[]{:S(2)}, u32[]{:S(2)}) %collective-permute-start.7) | collective-permute-done | bytes 786464 | tf_op jit(solution)/shard_map/ppermute | solution.py:506
  46.5 0.8 copy-done.6
  47.2 0.3 copy-done.7
  47.5 2.0 shard_map.61
  49.5 1.5 collective-permute-start.9
  51.0 0.3 collective-permute-start.10
  51.4 1.7 collective-permute-start.11
  53.1 6.2 %shard_map.62 = (f32[256,1536]{1,0:T(8,128)}, bf16[256,1536]{1,0:T(8,128)(2,1)}, bf16[3,3,256,512]{3,2,1,0:T(8,128)(2,1)}) custom-call(s32[5]{0:T(128)} %stack.23.at_ref, bf16[256,2048]{1,0:T(8,128)(2,1)} %get-tuple-element.50.mine_ref, bf16[256,2048]{1,0:T(8,128)(2,1)} %get-tuple-element.52.theirs_ref, bf16[3,256,512]{2,1,0:T(8,128)(2,1)} %get-tuple-element.58.refs_0_, ...), custom_call_target="tpu_custom_call" | custom-call | flops 1 | bytes 1 | tf_op jit(solution)/shard_map/pallas_call | solution.py:105
  59.3 0.7 copy-done.1
  60.2 0.3 collective-permute-start.12
  60.5 0.5 collective-permute-start.13
  61.1 2.3 %collective-permute-done.13.refs_3_ = bf16[1,256,512]{2,1,0:T(8,128)(2,1)S(1)} collective-permute-done((bf16[1,256,512]{2,1,0:T(8,128)(2,1)}, bf16[1,256,512]{2,1,0:T(8,128)(2,1)S(1)}, u32[]{:S(2)}, u32[]{:S(2)}) %collective-permute-start.13) | collective-permute-done | bytes 262176 | tf_op jit(solution)/shard_map/ppermute | solution.py:506
  63.5 0.2 collective-permute-done.14.refs_4_
  63.7 1.4 collective-permute-done.15.refs_5_
  65.1 0.7 copy-done.13
  65.8 0.3 copy-done.15
  66.0 4.3 %shard_map.64 = (bf16[4,256,512]{2,1,0:T(8,128)(2,1)}, bf16[4,3,256,512]{3,2,1,0:T(8,128)(2,1)}, bf16[3,3,256,512]{3,2,1,0:T(8,128)(2,1)}) custom-call(s32[5]{0:T(128)} %stack.23.at_ref, bf16[256,2048]{1,0:T(8,128)(2,1)} %get-tuple-element.50.mine_ref, ...), custom_call_target="tpu_custom_call", output_to_operand_aliasing={{1}: (12, {}), {2}: (13, {})} | custom-call | flops 1 | bytes 1 | tf_op jit(solution)/shard_map/pallas_call | solution.py:141
  70.4 4.3 %all-to-all-start = ((bf16[4,256,512]{2,1,0:T(8,128)(2,1)}), bf16[4,256,512]{2,1,0:T(8,128)(2,1)}, u32[]{:S(2)}, u32[]{:S(2)}) async-start(bf16[4,256,512]{2,1,0:T(8,128)(2,1)} %get-tuple-element.72.refs_2_.p_ref), calls=%async_computation | async-start | bytes 2097152 | tf_op jit(solution)/shard_map/all_to_all | solution.py:550
  74.9 0.4 collective-permute-start.19
  75.2 3.1 %collective-permute-done.1.refs_0_ = bf16[2,2048,256]{2,1,0:T(8,128)(2,1)} collective-permute-done((bf16[2,2048,256]{2,1,0:T(8,128)(2,1)}, bf16[2,2048,256]{2,1,0:T(8,128)(2,1)}, u32[]{:S(2)}, u32[]{:S(2)}) %collective-permute-start.1) | collective-permute-done | bytes 2097184 | tf_op jit(solution)/shard_map/ppermute | solution.py:506
  78.3 2.9 %shard_map.65 = (bf16[2,2048,256]{2,1,0:T(8,128)(2,1)}, bf16[2,2048,256]{2,1,0:T(8,128)(2,1)}, bf16[1,2048,256]{2,1,0:T(8,128)(2,1)}, bf16[1,2048,256]{2,1,0:T(8,128)(2,1)}) custom-call(bf16[2,2048,256]{2,1,0:T(8,128)(2,1)} %collective-permute-done.1.refs_0_, ...), custom_call_target="tpu_custom_call", output_to_operand_aliasing={{0}: (0, {}), {1}: (1, {})} | custom-call | flops 1 | bytes 1 | tf_op jit(solution)/shard_map/pallas_call | solution.py:491
  81.3 3.2 %collective-permute-start.17 = (bf16[1,2048,256]{2,1,0:T(8,128)(2,1)}, bf16[1,2048,256]{2,1,0:T(8,128)(2,1)}, u32[]{:S(2)}, u32[]{:S(2)}) collective-permute-start(bf16[1,2048,256]{2,1,0:T(8,128)(2,1)} %get-tuple-element.76), channel_id=1, source_target_pairs={{0,12},{4,0},{8,4},{12,8},{1,13},{5,1},{9,5},{13,9},{2,14},{6,2},{... | collective-permute-start | bytes 3145736 | tf_op jit(solution)/shard_map/ppermute | solution.py:506
  84.6 6.8 %all-to-all-done = bf16[4,256,512]{2,1,0:T(8,128)(2,1)} async-done(((bf16[4,256,512]{2,1,0:T(8,128)(2,1)}), bf16[4,256,512]{2,1,0:T(8,128)(2,1)}, u32[]{:S(2)}, u32[]{:S(2)}) %all-to-all-start) | async-done | bytes 1048608 | tf_op jit(solution)/shard_map/all_to_all | solution.py:550
  91.3 8.6 %shard_map.66 = (bf16[1024,128]{1,0:T(8,128)(2,1)}, bf16[1024,384]{1,0:T(8,128)(2,1)}) custom-call(bf16[1024,512]{1,0:T(8,128)(2,1)} %bitcast.8.qkv_ref, bf16[2,2048,256]{2,1,0:T(8,128)(2,1)} %get-tuple-element.73.refs_0_.refs_1_, bf16[2,2048,256]{2,1,0:T(8,128)(2,1)} %get-tuple-element.74.refs_1_.refs_2_), custom_call_target="tpu_custom_call" | custom-call | flops 20000000000 | bytes 1 | tf_op jit(solution)/shard_map/pallas_call | solution.py:193
  100.0 4.4 %all-to-all-start.2 = ((bf16[4,256,384]{2,1,0:T(8,128)(2,1)}), bf16[4,256,384]{2,1,0:T(8,128)(2,1)}, u32[]{:S(2)}, u32[]{:S(2)}) async-start(bf16[4,256,384]{2,1,0:T(8,128)(2,1)} %bitcast.18), calls=%async_computation.2 | async-start | bytes 1572864 | tf_op jit(solution)/shard_map/all_to_all | solution.py:561
  104.4 9.1 %collective-permute-done.16.refs_3_ = bf16[1,2048,256]{2,1,0:T(8,128)(2,1)} collective-permute-done((bf16[1,2048,256]{2,1,0:T(8,128)(2,1)}, bf16[1,2048,256]{2,1,0:T(8,128)(2,1)}, u32[]{:S(2)}, u32[]{:S(2)}) %collective-permute-start.16) | collective-permute-done | bytes 1048608 | tf_op jit(solution)/shard_map/ppermute | solution.py:506
  113.5 9.3 %shard_map.67 = bf16[2048,384]{1,0:T(8,128)(2,1)} custom-call(s32[5]{0:T(128)} %stack.23.at_ref, bf16[2,2048,256]{2,1,0:T(8,128)(2,1)} %get-tuple-element.49.refs_3_.refs_0_, bf16[2,2048,256]{2,1,0:T(8,128)(2,1)} %get-tuple-element.73.refs_0_.refs_1_, bf16[2,2048,256]{2,1,0:T(8,128)(2,1)} %get-tuple-element.74.refs_1_.refs_2_, ...), custom_call_target="tpu_custom_call" | custom-call | flops 1 | bytes 1 | tf_op jit(solution)/shard_map/pallas_call | solution.py:390
  122.8 7.5 %all-to-all-start.1 = ((bf16[4,512,384]{2,1,0:T(8,128)(2,1)}), bf16[4,512,384]{2,1,0:T(8,128)(2,1)}, u32[]{:S(2)}, u32[]{:S(2)}) async-start(bf16[4,512,384]{2,1,0:T(8,128)(2,1)} %bitcast.16), calls=%async_computation.1 | async-start | bytes 3145728 | tf_op jit(solution)/shard_map/all_to_all | solution.py:580
  130.4 1.7 copy-done
  132.0 7.7 %shard_map.68 = (bf16[1040,256]{1,0:T(8,128)(2,1)}, bf16[1024,256]{1,0:T(8,128)(2,1)}, f32[1,256]{1,0:T(1,128)}) custom-call(s32[5]{0:T(128)} %stack.23.at_ref, bf16[4,256,384]{2,1,0:T(8,128)(2,1)} %all-to-all-done.2.g_ref, bf16[4,256,512]{2,1,0:T(8,128)(2,1)} %get-tuple-element.72.refs_2_.p_ref, bf16[1,256,512]{2,1,0:T(8,128)(2,1)} %get-tuple-element.67.refs_0_, ...), custom_call_target="tpu_custom_call" | custom-call | flops 1 | bytes 1 | tf_op jit(solution)/shard_map/pallas_call | solution.py:278
  139.8 3.4 %collective-permute-start.22 = (bf16[1040,256]{1,0:T(8,128)(2,1)}, bf16[1040,256]{1,0:T(8,128)(2,1)S(1)}, u32[]{:S(2)}, u32[]{:S(2)}) collective-permute-start(bf16[1040,256]{1,0:T(8,128)(2,1)} %get-tuple-element.88), channel_id=1, source_target_pairs={{0,1},{1,2},{2,3},{3,0},{4,5},{5,6},{6,7},{7,4},{8,9},{9,10},{10,1... | collective-permute-start | bytes 1597448 | tf_op jit(solution)/shard_map/ppermute | solution.py:506
  143.1 2.2 %collective-permute-start.23 = (bf16[1024,256]{1,0:T(8,128)(2,1)}, bf16[1024,256]{1,0:T(8,128)(2,1)S(1)}, u32[]{:S(2)}, u32[]{:S(2)}) collective-permute-start(bf16[1024,256]{1,0:T(8,128)(2,1)} %get-tuple-element.90), channel_id=1, source_target_pairs={{0,3},{1,0},{2,1},{3,2},{4,7},{5,4},{6,5},{7,6},{8,11},{9,8},{10,9... | collective-permute-start | bytes 1572872 | tf_op jit(solution)/shard_map/ppermute | solution.py:506
  145.3 7.6 %shard_map.69 = (bf16[512,256]{1,0:T(8,128)(2,1)}, bf16[512,256]{1,0:T(8,128)(2,1)}, bf16[512,256]{1,0:T(8,128)(2,1)}, bf16[512,256]{1,0:T(8,128)(2,1)}, f32[1,256]{1,0:T(1,128)}) custom-call(s32[5]{0:T(128)} %stack.23.at_ref, bf16[4,256,384]{2,1,0:T(8,128)(2,1)} %all-to-all-done.2.g_ref, bf16[4,256,512]{2,1,0:T(8,128)(2,1)} %get-tuple-element.72.refs_2_.p_ref, ...), custom_call_target="tpu_custom_call" | custom-call | flops 1 | bytes 1 | tf_op jit(solution)/shard_map/pallas_call | solution.py:278
  153.0 2.3 %shard_map.70 = (f32[256,384]{1,0:T(8,128)}, bf16[256,384]{1,0:T(8,128)(2,1)}) custom-call(s32[5]{0:T(128)} %stack.23.at_ref, bf16[4,2,256,384]{3,2,1,0:T(8,128)(2,1)} %bitcast.11.part_ref, bf16[512,256]{1,0:T(8,128)(2,1)} %get-tuple-element.81.refs_0_.own0), custom_call_target="tpu_custom_call" | custom-call | flops 1 | bytes 1 | tf_op jit(solution)/shard_map/pallas_call | solution.py:417
  155.3 1.0 collective-permute-start.21
  156.2 15.5 %collective-permute-done.21.came_ref.refs_0_ = bf16[256,384]{1,0:T(8,128)(2,1)S(1)} collective-permute-done((bf16[256,384]{1,0:T(8,128)(2,1)}, bf16[256,384]{1,0:T(8,128)(2,1)S(1)}, u32[]{:S(2)}, u32[]{:S(2)}) %collective-permute-start.21) | collective-permute-done | bytes 196640 | tf_op jit(solution)/shard_map/ppermute | solution.py:506
  171.8 0.7 copy-done.16
  172.6 0.2 copy-done.14
  172.8 2.2 %shard_map.73 = (bf16[528,256]{1,0:T(8,128)(2,1)}, bf16[528,256]{1,0:T(8,128)(2,1)}) custom-call(bf16[512,256]{1,0:T(8,128)(2,1)} %get-tuple-element.87.up_part, bf16[1040,256]{1,0:T(8,128)(2,1)} %copy-done.14, bf16[1040,256]{1,0:T(8,128)(2,1)} %copy-done.14, bf16[512,256]{1,0:T(8,128)(2,1)} %get-tuple-element.89.down_part, bf16[1024,256]{1,0:T(8,128)(2,1)} %copy-done.17, ...), custom_call_target="tpu_custom_call" | custom-call | flops 1 | bytes 1 | tf_op jit(solution)/shard_map/pallas_call | solution.py:308
  175.0 1.5 collective-permute-start.24
  176.5 2.7 %collective-permute-start.25 = (bf16[528,256]{1,0:T(8,128)(2,1)}, bf16[528,256]{1,0:T(8,128)(2,1)S(1)}, u32[]{:S(2)}, u32[]{:S(2)}) collective-permute-start(bf16[528,256]{1,0:T(8,128)(2,1)} %get-tuple-element.92), channel_id=1, source_target_pairs={{0,3},{1,0},{2,1},{3,2},{4,7},{5,4},{6,5},{7,6},{8,11},{9,8},{10,9... | collective-permute-start | bytes 811016 | tf_op jit(solution)/shard_map/ppermute | solution.py:506
  179.2 2.2 %shard_map.71 = bf16[4,256,512]{2,1,0:T(8,128)(2,1)} custom-call(f32[256,384]{1,0:T(8,128)} %get-tuple-element.82.keep_ref, bf16[256,384]{1,0:T(8,128)(2,1)} %copy-done.16, bf16[4,256,128]{2,1,0:T(8,128)(2,1)} %bitcast.25), custom_call_target="tpu_custom_call" | custom-call | flops 1 | bytes 1 | tf_op jit(solution)/shard_map/pallas_call | solution.py:441
  181.4 3.5 %all-to-all-start.3 = ((bf16[4,256,512]{2,1,0:T(8,128)(2,1)}), bf16[4,256,512]{2,1,0:T(8,128)(2,1)S(1)}, u32[]{:S(2)}, u32[]{:S(2)}) async-start(bf16[4,256,512]{2,1,0:T(8,128)(2,1)} %shard_map.71), calls=%async_computation.3 | async-start | bytes 2097152 | tf_op jit(solution)/shard_map/all_to_all | solution.py:586
  184.9 3.3 %collective-permute-done.24.up0 = bf16[528,256]{1,0:T(8,128)(2,1)S(1)} collective-permute-done((bf16[528,256]{1,0:T(8,128)(2,1)}, bf16[528,256]{1,0:T(8,128)(2,1)S(1)}, u32[]{:S(2)}, u32[]{:S(2)}) %collective-permute-start.24) | collective-permute-done | bytes 270368 | tf_op jit(solution)/shard_map/ppermute | solution.py:506
  188.3 1.2 collective-permute-done.25.down1
  189.4 0.7 copy-done.19
  190.2 3.5 %shard_map.74 = bf16[256,1024]{1,0:T(8,128)(2,1)} custom-call(s32[5]{0:T(128)} %stack.23.at_ref, bf16[512,256]{1,0:T(8,128)(2,1)} %get-tuple-element.81.refs_0_.own0, bf16[512,256]{1,0:T(8,128)(2,1)} %get-tuple-element.86.own1, bf16[528,256]{1,0:T(8,128)(2,1)} %copy-done.18, bf16[1040,256]{1,0:T(8,128)(2,1)} %copy-done.14, bf16[1024,256]{1,0:T(8,128)(2,1)} %copy-done.17, ...), custom_call_target="tpu_custom_call" | custom-call | flops 20000000000 | bytes 1 | tf_op jit(solution)/shard_map/pallas_call | solution.py:342
  193.6 3.8 %all-to-all-done.3.in_ref = bf16[4,256,512]{2,1,0:T(8,128)(2,1)S(1)} async-done(((bf16[4,256,512]{2,1,0:T(8,128)(2,1)}), bf16[4,256,512]{2,1,0:T(8,128)(2,1)S(1)}, u32[]{:S(2)}, u32[]{:S(2)}) %all-to-all-start.3) | async-done | bytes 1048608 | tf_op jit(solution)/shard_map/all_to_all | solution.py:586
  197.4 1.0 copy-done.4
  198.4 3.5 %shard_map.72 = (f32[3,256,512]{2,1,0:T(8,128)}, bf16[256,512]{1,0:T(8,128)(2,1)}) custom-call(bf16[4,256,512]{2,1,0:T(8,128)(2,1)} %copy-done.4), custom_call_target="tpu_custom_call" | custom-call | flops 1 | bytes 1 | tf_op jit(solution)/shard_map/pallas_call | solution.py:462
  (54 shorter events, 1.2 us)
Async XLA Ops:
  0.6 4.7 %collective-permute-start = (bf16[256,4096]{1,0:T(8,128)(2,1)}, bf16[256,4096]{1,0:T(8,128)(2,1)}, u32[]{:S(2)}, u32[]{:S(2)}) collective-permute-start(bf16[256,4096]{1,0:T(8,128)(2,1)} %bitcast.26), channel_id=1, source_target_pairs={{0,16},{16,0},{1,17},{17,1},{2,18},{18,2},{3,19},{19,3},{4,20},{20... | collective-permute-start | bytes 6291464 | tf_op jit(solution)/shard_map/ppermute | solution.py:506
  0.7 20.3 %collective-permute-start.5 = (bf16[3,256,512]{2,1,0:T(8,128)(2,1)}, bf16[3,256,512]{2,1,0:T(8,128)(2,1)S(1)}, u32[]{:S(2)}, u32[]{:S(2)}) collective-permute-start(bf16[3,256,512]{2,1,0:T(8,128)(2,1)} %bitcast.20), channel_id=1, source_target_pairs={{0,32},{32,0},{1,33},{33,1},{2,34},{34,2},{3,35},{35,3},{4,36},{36... | collective-permute-start | bytes 2359304 | tf_op jit(solution)/shard_map/ppermute | solution.py:506
  2.7 19.8 %collective-permute-start.4 = (bf16[3,256,512]{2,1,0:T(8,128)(2,1)}, bf16[3,256,512]{2,1,0:T(8,128)(2,1)S(1)}, u32[]{:S(2)}, u32[]{:S(2)}) collective-permute-start(bf16[3,256,512]{2,1,0:T(8,128)(2,1)} %bitcast.21), channel_id=1, source_target_pairs={{0,192},{64,0},{128,64},{192,128},{1,193},{65,1},{129,65},{193,129... | collective-permute-start | bytes 2359304 | tf_op jit(solution)/shard_map/ppermute | solution.py:506
  3.2 20.8 %collective-permute-start.3 = (bf16[3,256,512]{2,1,0:T(8,128)(2,1)}, bf16[3,256,512]{2,1,0:T(8,128)(2,1)S(1)}, u32[]{:S(2)}, u32[]{:S(2)}) collective-permute-start(bf16[3,256,512]{2,1,0:T(8,128)(2,1)} %bitcast.22), channel_id=1, source_target_pairs={{0,64},{64,128},{128,192},{192,0},{1,65},{65,129},{129,193},{193,1... | collective-permute-start | bytes 2359304 | tf_op jit(solution)/shard_map/ppermute | solution.py:506
  21.1 3.0 %copy-start.8 = (bf16[3,256,512]{2,1,0:T(8,128)(2,1)}, bf16[3,256,512]{2,1,0:T(8,128)(2,1)S(1)}, u32[]{:S(2)}) copy-start(bf16[3,256,512]{2,1,0:T(8,128)(2,1)S(1)} %collective-permute-done.5.refs_2_) | copy-start | bytes 2359300
  22.5 1.5 copy-start.9
  24.0 0.9 copy-start.10
  24.9 19.3 %collective-permute-start.8 = (bf16[3,256,512]{2,1,0:T(8,128)(2,1)}, bf16[3,256,512]{2,1,0:T(8,128)(2,1)S(1)}, u32[]{:S(2)}, u32[]{:S(2)}) collective-permute-start(bf16[3,256,512]{2,1,0:T(8,128)(2,1)} %get-tuple-element.54.refs_3_), channel_id=1, source_target_pairs={{0,192},{64,0},{128,64},{192,128},{1,193},{65,1},{129,65},{193,129... | collective-permute-start | bytes 2359304 | tf_op jit(solution)/shard_map/ppermute | solution.py:506
  27.9 18.4 %collective-permute-start.7 = (bf16[3,256,512]{2,1,0:T(8,128)(2,1)}, bf16[3,256,512]{2,1,0:T(8,128)(2,1)S(1)}, u32[]{:S(2)}, u32[]{:S(2)}) collective-permute-start(bf16[3,256,512]{2,1,0:T(8,128)(2,1)} %get-tuple-element.53.refs_1_), channel_id=1, source_target_pairs={{0,32},{32,0},{1,33},{33,1},{2,34},{34,2},{3,35},{35,3},{4,36},{36... | collective-permute-start | bytes 2359304 | tf_op jit(solution)/shard_map/ppermute | solution.py:506
  28.2 18.3 %collective-permute-start.6 = (bf16[3,256,512]{2,1,0:T(8,128)(2,1)}, bf16[3,256,512]{2,1,0:T(8,128)(2,1)S(1)}, u32[]{:S(2)}, u32[]{:S(2)}) collective-permute-start(bf16[3,256,512]{2,1,0:T(8,128)(2,1)} %get-tuple-element.53.refs_1_), channel_id=1, source_target_pairs={{0,64},{64,128},{128,192},{192,0},{1,65},{65,129},{129,193},{193,1... | collective-permute-start | bytes 2359304 | tf_op jit(solution)/shard_map/ppermute | solution.py:506
  28.2 47.0 %collective-permute-start.2 = (bf16[2,2048,256]{2,1,0:T(8,128)(2,1)}, bf16[2,2048,256]{2,1,0:T(8,128)(2,1)}, u32[]{:S(2)}, u32[]{:S(2)}) collective-permute-start(bf16[2,2048,256]{2,1,0:T(8,128)(2,1)} %get-tuple-element.49.refs_3_.refs_0_), channel_id=1, source_target_pairs={{0,12},{4,0},{8,4},{12,8},{1,13},{5,1},{9,5},{13,9},{2,14},{6,2},{... | collective-permute-start | bytes 6291464 | tf_op jit(solution)/shard_map/ppermute | solution.py:506
  30.9 47.4 %collective-permute-start.1 = (bf16[2,2048,256]{2,1,0:T(8,128)(2,1)}, bf16[2,2048,256]{2,1,0:T(8,128)(2,1)}, u32[]{:S(2)}, u32[]{:S(2)}) collective-permute-start(bf16[2,2048,256]{2,1,0:T(8,128)(2,1)} %get-tuple-element.49.refs_3_.refs_0_), channel_id=1, source_target_pairs={{0,4},{4,8},{8,12},{12,0},{1,5},{5,9},{9,13},{13,1},{2,6},{6,10},{... | collective-permute-start | bytes 6291464 | tf_op jit(solution)/shard_map/ppermute | solution.py:506
  44.2 2.3 %copy-start.5 = (bf16[3,256,512]{2,1,0:T(8,128)(2,1)}, bf16[3,256,512]{2,1,0:T(8,128)(2,1)S(1)}, u32[]{:S(2)}) copy-start(bf16[3,256,512]{2,1,0:T(8,128)(2,1)S(1)} %collective-permute-done.8.refs_2_) | copy-start | bytes 2359300
  46.3 0.9 copy-start.6
  46.5 1.1 copy-start.7
  49.5 9.8 %collective-permute-start.9 = (bf16[1,256,512]{2,1,0:T(8,128)(2,1)}, bf16[1,256,512]{2,1,0:T(8,128)(2,1)S(1)}, u32[]{:S(2)}, u32[]{:S(2)}) collective-permute-start(bf16[1,256,512]{2,1,0:T(8,128)(2,1)} %get-tuple-element.62), channel_id=1, source_target_pairs={{0,32},{32,0},{1,33},{33,1},{2,34},{34,2},{3,35},{35,3},{4,36},{36... | collective-permute-start | bytes 786440 | tf_op jit(solution)/shard_map/ppermute | solution.py:506
  51.0 8.3 %collective-permute-start.10 = (bf16[1,256,512]{2,1,0:T(8,128)(2,1)}, bf16[1,256,512]{2,1,0:T(8,128)(2,1)S(1)}, u32[]{:S(2)}, u32[]{:S(2)}) collective-permute-start(bf16[1,256,512]{2,1,0:T(8,128)(2,1)} %get-tuple-element.63), channel_id=1, source_target_pairs={{0,64},{64,128},{128,192},{192,0},{1,65},{65,129},{129,193},{193,1... | collective-permute-start | bytes 786440 | tf_op jit(solution)/shard_map/ppermute | solution.py:506
  51.4 8.0 %collective-permute-start.11 = (bf16[1,256,512]{2,1,0:T(8,128)(2,1)}, bf16[1,256,512]{2,1,0:T(8,128)(2,1)S(1)}, u32[]{:S(2)}, u32[]{:S(2)}) collective-permute-start(bf16[1,256,512]{2,1,0:T(8,128)(2,1)} %get-tuple-element.64), channel_id=1, source_target_pairs={{0,192},{64,0},{128,64},{192,128},{1,193},{65,1},{129,65},{193,129... | collective-permute-start | bytes 786440 | tf_op jit(solution)/shard_map/ppermute | solution.py:506
  59.3 0.7 copy-start.1
  59.3 0.8 copy-start.2
  59.3 0.8 copy-start.3
  60.2 4.9 %collective-permute-start.12 = (bf16[256,1536]{1,0:T(8,128)(2,1)}, bf16[256,1536]{1,0:T(8,128)(2,1)S(1)}, u32[]{:S(2)}, u32[]{:S(2)}) collective-permute-start(bf16[256,1536]{1,0:T(8,128)(2,1)} %get-tuple-element.66), channel_id=1, source_target_pairs={{0,16},{16,0},{1,17},{17,1},{2,18},{18,2},{3,19},{19,3},{4,20},{20... | collective-permute-start | bytes 2359304 | tf_op jit(solution)/shard_map/ppermute | solution.py:506
  60.5 2.9 %collective-permute-start.13 = (bf16[1,256,512]{2,1,0:T(8,128)(2,1)}, bf16[1,256,512]{2,1,0:T(8,128)(2,1)S(1)}, u32[]{:S(2)}, u32[]{:S(2)}) collective-permute-start(bf16[1,256,512]{2,1,0:T(8,128)(2,1)} %get-tuple-element.67.refs_0_), channel_id=1, source_target_pairs={{0,16},{16,0},{1,17},{17,1},{2,18},{18,2},{3,19},{19,3},{4,20},{20... | collective-permute-start | bytes 786440 | tf_op jit(solution)/shard_map/ppermute | solution.py:506
  61.0 2.7 %collective-permute-start.14 = (bf16[1,256,512]{2,1,0:T(8,128)(2,1)}, bf16[1,256,512]{2,1,0:T(8,128)(2,1)S(1)}, u32[]{:S(2)}, u32[]{:S(2)}) collective-permute-start(bf16[1,256,512]{2,1,0:T(8,128)(2,1)} %get-tuple-element.68.refs_1_), channel_id=1, source_target_pairs={{0,16},{16,0},{1,17},{17,1},{2,18},{18,2},{3,19},{19,3},{4,20},{20... | collective-permute-start | bytes 786440 | tf_op jit(solution)/shard_map/ppermute | solution.py:506
  63.3 1.8 copy-start.11
  63.3 1.7 collective-permute-start.15
  63.7 1.4 copy-start.12
  65.1 0.7 copy-start.13
  65.1 1.0 copy-start.15
  70.4 20.9 %all-to-all-start = ((bf16[4,256,512]{2,1,0:T(8,128)(2,1)}), bf16[4,256,512]{2,1,0:T(8,128)(2,1)}, u32[]{:S(2)}, u32[]{:S(2)}) async-start(bf16[4,256,512]{2,1,0:T(8,128)(2,1)} %get-tuple-element.72.refs_2_.p_ref), calls=%async_computation | async-start | bytes 2097152 | tf_op jit(solution)/shard_map/all_to_all | solution.py:550
  74.7 55.7 %collective-permute-start.20 = (bf16[3,3,256,512]{3,2,1,0:T(8,128)(2,1)}, bf16[3,3,256,512]{3,2,1,0:T(8,128)(2,1)}, u32[]{:S(2)}, u32[]{:S(2)}) collective-permute-start(bf16[3,3,256,512]{3,2,1,0:T(8,128)(2,1)} %get-tuple-element.79.refs_8_), channel_id=1, source_target_pairs={{0,16},{16,0},{1,17},{17,1},{2,18},{18,2},{3,19},{19,3},{4,20},{20... | collective-permute-start | bytes 7077896 | tf_op jit(solution)/shard_map/ppermute | solution.py:506
  74.9 55.5 %collective-permute-start.19 = (bf16[4,3,256,512]{3,2,1,0:T(8,128)(2,1)}, bf16[4,3,256,512]{3,2,1,0:T(8,128)(2,1)S(1)}, u32[]{:S(2)}, u32[]{:S(2)}) collective-permute-start(bf16[4,3,256,512]{3,2,1,0:T(8,128)(2,1)} %get-tuple-element.78.refs_6_), channel_id=1, source_target_pairs={{0,16},{16,0},{1,17},{17,1},{2,18},{18,2},{3,19},{19,3},{4,20},{20... | collective-permute-start | bytes 9437192 | tf_op jit(solution)/shard_map/ppermute | solution.py:506
  81.3 32.2 %collective-permute-start.16 = (bf16[1,2048,256]{2,1,0:T(8,128)(2,1)}, bf16[1,2048,256]{2,1,0:T(8,128)(2,1)}, u32[]{:S(2)}, u32[]{:S(2)}) collective-permute-start(bf16[1,2048,256]{2,1,0:T(8,128)(2,1)} %get-tuple-element.75), channel_id=1, source_target_pairs={{0,4},{4,8},{8,12},{12,0},{1,5},{5,9},{9,13},{13,1},{2,6},{6,10},{... | collective-permute-start | bytes 3145736 | tf_op jit(solution)/shard_map/ppermute | solution.py:506
  81.3 32.1 %collective-permute-start.17 = (bf16[1,2048,256]{2,1,0:T(8,128)(2,1)}, bf16[1,2048,256]{2,1,0:T(8,128)(2,1)}, u32[]{:S(2)}, u32[]{:S(2)}) collective-permute-start(bf16[1,2048,256]{2,1,0:T(8,128)(2,1)} %get-tuple-element.76), channel_id=1, source_target_pairs={{0,12},{4,0},{8,4},{12,8},{1,13},{5,1},{9,5},{13,9},{2,14},{6,2},{... | collective-permute-start | bytes 3145736 | tf_op jit(solution)/shard_map/ppermute | solution.py:506
  100.0 13.5 %collective-permute-start.18 = (bf16[4,256,384]{2,1,0:T(8,128)(2,1)}, bf16[4,256,384]{2,1,0:T(8,128)(2,1)}, u32[]{:S(2)}, u32[]{:S(2)}) collective-permute-start(bf16[4,256,384]{2,1,0:T(8,128)(2,1)} %bitcast.17), channel_id=1, source_target_pairs={{0,16},{16,0},{1,17},{17,1},{2,18},{18,2},{3,19},{19,3},{4,20},{20... | collective-permute-start | bytes 2359304 | tf_op jit(solution)/shard_map/ppermute | solution.py:506
  100.0 22.9 %all-to-all-start.2 = ((bf16[4,256,384]{2,1,0:T(8,128)(2,1)}), bf16[4,256,384]{2,1,0:T(8,128)(2,1)}, u32[]{:S(2)}, u32[]{:S(2)}) async-start(bf16[4,256,384]{2,1,0:T(8,128)(2,1)} %bitcast.18), calls=%async_computation.2 | async-start | bytes 1572864 | tf_op jit(solution)/shard_map/all_to_all | solution.py:561
  122.8 30.1 %all-to-all-start.1 = ((bf16[4,512,384]{2,1,0:T(8,128)(2,1)}), bf16[4,512,384]{2,1,0:T(8,128)(2,1)}, u32[]{:S(2)}, u32[]{:S(2)}) async-start(bf16[4,512,384]{2,1,0:T(8,128)(2,1)} %bitcast.16), calls=%async_computation.1 | async-start | bytes 3145728 | tf_op jit(solution)/shard_map/all_to_all | solution.py:580
  130.4 1.7 copy-start
  139.8 32.0 %collective-permute-start.22 = (bf16[1040,256]{1,0:T(8,128)(2,1)}, bf16[1040,256]{1,0:T(8,128)(2,1)S(1)}, u32[]{:S(2)}, u32[]{:S(2)}) collective-permute-start(bf16[1040,256]{1,0:T(8,128)(2,1)} %get-tuple-element.88), channel_id=1, source_target_pairs={{0,1},{1,2},{2,3},{3,0},{4,5},{5,6},{6,7},{7,4},{8,9},{9,10},{10,1... | collective-permute-start | bytes 1597448 | tf_op jit(solution)/shard_map/ppermute | solution.py:506
  143.1 28.6 %collective-permute-start.23 = (bf16[1024,256]{1,0:T(8,128)(2,1)}, bf16[1024,256]{1,0:T(8,128)(2,1)S(1)}, u32[]{:S(2)}, u32[]{:S(2)}) collective-permute-start(bf16[1024,256]{1,0:T(8,128)(2,1)} %get-tuple-element.90), channel_id=1, source_target_pairs={{0,3},{1,0},{2,1},{3,2},{4,7},{5,4},{6,5},{7,6},{8,11},{9,8},{10,9... | collective-permute-start | bytes 1572872 | tf_op jit(solution)/shard_map/ppermute | solution.py:506
  155.3 16.5 %collective-permute-start.21 = (bf16[256,384]{1,0:T(8,128)(2,1)}, bf16[256,384]{1,0:T(8,128)(2,1)S(1)}, u32[]{:S(2)}, u32[]{:S(2)}) collective-permute-start(bf16[256,384]{1,0:T(8,128)(2,1)} %get-tuple-element.83), channel_id=1, source_target_pairs={{0,32},{32,0},{1,33},{33,1},{2,34},{34,2},{3,35},{35,3},{4,36},{36... | collective-permute-start | bytes 589832 | tf_op jit(solution)/shard_map/ppermute | solution.py:506
  171.7 0.7 copy-start.16
  171.7 0.8 copy-start.17
  171.7 1.0 copy-start.14
  175.0 13.2 %collective-permute-start.24 = (bf16[528,256]{1,0:T(8,128)(2,1)}, bf16[528,256]{1,0:T(8,128)(2,1)S(1)}, u32[]{:S(2)}, u32[]{:S(2)}) collective-permute-start(bf16[528,256]{1,0:T(8,128)(2,1)} %get-tuple-element.91), channel_id=1, source_target_pairs={{0,1},{1,2},{2,3},{3,0},{4,5},{5,6},{6,7},{7,4},{8,9},{9,10},{10,1... | collective-permute-start | bytes 811016 | tf_op jit(solution)/shard_map/ppermute | solution.py:506
  176.5 12.9 %collective-permute-start.25 = (bf16[528,256]{1,0:T(8,128)(2,1)}, bf16[528,256]{1,0:T(8,128)(2,1)S(1)}, u32[]{:S(2)}, u32[]{:S(2)}) collective-permute-start(bf16[528,256]{1,0:T(8,128)(2,1)} %get-tuple-element.92), channel_id=1, source_target_pairs={{0,3},{1,0},{2,1},{3,2},{4,7},{5,4},{6,5},{7,6},{8,11},{9,8},{10,9... | collective-permute-start | bytes 811016 | tf_op jit(solution)/shard_map/ppermute | solution.py:506
  181.4 16.0 %all-to-all-start.3 = ((bf16[4,256,512]{2,1,0:T(8,128)(2,1)}), bf16[4,256,512]{2,1,0:T(8,128)(2,1)S(1)}, u32[]{:S(2)}, u32[]{:S(2)}) async-start(bf16[4,256,512]{2,1,0:T(8,128)(2,1)} %shard_map.71), calls=%async_computation.3 | async-start | bytes 2097152 | tf_op jit(solution)/shard_map/all_to_all | solution.py:586
  188.3 1.2 copy-start.18
  189.4 0.7 copy-start.19
  197.4 1.0 copy-start.4

commit v8 on v7

--- a/solution.py
+++ b/solution.py
@@ -15,6 +15,7 @@
 BUSY = 2 * 10**10
 F32 = jnp.float32
 PARAMS = pltpu.CompilerParams(vmem_limit_bytes=60 * 1024 * 1024)
+SMALL = pltpu.CompilerParams(vmem_limit_bytes=24 * 1024 * 1024)
 
 
 def dot(a, b, ca, cb):
@@ -118,7 +119,14 @@
 
 
 def project_last_kernel(offset, carried, at_ref, mine_ref, given_ref, keep_ref, came_ref, cot_ref, *refs):
-    shards, heads_ref = refs[:6], refs[-1 - carried]
+    shards, x_refs = refs[:6], refs[6:8]
+    heads_ref, *cuts, sems = refs[-4 - carried : -1 - carried] + refs[-1:]
+    copies = [
+        pltpu.make_async_copy(ref.at[pl.ds(i, 1)], cut, sems.at[i])
+        for i, (ref, cut) in enumerate(zip(x_refs, cuts))
+    ]
+    for copy in copies:
+        copy.start()
     depth, cols = shards[0].shape[-2:]
     band = pl.ds(pl.multiple_of(place_of(at_ref, *offset) * depth, depth), depth)
     heads = range(heads_ref.shape[0])
@@ -131,9 +139,11 @@
             heads_ref[h, :, j * HS : (j + 1) * HS] = total[:, h * HS : (h + 1) * HS].astype(BF)
     for h in heads:
         heads_ref[h, :, 3 * HS :] = cot_ref[:, h * HS : (h + 1) * HS]
-
-
-def project_last(ids, mine, given, keep, came, cotangent, pieces, offset, heads, carry):
+    for copy in copies:
+        copy.wait()
+
+
+def project_last(ids, mine, given, keep, came, cotangent, pieces, offset, heads, cut, carry):
     rows, cols = keep.shape
     n = len(carry)
     vmem = pl.BlockSpec(memory_space=pltpu.VMEM)
@@ -142,13 +152,16 @@
         functools.partial(project_last_kernel, offset, n),
         in_specs=[pl.BlockSpec(memory_space=pltpu.SMEM)]
         + [vmem] * (5 + len(pieces))
-        + [free] * n,
-        out_specs=(vmem,) + (free,) * n,
-        out_shape=(shape(heads, rows, cols // heads + HS),) + tuple(shape(*c.shape) for c in carry),
-        input_output_aliases={6 + len(pieces) + i: 1 + i for i in range(n)},
-        compiler_params=PARAMS,
-        cost_estimate=cost(1, 1),
-    )(ids, mine, given, keep, came, cotangent, *pieces, *carry)
+        + [free] * (2 + n),
+        out_specs=(vmem,) * 3 + (free,) * n,
+        out_shape=(shape(heads, rows, cols // heads + HS),)
+        + tuple(shape(1, *c.shape[1:]) for c in cut)
+        + tuple(shape(*c.shape) for c in carry),
+        scratch_shapes=[pltpu.SemaphoreType.DMA((2,))],
+        input_output_aliases={8 + len(pieces) + i: 3 + i for i in range(n)},
+        compiler_params=PARAMS,
+        cost_estimate=cost(1, 1),
+    )(ids, mine, given, keep, came, cotangent, *pieces, *cut, *carry)
 
 
 def attention_kernel(q_rows, qkv_ref, *refs):
@@ -357,7 +370,9 @@
 
 
 def outer_kernel(tile, spots, at_ref, *refs):
-    arrays, (mine_ref, other_ref, out_ref, a_ref, g_ref, sems) = refs[:-6], refs[-6:]
+    out_ref, a_ref, g_ref, sems = refs[-4:]
+    m = max(spot[0] for spot in spots) + 1
+    arrays, (mine_ref, other_ref) = refs[:m], refs[m : m + 2]
     n, rows, _ = mine_ref.shape
     depth = a_ref.shape[0]
     copies = []
@@ -381,7 +396,7 @@
         ).astype(BF)
 
 
-def outer(ids, arrays, spots, mine, other):
+def outer(ids, arrays, spots, mine, other, after):
     _, depth, rows = arrays[0].shape
     cols = mine.shape[2]
     n = len(spots)
@@ -391,7 +406,8 @@
         functools.partial(outer_kernel, tile, spots),
         in_specs=[pl.BlockSpec(memory_space=pltpu.SMEM)]
         + [pl.BlockSpec(memory_space=pl.ANY)] * len(arrays)
-        + [vmem, vmem],
+        + [vmem, vmem]
+        + [pl.BlockSpec(memory_space=pl.ANY)] * len(after),
         out_specs=vmem,
         out_shape=shape(depth, cols),
         scratch_shapes=[
@@ -401,7 +417,7 @@
         ],
         compiler_params=PARAMS,
         cost_estimate=cost(1, 1),
-    )(ids, *arrays, mine, other)
+    )(ids, *arrays, mine, other, *after)
 
 
 def split_kernel(at_ref, part_ref, *refs):
@@ -468,7 +484,7 @@
             pl.BlockSpec((tile, heads * HS), lambda i: (i, 0)),
         ),
         out_shape=(shape(3, rows, heads * HS, dtype=F32), shape(rows, heads * HS)),
-        compiler_params=PARAMS,
+        compiler_params=SMALL,
         cost_estimate=cost(1, 1),
     )(last)
 
@@ -538,17 +554,16 @@
         (shift(pieces[0], "zl", 1), shift(pieces[1], "y", 1), shift(pieces[2], "y", -1), give)
     )
     pieces = (*pieces, *(swap(p) for p in pieces))
-    proj, stack_0, stack_1 = project_last(
+    proj, far_0, far_1, stack_0, stack_1 = project_last(
         ids, mine, given, keep, swap(give), cotangent.reshape(rows, cols), pieces, (2, 1), heads,
-        (stack_0, stack_1),
-    )
-
-    x_left, x_right, far_0, far_1 = gate((x_left, x_right), (proj,), ((0, 0), (1, 1)))
+        (x_left, x_right), (stack_0, stack_1),
+    )
+
     far_0, far_1 = shift(far_0, "x", 1), shift(far_1, "x", -1)
     blocks = (pair, x_left, x_right, far_0, far_1)
     spots = ((0, 0, 0, 0), (0, 1, 0, 1), (1, 0, 3, 0), (1, 1, 3, 1), (2, 0, 1, 0), (2, 1, 1, 1), (3, 0, 2, 0), (4, 0, 2, 1))
     qkv = lax.all_to_all(proj, "x", 0, 0, tiled=True).reshape(n_x * rows, 4 * HS)
-    att, head_grads = attention(qkv, (x_left, x_right))
+    att, head_grads = attention(qkv, ())
 
     shards = (*pieces, stack_0, swap(stack_0), stack_1, swap(stack_1))
     places = {(2, 1): [[(3 * core + j, (0,)) for j in range(3)] for core in range(2)]}
@@ -559,7 +574,7 @@
 
     head_grads = head_grads.reshape(n_x, rows, 3 * HS)
     grads = lax.all_to_all(head_grads, "x", 0, 0, tiled=True)
-    part = outer(ids, blocks, spots, head_grads, swap(head_grads))
+    part = outer(ids, blocks, spots, head_grads, swap(head_grads), (shards[7], shards[9]))
 
     up, down, stat = norm_halves(
         ids, grads, proj, shards, places,

time: 203 us -> 201 us (level)
  Pallas kernels: 74.3 us -> 71.5 us
  waiting for transfers between devices: 69 us -> 71.6 us
    all_to_all x1, waiting for transfers between devices: 6.76 us -> 13.1 us  [per_device(): lax.all_to_all(proj, 'x', 0, 0, tiled=True).reshape(n_x * rows, 4 * HS)]
    ppermute x26, waiting for transfers between devices: 58.4 us -> 54.8 us  [shift(): return lax.ppermute(x, axis, [(i, (i + by) % n) for i in range(n)])]
    pallas_call x4 -> x3, Pallas kernels: 4.91 us -> 2.03 us  [gate(): pl.pallas_call(kernel, in_specs=[free] * m, out_specs=(free,) * n + (pl.B...]
    unnamed x40 -> x36, local copies, waits for them, and re-layouts: 8.18 us -> 6.66 us
  transfers between devices with their start and end apart: 30 -> 30, of which waited for: 16 -> 17; matrix products, arithmetic and copies ran while one was open for 0% -> 0% of each run, Pallas kernels for 34% -> 31%
where the time goes in v8:
time: 201 us; the launch traced here: 200 us
  waiting for transfers between devices  71.6 us (36%)
  Pallas kernels  71.5 us (36%)
  starting transfers between devices  48.6 us (24%)
  local copies, waits for them, and re-layouts  7.27 us (4%)
    ppermute x26, waiting for transfers between devices, shift(): return lax.ppermute(x, axis, [(i, (i + by) % n) for i in range(n)])  54.8 us
    ppermute x26, starting transfers between devices, shift(): return lax.ppermute(x, axis, [(i, (i + by) % n) for i in range(n)])  29.7 us
    pallas_call x2, Pallas kernels, norm_halves(): pl.pallas_call(functools.partial(norm_kernel, width, halves, spots, place...  15.4 us
    all_to_all x1, waiting for transfers between devices, per_device(): lax.all_to_all(proj, 'x', 0, 0, tiled=True).reshape(n_x * rows, 4 * HS)  13.1 us
    pallas_call x2, Pallas kernels, project(): pl.pallas_call(functools.partial(project_kernel, offsets, not sums), in_s...  12.5 us
    pallas_call x1, Pallas kernels, outer(): pl.pallas_call(functools.partial(outer_kernel, tile, spots), in_specs=[pl...  9.34 us
    pallas_call x1, Pallas kernels, attention(): pl.pallas_call(functools.partial(attention_kernel, min(256, n)), out_shap...  8.68 us
    all_to_all x1, starting transfers between devices, per_device(): lax.all_to_all(part, 'y', 0, 0, tiled=True).reshape(n_y, 2, w_rows, 3 * HS)  6.77 us
  transfers between devices with their start and end apart: 30, of which 17 were waited for; matrix products, arithmetic and copies ran while one was open for 0% of the time, Pallas kernels for 31%

profile of v8, /device:TPU:8, one launch (start us, length us, event | category | flops | bytes accessed | tf_op | source)
XLA Modules:
  0.0 200.0 jit_solution(7752556164997536948)
XLA Ops:
  0.7 2.0 %collective-permute-start.5 = (bf16[3,256,512]{2,1,0:T(8,128)(2,1)}, bf16[3,256,512]{2,1,0:T(8,128)(2,1)S(1)}, u32[]{:S(2)}, u32[]{:S(2)}) collective-permute-start(bf16[3,256,512]{2,1,0:T(8,128)(2,1)} %bitcast.21), channel_id=1, source_target_pairs={{0,32},{32,0},{1,33},{33,1},{2,34},{34,2},{3,35},{35,3},{4,36},{36... | collective-permute-start | bytes 2359304 | tf_op jit(solution)/shard_map/ppermute | solution.py:522
  2.7 0.4 collective-permute-start.4
  3.2 1.6 collective-permute-start.3
  4.8 0.6 stack.23.at_ref
  5.4 5.5 %shard_map.58 = (f32[256,1]{1,0:T(8,128)}, bf16[256,2048]{1,0:T(8,128)(2,1)}, bf16[256,2048]{1,0:T(8,128)(2,1)}, bf16[256,2048]{1,0:T(8,128)(2,1)}, bf16[2,2048,256]{2,1,0:T(8,128)(2,1)}) custom-call(s32[5]{0:T(128)} %stack.23.at_ref, bf16[256,4096]{1,0:T(8,128)(2,1)} %bitcast.28, bf16[256,4096]{1,0:T(8,128)(2,1)} %collective-permute-done.other_ref), custom_call_target="tpu_custom_call" | custom-call | flops 20000000000 | bytes 1 | tf_op jit(solution)/shard_map/pallas_call | solution.py:56
  10.8 2.8 %collective-permute-start.2 = (bf16[2,2048,256]{2,1,0:T(8,128)(2,1)}, bf16[2,2048,256]{2,1,0:T(8,128)(2,1)S(1)}, u32[]{:S(2)}, u32[]{:S(2)}) collective-permute-start(bf16[2,2048,256]{2,1,0:T(8,128)(2,1)} %get-tuple-element.47.refs_3_.refs_0_), channel_id=1, source_target_pairs={{0,12},{4,0},{8,4},{12,8},{1,13},{5,1},{9,5},{13,9},{2,14},{6,2},{... | collective-permute-start | bytes 6291464 | tf_op jit(solution)/shard_map/ppermute | solution.py:522
  13.6 7.4 %collective-permute-done.5.refs_2_ = bf16[3,256,512]{2,1,0:T(8,128)(2,1)S(1)} collective-permute-done((bf16[3,256,512]{2,1,0:T(8,128)(2,1)}, bf16[3,256,512]{2,1,0:T(8,128)(2,1)S(1)}, u32[]{:S(2)}, u32[]{:S(2)}) %collective-permute-start.5) | collective-permute-done | bytes 786464 | tf_op jit(solution)/shard_map/ppermute | solution.py:522
  21.1 1.5 collective-permute-done.4.refs_1_
  22.5 1.6 collective-permute-done.3.refs_0_
  24.1 3.0 %collective-permute-start.8 = (bf16[3,256,512]{2,1,0:T(8,128)(2,1)}, bf16[3,256,512]{2,1,0:T(8,128)(2,1)S(1)}, u32[]{:S(2)}, u32[]{:S(2)}) collective-permute-start(bf16[3,256,512]{2,1,0:T(8,128)(2,1)} %get-tuple-element.52.refs_3_), channel_id=1, source_target_pairs={{0,192},{64,0},{128,64},{192,128},{1,193},{65,1},{129,65},{193,129... | collective-permute-start | bytes 2359304 | tf_op jit(solution)/shard_map/ppermute | solution.py:522
  27.1 0.3 collective-permute-start.7
  27.4 6.3 %shard_map.60 = (f32[256,1536]{1,0:T(8,128)}, f32[256,1536]{1,0:T(8,128)}, bf16[4,3,256,512]{3,2,1,0:T(8,128)(2,1)}) custom-call(s32[5]{0:T(128)} %stack.23.at_ref, bf16[256,2048]{1,0:T(8,128)(2,1)} %get-tuple-element.48.mine_ref, bf16[256,2048]{1,0:T(8,128)(2,1)} %get-tuple-element.50.theirs_ref, bf16[3,256,512]{2,1,0:T(8,128)(2,1)} %bitcast.24, ...), custom_call_target="tpu_custom_call" | custom-call | flops 1 | bytes 1 | tf_op jit(solution)/shard_map/pallas_call | solution.py:106
  33.7 9.7 %collective-permute-done.8.refs_2_ = bf16[3,256,512]{2,1,0:T(8,128)(2,1)S(1)} collective-permute-done((bf16[3,256,512]{2,1,0:T(8,128)(2,1)}, bf16[3,256,512]{2,1,0:T(8,128)(2,1)S(1)}, u32[]{:S(2)}, u32[]{:S(2)}) %collective-permute-start.8) | collective-permute-done | bytes 786464 | tf_op jit(solution)/shard_map/ppermute | solution.py:522
  43.4 2.2 %collective-permute-done.7.refs_1_ = bf16[3,256,512]{2,1,0:T(8,128)(2,1)} collective-permute-done((bf16[3,256,512]{2,1,0:T(8,128)(2,1)}, bf16[3,256,512]{2,1,0:T(8,128)(2,1)}, u32[]{:S(2)}, u32[]{:S(2)}) %collective-permute-start.7) | collective-permute-done | bytes 786464 | tf_op jit(solution)/shard_map/ppermute | solution.py:522
  45.6 0.2 collective-permute-done.6.refs_0_
  45.8 2.0 %shard_map.61 = (bf16[3,256,512]{2,1,0:T(8,128)(2,1)}, bf16[3,256,512]{2,1,0:T(8,128)(2,1)}, bf16[3,256,512]{2,1,0:T(8,128)(2,1)}, bf16[1,256,512]{2,1,0:T(8,128...) custom-call(bf16[3,256,512]{2,1,0:T(8,128)(2,1)} %collective-permute, ...), custom_call_target="tpu_custom_call", output_to_operand_aliasing={{0}: (0, {}), {1}: (1, {}), {2}: (2, {})} | custom-call | flops 1 | bytes 1 | tf_op jit(solution)/shard_map/pallas_call | solution.py:507
  47.8 1.7 collective-permute-start.9
  49.5 0.3 collective-permute-start.10
  49.8 2.4 %collective-permute-start.11 = (bf16[1,256,512]{2,1,0:T(8,128)(2,1)}, bf16[1,256,512]{2,1,0:T(8,128)(2,1)S(1)}, u32[]{:S(2)}, u32[]{:S(2)}) collective-permute-start(bf16[1,256,512]{2,1,0:T(8,128)(2,1)} %get-tuple-element.62), channel_id=1, source_target_pairs={{0,192},{64,0},{128,64},{192,128},{1,193},{65,1},{129,65},{193,129... | collective-permute-start | bytes 786440 | tf_op jit(solution)/shard_map/ppermute | solution.py:522
  52.2 6.1 %shard_map.62 = (f32[256,1536]{1,0:T(8,128)}, bf16[256,1536]{1,0:T(8,128)(2,1)}, bf16[3,3,256,512]{3,2,1,0:T(8,128)(2,1)}) custom-call(s32[5]{0:T(128)} %stack.23.at_ref, bf16[256,2048]{1,0:T(8,128)(2,1)} %get-tuple-element.48.mine_ref, bf16[256,2048]{1,0:T(8,128)(2,1)} %get-tuple-element.50.theirs_ref, bf16[3,256,512]{2,1,0:T(8,128)(2,1)} %get-tuple-element.56.refs_0_, ...), custom_call_target="tpu_custom_call" | custom-call | flops 1 | bytes 1 | tf_op jit(solution)/shard_map/pallas_call | solution.py:106
  58.4 0.7 copy-done.3
  59.3 0.3 collective-permute-start.12
  59.6 0.5 collective-permute-start.13
  60.2 2.3 %collective-permute-done.13.refs_3_ = bf16[1,256,512]{2,1,0:T(8,128)(2,1)S(1)} collective-permute-done((bf16[1,256,512]{2,1,0:T(8,128)(2,1)}, bf16[1,256,512]{2,1,0:T(8,128)(2,1)S(1)}, u32[]{:S(2)}, u32[]{:S(2)}) %collective-permute-start.13) | collective-permute-done | bytes 262176 | tf_op jit(solution)/shard_map/ppermute | solution.py:522
  62.4 0.1 collective-permute-start.15
  62.6 0.2 collective-permute-done.14.refs_4_
  62.8 1.4 collective-permute-done.15.refs_5_
  64.2 0.6 copy-done.11
  64.9 0.3 copy-done.13
  65.1 0.7 copy-done.1
  65.8 6.1 %shard_map.64 = (bf16[4,256,512]{2,1,0:T(8,128)(2,1)}, bf16[1,2048,256]{2,1,0:T(8,128)(2,1)}, bf16[1,2048,256]{2,1,0:T(8,128)(2,1)}, bf16[4,3,256,512]{3,2,1,0:T(8,128)(2,1)}, bf16[3,3,256,512]{3,2,1,0:T(8,128)(2,1)}) custom-call(s32[5]{0:T(128)} %stack.23.at_ref, ...), custom_call_target="tpu_custom_call", output_to_operand_aliasing={{3}: (14, {}), {4}: (15, {})} | custom-call | flops 1 | bytes 1 | tf_op jit(solution)/shard_map/pallas_call | solution.py:151
  71.9 4.2 %all-to-all-start = ((bf16[4,256,512]{2,1,0:T(8,128)(2,1)}), bf16[4,256,512]{2,1,0:T(8,128)(2,1)}, u32[]{:S(2)}, u32[]{:S(2)}) async-start(bf16[4,256,512]{2,1,0:T(8,128)(2,1)} %get-tuple-element.72.p_ref), calls=%async_computation | async-start | bytes 2097152 | tf_op jit(solution)/shard_map/all_to_all | solution.py:565
  76.2 0.2 collective-permute-start.19
  76.4 1.8 collective-permute-start.16
  78.1 1.5 collective-permute-start.17
  79.6 13.1 %all-to-all-done = bf16[4,256,512]{2,1,0:T(8,128)(2,1)} async-done(((bf16[4,256,512]{2,1,0:T(8,128)(2,1)}), bf16[4,256,512]{2,1,0:T(8,128)(2,1)}, u32[]{:S(2)}, u32[]{:S(2)}) %all-to-all-start) | async-done | bytes 1048608 | tf_op jit(solution)/shard_map/all_to_all | solution.py:565
  92.7 8.7 %shard_map.65 = (bf16[1024,128]{1,0:T(8,128)(2,1)}, bf16[1024,384]{1,0:T(8,128)(2,1)}) custom-call(bf16[1024,512]{1,0:T(8,128)(2,1)} %bitcast.8.qkv_ref), custom_call_target="tpu_custom_call" | custom-call | flops 20000000000 | bytes 1 | tf_op jit(solution)/shard_map/pallas_call | solution.py:206
  101.4 4.4 %all-to-all-start.2 = ((bf16[4,256,384]{2,1,0:T(8,128)(2,1)}), bf16[4,256,384]{2,1,0:T(8,128)(2,1)}, u32[]{:S(2)}, u32[]{:S(2)}) async-start(bf16[4,256,384]{2,1,0:T(8,128)(2,1)} %bitcast.19), calls=%async_computation.2 | async-start | bytes 1572864 | tf_op jit(solution)/shard_map/all_to_all | solution.py:576
  105.9 9.0 %collective-permute-done.16.refs_3_ = bf16[1,2048,256]{2,1,0:T(8,128)(2,1)} collective-permute-done((bf16[1,2048,256]{2,1,0:T(8,128)(2,1)}, bf16[1,2048,256]{2,1,0:T(8,128)(2,1)}, u32[]{:S(2)}, u32[]{:S(2)}) %collective-permute-start.16) | collective-permute-done | bytes 1048608 | tf_op jit(solution)/shard_map/ppermute | solution.py:522
  114.9 1.7 copy-done
  116.6 9.3 %shard_map.66 = bf16[2048,384]{1,0:T(8,128)(2,1)} custom-call(s32[5]{0:T(128)} %stack.23.at_ref, bf16[2,2048,256]{2,1,0:T(8,128)(2,1)} %get-tuple-element.47.refs_3_.refs_0_, bf16[2,2048,256]{2,1,0:T(8,128)(2,1)} %collective-permute-done.1.refs_6_.refs_1_, bf16[2,2048,256]{2,1,0:T(8,128)(2,1)} %copy-done.1, ...), custom_call_target="tpu_custom_call" | custom-call | flops 1 | bytes 1 | tf_op jit(solution)/shard_map/pallas_call | solution.py:405
  125.9 6.8 %all-to-all-start.1 = ((bf16[4,512,384]{2,1,0:T(8,128)(2,1)}), bf16[4,512,384]{2,1,0:T(8,128)(2,1)S(1)}, u32[]{:S(2)}, u32[]{:S(2)}) async-start(bf16[4,512,384]{2,1,0:T(8,128)(2,1)} %bitcast.16), calls=%async_computation.1 | async-start | bytes 3145728 | tf_op jit(solution)/shard_map/all_to_all | solution.py:595
  132.7 7.7 %shard_map.67 = (bf16[1040,256]{1,0:T(8,128)(2,1)}, bf16[1024,256]{1,0:T(8,128)(2,1)}, f32[1,256]{1,0:T(1,128)}) custom-call(s32[5]{0:T(128)} %stack.23.at_ref, bf16[4,256,384]{2,1,0:T(8,128)(2,1)} %all-to-all-done.2.g_ref, bf16[4,256,512]{2,1,0:T(8,128)(2,1)} %get-tuple-element.72.p_ref, bf16[1,256,512]{2,1,0:T(8,128)(2,1)} %get-tuple-element.65.refs_0_, ...), custom_call_target="tpu_custom_call" | custom-call | flops 1 | bytes 1 | tf_op jit(solution)/shard_map/pallas_call | solution.py:291
  140.4 3.4 %collective-permute-start.22 = (bf16[1040,256]{1,0:T(8,128)(2,1)}, bf16[1040,256]{1,0:T(8,128)(2,1)S(1)}, u32[]{:S(2)}, u32[]{:S(2)}) collective-permute-start(bf16[1040,256]{1,0:T(8,128)(2,1)} %get-tuple-element.84), channel_id=1, source_target_pairs={{0,1},{1,2},{2,3},{3,0},{4,5},{5,6},{6,7},{7,4},{8,9},{9,10},{10,1... | collective-permute-start | bytes 1597448 | tf_op jit(solution)/shard_map/ppermute | solution.py:522
  143.8 2.2 %collective-permute-start.23 = (bf16[1024,256]{1,0:T(8,128)(2,1)}, bf16[1024,256]{1,0:T(8,128)(2,1)S(1)}, u32[]{:S(2)}, u32[]{:S(2)}) collective-permute-start(bf16[1024,256]{1,0:T(8,128)(2,1)} %get-tuple-element.86), channel_id=1, source_target_pairs={{0,3},{1,0},{2,1},{3,2},{4,7},{5,4},{6,5},{7,6},{8,11},{9,8},{10,9... | collective-permute-start | bytes 1572872 | tf_op jit(solution)/shard_map/ppermute | solution.py:522
  146.0 7.6 %shard_map.68 = (bf16[512,256]{1,0:T(8,128)(2,1)}, bf16[512,256]{1,0:T(8,128)(2,1)}, bf16[512,256]{1,0:T(8,128)(2,1)}, bf16[512,256]{1,0:T(8,128)(2,1)}, f32[1,256]{1,0:T(1,128)}) custom-call(s32[5]{0:T(128)} %stack.23.at_ref, bf16[4,256,384]{2,1,0:T(8,128)(2,1)} %all-to-all-done.2.g_ref, bf16[4,256,512]{2,1,0:T(8,128)(2,1)} %get-tuple-element.72.p_ref, ...), custom_call_target="tpu_custom_call" | custom-call | flops 1 | bytes 1 | tf_op jit(solution)/shard_map/pallas_call | solution.py:291
  153.6 1.1 copy-done.2
  154.8 2.3 %shard_map.69 = (f32[256,384]{1,0:T(8,128)}, bf16[256,384]{1,0:T(8,128)(2,1)}) custom-call(s32[5]{0:T(128)} %stack.23.at_ref, bf16[4,2,256,384]{3,2,1,0:T(8,128)(2,1)} %bitcast.17, bf16[512,256]{1,0:T(8,128)(2,1)} %get-tuple-element.77.refs_0_.own0), custom_call_target="tpu_custom_call" | custom-call | flops 1 | bytes 1 | tf_op jit(solution)/shard_map/pallas_call | solution.py:433
  157.1 1.0 collective-permute-start.21
  158.1 10.5 %collective-permute-done.23.down_in.down0 = bf16[1024,256]{1,0:T(8,128)(2,1)S(1)} collective-permute-done((bf16[1024,256]{1,0:T(8,128)(2,1)}, bf16[1024,256]{1,0:T(8,128)(2,1)S(1)}, u32[]{:S(2)}, u32[]{:S(2)}) %collective-permute-start.23) | collective-permute-done | bytes 524320 | tf_op jit(solution)/shard_map/ppermute | solution.py:522
  168.5 0.9 collective-permute-done.22.up_in.stat_in.up1
  169.5 3.2 %collective-permute-done.21.came_ref.refs_0_ = bf16[256,384]{1,0:T(8,128)(2,1)S(1)} collective-permute-done((bf16[256,384]{1,0:T(8,128)(2,1)}, bf16[256,384]{1,0:T(8,128)(2,1)S(1)}, u32[]{:S(2)}, u32[]{:S(2)}) %collective-permute-start.21) | collective-permute-done | bytes 196640 | tf_op jit(solution)/shard_map/ppermute | solution.py:522
  172.6 0.7 copy-done.14
  173.3 2.2 %shard_map.72 = (bf16[528,256]{1,0:T(8,128)(2,1)}, bf16[528,256]{1,0:T(8,128)(2,1)}) custom-call(bf16[512,256]{1,0:T(8,128)(2,1)} %get-tuple-element.83.up_part, bf16[1040,256]{1,0:T(8,128)(2,1)} %copy-done.12, bf16[1040,256]{1,0:T(8,128)(2,1)} %copy-done.12, bf16[512,256]{1,0:T(8,128)(2,1)} %get-tuple-element.85.down_part, bf16[1024,256]{1,0:T(8,128)(2,1)} %copy-done.15, ...), custom_call_target="tpu_custom_call" | custom-call | flops 1 | bytes 1 | tf_op jit(solution)/shard_map/pallas_call | solution.py:321
  175.6 1.5 collective-permute-start.24
  177.0 2.7 %collective-permute-start.25 = (bf16[528,256]{1,0:T(8,128)(2,1)}, bf16[528,256]{1,0:T(8,128)(2,1)S(1)}, u32[]{:S(2)}, u32[]{:S(2)}) collective-permute-start(bf16[528,256]{1,0:T(8,128)(2,1)} %get-tuple-element.88), channel_id=1, source_target_pairs={{0,3},{1,0},{2,1},{3,2},{4,7},{5,4},{6,5},{7,6},{8,11},{9,8},{10,9... | collective-permute-start | bytes 811016 | tf_op jit(solution)/shard_map/ppermute | solution.py:522
  179.7 2.2 %shard_map.70 = bf16[4,256,512]{2,1,0:T(8,128)(2,1)} custom-call(f32[256,384]{1,0:T(8,128)} %get-tuple-element.78.keep_ref, bf16[256,384]{1,0:T(8,128)(2,1)} %copy-done.14, bf16[4,256,128]{2,1,0:T(8,128)(2,1)} %bitcast.26), custom_call_target="tpu_custom_call" | custom-call | flops 1 | bytes 1 | tf_op jit(solution)/shard_map/pallas_call | solution.py:457
  181.9 3.5 %all-to-all-start.3 = ((bf16[4,256,512]{2,1,0:T(8,128)(2,1)}), bf16[4,256,512]{2,1,0:T(8,128)(2,1)S(1)}, u32[]{:S(2)}, u32[]{:S(2)}) async-start(bf16[4,256,512]{2,1,0:T(8,128)(2,1)} %shard_map.70), calls=%async_computation.3 | async-start | bytes 2097152 | tf_op jit(solution)/shard_map/all_to_all | solution.py:601
  185.5 3.8 %collective-permute-done.24.up0 = bf16[528,256]{1,0:T(8,128)(2,1)S(1)} collective-permute-done((bf16[528,256]{1,0:T(8,128)(2,1)}, bf16[528,256]{1,0:T(8,128)(2,1)S(1)}, u32[]{:S(2)}, u32[]{:S(2)}) %collective-permute-start.24) | collective-permute-done | bytes 270368 | tf_op jit(solution)/shard_map/ppermute | solution.py:522
  189.2 1.0 collective-permute-done.25.down1
  190.2 0.7 copy-done.17
  190.9 3.5 %shard_map.73 = bf16[256,1024]{1,0:T(8,128)(2,1)} custom-call(s32[5]{0:T(128)} %stack.23.at_ref, bf16[512,256]{1,0:T(8,128)(2,1)} %get-tuple-element.77.refs_0_.own0, bf16[512,256]{1,0:T(8,128)(2,1)} %get-tuple-element.82.own1, bf16[528,256]{1,0:T(8,128)(2,1)} %copy-done.16, bf16[1040,256]{1,0:T(8,128)(2,1)} %copy-done.12, bf16[1024,256]{1,0:T(8,128)(2,1)} %copy-done.15, ...), custom_call_target="tpu_custom_call" | custom-call | flops 20000000000 | bytes 1 | tf_op jit(solution)/shard_map/pallas_call | solution.py:355
  194.4 3.7 %all-to-all-done.3.in_ref = bf16[4,256,512]{2,1,0:T(8,128)(2,1)S(1)} async-done(((bf16[4,256,512]{2,1,0:T(8,128)(2,1)}), bf16[4,256,512]{2,1,0:T(8,128)(2,1)S(1)}, u32[]{:S(2)}, u32[]{:S(2)}) %all-to-all-start.3) | async-done | bytes 1048608 | tf_op jit(solution)/shard_map/all_to_all | solution.py:601
  198.1 1.9 shard_map.71
  (49 shorter events, 0.5 us)
Async XLA Ops:
  0.6 4.8 %collective-permute-start = (bf16[256,4096]{1,0:T(8,128)(2,1)}, bf16[256,4096]{1,0:T(8,128)(2,1)}, u32[]{:S(2)}, u32[]{:S(2)}) collective-permute-start(bf16[256,4096]{1,0:T(8,128)(2,1)} %bitcast.27), channel_id=1, source_target_pairs={{0,16},{16,0},{1,17},{17,1},{2,18},{18,2},{3,19},{19,3},{4,20},{20... | collective-permute-start | bytes 6291464 | tf_op jit(solution)/shard_map/ppermute | solution.py:522
  0.7 20.3 %collective-permute-start.5 = (bf16[3,256,512]{2,1,0:T(8,128)(2,1)}, bf16[3,256,512]{2,1,0:T(8,128)(2,1)S(1)}, u32[]{:S(2)}, u32[]{:S(2)}) collective-permute-start(bf16[3,256,512]{2,1,0:T(8,128)(2,1)} %bitcast.21), channel_id=1, source_target_pairs={{0,32},{32,0},{1,33},{33,1},{2,34},{34,2},{3,35},{35,3},{4,36},{36... | collective-permute-start | bytes 2359304 | tf_op jit(solution)/shard_map/ppermute | solution.py:522
  2.7 19.8 %collective-permute-start.4 = (bf16[3,256,512]{2,1,0:T(8,128)(2,1)}, bf16[3,256,512]{2,1,0:T(8,128)(2,1)S(1)}, u32[]{:S(2)}, u32[]{:S(2)}) collective-permute-start(bf16[3,256,512]{2,1,0:T(8,128)(2,1)} %bitcast.22), channel_id=1, source_target_pairs={{0,192},{64,0},{128,64},{192,128},{1,193},{65,1},{129,65},{193,129... | collective-permute-start | bytes 2359304 | tf_op jit(solution)/shard_map/ppermute | solution.py:522
  3.2 20.9 %collective-permute-start.3 = (bf16[3,256,512]{2,1,0:T(8,128)(2,1)}, bf16[3,256,512]{2,1,0:T(8,128)(2,1)}, u32[]{:S(2)}, u32[]{:S(2)}) collective-permute-start(bf16[3,256,512]{2,1,0:T(8,128)(2,1)} %bitcast.23), channel_id=1, source_target_pairs={{0,64},{64,128},{128,192},{192,0},{1,65},{65,129},{129,193},{193,1... | collective-permute-start | bytes 2359304 | tf_op jit(solution)/shard_map/ppermute | solution.py:522
  10.8 53.3 %collective-permute-start.2 = (bf16[2,2048,256]{2,1,0:T(8,128)(2,1)}, bf16[2,2048,256]{2,1,0:T(8,128)(2,1)S(1)}, u32[]{:S(2)}, u32[]{:S(2)}) collective-permute-start(bf16[2,2048,256]{2,1,0:T(8,128)(2,1)} %get-tuple-element.47.refs_3_.refs_0_), channel_id=1, source_target_pairs={{0,12},{4,0},{8,4},{12,8},{1,13},{5,1},{9,5},{13,9},{2,14},{6,2},{... | collective-permute-start | bytes 6291464 | tf_op jit(solution)/shard_map/ppermute | solution.py:522
  13.6 50.6 %collective-permute-start.1 = (bf16[2,2048,256]{2,1,0:T(8,128)(2,1)}, bf16[2,2048,256]{2,1,0:T(8,128)(2,1)}, u32[]{:S(2)}, u32[]{:S(2)}) collective-permute-start(bf16[2,2048,256]{2,1,0:T(8,128)(2,1)} %get-tuple-element.47.refs_3_.refs_0_), channel_id=1, source_target_pairs={{0,4},{4,8},{8,12},{12,0},{1,5},{5,9},{9,13},{13,1},{2,6},{6,10},{... | collective-permute-start | bytes 6291464 | tf_op jit(solution)/shard_map/ppermute | solution.py:522
  21.1 3.1 %copy-start.7 = (bf16[3,256,512]{2,1,0:T(8,128)(2,1)}, bf16[3,256,512]{2,1,0:T(8,128)(2,1)S(1)}, u32[]{:S(2)}) copy-start(bf16[3,256,512]{2,1,0:T(8,128)(2,1)S(1)} %collective-permute-done.5.refs_2_) | copy-start | bytes 2359300
  22.5 1.6 copy-start.8
  24.1 19.3 %collective-permute-start.8 = (bf16[3,256,512]{2,1,0:T(8,128)(2,1)}, bf16[3,256,512]{2,1,0:T(8,128)(2,1)S(1)}, u32[]{:S(2)}, u32[]{:S(2)}) collective-permute-start(bf16[3,256,512]{2,1,0:T(8,128)(2,1)} %get-tuple-element.52.refs_3_), channel_id=1, source_target_pairs={{0,192},{64,0},{128,64},{192,128},{1,193},{65,1},{129,65},{193,129... | collective-permute-start | bytes 2359304 | tf_op jit(solution)/shard_map/ppermute | solution.py:522
  27.1 18.5 %collective-permute-start.7 = (bf16[3,256,512]{2,1,0:T(8,128)(2,1)}, bf16[3,256,512]{2,1,0:T(8,128)(2,1)}, u32[]{:S(2)}, u32[]{:S(2)}) collective-permute-start(bf16[3,256,512]{2,1,0:T(8,128)(2,1)} %get-tuple-element.51.refs_1_), channel_id=1, source_target_pairs={{0,32},{32,0},{1,33},{33,1},{2,34},{34,2},{3,35},{35,3},{4,36},{36... | collective-permute-start | bytes 2359304 | tf_op jit(solution)/shard_map/ppermute | solution.py:522
  27.4 18.4 %collective-permute-start.6 = (bf16[3,256,512]{2,1,0:T(8,128)(2,1)}, bf16[3,256,512]{2,1,0:T(8,128)(2,1)}, u32[]{:S(2)}, u32[]{:S(2)}) collective-permute-start(bf16[3,256,512]{2,1,0:T(8,128)(2,1)} %get-tuple-element.51.refs_1_), channel_id=1, source_target_pairs={{0,64},{64,128},{128,192},{192,0},{1,65},{65,129},{129,193},{193,1... | collective-permute-start | bytes 2359304 | tf_op jit(solution)/shard_map/ppermute | solution.py:522
  43.4 2.4 %copy-start.6 = (bf16[3,256,512]{2,1,0:T(8,128)(2,1)}, bf16[3,256,512]{2,1,0:T(8,128)(2,1)S(1)}, u32[]{:S(2)}) copy-start(bf16[3,256,512]{2,1,0:T(8,128)(2,1)S(1)} %collective-permute-done.8.refs_2_) | copy-start | bytes 2359300
  47.8 10.5 %collective-permute-start.9 = (bf16[1,256,512]{2,1,0:T(8,128)(2,1)}, bf16[1,256,512]{2,1,0:T(8,128)(2,1)S(1)}, u32[]{:S(2)}, u32[]{:S(2)}) collective-permute-start(bf16[1,256,512]{2,1,0:T(8,128)(2,1)} %get-tuple-element.60), channel_id=1, source_target_pairs={{0,32},{32,0},{1,33},{33,1},{2,34},{34,2},{3,35},{35,3},{4,36},{36... | collective-permute-start | bytes 786440 | tf_op jit(solution)/shard_map/ppermute | solution.py:522
  49.5 8.9 %collective-permute-start.10 = (bf16[1,256,512]{2,1,0:T(8,128)(2,1)}, bf16[1,256,512]{2,1,0:T(8,128)(2,1)S(1)}, u32[]{:S(2)}, u32[]{:S(2)}) collective-permute-start(bf16[1,256,512]{2,1,0:T(8,128)(2,1)} %get-tuple-element.61), channel_id=1, source_target_pairs={{0,64},{64,128},{128,192},{192,0},{1,65},{65,129},{129,193},{193,1... | collective-permute-start | bytes 786440 | tf_op jit(solution)/shard_map/ppermute | solution.py:522
  49.8 8.6 %collective-permute-start.11 = (bf16[1,256,512]{2,1,0:T(8,128)(2,1)}, bf16[1,256,512]{2,1,0:T(8,128)(2,1)S(1)}, u32[]{:S(2)}, u32[]{:S(2)}) collective-permute-start(bf16[1,256,512]{2,1,0:T(8,128)(2,1)} %get-tuple-element.62), channel_id=1, source_target_pairs={{0,192},{64,0},{128,64},{192,128},{1,193},{65,1},{129,65},{193,129... | collective-permute-start | bytes 786440 | tf_op jit(solution)/shard_map/ppermute | solution.py:522
  58.4 0.7 copy-start.3
  58.4 0.8 copy-start.4
  58.4 0.9 copy-start.5
  59.3 4.9 %collective-permute-start.12 = (bf16[256,1536]{1,0:T(8,128)(2,1)}, bf16[256,1536]{1,0:T(8,128)(2,1)S(1)}, u32[]{:S(2)}, u32[]{:S(2)}) collective-permute-start(bf16[256,1536]{1,0:T(8,128)(2,1)} %get-tuple-element.64), channel_id=1, source_target_pairs={{0,16},{16,0},{1,17},{17,1},{2,18},{18,2},{3,19},{19,3},{4,20},{20... | collective-permute-start | bytes 2359304 | tf_op jit(solution)/shard_map/ppermute | solution.py:522
  59.6 2.9 %collective-permute-start.13 = (bf16[1,256,512]{2,1,0:T(8,128)(2,1)}, bf16[1,256,512]{2,1,0:T(8,128)(2,1)S(1)}, u32[]{:S(2)}, u32[]{:S(2)}) collective-permute-start(bf16[1,256,512]{2,1,0:T(8,128)(2,1)} %get-tuple-element.65.refs_0_), channel_id=1, source_target_pairs={{0,16},{16,0},{1,17},{17,1},{2,18},{18,2},{3,19},{19,3},{4,20},{20... | collective-permute-start | bytes 786440 | tf_op jit(solution)/shard_map/ppermute | solution.py:522
  60.1 2.7 %collective-permute-start.14 = (bf16[1,256,512]{2,1,0:T(8,128)(2,1)}, bf16[1,256,512]{2,1,0:T(8,128)(2,1)S(1)}, u32[]{:S(2)}, u32[]{:S(2)}) collective-permute-start(bf16[1,256,512]{2,1,0:T(8,128)(2,1)} %get-tuple-element.66.refs_1_), channel_id=1, source_target_pairs={{0,16},{16,0},{1,17},{17,1},{2,18},{18,2},{3,19},{19,3},{4,20},{20... | collective-permute-start | bytes 786440 | tf_op jit(solution)/shard_map/ppermute | solution.py:522
  62.4 1.8 copy-start.9
  62.4 1.7 collective-permute-start.15
  62.8 1.4 copy-start.10
  64.2 0.7 copy-start.11
  64.2 1.0 copy-start.13
  64.2 1.6 copy-start.1
  71.9 20.8 %all-to-all-start = ((bf16[4,256,512]{2,1,0:T(8,128)(2,1)}), bf16[4,256,512]{2,1,0:T(8,128)(2,1)}, u32[]{:S(2)}, u32[]{:S(2)}) async-start(bf16[4,256,512]{2,1,0:T(8,128)(2,1)} %get-tuple-element.72.p_ref), calls=%async_computation | async-start | bytes 2097152 | tf_op jit(solution)/shard_map/all_to_all | solution.py:565
  76.2 38.7 %collective-permute-start.19 = (bf16[4,3,256,512]{3,2,1,0:T(8,128)(2,1)}, bf16[4,3,256,512]{3,2,1,0:T(8,128)(2,1)S(1)}, u32[]{:S(2)}, u32[]{:S(2)}) collective-permute-start(bf16[4,3,256,512]{3,2,1,0:T(8,128)(2,1)} %get-tuple-element.74.refs_6_), channel_id=1, source_target_pairs={{0,16},{16,0},{1,17},{17,1},{2,18},{18,2},{3,19},{19,3},{4,20},{20... | collective-permute-start | bytes 9437192 | tf_op jit(solution)/shard_map/ppermute | solution.py:522
  76.4 38.5 %collective-permute-start.16 = (bf16[1,2048,256]{2,1,0:T(8,128)(2,1)}, bf16[1,2048,256]{2,1,0:T(8,128)(2,1)}, u32[]{:S(2)}, u32[]{:S(2)}) collective-permute-start(bf16[1,2048,256]{2,1,0:T(8,128)(2,1)} %get-tuple-element.70), channel_id=1, source_target_pairs={{0,4},{4,8},{8,12},{12,0},{1,5},{5,9},{9,13},{13,1},{2,6},{6,10},{... | collective-permute-start | bytes 3145736 | tf_op jit(solution)/shard_map/ppermute | solution.py:522
  78.1 36.7 %collective-permute-start.17 = (bf16[1,2048,256]{2,1,0:T(8,128)(2,1)}, bf16[1,2048,256]{2,1,0:T(8,128)(2,1)}, u32[]{:S(2)}, u32[]{:S(2)}) collective-permute-start(bf16[1,2048,256]{2,1,0:T(8,128)(2,1)} %get-tuple-element.71), channel_id=1, source_target_pairs={{0,12},{4,0},{8,4},{12,8},{1,13},{5,1},{9,5},{13,9},{2,14},{6,2},{... | collective-permute-start | bytes 3145736 | tf_op jit(solution)/shard_map/ppermute | solution.py:522
  79.6 35.2 %collective-permute-start.20 = (bf16[3,3,256,512]{3,2,1,0:T(8,128)(2,1)}, bf16[3,3,256,512]{3,2,1,0:T(8,128)(2,1)}, u32[]{:S(2)}, u32[]{:S(2)}) collective-permute-start(bf16[3,3,256,512]{3,2,1,0:T(8,128)(2,1)} %get-tuple-element.75.refs_8_), channel_id=1, source_target_pairs={{0,16},{16,0},{1,17},{17,1},{2,18},{18,2},{3,19},{19,3},{4,20},{20... | collective-permute-start | bytes 7077896 | tf_op jit(solution)/shard_map/ppermute | solution.py:522
  101.4 13.5 %collective-permute-start.18 = (bf16[4,256,384]{2,1,0:T(8,128)(2,1)}, bf16[4,256,384]{2,1,0:T(8,128)(2,1)}, u32[]{:S(2)}, u32[]{:S(2)}) collective-permute-start(bf16[4,256,384]{2,1,0:T(8,128)(2,1)} %bitcast.18), channel_id=1, source_target_pairs={{0,16},{16,0},{1,17},{17,1},{2,18},{18,2},{3,19},{19,3},{4,20},{20... | collective-permute-start | bytes 2359304 | tf_op jit(solution)/shard_map/ppermute | solution.py:522
  101.4 24.5 %all-to-all-start.2 = ((bf16[4,256,384]{2,1,0:T(8,128)(2,1)}), bf16[4,256,384]{2,1,0:T(8,128)(2,1)}, u32[]{:S(2)}, u32[]{:S(2)}) async-start(bf16[4,256,384]{2,1,0:T(8,128)(2,1)} %bitcast.19), calls=%async_computation.2 | async-start | bytes 1572864 | tf_op jit(solution)/shard_map/all_to_all | solution.py:576
  114.9 1.7 copy-start
  125.9 27.7 %all-to-all-start.1 = ((bf16[4,512,384]{2,1,0:T(8,128)(2,1)}), bf16[4,512,384]{2,1,0:T(8,128)(2,1)S(1)}, u32[]{:S(2)}, u32[]{:S(2)}) async-start(bf16[4,512,384]{2,1,0:T(8,128)(2,1)} %bitcast.16), calls=%async_computation.1 | async-start | bytes 3145728 | tf_op jit(solution)/shard_map/all_to_all | solution.py:595
  140.4 29.0 %collective-permute-start.22 = (bf16[1040,256]{1,0:T(8,128)(2,1)}, bf16[1040,256]{1,0:T(8,128)(2,1)S(1)}, u32[]{:S(2)}, u32[]{:S(2)}) collective-permute-start(bf16[1040,256]{1,0:T(8,128)(2,1)} %get-tuple-element.84), channel_id=1, source_target_pairs={{0,1},{1,2},{2,3},{3,0},{4,5},{5,6},{6,7},{7,4},{8,9},{9,10},{10,1... | collective-permute-start | bytes 1597448 | tf_op jit(solution)/shard_map/ppermute | solution.py:522
  143.8 24.7 %collective-permute-start.23 = (bf16[1024,256]{1,0:T(8,128)(2,1)}, bf16[1024,256]{1,0:T(8,128)(2,1)S(1)}, u32[]{:S(2)}, u32[]{:S(2)}) collective-permute-start(bf16[1024,256]{1,0:T(8,128)(2,1)} %get-tuple-element.86), channel_id=1, source_target_pairs={{0,3},{1,0},{2,1},{3,2},{4,7},{5,4},{6,5},{7,6},{8,11},{9,8},{10,9... | collective-permute-start | bytes 1572872 | tf_op jit(solution)/shard_map/ppermute | solution.py:522
  153.6 1.1 copy-start.2
  157.1 15.6 %collective-permute-start.21 = (bf16[256,384]{1,0:T(8,128)(2,1)}, bf16[256,384]{1,0:T(8,128)(2,1)S(1)}, u32[]{:S(2)}, u32[]{:S(2)}) collective-permute-start(bf16[256,384]{1,0:T(8,128)(2,1)} %get-tuple-element.79), channel_id=1, source_target_pairs={{0,32},{32,0},{1,33},{33,1},{2,34},{34,2},{3,35},{35,3},{4,36},{36... | collective-permute-start | bytes 589832 | tf_op jit(solution)/shard_map/ppermute | solution.py:522
  168.5 4.1 %copy-start.15 = (bf16[1024,256]{1,0:T(8,128)(2,1)}, bf16[1024,256]{1,0:T(8,128)(2,1)S(1)}, u32[]{:S(2)}) copy-start(bf16[1024,256]{1,0:T(8,128)(2,1)S(1)} %collective-permute-done.23.down_in.down0) | copy-start | bytes 1572868
  169.5 3.2 %copy-start.12 = (bf16[1040,256]{1,0:T(8,128)(2,1)}, bf16[1040,256]{1,0:T(8,128)(2,1)S(1)}, u32[]{:S(2)}) copy-start(bf16[1040,256]{1,0:T(8,128)(2,1)S(1)} %collective-permute-done.22.up_in.stat_in.up1) | copy-start | bytes 1597444
  172.6 0.7 copy-start.14
  175.6 13.7 %collective-permute-start.24 = (bf16[528,256]{1,0:T(8,128)(2,1)}, bf16[528,256]{1,0:T(8,128)(2,1)S(1)}, u32[]{:S(2)}, u32[]{:S(2)}) collective-permute-start(bf16[528,256]{1,0:T(8,128)(2,1)} %get-tuple-element.87), channel_id=1, source_target_pairs={{0,1},{1,2},{2,3},{3,0},{4,5},{5,6},{6,7},{7,4},{8,9},{9,10},{10,1... | collective-permute-start | bytes 811016 | tf_op jit(solution)/shard_map/ppermute | solution.py:522
  177.0 13.2 %collective-permute-start.25 = (bf16[528,256]{1,0:T(8,128)(2,1)}, bf16[528,256]{1,0:T(8,128)(2,1)S(1)}, u32[]{:S(2)}, u32[]{:S(2)}) collective-permute-start(bf16[528,256]{1,0:T(8,128)(2,1)} %get-tuple-element.88), channel_id=1, source_target_pairs={{0,3},{1,0},{2,1},{3,2},{4,7},{5,4},{6,5},{7,6},{8,11},{9,8},{10,9... | collective-permute-start | bytes 811016 | tf_op jit(solution)/shard_map/ppermute | solution.py:522
  181.9 16.2 %all-to-all-start.3 = ((bf16[4,256,512]{2,1,0:T(8,128)(2,1)}), bf16[4,256,512]{2,1,0:T(8,128)(2,1)S(1)}, u32[]{:S(2)}, u32[]{:S(2)}) async-start(bf16[4,256,512]{2,1,0:T(8,128)(2,1)} %shard_map.70), calls=%async_computation.3 | async-start | bytes 2097152 | tf_op jit(solution)/shard_map/all_to_all | solution.py:601
  189.2 1.0 copy-start.16
  190.2 0.7 copy-start.17
